TPU v7x, 32 devices: a whole 2x2x4 slice. The times are simulated.
32 devices in a mesh: dp: 8 (over z, y), ctx: 4 (over x, core).
Axes of the slice: x: 2, y: 2, z: 4, core: 2. Of those that a mesh axis runs over, the one named last changes fastest.
Arguments:
- tokens: bfloat16 [8192, 2048], P(('dp', 'ctx')), may hold values from -6 to 6
- segments: int32 [8192], P(('dp', 'ctx')), may hold values from 0 to 2, as said below
- positions: int32 [8192], P(('dp', 'ctx')), may hold values from 0 to 1023, as said below
- out_grad: bfloat16 [8192, 2048], P(('dp', 'ctx')), may hold values from -6 to 6
- ln1_gain: bfloat16 [2048], P(('dp', 'ctx')), may hold values from 0.5 to 1.5
- ln1_bias: bfloat16 [2048], P(('dp', 'ctx')), may hold values from -1 to 1
- qkv_weight: bfloat16 [2048, 6144], P(('dp', 'ctx')), may hold values from -0.125 to 0.125
- qkv_bias: bfloat16 [2048, 3], P(('dp', 'ctx')), may hold values from -1.5 to 1.5
- o_weight: bfloat16 [2048, 2048], P(('dp', 'ctx')), may hold values from -0.5 to 0.5
- ln2_gain: bfloat16 [2048], P(('dp', 'ctx')), may hold values from 0.5 to 1.5
- ln2_bias: bfloat16 [2048], P(('dp', 'ctx')), may hold values from -1 to 1
- gate_weight: bfloat16 [2048, 5632], P(('dp', 'ctx')), may hold values from -0.125 to 0.125
- up_weight: bfloat16 [2048, 5632], P(('dp', 'ctx')), may hold values from -0.125 to 0.125
- down_weight: bfloat16 [2048, 5632], P(('dp', 'ctx')), may hold values from -0.078125 to 0.078125
Outputs:
- output: bfloat16 [8192, 2048], P(('dp', 'ctx'))
- input_grad: bfloat16 [8192, 2048], P(('dp', 'ctx'))
- ln1_gain_grad: float32 [2048], P(('dp', 'ctx'))
- ln1_bias_grad: float32 [2048], P(('dp', 'ctx'))
- qkv_weight_grad: float32 [2048, 6144], P(('dp', 'ctx'))
- qkv_bias_grad: float32 [2048, 3], P(('dp', 'ctx'))
- o_weight_grad: float32 [2048, 2048], P(('dp', 'ctx'))
- ln2_gain_grad: float32 [2048], P(('dp', 'ctx'))
- ln2_bias_grad: float32 [2048], P(('dp', 'ctx'))
- gate_weight_grad: float32 [2048, 5632], P(('dp', 'ctx'))
- up_weight_grad: float32 [2048, 5632], P(('dp', 'ctx'))
- down_weight_grad: float32 [2048, 5632], P(('dp', 'ctx'))
Inputs may be any that keep to these rules, and one draw needn't show every extreme that they name: `segments`: within each pack of 1024 consecutive tokens the numbers never fall, and the first token of a pack has number 0. Within a run of equal segment numbers inside a pack, positions rise by one from token to token; the first token of every pack has position 0.
All inputs are finite; a program needn't handle non-finite values.
Results may differ from a plain program's by a relative error of at most 0.014.
Values may be sent and summed in bfloat16 or wider, within the bound.
No kernel may reach another device: no remote copies, remote signals or barrier semaphores. Data moves between devices by JAX's collectives and lax.ppermute only.
A program may use at most 832 MiB of HBM per device.

v0:
```python
import math

import jax
import jax.numpy as jnp
from jax import lax
from jax.sharding import PartitionSpec as P

HEAD_DIM = 64
ROT_DIMS = 16


epsilon = 1e-05
neg_large = -1e30
rope_base = 10000.0
score_scale = 0.125


def layer_stats(values):
    mean_value = jnp.mean(values, axis=-1, keepdims=True)
    centered = values - mean_value
    inv_std = lax.rsqrt(jnp.mean(centered * centered, axis=-1, keepdims=True) + epsilon)
    return (centered * inv_std, inv_std)


def norm_back(grad_rows, normed, inv_std, gain_row):
    scaled = grad_rows * gain_row
    inner = jnp.mean(scaled * normed, axis=-1, keepdims=True)
    return inv_std * (scaled - jnp.mean(scaled, axis=-1, keepdims=True) - normed * inner)


def angles(position_ids):
    frequency = rope_base ** (-jnp.arange(0, ROT_DIMS, 2, dtype=jnp.float32) / ROT_DIMS)
    phases = position_ids.astype(jnp.float32)[:, None] * frequency[None, :]
    phases = jnp.concatenate([phases, phases], axis=1)
    return (jnp.cos(phases)[:, None, :], jnp.sin(phases)[:, None, :])


def half_turn(leading):
    middle = leading.shape[-1] // 2
    return jnp.concatenate([-leading[..., middle:], leading[..., :middle]], axis=-1)


def rotate(head_rows, cosine, sine_rows, direction):
    leading = head_rows[..., :ROT_DIMS]
    turned = leading * cosine + direction * half_turn(leading) * sine_rows
    return jnp.concatenate([turned, head_rows[..., ROT_DIMS:]], axis=-1)


def contract_rows(left_part, right_part):
    return lax.dot_general(
        left_part, right_part, (((0,), (0,)), ((), ())), preferred_element_type=jnp.float32
    )


def contract_cols(left_part, right_part):
    return lax.dot_general(
        left_part, right_part, (((1,), (1,)), ((), ())), preferred_element_type=jnp.float32
    )


def head_groups(flat_rows, group_size):
    grouped = flat_rows.reshape(flat_rows.shape[0], -1, group_size, HEAD_DIM)
    return jnp.transpose(grouped, (1, 0, 2, 3))


def merge_groups(grouped):
    return jnp.transpose(grouped, (1, 0, 2, 3)).reshape(grouped.shape[1], -1)


def local(
    tokens,
    segments,
    positions,
    out_grad,
    ln1_gain,
    ln1_bias,
    qkv_weight,
    qkv_bias,
    o_weight,
    ln2_gain,
    ln2_bias,
    gate_weight,
    up_weight,
    down_weight,
):
    row_count = tokens.shape[0]
    model_width = tokens.shape[1]
    ffn_width = gate_weight.shape[1]
    head_count = model_width // HEAD_DIM
    group_size = math.gcd(head_count, 8)
    ctx_index = lax.axis_index("ctx")
    ctx_count = lax.axis_size("ctx")
    seq_len = row_count * ctx_count
    qkv_full, out_full, gain_one, shift_one, bias_full = (
        lax.all_gather(qkv_weight, ("dp", "ctx"), axis=0, tiled=True),
        lax.all_gather(o_weight, ("dp", "ctx"), axis=0, tiled=True),
        lax.all_gather(ln1_gain, ("dp", "ctx"), axis=0, tiled=True),
        lax.all_gather(ln1_bias, ("dp", "ctx"), axis=0, tiled=True),
        lax.all_gather(qkv_bias, ("dp", "ctx"), axis=0, tiled=True),
    )
    inputs = tokens.astype(jnp.float32)
    normed_one, inv_one = layer_stats(inputs)
    act_one = (normed_one * gain_one.astype(jnp.float32) + shift_one.astype(jnp.float32)).astype(
        jnp.bfloat16
    )
    bias_flat = jnp.transpose(bias_full.astype(jnp.float32)).reshape(-1)
    projected = jnp.dot(act_one, qkv_full, preferred_element_type=jnp.float32) + bias_flat
    cosine, sine_rows = angles(positions)
    query_heads = projected[:, :model_width].reshape(row_count, head_count, HEAD_DIM)
    key_heads = projected[:, model_width : 2 * model_width].reshape(row_count, head_count, HEAD_DIM)
    query_low = (
        rotate(query_heads, cosine, sine_rows, 1.0)
        .astype(jnp.bfloat16)
        .reshape(row_count, model_width)
    )
    key_low = (
        rotate(key_heads, cosine, sine_rows, 1.0)
        .astype(jnp.bfloat16)
        .reshape(row_count, model_width)
    )
    value_low = projected[:, 2 * model_width :].astype(jnp.bfloat16)
    segment_low = segments.astype(jnp.bfloat16)
    key_all, value_all, segment_all = (
        lax.all_gather(key_low, "ctx", axis=0, tiled=True),
        lax.all_gather(value_low, "ctx", axis=0, tiled=True),
        lax.all_gather(segment_low, "ctx", axis=0, tiled=True),
    )
    query_index = ctx_index * row_count + jnp.arange(row_count, dtype=jnp.int32)
    key_index = jnp.arange(seq_len, dtype=jnp.int32)
    allowed = (key_index[None, :] <= query_index[:, None]) & (
        segment_all[None, :] == segment_low[:, None]
    )

    def masked_scores(query_block, key_block):
        scores = (
            jnp.einsum("qhd,khd->hqk", query_block, key_block, preferred_element_type=jnp.float32)
            * score_scale
        )
        return jnp.where(allowed[None], scores, neg_large)

    def attend(group_block):
        query_block, key_block, value_block = group_block
        scores = masked_scores(query_block, key_block)
        row_max = jnp.max(scores, axis=-1, keepdims=True)
        weights = jnp.exp(scores - row_max)
        totals = jnp.sum(weights, axis=-1, keepdims=True)
        attn_probs = (weights / totals).astype(jnp.bfloat16)
        mixed_out = jnp.einsum(
            "hqk,khd->qhd", attn_probs, value_block, preferred_element_type=jnp.float32
        )
        return (mixed_out, (row_max + jnp.log(totals))[..., 0])

    query_groups = head_groups(query_low, group_size)
    mixed_groups, log_totals = lax.map(
        attend, (query_groups, head_groups(key_all, group_size), head_groups(value_all, group_size))
    )
    mixed_low = merge_groups(mixed_groups).astype(jnp.bfloat16)
    hidden = inputs + jnp.dot(mixed_low, out_full, preferred_element_type=jnp.float32)
    gate_full, up_full, down_full, gain_two, shift_two = (
        lax.all_gather(gate_weight, ("dp", "ctx"), axis=0, tiled=True),
        lax.all_gather(up_weight, ("dp", "ctx"), axis=0, tiled=True),
        lax.all_gather(down_weight, ("dp", "ctx"), axis=0, tiled=True),
        lax.all_gather(ln2_gain, ("dp", "ctx"), axis=0, tiled=True),
        lax.all_gather(ln2_bias, ("dp", "ctx"), axis=0, tiled=True),
    )
    normed_two, inv_two = layer_stats(hidden)
    act_two = (normed_two * gain_two.astype(jnp.float32) + shift_two.astype(jnp.float32)).astype(
        jnp.bfloat16
    )
    gate_value = jnp.dot(act_two, gate_full, preferred_element_type=jnp.float32)
    up_value = jnp.dot(act_two, up_full, preferred_element_type=jnp.float32)
    gate_sigmoid = jax.nn.sigmoid(gate_value)
    gate_silu = gate_value * gate_sigmoid
    middle_low = (gate_silu * up_value).astype(jnp.bfloat16)
    output = (hidden + contract_cols(middle_low, down_full)).astype(jnp.bfloat16)
    gate_back, up_back, down_back, gain_back = (
        lax.all_gather(gate_weight, ("dp", "ctx"), axis=0, tiled=True),
        lax.all_gather(up_weight, ("dp", "ctx"), axis=0, tiled=True),
        lax.all_gather(down_weight, ("dp", "ctx"), axis=0, tiled=True),
        lax.all_gather(ln2_gain, ("dp", "ctx"), axis=0, tiled=True),
    )
    cotangent = out_grad.astype(jnp.float32)
    middle_grad = jnp.dot(out_grad, down_back, preferred_element_type=jnp.float32)
    gate_grad = (
        middle_grad * up_value * (gate_sigmoid * (1.0 + gate_value * (1.0 - gate_sigmoid)))
    ).astype(jnp.bfloat16)
    up_grad = (middle_grad * gate_silu).astype(jnp.bfloat16)
    norm_grad_two = contract_cols(gate_grad, gate_back) + contract_cols(up_grad, up_back)
    hidden_grad = cotangent + norm_back(
        norm_grad_two, normed_two, inv_two, gain_back.astype(jnp.float32)
    )
    hidden_low = hidden_grad.astype(jnp.bfloat16)
    gate_up_grad = jnp.concatenate([gate_grad, up_grad], axis=1)
    ffn_share = lax.psum_scatter(
        jnp.concatenate(
            [contract_rows(act_two, gate_up_grad), contract_rows(out_grad, middle_low)], axis=1
        ),
        ("dp", "ctx"),
        scatter_dimension=0,
        tiled=True,
    )
    qkv_back, out_back, gain_first = (
        lax.all_gather(qkv_weight, ("dp", "ctx"), axis=0, tiled=True),
        lax.all_gather(o_weight, ("dp", "ctx"), axis=0, tiled=True),
        lax.all_gather(ln1_gain, ("dp", "ctx"), axis=0, tiled=True),
    )
    mixed_grad = contract_cols(hidden_low, out_back).astype(jnp.bfloat16)
    key_back, value_back = (
        lax.all_gather(key_low, "ctx", axis=0, tiled=True),
        lax.all_gather(value_low, "ctx", axis=0, tiled=True),
    )

    def attend_back(group_block):
        query_block, key_block, value_block, grad_block, total_block = group_block
        scores = masked_scores(query_block, key_block)
        attn_probs = jnp.exp(scores - total_block[..., None])
        prob_grad = jnp.einsum(
            "qhd,khd->hqk", grad_block, value_block, preferred_element_type=jnp.float32
        )
        row_inner = jnp.sum(attn_probs * prob_grad, axis=-1, keepdims=True)
        score_grad = (attn_probs * (prob_grad - row_inner)).astype(jnp.bfloat16)
        query_grad = (
            jnp.einsum("hqk,khd->qhd", score_grad, key_block, preferred_element_type=jnp.float32)
            * score_scale
        )
        key_grad = (
            jnp.einsum("hqk,qhd->khd", score_grad, query_block, preferred_element_type=jnp.float32)
            * score_scale
        )
        value_grad = jnp.einsum(
            "hqk,qhd->khd",
            attn_probs.astype(jnp.bfloat16),
            grad_block,
            preferred_element_type=jnp.float32,
        )
        return (query_grad, key_grad, value_grad)

    query_parts, key_parts, value_parts = lax.map(
        attend_back,
        (
            query_groups,
            head_groups(key_back, group_size),
            head_groups(value_back, group_size),
            head_groups(mixed_grad, group_size),
            log_totals,
        ),
    )
    key_sum, value_sum = (
        lax.psum_scatter(
            merge_groups(key_parts).astype(jnp.bfloat16), "ctx", scatter_dimension=0, tiled=True
        ).astype(jnp.float32),
        lax.psum_scatter(
            merge_groups(value_parts).astype(jnp.bfloat16), "ctx", scatter_dimension=0, tiled=True
        ).astype(jnp.float32),
    )
    query_turn = rotate(
        merge_groups(query_parts).reshape(row_count, head_count, HEAD_DIM), cosine, sine_rows, -1.0
    )
    key_turn = rotate(key_sum.reshape(row_count, head_count, HEAD_DIM), cosine, sine_rows, -1.0)
    qkv_grad = jnp.concatenate(
        [
            query_turn.reshape(row_count, model_width),
            key_turn.reshape(row_count, model_width),
            value_sum,
        ],
        axis=1,
    ).astype(jnp.bfloat16)
    bias_grad = jnp.transpose(jnp.sum(qkv_grad.astype(jnp.float32), axis=0).reshape(3, model_width))
    norm_grad_one = contract_cols(qkv_grad, qkv_back)
    input_grad = (
        hidden_grad + norm_back(norm_grad_one, normed_one, inv_one, gain_first.astype(jnp.float32))
    ).astype(jnp.bfloat16)
    attn_share = lax.psum_scatter(
        jnp.concatenate(
            [contract_rows(act_one, qkv_grad), contract_rows(mixed_low, hidden_low)], axis=1
        ),
        ("dp", "ctx"),
        scatter_dimension=0,
        tiled=True,
    )
    vector_terms = jnp.concatenate(
        [
            jnp.sum(norm_grad_one * normed_one, axis=0)[:, None],
            jnp.sum(norm_grad_one, axis=0)[:, None],
            bias_grad,
            jnp.sum(norm_grad_two * normed_two, axis=0)[:, None],
            jnp.sum(norm_grad_two, axis=0)[:, None],
        ],
        axis=1,
    )
    vector_share = lax.psum_scatter(vector_terms, ("dp", "ctx"), scatter_dimension=0, tiled=True)
    return (
        output,
        input_grad,
        vector_share[:, 0],
        vector_share[:, 1],
        attn_share[:, : 3 * model_width],
        vector_share[:, 2:5],
        attn_share[:, 3 * model_width :],
        vector_share[:, 5],
        vector_share[:, 6],
        ffn_share[:, :ffn_width],
        ffn_share[:, ffn_width : 2 * ffn_width],
        ffn_share[:, 2 * ffn_width :],
    )


def solution(mesh):
    return jax.shard_map(
        local,
        mesh=mesh,
        in_specs=(
            P(("dp", "ctx"), None),
            P(("dp", "ctx")),
            P(("dp", "ctx")),
            P(("dp", "ctx"), None),
            P(("dp", "ctx")),
            P(("dp", "ctx")),
            P(("dp", "ctx"), None),
            P(("dp", "ctx"), None),
            P(("dp", "ctx"), None),
            P(("dp", "ctx")),
            P(("dp", "ctx")),
            P(("dp", "ctx"), None),
            P(("dp", "ctx"), None),
            P(("dp", "ctx"), None),
        ),
        out_specs=(
            P(("dp", "ctx"), None),
            P(("dp", "ctx"), None),
            P(("dp", "ctx")),
            P(("dp", "ctx")),
            P(("dp", "ctx"), None),
            P(("dp", "ctx"), None),
            P(("dp", "ctx"), None),
            P(("dp", "ctx")),
            P(("dp", "ctx")),
            P(("dp", "ctx"), None),
            P(("dp", "ctx"), None),
            P(("dp", "ctx"), None),
        ),
        check_vma=False,
    )
```

profile of v0, /device:TPU:0, one launch (start us, length us, event | category | flops | bytes accessed | tf_op | source)
XLA Modules:
  0.0 3813.0 jit_solution(12587906149706051192)
XLA Ops:
  8.0 43.7 %all-gather = bf16[32,64,3]{1,2,0:T(4,128)(2,1)S(1)} all-gather(bf16[1,64,3]{1,2,0:T(4,128)(2,1)} %bitcast.218), channel_id=1, replica_groups=mesh['dp'=8,'ctx'=4] {'dp','ctx'}, dimensions={0}, use_global_device_ids=true | all-gather | bytes 12672 | tf_op jit(solution)/shard_map/all_gather | solution.py:99
  55.3 39.0 %all-reduce.5 = (bf16[2048]{0:T(1024)(128)(2,1)S(1)}, bf16[2048]{0:T(1024)(128)(2,1)S(1)}, bf16[2048]{0:T(1024)(128)(2,1)S(1)}, bf16[2048]{0:T(1024)(128)(2,1)S(1)}) all-reduce(bf16[2048]{0:T(1024)(128)(2,1)S(1)} %dynamic-update-slice.1, bf16[2048]{0:T(1024)(128)(2,1)S(1)} %dynamic-update-slice, ...), channel_id=1, replica_groups=mesh['dp'=8,'ctx'=4] {'dp','ctx'}, use_global_device_ids=true, to_apply=%add.1 | all-reduce | flops 8192 | bytes 32768
  97.8 71.9 %all-gather.10.cloned.1.call-done = bf16[2048,6144]{1,0:T(8,128)(2,1)} async-done(((bf16[64,6144]{1,0:T(8,128)(2,1)}), bf16[2048,6144]{1,0:T(8,128)(2,1)}) %all-gather.10.cloned.1.call-update) | async-done | bytes 25165840 | tf_op jit(solution)/shard_map/all_gather | solution.py:95
  169.6 11.8 convolution_add_fusion
  181.5 2.7 copy-done.14
  186.1 4.0 fusion.93
  190.1 3.2 copy.55
  203.1 5.3 all-gather.1
  210.2 7.9 all-gather.12.cloned.1.call-done
  218.1 6.4 copy.54
  224.5 30.8 all-gather.14.cloned.1.call-done
  255.3 35.9 while.30
  255.6 2.8 fusion.153
  260.6 3.7 fusion.155
  264.6 2.9 fusion.153
  269.6 3.7 fusion.155
  273.6 2.8 fusion.153
  278.6 3.7 fusion.155
  282.6 2.8 fusion.153
  287.6 3.7 fusion.155
  291.3 44.3 %all-gather.16.cloned.1.call-done = bf16[2048,2048]{1,0:T(8,128)(2,1)} async-done(((bf16[64,2048]{1,0:T(8,128)(2,1)}), bf16[2048,2048]{1,0:T(8,128)(2,1)}) %all-gather.16.cloned.1.call-update) | async-done | bytes 8388624 | tf_op jit(solution)/shard_map/all_gather | solution.py:96
  335.5 6.1 fusion.95
  342.1 139.4 %all-gather.18.cloned.1.call-done = bf16[2048,5632]{1,0:T(8,128)(2,1)} async-done(((bf16[64,5632]{1,0:T(8,128)(2,1)}), bf16[2048,5632]{1,0:T(8,128)(2,1)}) %all-gather.18.cloned.1.call-update) | async-done | bytes 23068688 | tf_op jit(solution)/shard_map/all_gather | solution.py:160
  481.5 13.3 fusion.97
  494.8 132.2 %all-gather.20.cloned.1.call-done = bf16[2048,5632]{1,0:T(8,128)(2,1)} async-done(((bf16[64,5632]{1,0:T(8,128)(2,1)}), bf16[2048,5632]{1,0:T(8,128)(2,1)}) %all-gather.20.cloned.1.call-update) | async-done | bytes 23068688 | tf_op jit(solution)/shard_map/all_gather | solution.py:161
  627.0 13.3 fusion.96
  640.2 132.4 %all-gather.22.cloned.1.call-done = bf16[2048,5632]{1,0:T(8,128)(2,1)} async-done(((bf16[64,5632]{1,0:T(8,128)(2,1)}), bf16[2048,5632]{1,0:T(8,128)(2,1)}) %all-gather.22.cloned.1.call-update) | async-done | bytes 23068688 | tf_op jit(solution)/shard_map/all_gather | solution.py:162
  772.6 20.1 multiply_convert_fusion.1
  792.7 12.5 fusion.98
  805.2 13.9 multiply_reduce_fusion.1
  819.2 2.5 multiply_add_fusion
  823.0 6.8 convolution_convert_fusion
  832.0 84.3 %while.31 = (s32[]{:T(128)}, f32[4,256,8,64]{1,3,2,0:T(8,128)}, bf16[4,1024,8,64]{1,3,2,0:T(8,128)(2,1)}, bf16[4,1024,8,64]{1,3,2,0:T(8,128)(2,1)}, bf16[4,1024,...) while((s32[]{:T(128)}, f32[4,256,8,64]{1,3,2,0:T(8,128)}, ...), condition=%wide.region_12.13_spmd.clone.clone, body=%wide.region_10.12_spmd.clone.sunk.clone | while | flops 1375598592 | bytes 144245520 | solution.py:238
  832.2 2.6 fusion.164
  835.1 4.5 multiply_reduce_fusion.8
  842.0 3.6 fusion.166
  848.7 2.6 bitcast_dynamic-update-slice_fusion.11
  853.3 2.6 fusion.164
  856.2 4.5 multiply_reduce_fusion.8
  863.0 3.6 fusion.166
  869.7 2.6 bitcast_dynamic-update-slice_fusion.11
  874.3 2.6 fusion.164
  877.2 4.5 multiply_reduce_fusion.8
  884.0 3.6 fusion.166
  890.8 2.6 bitcast_dynamic-update-slice_fusion.11
  895.3 2.6 fusion.164
  898.2 4.5 multiply_reduce_fusion.8
  905.1 3.6 fusion.166
  911.8 2.6 bitcast_dynamic-update-slice_fusion.11
  916.5 2.5 slice.184
  920.8 20.8 convolution_bitcast_fusion
  941.6 36.9 fusion.53
  984.1 22.4 reduce-scatter.9.cloned.1.call-done
  1008.7 13.8 fusion.72
  1024.0 90.0 %pad_maximum_fusion = f32[2048,16896]{1,0:T(8,128)} fusion(f32[2048,5632]{1,0:T(8,128)} %convolution_bitcast_fusion, f32[2048,11264]{1,0:T(8,128)} %fusion.53), kind=kLoop, calls=%fused_computation.61 | loop fusion | flops 34603008 | bytes 276824064 | tf_op jit(solution)/shard_map/concatenate | solution.py:195
  1115.6 9.6 fusion.82
  1125.2 19.9 fusion.88
  1145.1 44.0 %pad_maximum_fusion.1 = f32[2048,8192]{1,0:T(8,128)} fusion(f32[2048,2048]{1,0:T(8,128)} %fusion.82, f32[2048,6144]{1,0:T(8,128)} %fusion.88), kind=kLoop, calls=%fused_computation.62 | loop fusion | flops 16777216 | bytes 134217728 | tf_op jit(solution)/shard_map/concatenate | solution.py:274
  1190.7 12.7 fusion.58
  1203.4 4.0 fusion.71
  1212.3 1882.9 %all-reduce.8.cloned.1.call-done = f32[2048,16896]{1,0:T(8,128)} async-done(((f32[2048,16896]{1,0:T(8,128)}), f32[2048,16896]{1,0:T(8,128)}) %all-reduce.8.cloned.1.call-update) | async-done | bytes 138412048
  3095.2 5.1 fusion.92
  3100.3 700.9 %reduce-scatter.11.cloned.1.call-done = f32[64,8192]{1,0:T(8,128)} async-done(((f32[2048,8192]{1,0:T(8,128)}), f32[64,8192]{1,0:T(8,128)}) %reduce-scatter.11.cloned.1.call-update) | async-done | bytes 2097168 | tf_op jit(solution)/shard_map/reduce_scatter | solution.py:273
  3801.2 2.7 slice.150
  (238 shorter events, 86.4 us)
Async XLA Ops:
  7.2 162.5 %copy-start.2 = (bf16[256,2048]{1,0:T(8,128)(2,1)S(1)}, bf16[256,2048]{1,0:T(8,128)(2,1)}, u32[]{:S(2)}) copy-start(bf16[256,2048]{1,0:T(8,128)(2,1)} %param.18) | copy-start | bytes 3145732
  7.2 162.4 %all-gather.10.cloned.1.call-start = ((), (), s32[]{:S(2)}) async-start(), calls=%async_computation.4 | async-start | bytes 25952256 | tf_op jit(solution)/shard_map/all_gather | solution.py:95
  7.9 210.2 %all-gather.12.cloned.1.call-start = ((), (), s32[]{:S(2)}) async-start(), calls=%async_computation.5 | async-start | bytes 5242880 | tf_op jit(solution)/shard_map/all_gather | solution.py:125
  94.3 87.1 %copy-start.26 = (f32[2048]{0:T(1024)}, f32[2048]{0:T(1024)S(1)}, u32[]{:S(2)}) copy-start(f32[2048]{0:T(1024)S(1)} %convert_element_type.106) | copy-start | bytes 24580
  94.3 87.2 %copy-start.24 = (f32[2048]{0:T(1024)}, f32[2048]{0:T(1024)S(1)}, u32[]{:S(2)}) copy-start(f32[2048]{0:T(1024)S(1)} %convert_element_type.105) | copy-start | bytes 24580
  96.0 85.4 %copy-start.32 = (f32[256]{0:T(256)}, f32[256]{0:T(256)S(1)}, u32[]{:S(2)}) copy-start(f32[256]{0:T(256)S(1)} %broadcast_multiply_fusion.7) | copy-start | bytes 3076
  97.7 83.7 %copy-start.34 = (f32[256]{0:T(256)}, f32[256]{0:T(256)S(1)}, u32[]{:S(2)}) copy-start(f32[256]{0:T(256)S(1)} %add_rsqrt_fusion.1) | copy-start | bytes 3076
  181.5 2.7 copy-start.14
  185.3 70.0 %all-gather.14.cloned.1.call-start = ((), (), s32[]{:S(2)}) async-start(), calls=%async_computation.6 | async-start | bytes 5242880 | tf_op jit(solution)/shard_map/all_gather | solution.py:124
  186.1 11.8 copy-start.30
  199.4 3.7 copy-start.42
  200.5 135.1 %all-gather.16.cloned.1.call-start = ((), (), s32[]{:S(2)}) async-start(), calls=%async_computation.7 | async-start | bytes 8650752 | tf_op jit(solution)/shard_map/all_gather | solution.py:96
  201.1 280.4 %all-gather.18.cloned.1.call-start = ((), (), s32[]{:S(2)}) async-start(), calls=%async_computation.8 | async-start | bytes 23789568 | tf_op jit(solution)/shard_map/all_gather | solution.py:160
  201.6 425.3 %all-gather.20.cloned.1.call-start = ((), (), s32[]{:S(2)}) async-start(), calls=%async_computation.9 | async-start | bytes 23789568 | tf_op jit(solution)/shard_map/all_gather | solution.py:161
  202.2 570.4 %all-gather.22.cloned.1.call-start = ((), (), s32[]{:S(2)}) async-start(), calls=%async_computation.10 | async-start | bytes 23789568 | tf_op jit(solution)/shard_map/all_gather | solution.py:162
  203.0 775.5 %reduce-scatter.7.cloned.1.call-start = ((), (), s32[]{:S(2)}) async-start(), calls=%async_computation.11 | async-start | bytes 5242880 | tf_op jit(solution)/shard_map/reduce_scatter | solution.py:249
  208.4 418.5 %copy-start.28 = (f32[2048]{0:T(1024)}, f32[2048]{0:T(1024)S(1)}, u32[]{:S(2)}) copy-start(f32[2048]{0:T(1024)S(1)} %convert_element_type.115) | copy-start | bytes 24580
  291.3 44.3 %copy-start.4 = (bf16[4,256,8,64]{1,3,2,0:T(8,128)(2,1)}, bf16[4,256,8,64]{1,3,2,0:T(8,128)(2,1)S(1)}, u32[]{:S(2)}) copy-start(bf16[4,256,8,64]{1,3,2,0:T(8,128)(2,1)S(1)} %get-tuple-element.513) | copy-start | bytes 3145732
  291.3 44.3 %copy-start.8 = (bf16[4,256,8,64]{1,3,2,0:T(8,128)(2,1)}, bf16[4,256,8,64]{1,3,2,0:T(8,128)(2,1)S(1)}, u32[]{:S(2)}) copy-start(bf16[4,256,8,64]{1,3,2,0:T(8,128)(2,1)S(1)} %get-tuple-element.104) | copy-start | bytes 3145732
  341.7 599.9 %copy-start = (f32[256,2048]{1,0:T(8,128)}, f32[256,2048]{1,0:T(8,128)S(1)}, u32[]{:S(2)}) copy-start(f32[256,2048]{1,0:T(8,128)S(1)} %get-tuple-element.245) | copy-start | bytes 6291460
  494.8 277.9 %copy-start.15 = (bf16[256,2048]{1,0:T(8,128)(2,1)S(1)}, bf16[256,2048]{1,0:T(8,128)(2,1)}, u32[]{:S(2)}) copy-start(bf16[256,2048]{1,0:T(8,128)(2,1)} %param.21) | copy-start | bytes 3145732
  823.0 9.1 copy-start.5
  832.2 2.9 copy-start.13
  842.0 3.6 copy-start.18
  845.5 3.2 copy-start.20
  846.4 4.9 copy-start.19
  851.3 1.9 copy-start.21
  853.3 2.9 copy-start.13
  863.0 3.6 copy-start.18
  866.6 3.2 copy-start.20
  867.4 4.9 copy-start.19
  872.3 1.9 copy-start.21
  874.3 2.9 copy-start.13
  884.0 3.6 copy-start.18
  887.6 3.2 copy-start.20
  888.5 4.9 copy-start.19
  893.4 1.9 copy-start.21
  895.3 2.9 copy-start.13
  905.1 3.6 copy-start.18
  908.7 3.2 copy-start.20
  909.5 4.9 copy-start.19
  916.4 90.1 %reduce-scatter.9.cloned.1.call-start = ((), (), s32[]{:S(2)}) async-start(), calls=%async_computation.12 | async-start | bytes 5242880 | tf_op jit(solution)/shard_map/reduce_scatter | solution.py:252
  916.4 4.3 copy-start.16
  920.7 286.7 %reduce-scatter.13.cloned.1.call-start = ((), (), s32[]{:S(2)}) async-start(), calls=%async_computation.14 | async-start | bytes 1081344
  920.8 20.8 copy-start.29
  978.5 3.9 copy-start.23
  978.5 3.9 copy-start.31
  978.5 3.9 copy-start.36
  983.9 38.6 %copy-start.9 = (bf16[256,32,64]{0,2,1:T(8,128)(2,1)}, bf16[256,32,64]{0,2,1:T(8,128)(2,1)S(1)}, u32[]{:S(2)}) copy-start(bf16[256,32,64]{0,2,1:T(8,128)(2,1)S(1)} %pad_maximum_fusion.5) | copy-start | bytes 3145732
  983.9 24.7 copy-start.3
  983.9 24.7 copy-start.25
  983.9 24.7 copy-start.33
  983.9 24.7 copy-start.35
  984.1 38.4 %copy-start.11 = (bf16[256,32,64]{0,2,1:T(8,128)(2,1)}, bf16[256,32,64]{0,2,1:T(8,128)(2,1)S(1)}, u32[]{:S(2)}) copy-start(bf16[256,32,64]{0,2,1:T(8,128)(2,1)S(1)} %pad_maximum_fusion.4) | copy-start | bytes 3145732
  1008.6 13.9 copy-start.37
  1008.6 13.9 copy-start.38
  1024.0 2071.2 %all-reduce.8.cloned.1.call-start = ((), (), s32[]{:S(2)}) async-start(), calls=%async_computation.15 | async-start | bytes 276824064
  1114.1 11.1 copy-start.27
  1114.1 2687.1 %reduce-scatter.11.cloned.1.call-start = ((), (), s32[]{:S(2)}) async-start(), calls=%async_computation.13 | async-start | bytes 69206016 | tf_op jit(solution)/shard_map/reduce_scatter | solution.py:273
  1115.6 9.6 copy-start.10
  1115.6 9.6 copy-start.12
  1115.6 9.6 copy-start.17
  1190.7 12.7 copy-start.41
  1190.7 12.7 copy-start.40
  (6 other events, 9.3 us)
Sparse Core Ops, SparseCore 0:
  10.9 158.7 all-gather.9
  185.4 32.6 all-gather.11
  220.3 35.0 all-gather.13
  258.0 77.4 all-gather.15
  338.2 143.1 all-gather.17
  484.1 142.7 all-gather.19
  629.8 142.7 all-gather.21
  916.5 42.7 reduce-scatter.6
  962.0 44.5 reduce-scatter.8
  1024.1 135.1 reduce-scatter.12
  1166.9 1928.2 all-reduce.7
  3097.5 703.6 reduce-scatter.10
where the time goes:
time: 3830 us; the launch traced here: 3810 us
  waiting for transfers between devices  3170 us (83%)
  matrix products  294 us (8%)
  other arithmetic  176 us (5%)
  blocking collectives  88 us (2%)
  local copies, waits for them, and re-layouts  69.9 us (2%)
    unnamed x14, waiting for transfers between devices  1890 us
    reduce_scatter x1, waiting for transfers between devices, local(): lax.psum_scatter(jnp.concatenate([contract_rows(act_one, qkv_grad), contr...  701 us
    all_gather x1, waiting for transfers between devices, local(): lax.all_gather(gate_weight, ('dp', 'ctx'), axis=0, tiled=True)  139 us
    all_gather x1, waiting for transfers between devices, local(): lax.all_gather(down_weight, ('dp', 'ctx'), axis=0, tiled=True)  132 us
    all_gather x1, waiting for transfers between devices, local(): lax.all_gather(up_weight, ('dp', 'ctx'), axis=0, tiled=True)  132 us
    concatenate x1, other arithmetic, local(): jnp.concatenate([contract_rows(act_two, gate_up_grad), contract_rows(out_...  90 us
    dot_general x4, matrix products, contract_rows(): lax.dot_general(left_part, right_part, (((0,), (0,)), ((), ())), preferre...  87.1 us
  transfers between devices with their start and end apart: 12, of which 10 were waited for; matrix products, arithmetic and copies ran while one was open for 9% of the time, Pallas kernels for 0%

commit v1 on v0

v1 whole, which is shorter than its diff:
```python
import functools

import jax
import jax.numpy as jnp
from jax import lax
from jax.experimental import pallas as pl
from jax.experimental.pallas import tpu as pltpu
from jax.sharding import Mesh
from jax.sharding import PartitionSpec as P

HEAD_DIM = 64
ROT_DIMS = 16
PAIR = 2 * HEAD_DIM
PLANE = ("y", "x", "c")
ALL = ("g", "y", "x", "c")
bf16 = jnp.bfloat16
f32 = jnp.float32

epsilon = 1e-05
neg_large = -1e30
rope_base = 10000.0
score_scale = 0.125


def layer_stats(values):
    mean_value = jnp.mean(values, axis=-1, keepdims=True)
    centered = values - mean_value
    inv_std = lax.rsqrt(jnp.mean(centered * centered, axis=-1, keepdims=True) + epsilon)
    return (centered * inv_std, inv_std)


def norm_back(grad_rows, normed, inv_std, gain_row):
    scaled = grad_rows * gain_row
    inner = jnp.mean(scaled * normed, axis=-1, keepdims=True)
    return inv_std * (scaled - jnp.mean(scaled, axis=-1, keepdims=True) - normed * inner)


def contract(left, right, left_dim, right_dim, kind=f32):
    return lax.dot_general(
        left, right, (((left_dim,), (right_dim,)), ((), ())), preferred_element_type=f32
    ).astype(kind)


def swap(values, axis):
    return lax.ppermute(values, axis, [(0, 1), (1, 0)])


def plane_gather(rows):
    half = rows.shape[0] // 2
    over_x = swap(rows, "x")
    over_y = swap(rows, "y")
    corner_a = swap(over_y[:half], "x")
    corner_b = swap(over_x[half:], "y")
    pieces = []
    for chip in ((rows,), (over_x,), (over_y,), (corner_a, corner_b)):
        pieces += list(chip) + [swap(part, "c") for part in chip]
    return jnp.concatenate(pieces, axis=0)


def plane_reduce(slots):
    half = slots[0].shape[0] // 2
    chip = [
        slots[s].astype(f32) + swap(slots[s + 1], "c").astype(f32) for s in (0, 2, 4, 6)
    ]
    corner = chip[3].astype(bf16)
    from_x = swap(corner[:half], "x").astype(f32)
    from_y = swap(corner[half:], "y").astype(f32)
    to_x = jnp.concatenate([chip[1][:half], chip[1][half:] + from_y], axis=0)
    to_y = jnp.concatenate([chip[2][:half] + from_x, chip[2][half:]], axis=0)
    got_x = swap(to_x.astype(bf16), "x").astype(f32)
    got_y = swap(to_y.astype(bf16), "y").astype(f32)
    return chip[0] + got_x + got_y


def plane_exchange(slots):
    count = len(slots)
    return [slots[0]] + [
        lax.ppermute(slots[s], PLANE, [(i, i ^ s) for i in range(count)]) for s in range(1, count)
    ]


def plane_all_to_all(blocks):
    return lax.all_to_all(blocks, PLANE, 0, 0, tiled=True)


def turned(rows, cosine, sine, first):
    partner = jnp.where(first, pltpu.roll(rows, PAIR - ROT_DIMS // 2, 1), pltpu.roll(rows, ROT_DIMS // 2, 1))
    return rows * cosine + partner * sine


def lanes_of(rows):
    return lax.broadcasted_iota(jnp.int32, (rows, PAIR), 1)


def keep_head(values, head):
    lane = lanes_of(values.shape[0])
    inside = lane < HEAD_DIM if head == 0 else lane >= HEAD_DIM
    return jnp.where(inside, values, jnp.zeros_like(values))


def allowed_block(seg_col, seg_row, block, rows):
    same = seg_col[0, : (block + 1) * rows, :] == seg_row[0, :, block * rows : (block + 1) * rows]
    key_at = lax.broadcasted_iota(jnp.int32, same.shape, 0)
    query_at = lax.broadcasted_iota(jnp.int32, same.shape, 1) + block * rows
    return same & (key_at <= query_at)


def nt(left, right):
    return lax.dot_general(left, right, (((1,), (1,)), ((), ())), preferred_element_type=f32)


def tn(left, right):
    return lax.dot_general(left, right, (((0,), (0,)), ((), ())), preferred_element_type=f32)


def nn(left, right):
    return lax.dot_general(left, right, (((1,), (0,)), ((), ())), preferred_element_type=f32)


def attend_kernel(
    blocks, place, q_ref, k_ref, v_ref, bq_ref, bk_ref, bv_ref, cos_ref, sin_ref, col_ref, row_ref,
    mixed_ref, query_ref, key_ref, value_ref, total_ref,
):
    own = place[0]
    rows = q_ref.shape[2]
    first = lanes_of(rows) % HEAD_DIM < ROT_DIMS // 2
    for block in range(blocks):
        slot = jnp.bitwise_xor(own, block)
        span = slice(block * rows, (block + 1) * rows)
        cosine, sine = cos_ref[0, span, :], sin_ref[0, span, :]
        query_ref[0, span, :] = turned(q_ref[0, slot] + bq_ref[...], cosine, sine, first).astype(bf16)
        key_ref[0, span, :] = turned(k_ref[0, slot] + bk_ref[...], cosine, sine, first).astype(bf16)
        value_ref[0, span, :] = (v_ref[0, slot] + bv_ref[...]).astype(bf16)
    for block in range(blocks):
        slot = jnp.bitwise_xor(own, block)
        span = slice(block * rows, (block + 1) * rows)
        upto = (block + 1) * rows
        allowed = allowed_block(col_ref, row_ref, block, rows)
        mixed = jnp.zeros((PAIR, rows), f32)
        for head in range(2):
            query = keep_head(query_ref[0, span, :], head) * score_scale
            scores = jnp.where(allowed, nt(key_ref[0, :upto, :], query), neg_large)
            top = jnp.max(scores, axis=0, keepdims=True)
            weights = jnp.exp(scores - top)
            total = jnp.sum(weights, axis=0, keepdims=True)
            probs = (weights * (1.0 / total)).astype(bf16)
            mixed = mixed + tn(keep_head(value_ref[0, :upto, :], head), probs)
            total_ref[0, 0, head : head + 1, span] = top + jnp.log(total)
        mixed_ref[0, slot] = jnp.transpose(mixed).astype(bf16)


def attend_back_kernel(
    blocks, place, query_ref, key_ref, value_ref, grad_ref, total_ref, cos_ref, sin_ref, col_ref, row_ref,
    out_ref, dk_ref, dv_ref,
):
    own = place[0]
    pair = pl.program_id(1)
    rows = grad_ref.shape[2]
    width = out_ref.shape[3] // 3
    first = lanes_of(rows) % HEAD_DIM < ROT_DIMS // 2

    def put(slot, which, values):
        at = pl.multiple_of(which * width + pair * PAIR, PAIR)
        out_ref[0, slot, :, pl.ds(at, PAIR)] = values.astype(bf16)

    dk_ref[...] = jnp.zeros_like(dk_ref)
    dv_ref[...] = jnp.zeros_like(dv_ref)
    for block in range(blocks):
        slot = jnp.bitwise_xor(own, block)
        span = slice(block * rows, (block + 1) * rows)
        upto = (block + 1) * rows
        allowed = allowed_block(col_ref, row_ref, block, rows)
        dq = jnp.zeros((PAIR, rows), f32)
        for head in range(2):
            query = keep_head(query_ref[0, span, :], head) * score_scale
            grad = keep_head(grad_ref[0, slot], head)
            scores = jnp.where(allowed, nt(key_ref[0, :upto, :], query), neg_large)
            probs = jnp.exp(scores - total_ref[0, 0, head : head + 1, span])
            prob_grad = nt(value_ref[0, :upto, :], grad)
            inner = jnp.sum(probs * prob_grad, axis=0, keepdims=True)
            score_grad = (probs * (prob_grad - inner)).astype(bf16)
            dk_ref[:upto, :] += nn(score_grad, query)
            dv_ref[:upto, :] += nn(probs.astype(bf16), grad)
            dq = dq + tn(keep_head(key_ref[0, :upto, :], head), score_grad)
        put(slot, 0, turned(jnp.transpose(dq) * score_scale, cos_ref[0, span, :], -sin_ref[0, span, :], first))
    for block in range(blocks):
        slot = jnp.bitwise_xor(own, block)
        span = slice(block * rows, (block + 1) * rows)
        put(slot, 1, turned(dk_ref[span, :], cos_ref[0, span, :], -sin_ref[0, span, :], first))
        put(slot, 2, dv_ref[span, :])


def attention(place, projected, bias, cosine, sine, seg_col, seg_row):
    packs, blocks, rows, width = projected.shape
    width //= 3
    pairs, seq = width // PAIR, blocks * rows

    def part(which):
        return pl.BlockSpec((1, blocks, rows, PAIR), lambda p, h, place: (p, 0, 0, which * pairs + h))

    def part_bias(which):
        return pl.BlockSpec((1, PAIR), lambda p, h, place: (0, which * pairs + h))

    def at_pack(*shape):
        return pl.BlockSpec((1, *shape), lambda p, h, place: (jnp.bitwise_xor(p, place[1]), 0, 0))

    kept = pl.BlockSpec((1, seq, PAIR), lambda p, h, place: (p, 0, h))
    return pl.pallas_call(
        functools.partial(attend_kernel, blocks),
        grid_spec=pltpu.PrefetchScalarGridSpec(
            num_scalar_prefetch=1,
            grid=(packs, pairs),
            in_specs=[part(0), part(1), part(2), part_bias(0), part_bias(1), part_bias(2),
                      at_pack(seq, PAIR), at_pack(seq, PAIR), at_pack(seq, 1), at_pack(1, seq)],
            out_specs=[
                pl.BlockSpec((1, blocks, rows, PAIR), lambda p, h, place: (p, 0, 0, h)),
                kept, kept, kept,
                pl.BlockSpec((1, 1, 2, seq), lambda p, h, place: (p, h, 0, 0)),
            ],
        ),
        out_shape=[
            jax.ShapeDtypeStruct((packs, blocks, rows, width), bf16),
            *[jax.ShapeDtypeStruct((packs, seq, width), bf16)] * 3,
            jax.ShapeDtypeStruct((packs, pairs, 2, seq), f32),
        ],
        compiler_params=pltpu.CompilerParams(vmem_limit_bytes=48 * 1024 * 1024),
        cost_estimate=pl.CostEstimate(
            flops=packs * seq * seq * width * 4, bytes_accessed=packs * seq * width * 24,
            transcendentals=packs * seq * seq * pairs,
        ),
    )(place, projected, projected, projected, bias, bias, bias, cosine, sine, seg_col, seg_row)


def attention_back(place, query, key, value, grad, totals, cosine, sine, seg_col, seg_row):
    packs, blocks, rows, width = grad.shape
    pairs, seq = width // PAIR, blocks * rows

    def at_pack(*shape):
        return pl.BlockSpec((1, *shape), lambda p, h, place: (jnp.bitwise_xor(p, place[1]), 0, 0))

    kept = pl.BlockSpec((1, seq, PAIR), lambda p, h, place: (p, 0, h))
    return pl.pallas_call(
        functools.partial(attend_back_kernel, blocks),
        grid_spec=pltpu.PrefetchScalarGridSpec(
            num_scalar_prefetch=1,
            grid=(packs, pairs),
            in_specs=[
                kept, kept, kept,
                pl.BlockSpec((1, blocks, rows, PAIR), lambda p, h, place: (p, 0, 0, h)),
                pl.BlockSpec((1, 1, 2, seq), lambda p, h, place: (p, h, 0, 0)),
                at_pack(seq, PAIR), at_pack(seq, PAIR), at_pack(seq, 1), at_pack(1, seq),
            ],
            out_specs=pl.BlockSpec((1, blocks, rows, 3 * width), lambda p, h, place: (p, 0, 0, 0)),
            scratch_shapes=[pltpu.VMEM((seq, PAIR), f32), pltpu.VMEM((seq, PAIR), f32)],
        ),
        out_shape=jax.ShapeDtypeStruct((packs, blocks, rows, 3 * width), bf16),
        compiler_params=pltpu.CompilerParams(vmem_limit_bytes=48 * 1024 * 1024),
        cost_estimate=pl.CostEstimate(
            flops=packs * seq * seq * width * 10, bytes_accessed=packs * seq * width * 16,
            transcendentals=packs * seq * seq * pairs,
        ),
    )(place, query, key, value, grad, totals, cosine, sine, seg_col, seg_row)


def local(
    tokens, segments, positions, out_grad, ln1_gain, ln1_bias, qkv_weight, qkv_bias, o_weight,
    ln2_gain, ln2_bias, gate_weight, up_weight, down_weight,
):
    rows, width = tokens.shape
    shard = qkv_weight.shape[0]
    ffn = gate_weight.shape[1]
    heads = width // HEAD_DIM
    team = lax.axis_size(PLANE)
    depth = lax.axis_size("g")
    devices = team * depth
    packs = lax.axis_size("y")
    blocks = team // packs
    seq = blocks * rows
    my_heads = heads // team
    my_width = my_heads * HEAD_DIM
    my_ffn = ffn // team
    pad_ffn = -(-my_ffn // 128) * 128
    me = lax.axis_index(PLANE)
    own_block = lax.axis_index("x") * 2 + lax.axis_index("c")
    place = jnp.stack([own_block, lax.axis_index("y")]).astype(jnp.int32)
    aligned = shard == HEAD_DIM

    vectors = jnp.stack([ln1_gain, ln1_bias, ln2_gain, ln2_bias], axis=0)
    vectors = jnp.concatenate([vectors, jnp.transpose(qkv_bias)], axis=0).astype(f32).reshape(-1)
    small = jnp.concatenate([vectors, segments.astype(f32), positions.astype(f32)])
    small = lax.all_to_all(
        jnp.broadcast_to(small[None], (devices, small.shape[0])), ALL, 0, 0, tiled=True
    )
    vectors = jnp.transpose(small[:, : 7 * shard].reshape(devices, 7, shard), (1, 0, 2)).reshape(7, width)
    gain_one, shift_one, gain_two, shift_two = (vectors[i][None, :] for i in range(4))
    my_plane = lax.dynamic_slice_in_dim(small[:, 7 * shard :], lax.axis_index("g") * team, team, 0)
    segment_all = my_plane[:, :rows].reshape(packs, seq)
    position_all = my_plane[:, rows:].reshape(packs, seq)
    bias_mine = lax.dynamic_slice_in_dim(
        vectors[4:7].reshape(3, my_heads, team, HEAD_DIM), me, 1, 2
    ).reshape(1, 3 * my_width)

    qkv_send = jnp.transpose(
        qkv_weight.reshape(shard, 3 * my_heads, team, HEAD_DIM), (2, 0, 1, 3)
    ).reshape(team, shard, 3 * my_width)
    qkv_mine = plane_all_to_all(qkv_send).reshape(team * shard, 3 * my_width)

    def ffn_columns(weight):
        split = jnp.transpose(weight.reshape(shard, team, my_ffn), (1, 0, 2))
        return jnp.pad(split, ((0, 0), (0, 0), (0, pad_ffn - my_ffn)))

    ffn_send = jnp.concatenate(
        [ffn_columns(gate_weight), ffn_columns(up_weight), ffn_columns(down_weight)], axis=2
    )
    ffn_mine = plane_all_to_all(ffn_send).reshape(team * shard, 3 * pad_ffn)

    def over_g(piece):
        return lax.all_gather(piece, "g", axis=0, tiled=True)

    if aligned:
        out_rows = over_g(o_weight)
        out_full = plane_gather(out_rows)
    else:
        out_abs = lax.all_gather(o_weight, ALL, axis=0, tiled=True)
        out_abs = out_abs.reshape(my_heads, team, HEAD_DIM, width)
        out_full = jnp.concatenate(
            [jnp.take(out_abs, jnp.bitwise_xor(me, s), axis=1).reshape(my_width, width) for s in range(team)],
            axis=0,
        )
    qkv_full = over_g(qkv_mine)
    gate_up_full = over_g(ffn_mine[:, : 2 * pad_ffn])
    down_full = over_g(ffn_mine[:, 2 * pad_ffn :])

    inputs = tokens.astype(f32)
    normed_one, inv_one = layer_stats(inputs)
    act_one = plane_gather((normed_one * gain_one + shift_one).astype(bf16))
    projected = contract(act_one, qkv_full, 1, 0)
    frequency = rope_base ** (-jnp.arange(0, ROT_DIMS, 2, dtype=f32) / ROT_DIMS)
    within = jnp.arange(PAIR) % HEAD_DIM
    phases = position_all[:, :, None] * jnp.where(within < ROT_DIMS, frequency[within % (ROT_DIMS // 2)], 0.0)
    cosine = jnp.cos(phases)
    sine = jnp.sin(phases) * jnp.where(within < ROT_DIMS // 2, -1.0, 1.0)
    seg_col, seg_row = segment_all[:, :, None], segment_all[:, None, :]
    mixed, query, key, value, totals = attention(
        place, projected.reshape(packs, blocks, rows, 3 * my_width), bias_mine, cosine, sine, seg_col, seg_row
    )
    mixed = mixed.reshape(team, rows, my_width)
    mixed_own = jnp.concatenate(plane_exchange([mixed[s] for s in range(team)]), axis=1)
    hidden = inputs + contract(mixed_own, out_full, 1, 0)

    normed_two, inv_two = layer_stats(hidden)
    act_two = plane_gather((normed_two * gain_two + shift_two).astype(bf16))
    cotangent = plane_gather(out_grad)
    gate_up = contract(act_two, gate_up_full, 1, 0)
    gate_value, up_value = gate_up[:, :pad_ffn], gate_up[:, pad_ffn:]
    gate_sigmoid = jax.nn.sigmoid(gate_value)
    gate_silu = gate_value * gate_sigmoid
    middle_low = (gate_silu * up_value).astype(bf16)

    def slots_of(left, right):
        return [
            contract(left[s * rows : (s + 1) * rows], right, 1, 1, bf16) for s in range(team)
        ]

    output = (hidden + plane_reduce(slots_of(middle_low, down_full))).astype(bf16)

    middle_grad = contract(cotangent, down_full, 1, 0)
    gate_grad = middle_grad * up_value * (gate_sigmoid * (1.0 + gate_value * (1.0 - gate_sigmoid)))
    gate_up_grad = jnp.concatenate([gate_grad.astype(bf16), (middle_grad * gate_silu).astype(bf16)], axis=1)
    norm_grad_two = plane_reduce(slots_of(gate_up_grad, gate_up_full))
    hidden_grad = out_grad.astype(f32) + norm_back(norm_grad_two, normed_two, inv_two, gain_two)
    hidden_low = hidden_grad.astype(bf16)

    def own_rows(grad_sum):
        return lax.psum_scatter(grad_sum, "g", scatter_dimension=0, tiled=True)

    def back_to_rows(columns):
        return plane_all_to_all(columns.reshape(team, shard, columns.shape[1]))

    def ffn_rows(received, which):
        part = received[:, :, which * pad_ffn : which * pad_ffn + my_ffn].astype(f32)
        return jnp.transpose(part, (1, 0, 2)).reshape(shard, ffn)

    down_share = back_to_rows(own_rows(contract(cotangent, middle_low, 0, 0, bf16)))
    gate_up_share = back_to_rows(own_rows(contract(act_two, gate_up_grad, 0, 0, bf16)))

    mixed_grad = contract(hidden_low, out_full, 1, 1, bf16)
    mixed_grad = plane_exchange([mixed_grad[:, s * my_width : (s + 1) * my_width] for s in range(team)])
    mixed_grad = jnp.stack(mixed_grad).reshape(packs, blocks, rows, my_width)
    hidden_all = plane_gather(hidden_low)
    out_sum = contract(mixed.reshape(team * rows, my_width), hidden_all, 0, 0, bf16)
    if aligned:
        out_share = own_rows(out_sum).astype(f32)
    else:
        spread = jnp.zeros((my_heads, team, HEAD_DIM, width), bf16)
        spread = lax.dynamic_update_slice_in_dim(
            spread, out_sum.reshape(my_heads, 1, HEAD_DIM, width), me, 1
        )
        out_share = lax.psum_scatter(
            spread.reshape(width, width).astype(f32), ALL, scatter_dimension=0, tiled=True
        )
    qkv_grad = attention_back(
        place, query, key, value, mixed_grad, totals, cosine, sine, seg_col, seg_row
    ).reshape(team * rows, 3 * my_width)
    norm_grad_one = plane_reduce(slots_of(qkv_grad, qkv_full))
    input_grad = (hidden_grad + norm_back(norm_grad_one, normed_one, inv_one, gain_one)).astype(bf16)
    qkv_share = back_to_rows(own_rows(contract(act_one, qkv_grad, 0, 0, bf16)))
    qkv_share = jnp.transpose(
        qkv_share.reshape(team, shard, 3 * my_heads, HEAD_DIM), (1, 2, 0, 3)
    ).reshape(shard, 3 * width).astype(f32)

    bias_sum = jnp.sum(qkv_grad.astype(f32), axis=0).reshape(3, my_heads, 1, HEAD_DIM)
    mine = (jnp.arange(team) == me).astype(f32)[None, None, :, None]
    terms = jnp.concatenate(
        [
            jnp.sum(norm_grad_one * normed_one, axis=0)[None],
            jnp.sum(norm_grad_one, axis=0)[None],
            (bias_sum * mine).reshape(3, width),
            jnp.sum(norm_grad_two * normed_two, axis=0)[None],
            jnp.sum(norm_grad_two, axis=0)[None],
        ],
        axis=0,
    )
    terms = jnp.transpose(terms.reshape(7, devices, shard), (1, 0, 2)).reshape(devices, 7 * shard)
    vector_share = jnp.sum(lax.all_to_all(terms, ALL, 0, 0, tiled=True), axis=0).reshape(7, shard)
    return (
        output,
        input_grad,
        vector_share[0],
        vector_share[1],
        qkv_share,
        jnp.transpose(vector_share[2:5]),
        out_share,
        vector_share[5],
        vector_share[6],
        ffn_rows(gate_up_share, 0),
        ffn_rows(gate_up_share, 1),
        ffn_rows(down_share, 0),
    )


def solution(mesh):
    dp, ctx = mesh.shape["dp"], mesh.shape["ctx"]
    split = Mesh(mesh.devices.reshape(dp // 2, 2, ctx // 2, 2), ALL)
    row, flat = P(ALL, None), P(ALL)
    return jax.shard_map(
        local,
        mesh=split,
        in_specs=(row, flat, flat, row, flat, flat, row, row, row, flat, flat, row, row, row),
        out_specs=(row, row, flat, flat, row, row, row, flat, flat, row, row, row),
        check_vma=False,
    )
```

time: 3830 us -> 775 us (0.20)
  waiting for transfers between devices: 3170 us -> 262 us
  other arithmetic: 176 us -> 42.3 us
  matrix products: 294 us -> 163 us
  starting transfers between devices: 0.73 us -> 77.3 us
  local copies, waits for them, and re-layouts: 69.9 us -> 127 us
  blocking collectives: 88 us -> 34 us
  Pallas kernels: 0 us -> 42.8 us
    unnamed x14 -> x8, waiting for transfers between devices: 1890 us -> 0.8 us
    reduce_scatter x3 -> x4, waiting for transfers between devices: 723 us -> 40.6 us  [own_rows(): return lax.psum_scatter(grad_sum, 'g', scatter_dimension=0, tiled=True)]
    all_gather x7 -> x4, waiting for transfers between devices: 559 us -> 0.01 us  [over_g(): return lax.all_gather(piece, 'g', axis=0, tiled=True)]
    ppermute x0 -> x83, waiting for transfers between devices: none -> 192 us  [the longest x69 167 us: swap(): return lax.ppermute(values, axis, [(0, 1), (1, 0)])]
    dot_general x42 -> x33, matrix products: 294 us -> 163 us  [contract(): lax.dot_general(left, right, (((left_dim,), (right_dim,)), ((), ())), pre...]
    concatenate x5 -> x8, other arithmetic: 135 us -> 4.66 us  [the longest x3 2.19 us: plane_reduce(): to_x = jnp.concatenate([chip[1][:half], chip[1][half:] + from_y], axis=0)]
    ppermute x0 -> x83, starting transfers between devices: none -> 53 us  [the longest x69 41.5 us: swap(): return lax.ppermute(values, axis, [(0, 1), (1, 0)])]
    unnamed x92 -> x145, local copies, waits for them, and re-layouts: 14.8 us -> 64 us
  transfers between devices with their start and end apart: 12 -> 96, of which waited for: 10 -> 35; matrix products, arithmetic and copies ran while one was open for 9% -> 39% of each run, Pallas kernels for 0% -> 6%
where the time goes in v1:
time: 775 us; the launch traced here: 764 us
  waiting for transfers between devices  262 us (34%)
  matrix products  163 us (21%)
  local copies, waits for them, and re-layouts  127 us (16%)
  starting transfers between devices  77.3 us (10%)
  Pallas kernels  42.8 us (6%)
  other arithmetic  42.3 us (5%)
  blocking collectives  34 us (4%)
  between operations  15.8 us (2%)
    ppermute x69, waiting for transfers between devices, swap(): return lax.ppermute(values, axis, [(0, 1), (1, 0)])  167 us
    dot_general x33, matrix products, contract(): lax.dot_general(left, right, (((left_dim,), (right_dim,)), ((), ())), pre...  163 us
    unnamed x145, local copies, waits for them, and re-layouts  64 us
    ppermute x69, starting transfers between devices, swap(): return lax.ppermute(values, axis, [(0, 1), (1, 0)])  41.5 us
    reduce_scatter x4, waiting for transfers between devices, own_rows(): return lax.psum_scatter(grad_sum, 'g', scatter_dimension=0, tiled=True)  40.6 us
    all_to_all x2, blocking collectives, plane_all_to_all(): return lax.all_to_all(blocks, PLANE, 0, 0, tiled=True)  34 us
    pallas_call x1, Pallas kernels, attention_back(): pl.pallas_call(functools.partial(attend_back_kernel, blocks), grid_spec=p...  25.5 us
    ppermute x14, waiting for transfers between devices, plane_exchange(): lax.ppermute(slots[s], PLANE, [(i, i ^ s) for i in range(count)])  24.6 us
  transfers between devices with their start and end apart: 96, of which 35 were waited for; matrix products, arithmetic and copies ran while one was open for 39% of the time, Pallas kernels for 6%

profile of v1, /device:TPU:0, one launch (start us, length us, event | category | flops | bytes accessed | tf_op | source)
XLA Modules:
  0.0 764.2 jit_solution(18015356675843129909)
XLA Ops:
  8.0 3.4 reshape.292
  15.3 18.0 %all_to_all.44 = bf16[8,64,768]{2,1,0:T(8,128)(2,1)} all-to-all(bf16[8,64,768]{2,1,0:T(8,128)(2,1)} %reshape.293), channel_id=1, replica_groups=mesh['g'=4,'y'=2,'x'=2,'c'=2] {'y','x','c'}, dimensions={0} | all-to-all | bytes 1572864 | tf_op jit(solution)/shard_map/all_to_all | solution.py:83
  35.5 6.1 all-to-all-start
  45.6 15.6 %all-to-all-done = f32[32,1,960]{2,1,0:T(1,128)S(1)} async-done(((f32[32,1,960]{2,1,0:T(1,128)}), f32[32,1,960]{2,1,0:T(1,128)S(1)}, u32[]{:S(2)}, u32[]{:S(2)}) %all-to-all-start) | async-done | bytes 122912 | tf_op jit(solution)/shard_map/all_to_all | solution.py:291
  66.4 2.5 constant_dynamic-update-slice_fusion.9
  72.4 4.5 all-to-all-start.2
  79.7 5.1 compare_select_fusion.9
  86.0 9.2 %collective-permute-done.1 = bf16[256,2048]{1,0:T(8,128)(2,1)} collective-permute-done((bf16[256,2048]{1,0:T(8,128)(2,1)}, bf16[256,2048]{1,0:T(8,128)(2,1)}, u32[]{:S(2)}, u32[]{:S(2)}) %collective-permute-start.1) | collective-permute-done | bytes 1048608 | tf_op jit(solution)/shard_map/ppermute | solution.py:45
  95.2 4.7 fusion.34
  108.1 19.7 %collective-permute-done.3 = bf16[256,2048]{1,0:T(8,128)(2,1)S(1)} collective-permute-done((bf16[256,2048]{1,0:T(8,128)(2,1)}, bf16[256,2048]{1,0:T(8,128)(2,1)S(1)}, u32[]{:S(2)}, u32[]{:S(2)}) %collective-permute-start.3) | collective-permute-done | bytes 1048608 | tf_op jit(solution)/shard_map/ppermute | solution.py:45
  139.9 2.7 slice.413
  152.6 12.2 %collective-permute-done.17 = bf16[256,2048]{1,0:T(8,128)(2,1)S(1)} collective-permute-done((bf16[256,2048]{1,0:T(8,128)(2,1)}, bf16[256,2048]{1,0:T(8,128)(2,1)S(1)}, u32[]{:S(2)}, u32[]{:S(2)}) %collective-permute-start.17) | collective-permute-done | bytes 1048608 | tf_op jit(solution)/shard_map/ppermute | solution.py:45
  177.2 6.8 collective-permute-done.21
  184.0 8.5 %collective-permute-done.22 = bf16[128,2048]{1,0:T(8,128)(2,1)S(1)} collective-permute-done((bf16[128,2048]{1,0:T(8,128)(2,1)S(1)}, bf16[128,2048]{1,0:T(8,128)(2,1)S(1)}, u32[]{:S(2)}, u32[]{:S(2)}) %collective-permute-start.22) | collective-permute-done | bytes 524320 | tf_op jit(solution)/shard_map/ppermute | solution.py:45
  197.4 12.1 %fusion.110 = f32[2048,768]{1,0:T(8,128)} fusion(bf16[2048,2048]{1,0:T(8,128)(2,1)} %constant_dynamic-update-slice_fusion, bf16[2048,768]{1,0:T(8,128)(2,1)} %all-gather.5.cloned.1.call-done), kind=kOutput, calls=%fused_computation.296 | convolution fusion | flops 6442450944 | bytes 17825792 | tf_op jit(solution)/shard_map/dot_general | solution.py:39
  209.5 17.3 %shard_map.229 = (bf16[2,4,256,256]{3,2,1,0:T(8,128)(2,1)S(1)}, bf16[2,1024,256]{2,1,0:T(8,128)(2,1)S(1)}, bf16[2,1024,256]{2,1,0:T(8,128)(2,1)S(1)}, bf16[2,102...) custom-call(s32[2]{0:T(128)S(1)} %pad_add_fusion.place, f32[2,4,256,768]{3,2,1,0:T(8,128)} %bitcast.144, ...), custom_call_target="tpu_custom_call" | custom-call | flops 2147483648 | bytes 12582912 | tf_op jit(solution)/shard_map/pallas_call | solution.py:208
  239.3 2.7 collective-permute-done.13
  244.2 3.1 collective-permute-done.15
  247.2 5.9 fusion.109
  273.2 7.5 collective-permute-done.26
  285.6 4.9 collective-permute-done.28
  299.4 4.8 collective-permute-done.30
  304.2 2.6 collective-permute-done.31
  313.4 19.2 %fusion.111 = f32[2048,1536]{0,1:T(8,128)} fusion(bf16[2048,2048]{1,0:T(8,128)(2,1)} %constant_dynamic-update-slice_fusion.28, bf16[2048,1536]{1,0:T(8,128)(2,1)} %all-gather.9.cloned.1.call-done), kind=kOutput, calls=%fused_computation.297 | convolution fusion | flops 12884901888 | bytes 27262976 | tf_op jit(solution)/shard_map/dot_general | solution.py:39
  332.5 17.9 %multiply_convert_fusion = (bf16[2048,768]{0,1:T(8,128)(2,1)}, bf16[2048,768]{0,1:T(8,128)(2,1)}, bf16[2048,768]{0,1:T(8,128)(2,1)}) fusion(f32[2048,1536]{0,1:T(8,128)} %fusion.111, bf16[2048,2048]{1,0:T(8,128)(2,1)} %constant_dynamic-update-slice_fusion.38, bf16[2048,768]{1,0:T(8,128)(2,1)} %all-gather.11.cloned.1.call-done), kind=kOutput, calls=%fused_computation.21 | convolution fusion | flops 6466043904 | bytes 33554432 | tf_op jit(solution)/shard_map/dot_general | solution.py:39
  350.4 4.2 convolution_convert_fusion.27
  357.4 3.2 convolution_convert_fusion.23
  366.0 2.9 convolution_convert_fusion.9
  372.8 2.5 convert_add_fusion.8
  382.2 3.2 convert_add_fusion.5
  391.3 5.2 collective-permute-done.37
  402.4 9.4 %collective-permute-done.57 = bf16[128,2048]{1,0:T(8,128)(2,1)S(1)} collective-permute-done((bf16[128,2048]{1,0:T(8,128)(2,1)S(1)}, bf16[128,2048]{1,0:T(8,128)(2,1)S(1)}, u32[]{:S(2)}, u32[]{:S(2)}) %collective-permute-start.57) | collective-permute-done | bytes 524320 | tf_op jit(solution)/shard_map/ppermute | solution.py:45
  416.8 10.5 %convolution_convert_fusion.1 = bf16[2048,768]{1,0:T(8,128)(2,1)} fusion(bf16[2048,2048]{1,0:T(8,128)(2,1)} %constant_dynamic-update-slice_fusion.38, bf16[2048,768]{0,1:T(8,128)(2,1)S(1)} %copy-done.24), kind=kOutput, calls=%fused_computation.32 | convolution fusion | flops 6444023808 | bytes 14680064 | tf_op jit(solution)/shard_map/dot_general | solution.py:39
  427.4 3.2 fusion.16
  430.6 4.9 fusion.8
  435.5 2.6 collective-permute-done.41
  438.1 20.1 %collective-permute-done.58 = bf16[256,2048]{1,0:T(8,128)(2,1)} collective-permute-done((bf16[256,2048]{1,0:T(8,128)(2,1)}, bf16[256,2048]{1,0:T(8,128)(2,1)}, u32[]{:S(2)}, u32[]{:S(2)}) %collective-permute-start.58) | collective-permute-done | bytes 1048608 | tf_op jit(solution)/shard_map/ppermute | solution.py:45
  458.2 5.4 multiply_reduce_fusion
  466.1 6.2 convolution_convert_fusion.20
  473.7 2.5 collective-permute-start.63
  478.9 4.8 collective-permute-done.60
  483.8 5.4 collective-permute-done.61
  489.3 25.5 %shard_map.230 = bf16[2,4,256,768]{3,2,1,0:T(8,128)(2,1)} custom-call(s32[2]{0:T(128)S(1)} %pad_add_fusion.place, bf16[2,1024,256]{2,1,0:T(8,128)(2,1)S(1)} %get-tuple-element.18.query_ref, bf16[2,1024,256]{2,1,0:T(8,128)(2,1)S(1)} %get-tuple-element.19.key_ref, bf16[2,1024,256]{2,1,0:T(8,128)(2,1)S(1)} %copy-done.3, bf16[2,4,256,256]{3,2,1,0:T(8,128)(2,1)S(1)} %bitcast.141, ...), custom_call_target="tpu_custom_call" | custom-call | flops 5368709120 | bytes 8388608 | tf_op jit(solution)/shard_map/pallas_call | solution.py:242
  514.8 10.6 %convolution_convert_fusion.2 = bf16[2048,768]{1,0:T(8,128)(2,1)} fusion(bf16[2048,2048]{1,0:T(8,128)(2,1)S(1)} %bitcast.171, bf16[2048,768]{1,0:T(8,128)(2,1)} %bitcast.149), kind=kOutput, calls=%fused_computation.33 | convolution fusion | flops 6444023808 | bytes 14680064 | tf_op jit(solution)/shard_map/dot_general | solution.py:39
  525.4 19.5 %convolution_convert_fusion = bf16[2048,1536]{1,0:T(8,128)(2,1)} fusion(bf16[2048,2048]{1,0:T(8,128)(2,1)} %constant_dynamic-update-slice_fusion.28, bf16[2048,768]{0,1:T(8,128)(2,1)} %get-tuple-element.43, bf16[2048,768]{0,1:T(8,128)(2,1)} %get-tuple-element.44), kind=kOutput, calls=%fused_computation.17 | convolution fusion | flops 12900630528 | bytes 20971520 | tf_op jit(solution)/shard_map/dot_general | solution.py:39
  551.4 3.2 convolution_convert_fusion.18
  560.7 10.4 %collective-permute-done.77 = bf16[256,2048]{1,0:T(8,128)(2,1)S(1)} collective-permute-done((bf16[256,2048]{1,0:T(8,128)(2,1)S(1)}, bf16[256,2048]{1,0:T(8,128)(2,1)S(1)}, u32[]{:S(2)}, u32[]{:S(2)}) %collective-permute-start.77) | collective-permute-done | bytes 1048608 | tf_op jit(solution)/shard_map/ppermute | solution.py:45
  583.2 19.0 %collective-permute-done.69 = bf16[128,2048]{1,0:T(8,128)(2,1)S(1)} collective-permute-done((bf16[128,2048]{1,0:T(8,128)(2,1)S(1)}, bf16[128,2048]{1,0:T(8,128)(2,1)S(1)}, u32[]{:S(2)}, u32[]{:S(2)}) %collective-permute-start.69) | collective-permute-done | bytes 524320 | tf_op jit(solution)/shard_map/ppermute | solution.py:45
  612.7 17.3 %collective-permute-done.70 = bf16[256,2048]{1,0:T(8,128)(2,1)S(1)} collective-permute-done((bf16[256,2048]{1,0:T(8,128)(2,1)S(1)}, bf16[256,2048]{1,0:T(8,128)(2,1)S(1)}, u32[]{:S(2)}, u32[]{:S(2)}) %collective-permute-start.70) | collective-permute-done | bytes 1048608 | tf_op jit(solution)/shard_map/ppermute | solution.py:45
  631.8 2.6 fusion.32
  635.5 5.3 all-to-all-start.3
  641.6 7.8 %all-to-all-done.3 = f32[32,1,448]{2,1,0:T(1,128)S(1)} async-done(((f32[32,1,448]{2,1,0:T(1,128)}), f32[32,1,448]{2,1,0:T(1,128)S(1)}, u32[]{:S(2)}, u32[]{:S(2)}) %all-to-all-start.3) | async-done | bytes 57376 | tf_op jit(solution)/shard_map/all_to_all | solution.py:425
  649.5 3.5 all-to-all-start.6
  653.3 6.7 convolution_convert_fusion.11
  660.0 5.6 all-to-all-done.6
  665.6 16.0 %all_to_all.45 = bf16[8,64,768]{2,1,0:T(8,128)(2,1)S(1)} all-to-all(bf16[8,64,768]{2,1,0:T(8,128)(2,1)} %bitcast.164), channel_id=1, replica_groups=mesh['g'=4,'y'=2,'x'=2,'c'=2] {'y','x','c'}, dimensions={0} | all-to-all | bytes 1572864 | tf_op jit(solution)/shard_map/all_to_all | solution.py:83
  681.6 19.7 %reduce-scatter.9.cloned.1.call-done = bf16[512,1536]{1,0:T(8,128)(2,1)} async-done(((bf16[2048,1536]{1,0:T(8,128)(2,1)}), bf16[512,1536]{1,0:T(8,128)(2,1)}) %reduce-scatter.9.cloned.1.call-update) | async-done | bytes 1572880 | tf_op jit(solution)/shard_map/reduce_scatter | solution.py:375
  701.2 4.3 all-to-all-start.5
  705.5 4.0 fusion.31
  710.9 20.9 %reduce-scatter.7.cloned.1.call-done = bf16[64,2048]{1,0:T(8,128)(2,1)} async-done(((bf16[256,2048]{1,0:T(8,128)(2,1)}), bf16[64,2048]{1,0:T(8,128)(2,1)}) %reduce-scatter.7.cloned.1.call-update) | async-done | bytes 262160 | tf_op jit(solution)/shard_map/reduce_scatter | solution.py:375
  736.3 2.6 reshape.325
  738.8 5.7 copy.54
  744.6 3.3 reshape.315
  747.9 2.7 convert_bitcast_fusion.1
  (443 shorter events, 219.5 us)
Async XLA Ops:
  7.2 130.0 %all-gather.7.cloned.1.call-start = ((), (), s32[]{:S(2)}) async-start(), calls=%async_computation.12 | async-start | bytes 1310720 | tf_op jit(solution)/shard_map/all_gather | solution.py:318
  7.9 189.5 %all-gather.5.cloned.1.call-start = ((), (), s32[]{:S(2)}) async-start(), calls=%async_computation.11 | async-start | bytes 3932160 | tf_op jit(solution)/shard_map/all_gather | solution.py:318
  33.3 46.3 %collective-permute-start.43 = (bf16[256,2048]{1,0:T(8,128)(2,1)}, bf16[256,2048]{1,0:T(8,128)(2,1)}, u32[]{:S(2)}, u32[]{:S(2)}) collective-permute-start(bf16[256,2048]{1,0:T(8,128)(2,1)} %param.17), channel_id=1, source_target_pairs={{0,2},{2,0},{1,3},{3,1},{4,6},{6,4},{5,7},{7,5},{8,10},{10,8},{9,1... | collective-permute-start | bytes 3145736 | tf_op jit(solution)/shard_map/ppermute | solution.py:45
  33.9 71.9 %collective-permute-start.42 = (bf16[256,2048]{1,0:T(8,128)(2,1)}, bf16[256,2048]{1,0:T(8,128)(2,1)}, u32[]{:S(2)}, u32[]{:S(2)}) collective-permute-start(bf16[256,2048]{1,0:T(8,128)(2,1)} %param.17), channel_id=1, source_target_pairs={{0,1},{1,0},{2,3},{3,2},{4,5},{5,4},{6,7},{7,6},{8,9},{9,8},{10,11... | collective-permute-start | bytes 3145736 | tf_op jit(solution)/shard_map/ppermute | solution.py:45
  34.0 70.0 %collective-permute-start.45 = (bf16[256,2048]{1,0:T(8,128)(2,1)}, bf16[256,2048]{1,0:T(8,128)(2,1)}, u32[]{:S(2)}, u32[]{:S(2)}) collective-permute-start(bf16[256,2048]{1,0:T(8,128)(2,1)} %param.17), channel_id=1, source_target_pairs={{0,4},{4,0},{1,5},{5,1},{2,6},{6,2},{3,7},{7,3},{8,12},{12,8},{9,1... | collective-permute-start | bytes 3145736 | tf_op jit(solution)/shard_map/ppermute | solution.py:45
  35.5 25.7 %all-to-all-start = ((f32[32,1,960]{2,1,0:T(1,128)}), f32[32,1,960]{2,1,0:T(1,128)S(1)}, u32[]{:S(2)}, u32[]{:S(2)}) async-start(f32[32,1,960]{2,1,0:T(1,128)} %broadcast_in_dim.14), calls=%async_computation | async-start | bytes 262144 | tf_op jit(solution)/shard_map/all_to_all | solution.py:291
  68.9 26.3 %collective-permute-start.1 = (bf16[256,2048]{1,0:T(8,128)(2,1)}, bf16[256,2048]{1,0:T(8,128)(2,1)}, u32[]{:S(2)}, u32[]{:S(2)}) collective-permute-start(bf16[256,2048]{1,0:T(8,128)(2,1)} %get-tuple-element.42), channel_id=1, source_target_pairs={{0,2},{2,0},{1,3},{3,1},{4,6},{6,4},{5,7},{7,5},{8,10},{10,8},{9,1... | collective-permute-start | bytes 3145736 | tf_op jit(solution)/shard_map/ppermute | solution.py:45
  72.4 67.5 %all-to-all-start.2 = ((bf16[8,64,2304]{2,1,0:T(8,128)(2,1)}), bf16[8,64,2304]{2,1,0:T(8,128)(2,1)}, u32[]{:S(2)}, u32[]{:S(2)}) async-start(bf16[8,64,2304]{2,1,0:T(8,128)(2,1)} %copy.50), calls=%async_computation.2 | async-start | bytes 4718592 | tf_op jit(solution)/shard_map/all_to_all | solution.py:83
  76.9 236.4 %all-gather.9.cloned.1.call-start = ((), (), s32[]{:S(2)}) async-start(), calls=%async_computation.13 | async-start | bytes 7864320 | tf_op jit(solution)/shard_map/all_gather | solution.py:318
  77.7 50.1 %collective-permute-start.3 = (bf16[256,2048]{1,0:T(8,128)(2,1)}, bf16[256,2048]{1,0:T(8,128)(2,1)S(1)}, u32[]{:S(2)}, u32[]{:S(2)}) collective-permute-start(bf16[256,2048]{1,0:T(8,128)(2,1)} %get-tuple-element.42), channel_id=1, source_target_pairs={{0,4},{4,0},{1,5},{5,1},{2,6},{6,2},{3,7},{7,3},{8,12},{12,8},{9,1... | collective-permute-start | bytes 3145736 | tf_op jit(solution)/shard_map/ppermute | solution.py:45
  79.6 52.9 %collective-permute-start = (bf16[256,2048]{1,0:T(8,128)(2,1)}, bf16[256,2048]{1,0:T(8,128)(2,1)}, u32[]{:S(2)}, u32[]{:S(2)}) collective-permute-start(bf16[256,2048]{1,0:T(8,128)(2,1)} %get-tuple-element.42), channel_id=1, source_target_pairs={{0,1},{1,0},{2,3},{3,2},{4,5},{5,4},{6,7},{7,6},{8,9},{9,8},{10,11... | collective-permute-start | bytes 3145736 | tf_op jit(solution)/shard_map/ppermute | solution.py:45
  95.2 47.4 %collective-permute-start.2 = (bf16[256,2048]{1,0:T(8,128)(2,1)}, bf16[256,2048]{1,0:T(8,128)(2,1)}, u32[]{:S(2)}, u32[]{:S(2)}) collective-permute-start(bf16[256,2048]{1,0:T(8,128)(2,1)} %collective-permute-done.1), channel_id=1, source_target_pairs={{0,1},{1,0},{2,3},{3,2},{4,5},{5,4},{6,7},{7,6},{8,9},{9,8},{10,11... | collective-permute-start | bytes 3145736 | tf_op jit(solution)/shard_map/ppermute | solution.py:45
  128.6 19.1 %collective-permute-start.5 = (bf16[128,2048]{1,0:T(8,128)(2,1)}, bf16[128,2048]{1,0:T(8,128)(2,1)}, u32[]{:S(2)}, u32[]{:S(2)}) collective-permute-start(bf16[128,2048]{1,0:T(8,128)(2,1)} %slice.395), channel_id=1, source_target_pairs={{0,2},{2,0},{1,3},{3,1},{4,6},{6,4},{5,7},{7,5},{8,10},{10,8},{9,1... | collective-permute-start | bytes 1572872 | tf_op jit(solution)/shard_map/ppermute | solution.py:45
  132.0 15.7 %collective-permute-start.6 = (bf16[128,2048]{1,0:T(8,128)(2,1)}, bf16[128,2048]{1,0:T(8,128)(2,1)}, u32[]{:S(2)}, u32[]{:S(2)}) collective-permute-start(bf16[128,2048]{1,0:T(8,128)(2,1)} %slice.396), channel_id=1, source_target_pairs={{0,4},{4,0},{1,5},{5,1},{2,6},{6,2},{3,7},{7,3},{8,12},{12,8},{9,1... | collective-permute-start | bytes 1572872 | tf_op jit(solution)/shard_map/ppermute | solution.py:45
  132.5 15.7 %collective-permute-start.4 = (bf16[256,2048]{1,0:T(8,128)(2,1)S(1)}, bf16[256,2048]{1,0:T(8,128)(2,1)}, u32[]{:S(2)}, u32[]{:S(2)}) collective-permute-start(bf16[256,2048]{1,0:T(8,128)(2,1)S(1)} %collective-permute-done.3), channel_id=1, source_target_pairs={{0,1},{1,0},{2,3},{3,2},{4,5},{5,4},{6,7},{7,6},{8,9},{9,8},{10,11... | collective-permute-start | bytes 3145736 | tf_op jit(solution)/shard_map/ppermute | solution.py:45
  137.2 27.6 %collective-permute-start.17 = (bf16[256,2048]{1,0:T(8,128)(2,1)}, bf16[256,2048]{1,0:T(8,128)(2,1)S(1)}, u32[]{:S(2)}, u32[]{:S(2)}) collective-permute-start(bf16[256,2048]{1,0:T(8,128)(2,1)} %all-gather.7.cloned.1.call-done), channel_id=1, source_target_pairs={{0,2},{2,0},{1,3},{3,1},{4,6},{6,4},{5,7},{7,5},{8,10},{10,8},{9,1... | collective-permute-start | bytes 3145736 | tf_op jit(solution)/shard_map/ppermute | solution.py:45
  142.5 190.0 %all-gather.11.cloned.1.call-start = ((), (), s32[]{:S(2)}) async-start(), calls=%async_computation.14 | async-start | bytes 3932160 | tf_op jit(solution)/shard_map/all_gather | solution.py:318
  142.6 25.6 %collective-permute-start.19 = (bf16[256,2048]{1,0:T(8,128)(2,1)}, bf16[256,2048]{1,0:T(8,128)(2,1)S(1)}, u32[]{:S(2)}, u32[]{:S(2)}) collective-permute-start(bf16[256,2048]{1,0:T(8,128)(2,1)} %all-gather.7.cloned.1.call-done), channel_id=1, source_target_pairs={{0,4},{4,0},{1,5},{5,1},{2,6},{6,2},{3,7},{7,3},{8,12},{12,8},{9,1... | collective-permute-start | bytes 3145736 | tf_op jit(solution)/shard_map/ppermute | solution.py:45
  147.7 23.1 %collective-permute-start.16 = (bf16[256,2048]{1,0:T(8,128)(2,1)S(1)}, bf16[256,2048]{1,0:T(8,128)(2,1)S(1)}, u32[]{:S(2)}, u32[]{:S(2)}) collective-permute-start(bf16[256,2048]{1,0:T(8,128)(2,1)S(1)} %copy-done.19), channel_id=1, source_target_pairs={{0,1},{1,0},{2,3},{3,2},{4,5},{5,4},{6,7},{7,6},{8,9},{9,8},{10,11... | collective-permute-start | bytes 3145736 | tf_op jit(solution)/shard_map/ppermute | solution.py:45
  147.7 18.9 %collective-permute-start.7 = (bf16[128,2048]{1,0:T(8,128)(2,1)}, bf16[128,2048]{1,0:T(8,128)(2,1)S(1)}, u32[]{:S(2)}, u32[]{:S(2)}) collective-permute-start(bf16[128,2048]{1,0:T(8,128)(2,1)} %collective-permute-done.5), channel_id=1, source_target_pairs={{0,1},{1,0},{2,3},{3,2},{4,5},{5,4},{6,7},{7,6},{8,9},{9,8},{10,11... | collective-permute-start | bytes 1572872 | tf_op jit(solution)/shard_map/ppermute | solution.py:45
  148.2 20.1 %collective-permute-start.8 = (bf16[128,2048]{1,0:T(8,128)(2,1)}, bf16[128,2048]{1,0:T(8,128)(2,1)S(1)}, u32[]{:S(2)}, u32[]{:S(2)}) collective-permute-start(bf16[128,2048]{1,0:T(8,128)(2,1)} %collective-permute-done.6), channel_id=1, source_target_pairs={{0,1},{1,0},{2,3},{3,2},{4,5},{5,4},{6,7},{7,6},{8,9},{9,8},{10,11... | collective-permute-start | bytes 1572872 | tf_op jit(solution)/shard_map/ppermute | solution.py:45
  166.6 92.7 %collective-permute-start.48 = (bf16[128,2048]{1,0:T(8,128)(2,1)}, bf16[128,2048]{1,0:T(8,128)(2,1)}, u32[]{:S(2)}, u32[]{:S(2)}) collective-permute-start(bf16[128,2048]{1,0:T(8,128)(2,1)} %slice.432), channel_id=1, source_target_pairs={{0,4},{4,0},{1,5},{5,1},{2,6},{6,2},{3,7},{7,3},{8,12},{12,8},{9,1... | collective-permute-start | bytes 1572872 | tf_op jit(solution)/shard_map/ppermute | solution.py:45
  168.2 24.3 %collective-permute-start.20 = (bf16[256,2048]{1,0:T(8,128)(2,1)S(1)}, bf16[256,2048]{1,0:T(8,128)(2,1)S(1)}, u32[]{:S(2)}, u32[]{:S(2)}) collective-permute-start(bf16[256,2048]{1,0:T(8,128)(2,1)S(1)} %collective-permute-done.19), channel_id=1, source_target_pairs={{0,1},{1,0},{2,3},{3,2},{4,5},{5,4},{6,7},{7,6},{8,9},{9,8},{10,11... | collective-permute-start | bytes 3145736 | tf_op jit(solution)/shard_map/ppermute | solution.py:45
  170.9 21.6 %collective-permute-start.22 = (bf16[128,2048]{1,0:T(8,128)(2,1)S(1)}, bf16[128,2048]{1,0:T(8,128)(2,1)S(1)}, u32[]{:S(2)}, u32[]{:S(2)}) collective-permute-start(bf16[128,2048]{1,0:T(8,128)(2,1)S(1)} %slice.408), channel_id=1, source_target_pairs={{0,4},{4,0},{1,5},{5,1},{2,6},{6,2},{3,7},{7,3},{8,12},{12,8},{9,1... | collective-permute-start | bytes 1572872 | tf_op jit(solution)/shard_map/ppermute | solution.py:45
  174.6 85.7 %collective-permute-start.47 = (bf16[128,2048]{1,0:T(8,128)(2,1)}, bf16[128,2048]{1,0:T(8,128)(2,1)}, u32[]{:S(2)}, u32[]{:S(2)}) collective-permute-start(bf16[128,2048]{1,0:T(8,128)(2,1)} %slice.431), channel_id=1, source_target_pairs={{0,2},{2,0},{1,3},{3,1},{4,6},{6,4},{5,7},{7,5},{8,10},{10,8},{9,1... | collective-permute-start | bytes 1572872 | tf_op jit(solution)/shard_map/ppermute | solution.py:45
  184.0 78.5 %collective-permute-start.44 = (bf16[256,2048]{1,0:T(8,128)(2,1)}, bf16[256,2048]{1,0:T(8,128)(2,1)}, u32[]{:S(2)}, u32[]{:S(2)}) collective-permute-start(bf16[256,2048]{1,0:T(8,128)(2,1)} %collective-permute-done.43), channel_id=1, source_target_pairs={{0,1},{1,0},{2,3},{3,2},{4,5},{5,4},{6,7},{7,6},{8,9},{9,8},{10,11... | collective-permute-start | bytes 3145736 | tf_op jit(solution)/shard_map/ppermute | solution.py:45
  243.3 25.6 %collective-permute-start.46 = (bf16[256,2048]{1,0:T(8,128)(2,1)}, bf16[256,2048]{1,0:T(8,128)(2,1)}, u32[]{:S(2)}, u32[]{:S(2)}) collective-permute-start(bf16[256,2048]{1,0:T(8,128)(2,1)} %collective-permute-done.45), channel_id=1, source_target_pairs={{0,1},{1,0},{2,3},{3,2},{4,5},{5,4},{6,7},{7,6},{8,9},{9,8},{10,11... | collective-permute-start | bytes 3145736 | tf_op jit(solution)/shard_map/ppermute | solution.py:45
  255.4 25.3 %collective-permute-start.26 = (bf16[256,2048]{1,0:T(8,128)(2,1)}, bf16[256,2048]{1,0:T(8,128)(2,1)}, u32[]{:S(2)}, u32[]{:S(2)}) collective-permute-start(bf16[256,2048]{1,0:T(8,128)(2,1)} %get-tuple-element.40), channel_id=1, source_target_pairs={{0,2},{2,0},{1,3},{3,1},{4,6},{6,4},{5,7},{7,5},{8,10},{10,8},{9,1... | collective-permute-start | bytes 3145736 | tf_op jit(solution)/shard_map/ppermute | solution.py:45
  259.4 34.7 %collective-permute-start.50 = (bf16[128,2048]{1,0:T(8,128)(2,1)}, bf16[128,2048]{1,0:T(8,128)(2,1)}, u32[]{:S(2)}, u32[]{:S(2)}) collective-permute-start(bf16[128,2048]{1,0:T(8,128)(2,1)} %collective-permute-done.48), channel_id=1, source_target_pairs={{0,1},{1,0},{2,3},{3,2},{4,5},{5,4},{6,7},{7,6},{8,9},{9,8},{10,11... | collective-permute-start | bytes 1572872 | tf_op jit(solution)/shard_map/ppermute | solution.py:45
  260.3 23.5 %collective-permute-start.49 = (bf16[128,2048]{1,0:T(8,128)(2,1)}, bf16[128,2048]{1,0:T(8,128)(2,1)}, u32[]{:S(2)}, u32[]{:S(2)}) collective-permute-start(bf16[128,2048]{1,0:T(8,128)(2,1)} %collective-permute-done.47), channel_id=1, source_target_pairs={{0,1},{1,0},{2,3},{3,2},{4,5},{5,4},{6,7},{7,6},{8,9},{9,8},{10,11... | collective-permute-start | bytes 1572872 | tf_op jit(solution)/shard_map/ppermute | solution.py:45
  262.4 387.0 %reduce-scatter.11.cloned.1.call-start = ((), (), s32[]{:S(2)}) async-start(), calls=%async_computation.18 | async-start | bytes 3932160 | tf_op jit(solution)/shard_map/reduce_scatter | solution.py:375
  264.8 25.7 %collective-permute-start.28 = (bf16[256,2048]{1,0:T(8,128)(2,1)}, bf16[256,2048]{1,0:T(8,128)(2,1)S(1)}, u32[]{:S(2)}, u32[]{:S(2)}) collective-permute-start(bf16[256,2048]{1,0:T(8,128)(2,1)} %get-tuple-element.40), channel_id=1, source_target_pairs={{0,4},{4,0},{1,5},{5,1},{2,6},{6,2},{3,7},{7,3},{8,12},{12,8},{9,1... | collective-permute-start | bytes 3145736 | tf_op jit(solution)/shard_map/ppermute | solution.py:45
  268.9 27.1 %collective-permute-start.25 = (bf16[256,2048]{1,0:T(8,128)(2,1)}, bf16[256,2048]{1,0:T(8,128)(2,1)S(1)}, u32[]{:S(2)}, u32[]{:S(2)}) collective-permute-start(bf16[256,2048]{1,0:T(8,128)(2,1)} %get-tuple-element.40), channel_id=1, source_target_pairs={{0,1},{1,0},{2,3},{3,2},{4,5},{5,4},{6,7},{7,6},{8,9},{9,8},{10,11... | collective-permute-start | bytes 3145736 | tf_op jit(solution)/shard_map/ppermute | solution.py:45
  280.7 26.1 %collective-permute-start.27 = (bf16[256,2048]{1,0:T(8,128)(2,1)}, bf16[256,2048]{1,0:T(8,128)(2,1)S(1)}, u32[]{:S(2)}, u32[]{:S(2)}) collective-permute-start(bf16[256,2048]{1,0:T(8,128)(2,1)} %collective-permute-done.26), channel_id=1, source_target_pairs={{0,1},{1,0},{2,3},{3,2},{4,5},{5,4},{6,7},{7,6},{8,9},{9,8},{10,11... | collective-permute-start | bytes 3145736 | tf_op jit(solution)/shard_map/ppermute | solution.py:45
  354.6 61.5 %collective-permute-start.34 = (bf16[256,2048]{1,0:T(8,128)(2,1)}, bf16[256,2048]{1,0:T(8,128)(2,1)}, u32[]{:S(2)}, u32[]{:S(2)}) collective-permute-start(bf16[256,2048]{1,0:T(8,128)(2,1)} %convolution_convert_fusion.27), channel_id=1, source_target_pairs={{0,1},{1,0},{2,3},{3,2},{4,5},{5,4},{6,7},{7,6},{8,9},{9,8},{10,11... | collective-permute-start | bytes 3145736 | tf_op jit(solution)/shard_map/ppermute | solution.py:45
  357.3 15.3 %collective-permute-start.35 = (bf16[256,2048]{1,0:T(8,128)(2,1)S(1)}, bf16[256,2048]{1,0:T(8,128)(2,1)S(1)}, u32[]{:S(2)}, u32[]{:S(2)}) collective-permute-start(bf16[256,2048]{1,0:T(8,128)(2,1)S(1)} %convolution_convert_fusion.25), channel_id=1, source_target_pairs={{0,1},{1,0},{2,3},{3,2},{4,5},{5,4},{6,7},{7,6},{8,9},{9,8},{10,11... | collective-permute-start | bytes 3145736 | tf_op jit(solution)/shard_map/ppermute | solution.py:45
  360.6 17.4 %collective-permute-start.36 = (bf16[256,2048]{1,0:T(8,128)(2,1)}, bf16[256,2048]{1,0:T(8,128)(2,1)}, u32[]{:S(2)}, u32[]{:S(2)}) collective-permute-start(bf16[256,2048]{1,0:T(8,128)(2,1)} %convolution_convert_fusion.23), channel_id=1, source_target_pairs={{0,1},{1,0},{2,3},{3,2},{4,5},{5,4},{6,7},{7,6},{8,9},{9,8},{10,11... | collective-permute-start | bytes 3145736 | tf_op jit(solution)/shard_map/ppermute | solution.py:45
  365.4 16.2 %collective-permute-start.56 = (bf16[256,2048]{1,0:T(8,128)(2,1)S(1)}, bf16[256,2048]{1,0:T(8,128)(2,1)}, u32[]{:S(2)}, u32[]{:S(2)}) collective-permute-start(bf16[256,2048]{1,0:T(8,128)(2,1)S(1)} %convolution_convert_fusion.3), channel_id=1, source_target_pairs={{0,1},{1,0},{2,3},{3,2},{4,5},{5,4},{6,7},{7,6},{8,9},{9,8},{10,11... | collective-permute-start | bytes 3145736 | tf_op jit(solution)/shard_map/ppermute | solution.py:45
  378.1 57.4 %collective-permute-start.51 = (bf16[256,2048]{1,0:T(8,128)(2,1)}, bf16[256,2048]{1,0:T(8,128)(2,1)}, u32[]{:S(2)}, u32[]{:S(2)}) collective-permute-start(bf16[256,2048]{1,0:T(8,128)(2,1)} %convolution_convert_fusion.9), channel_id=1, source_target_pairs={{0,1},{1,0},{2,3},{3,2},{4,5},{5,4},{6,7},{7,6},{8,9},{9,8},{10,11... | collective-permute-start | bytes 3145736 | tf_op jit(solution)/shard_map/ppermute | solution.py:45
  388.3 26.1 %collective-permute-start.54 = (bf16[128,2048]{1,0:T(8,128)(2,1)S(1)}, bf16[128,2048]{1,0:T(8,128)(2,1)S(1)}, u32[]{:S(2)}, u32[]{:S(2)}) collective-permute-start(bf16[128,2048]{1,0:T(8,128)(2,1)S(1)} %get-tuple-element.58), channel_id=1, source_target_pairs={{0,4},{4,0},{1,5},{5,1},{2,6},{6,2},{3,7},{7,3},{8,12},{12,8},{9,1... | collective-permute-start | bytes 1572872 | tf_op jit(solution)/shard_map/ppermute | solution.py:45
  400.5 35.0 %collective-permute-start.38 = (bf16[256,2048]{1,0:T(8,128)(2,1)}, bf16[256,2048]{1,0:T(8,128)(2,1)}, u32[]{:S(2)}, u32[]{:S(2)}) collective-permute-start(bf16[256,2048]{1,0:T(8,128)(2,1)} %pad_maximum_fusion.2), channel_id=1, source_target_pairs={{0,2},{2,0},{1,3},{3,1},{4,6},{6,4},{5,7},{7,5},{8,10},{10,8},{9,1... | collective-permute-start | bytes 3145736 | tf_op jit(solution)/shard_map/ppermute | solution.py:45
  411.7 26.4 %collective-permute-start.41 = (bf16[256,2048]{1,0:T(8,128)(2,1)}, bf16[256,2048]{1,0:T(8,128)(2,1)}, u32[]{:S(2)}, u32[]{:S(2)}) collective-permute-start(bf16[256,2048]{1,0:T(8,128)(2,1)} %pad_maximum_fusion.3), channel_id=1, source_target_pairs={{0,4},{4,0},{1,5},{5,1},{2,6},{6,2},{3,7},{7,3},{8,12},{12,8},{9,1... | collective-permute-start | bytes 3145736 | tf_op jit(solution)/shard_map/ppermute | solution.py:45
  414.4 43.9 %collective-permute-start.58 = (bf16[256,2048]{1,0:T(8,128)(2,1)}, bf16[256,2048]{1,0:T(8,128)(2,1)}, u32[]{:S(2)}, u32[]{:S(2)}) collective-permute-start(bf16[256,2048]{1,0:T(8,128)(2,1)} %pad_maximum_fusion.5), channel_id=1, source_target_pairs={{0,4},{4,0},{1,5},{5,1},{2,6},{6,2},{3,7},{7,3},{8,12},{12,8},{9,1... | collective-permute-start | bytes 3145736 | tf_op jit(solution)/shard_map/ppermute | solution.py:45
  416.1 42.1 %collective-permute-start.55 = (bf16[256,2048]{1,0:T(8,128)(2,1)}, bf16[256,2048]{1,0:T(8,128)(2,1)}, u32[]{:S(2)}, u32[]{:S(2)}) collective-permute-start(bf16[256,2048]{1,0:T(8,128)(2,1)} %pad_maximum_fusion.4), channel_id=1, source_target_pairs={{0,2},{2,0},{1,3},{3,1},{4,6},{6,4},{5,7},{7,5},{8,10},{10,8},{9,1... | collective-permute-start | bytes 3145736 | tf_op jit(solution)/shard_map/ppermute | solution.py:45
  427.3 238.3 %reduce-scatter.5.cloned.1.call-start = ((), (), s32[]{:S(2)}) async-start(), calls=%async_computation.15 | async-start | bytes 3932160 | tf_op jit(solution)/shard_map/reduce_scatter | solution.py:375
  472.4 16.9 %collective-permute-start.65 = (bf16[256,256]{1,0:T(8,128)(2,1)S(1)}, bf16[256,256]{1,0:T(8,128)(2,1)S(1)}, u32[]{:S(2)}, u32[]{:S(2)}) collective-permute-start(bf16[256,256]{1,0:T(8,128)(2,1)S(1)} %get-tuple-element.51), channel_id=1, source_target_pairs={{0,7},{1,6},{2,5},{3,4},{4,3},{5,2},{6,1},{7,0},{8,15},{9,14},{10,... | collective-permute-start | bytes 393224 | tf_op jit(solution)/shard_map/ppermute | solution.py:78
  472.5 16.8 %collective-permute-start.64 = (bf16[256,256]{1,0:T(8,128)(2,1)S(1)}, bf16[256,256]{1,0:T(8,128)(2,1)S(1)}, u32[]{:S(2)}, u32[]{:S(2)}) collective-permute-start(bf16[256,256]{1,0:T(8,128)(2,1)S(1)} %get-tuple-element.52), channel_id=1, source_target_pairs={{0,6},{1,7},{2,4},{3,5},{4,2},{5,3},{6,0},{7,1},{8,14},{9,15},{10,... | collective-permute-start | bytes 393224 | tf_op jit(solution)/shard_map/ppermute | solution.py:78
  473.7 15.5 %collective-permute-start.63 = (bf16[256,256]{1,0:T(8,128)(2,1)S(1)}, bf16[256,256]{1,0:T(8,128)(2,1)S(1)}, u32[]{:S(2)}, u32[]{:S(2)}) collective-permute-start(bf16[256,256]{1,0:T(8,128)(2,1)S(1)} %get-tuple-element.53), channel_id=1, source_target_pairs={{0,5},{1,4},{2,7},{3,6},{4,1},{5,0},{6,3},{7,2},{8,13},{9,12},{10,... | collective-permute-start | bytes 393224 | tf_op jit(solution)/shard_map/ppermute | solution.py:78
  525.4 175.8 %reduce-scatter.9.cloned.1.call-start = ((), (), s32[]{:S(2)}) async-start(), calls=%async_computation.17 | async-start | bytes 7864320 | tf_op jit(solution)/shard_map/reduce_scatter | solution.py:375
  546.2 24.9 %collective-permute-start.77 = (bf16[256,2048]{1,0:T(8,128)(2,1)S(1)}, bf16[256,2048]{1,0:T(8,128)(2,1)S(1)}, u32[]{:S(2)}, u32[]{:S(2)}) collective-permute-start(bf16[256,2048]{1,0:T(8,128)(2,1)S(1)} %copy-done.18), channel_id=1, source_target_pairs={{0,4},{4,0},{1,5},{5,1},{2,6},{6,2},{3,7},{7,3},{8,12},{12,8},{9,1... | collective-permute-start | bytes 3145736 | tf_op jit(solution)/shard_map/ppermute | solution.py:45
  547.6 24.6 %collective-permute-start.75 = (bf16[256,2048]{1,0:T(8,128)(2,1)S(1)}, bf16[256,2048]{1,0:T(8,128)(2,1)S(1)}, u32[]{:S(2)}, u32[]{:S(2)}) collective-permute-start(bf16[256,2048]{1,0:T(8,128)(2,1)S(1)} %copy-done.18), channel_id=1, source_target_pairs={{0,2},{2,0},{1,3},{3,1},{4,6},{6,4},{5,7},{7,5},{8,10},{10,8},{9,1... | collective-permute-start | bytes 3145736 | tf_op jit(solution)/shard_map/ppermute | solution.py:45
  548.7 23.5 %collective-permute-start.74 = (bf16[256,2048]{1,0:T(8,128)(2,1)S(1)}, bf16[256,2048]{1,0:T(8,128)(2,1)}, u32[]{:S(2)}, u32[]{:S(2)}) collective-permute-start(bf16[256,2048]{1,0:T(8,128)(2,1)S(1)} %copy-done.18), channel_id=1, source_target_pairs={{0,1},{1,0},{2,3},{3,2},{4,5},{5,4},{6,7},{7,6},{8,9},{9,8},{10,11... | collective-permute-start | bytes 3145736 | tf_op jit(solution)/shard_map/ppermute | solution.py:45
  554.5 58.2 %collective-permute-start.66 = (bf16[256,2048]{1,0:T(8,128)(2,1)S(1)}, bf16[256,2048]{1,0:T(8,128)(2,1)S(1)}, u32[]{:S(2)}, u32[]{:S(2)}) collective-permute-start(bf16[256,2048]{1,0:T(8,128)(2,1)S(1)} %convolution_convert_fusion.18), channel_id=1, source_target_pairs={{0,1},{1,0},{2,3},{3,2},{4,5},{5,4},{6,7},{7,6},{8,9},{9,8},{10,11... | collective-permute-start | bytes 3145736 | tf_op jit(solution)/shard_map/ppermute | solution.py:45
  557.4 19.5 %collective-permute-start.68 = (bf16[256,2048]{1,0:T(8,128)(2,1)S(1)}, bf16[256,2048]{1,0:T(8,128)(2,1)S(1)}, u32[]{:S(2)}, u32[]{:S(2)}) collective-permute-start(bf16[256,2048]{1,0:T(8,128)(2,1)S(1)} %convolution_convert_fusion.14), channel_id=1, source_target_pairs={{0,1},{1,0},{2,3},{3,2},{4,5},{5,4},{6,7},{7,6},{8,9},{9,8},{10,11... | collective-permute-start | bytes 3145736 | tf_op jit(solution)/shard_map/ppermute | solution.py:45
  572.2 34.5 %collective-permute-start.79 = (bf16[128,2048]{1,0:T(8,128)(2,1)S(1)}, bf16[128,2048]{1,0:T(8,128)(2,1)S(1)}, u32[]{:S(2)}, u32[]{:S(2)}) collective-permute-start(bf16[128,2048]{1,0:T(8,128)(2,1)S(1)} %slice.477), channel_id=1, source_target_pairs={{0,2},{2,0},{1,3},{3,1},{4,6},{6,4},{5,7},{7,5},{8,10},{10,8},{9,1... | collective-permute-start | bytes 1572872 | tf_op jit(solution)/shard_map/ppermute | solution.py:45
  576.9 31.6 %collective-permute-start.80 = (bf16[128,2048]{1,0:T(8,128)(2,1)S(1)}, bf16[128,2048]{1,0:T(8,128)(2,1)S(1)}, u32[]{:S(2)}, u32[]{:S(2)}) collective-permute-start(bf16[128,2048]{1,0:T(8,128)(2,1)S(1)} %slice.478), channel_id=1, source_target_pairs={{0,4},{4,0},{1,5},{5,1},{2,6},{6,2},{3,7},{7,3},{8,12},{12,8},{9,1... | collective-permute-start | bytes 1572872 | tf_op jit(solution)/shard_map/ppermute | solution.py:45
  578.9 23.3 %collective-permute-start.69 = (bf16[128,2048]{1,0:T(8,128)(2,1)S(1)}, bf16[128,2048]{1,0:T(8,128)(2,1)S(1)}, u32[]{:S(2)}, u32[]{:S(2)}) collective-permute-start(bf16[128,2048]{1,0:T(8,128)(2,1)S(1)} %get-tuple-element.49), channel_id=1, source_target_pairs={{0,4},{4,0},{1,5},{5,1},{2,6},{6,2},{3,7},{7,3},{8,12},{12,8},{9,1... | collective-permute-start | bytes 1572872 | tf_op jit(solution)/shard_map/ppermute | solution.py:45
  581.2 21.1 %collective-permute-start.72 = (bf16[128,2048]{1,0:T(8,128)(2,1)S(1)}, bf16[128,2048]{1,0:T(8,128)(2,1)S(1)}, u32[]{:S(2)}, u32[]{:S(2)}) collective-permute-start(bf16[128,2048]{1,0:T(8,128)(2,1)S(1)} %get-tuple-element.50), channel_id=1, source_target_pairs={{0,2},{2,0},{1,3},{3,1},{4,6},{6,4},{5,7},{7,5},{8,10},{10,8},{9,1... | collective-permute-start | bytes 1572872 | tf_op jit(solution)/shard_map/ppermute | solution.py:45
  604.9 25.2 %collective-permute-start.70 = (bf16[256,2048]{1,0:T(8,128)(2,1)S(1)}, bf16[256,2048]{1,0:T(8,128)(2,1)S(1)}, u32[]{:S(2)}, u32[]{:S(2)}) collective-permute-start(bf16[256,2048]{1,0:T(8,128)(2,1)S(1)} %pad_maximum_fusion.6), channel_id=1, source_target_pairs={{0,2},{2,0},{1,3},{3,1},{4,6},{6,4},{5,7},{7,5},{8,10},{10,8},{9,1... | collective-permute-start | bytes 3145736 | tf_op jit(solution)/shard_map/ppermute | solution.py:45
  606.8 25.0 %collective-permute-start.73 = (bf16[256,2048]{1,0:T(8,128)(2,1)S(1)}, bf16[256,2048]{1,0:T(8,128)(2,1)S(1)}, u32[]{:S(2)}, u32[]{:S(2)}) collective-permute-start(bf16[256,2048]{1,0:T(8,128)(2,1)S(1)} %pad_maximum_fusion.7), channel_id=1, source_target_pairs={{0,4},{4,0},{1,5},{5,1},{2,6},{6,2},{3,7},{7,3},{8,12},{12,8},{9,1... | collective-permute-start | bytes 3145736 | tf_op jit(solution)/shard_map/ppermute | solution.py:45
  608.5 32.3 %collective-permute-start.82 = (bf16[128,2048]{1,0:T(8,128)(2,1)S(1)}, bf16[128,2048]{1,0:T(8,128)(2,1)S(1)}, u32[]{:S(2)}, u32[]{:S(2)}) collective-permute-start(bf16[128,2048]{1,0:T(8,128)(2,1)S(1)} %collective-permute-done.80), channel_id=1, source_target_pairs={{0,1},{1,0},{2,3},{3,2},{4,5},{5,4},{6,7},{7,6},{8,9},{9,8},{10,11... | collective-permute-start | bytes 1572872 | tf_op jit(solution)/shard_map/ppermute | solution.py:45
  649.5 16.1 %all-to-all-start.6 = ((bf16[8,64,768]{2,1,0:T(8,128)(2,1)}), bf16[8,64,768]{2,1,0:T(8,128)(2,1)S(1)}, u32[]{:S(2)}, u32[]{:S(2)}) async-start(bf16[8,64,768]{2,1,0:T(8,128)(2,1)} %bitcast.163), calls=%async_computation.10 | async-start | bytes 1572864 | tf_op jit(solution)/shard_map/all_to_all | solution.py:83
  653.0 78.8 %reduce-scatter.7.cloned.1.call-start = ((), (), s32[]{:S(2)}) async-start(), calls=%async_computation.16 | async-start | bytes 1310720 | tf_op jit(solution)/shard_map/reduce_scatter | solution.py:375
  701.2 46.6 %all-to-all-start.5 = ((bf16[8,64,1536]{2,1,0:T(8,128)(2,1)}), bf16[8,64,1536]{2,1,0:T(8,128)(2,1)}, u32[]{:S(2)}, u32[]{:S(2)}) async-start(bf16[8,64,1536]{2,1,0:T(8,128)(2,1)} %bitcast.162), calls=%async_computation.8 | async-start | bytes 3145728 | tf_op jit(solution)/shard_map/all_to_all | solution.py:83
  (76 other events, 1033.4 us)
Sparse Core Ops, SparseCore 0:
  9.6 30.6 all-gather.6
  41.8 62.9 all-gather.4
  142.7 117.1 all-gather.8
  262.5 64.5 all-gather.10
  427.4 61.6 reduce-scatter.10
  525.5 61.5 reduce-scatter.4
  589.4 111.8 reduce-scatter.8
  704.1 27.6 reduce-scatter.6

commit v2 on v1

v2 whole, which is shorter than its diff:
```python
import functools

import jax
import jax.numpy as jnp
from jax import lax
from jax.experimental import pallas as pl
from jax.experimental.pallas import tpu as pltpu
from jax.sharding import Mesh
from jax.sharding import PartitionSpec as P

HEAD_DIM = 64
ROT_DIMS = 16
PAIR = 2 * HEAD_DIM
PLANE = ("y", "x", "c")
ALL = ("g", "y", "x", "c")
bf16 = jnp.bfloat16
f32 = jnp.float32

epsilon = 1e-05
neg_large = -1e30
rope_base = 10000.0
score_scale = 0.125


def layer_stats(values):
    mean_value = jnp.mean(values, axis=-1, keepdims=True)
    centered = values - mean_value
    inv_std = lax.rsqrt(jnp.mean(centered * centered, axis=-1, keepdims=True) + epsilon)
    return (centered * inv_std, inv_std)


def norm_back(grad_rows, normed, inv_std, gain_row):
    scaled = grad_rows * gain_row
    inner = jnp.mean(scaled * normed, axis=-1, keepdims=True)
    return inv_std * (scaled - jnp.mean(scaled, axis=-1, keepdims=True) - normed * inner)


def contract(left, right, left_dim, right_dim, kind=f32):
    return lax.dot_general(
        left, right, (((left_dim,), (right_dim,)), ((), ())), preferred_element_type=f32
    ).astype(kind)


def after(values, *others):
    return lax.optimization_barrier((values, *others))[0]


def fenced(function, *operands):
    shapes = jax.eval_shape(function, *operands)
    return lax.cond(
        lax.axis_index("g") < lax.axis_size("g"),
        function,
        lambda *_: jax.tree.map(lambda leaf: jnp.zeros(leaf.shape, leaf.dtype), shapes),
        *operands,
    )


def swap(values, axis):
    return lax.ppermute(values, axis, [(0, 1), (1, 0)])


def join_kernel(*refs):
    *piece_refs, out_ref = refs
    at = 0
    for piece in piece_refs:
        out_ref[at : at + piece.shape[0], :] = piece[...]
        at += piece.shape[0]


def join(pieces, lead=0):
    rows, width = sum(piece.shape[0] for piece in pieces), pieces[0].shape[1]
    return pl.pallas_call(
        join_kernel,
        grid=(4,),
        in_specs=[pl.BlockSpec((piece.shape[0], width // 4), lambda i: (0, i)) for piece in pieces],
        out_specs=pl.BlockSpec((rows, width // 4), lambda i: (0, i)),
        out_shape=jax.ShapeDtypeStruct((rows, width), pieces[0].dtype),
        **limits(lead),
    )(*pieces)


def chip_pieces(rows, *first):
    half = rows.shape[0] // 2
    over_x = swap(rows, "x")
    over_y = swap(rows, "y")
    if first:
        over_x, over_y = lax.optimization_barrier((over_x, over_y, *first))[:2]
    return [rows, over_x, over_y, swap(over_y[:half], "x"), swap(over_x[half:], "y")]


def halves_of(pieces, *first, lead=0):
    if first:
        pieces = lax.optimization_barrier((*pieces, *first))[: len(pieces)]
    mine = join(pieces, lead)
    return mine, swap(mine, "c")


def send_kernel(left_ref, right_ref, out_ref):
    out_ref[...] = nt(left_ref[...], right_ref[...]).astype(bf16)


def keep_kernel(left_ref, right_ref, other_ref, corner_ref, x_ref, y_ref, own_ref):
    s = pl.program_id(0)
    total = nt(left_ref[...], right_ref[...]) + other_ref[...].astype(f32)

    @pl.when(s == 0)
    def _():
        corner_ref[...] = total.astype(bf16)

    for which, ref in ((1, x_ref), (2, y_ref), (3, own_ref)):

        @pl.when(s == which)
        def _(ref=ref):
            ref[...] = total.astype(ref.dtype)


def corner_first(s):
    return jnp.where(s == 0, 3, jnp.where(s == 3, 0, s))


def plane_send(left, right, at, lead=0):
    rows, depth, width = left.shape[0] // 8, left.shape[1], right.shape[0]
    terms = pl.pallas_call(
        send_kernel,
        grid=(2,),
        in_specs=[
            pl.BlockSpec((2 * rows, depth), lambda s: (s + 2, 0)),
            pl.BlockSpec((width, depth), lambda s: (0, at)),
        ],
        out_specs=pl.BlockSpec((2 * rows, width), lambda s: (s, 0)),
        out_shape=jax.ShapeDtypeStruct((4 * rows, width), bf16),
        **limits(lead),
    )(left, right)
    return swap(terms, "c")


def plane_keep(left, right, at, other, kind=f32, lead=0):
    rows, depth, width = left.shape[0] // 8, left.shape[1], right.shape[0]
    whole = pl.BlockSpec((rows, width), lambda s: (0, 0))
    return pl.pallas_call(
        keep_kernel,
        grid=(4,),
        in_specs=[
            pl.BlockSpec((rows, depth), lambda s: (corner_first(s), 0)),
            pl.BlockSpec((width, depth), lambda s: (0, at)),
            pl.BlockSpec((rows, width), lambda s: (corner_first(s), 0)),
        ],
        out_specs=[whole] * 4,
        out_shape=[jax.ShapeDtypeStruct((rows, width), kind) for kind in (bf16, kind, kind, f32)],
        **limits(lead),
    )(left, right, other)


def plane_direct(kept):
    corner, for_x, for_y, own = kept
    far = lax.ppermute(corner, ("y", "x"), [(0, 3), (1, 2), (2, 1), (3, 0)])
    return own, swap(for_x, "x"), swap(for_y, "y"), far


def plane_corner(kept):
    corner, for_x, for_y, own = kept
    half = corner.shape[0] // 2
    from_x = swap(corner[:half], "x")
    from_y = swap(corner[half:], "y")
    to_x = jnp.concatenate([for_x[:half], for_x[half:] + from_y.astype(f32)], axis=0).astype(bf16)
    to_y = jnp.concatenate([for_y[:half] + from_x.astype(f32), for_y[half:]], axis=0).astype(bf16)
    return own, to_x, to_y


def plane_neighbours(terms):
    own, to_x, to_y = terms
    return own, swap(to_x, "x"), swap(to_y, "y")


def total_of(terms):
    return sum(term.astype(f32) for term in terms[1:]) + terms[0]


def sum_kernel(count, *refs):
    *in_refs, out_ref = refs
    total = tn(in_refs[0][...], in_refs[count][...])
    for left_ref, right_ref in zip(in_refs[1:count], in_refs[count + 1 :]):
        total += tn(left_ref[...], right_ref[...])
    out_ref[...] = total.astype(bf16)


def row_sum(left, right, lead=0):
    width, columns = left[0].shape[1], right[0].shape[1]
    step = min(width, 512)
    rows = sum(piece.shape[0] for piece in left)
    return pl.pallas_call(
        functools.partial(sum_kernel, len(left)),
        grid=(width // step,),
        in_specs=[
            *[pl.BlockSpec((piece.shape[0], step), lambda i: (0, i)) for piece in left],
            *[pl.BlockSpec(piece.shape, lambda i: (0, 0)) for piece in right],
        ],
        out_specs=pl.BlockSpec((step, columns), lambda i: (i, 0)),
        out_shape=jax.ShapeDtypeStruct((width, columns), bf16),
        **limits(lead),
    )(*left, *right)


def deep_reduce(blocks):
    depth = lax.axis_index("g")
    slots = [lax.dynamic_index_in_dim(blocks, jnp.bitwise_xor(depth, j), 0, False) for j in range(4)]
    ends = lax.ppermute(slots[3], "g", [(0, 1), (3, 2)])
    middle = lax.ppermute(slots[3], "g", [(1, 2), (2, 1)])
    near = lax.ppermute(slots[1], "g", [(0, 1), (1, 0), (2, 3), (3, 2)])
    far = lax.ppermute(
        (slots[2].astype(f32) + ends.astype(f32)).astype(bf16), "g", [(0, 2), (1, 3), (2, 0), (3, 1)]
    )
    return slots[0].astype(f32) + middle.astype(f32) + near.astype(f32) + far.astype(f32)


def plane_all_to_all(blocks):
    return lax.all_to_all(blocks, PLANE, 0, 0, tiled=True)


def turned(rows, cosine, sine, first):
    partner = jnp.where(first, pltpu.roll(rows, PAIR - ROT_DIMS // 2, 1), pltpu.roll(rows, ROT_DIMS // 2, 1))
    return rows * cosine + partner * sine


def lanes_of(rows):
    return lax.broadcasted_iota(jnp.int32, (rows, PAIR), 1)


def keep_head(values, head):
    lane = lanes_of(values.shape[0])
    inside = lane < HEAD_DIM if head == 0 else lane >= HEAD_DIM
    return jnp.where(inside, values, jnp.zeros_like(values))


def allowed_block(seg_col, seg_row, block, rows):
    same = seg_col[0, : (block + 1) * rows, :] == seg_row[0, :, block * rows : (block + 1) * rows]
    key_at = lax.broadcasted_iota(jnp.int32, same.shape, 0)
    query_at = lax.broadcasted_iota(jnp.int32, same.shape, 1) + block * rows
    return same & (key_at <= query_at)


def where_is(place, block):
    return jnp.bitwise_xor(place[1], block % 2), jnp.bitwise_xor(place[0], block // 2)


def nt(left, right):
    return lax.dot_general(left, right, (((1,), (1,)), ((), ())), preferred_element_type=f32)


def tn(left, right):
    return lax.dot_general(left, right, (((0,), (0,)), ((), ())), preferred_element_type=f32)


def nn(left, right):
    return lax.dot_general(left, right, (((1,), (0,)), ((), ())), preferred_element_type=f32)


def attend_kernel(
    blocks, place, query_ref, key_ref, value_ref, col_ref, row_ref, mixed_ref, halves_ref, total_ref,
):
    rows = mixed_ref.shape[2]
    for block in range(blocks):
        span = slice(block * rows, (block + 1) * rows)
        upto = (block + 1) * rows
        allowed = allowed_block(col_ref, row_ref, block, rows)
        mixed = jnp.zeros((PAIR, rows), f32)
        for head in range(2):
            query = keep_head(query_ref[0, span, :], head) * score_scale
            scores = jnp.where(allowed, nt(key_ref[0, :upto, :], query), neg_large)
            top = jnp.max(scores, axis=0, keepdims=True)
            weights = jnp.exp(scores - top)
            total = jnp.sum(weights, axis=0, keepdims=True)
            probs = (weights * (1.0 / total)).astype(bf16)
            mixed = mixed + tn(keep_head(value_ref[0, :upto, :], head), probs)
            total_ref[0, 0, head : head + 1, span] = top + jnp.log(total)
        mixed = jnp.transpose(mixed).astype(bf16)
        mixed_ref[0, block] = mixed
        half, entry = where_is(place, block)
        halves_ref[half, 0, entry] = mixed


def attend_back_kernel(
    blocks, place, query_ref, key_ref, value_ref, grad_ref, total_ref, cos_ref, sin_ref, col_ref, row_ref,
    out_ref, dk_ref, dv_ref,
):
    pair = pl.program_id(1)
    rows = grad_ref.shape[2]
    width = out_ref.shape[4] // 3
    first = lanes_of(rows) % HEAD_DIM < ROT_DIMS // 2

    def put(block, which, values):
        half, entry = where_is(place, block)
        at = pl.multiple_of(which * width + pair * PAIR, PAIR)
        out_ref[half, 0, entry, :, pl.ds(at, PAIR)] = values.astype(bf16)

    dk_ref[...] = jnp.zeros_like(dk_ref)
    dv_ref[...] = jnp.zeros_like(dv_ref)
    for block in range(blocks):
        span = slice(block * rows, (block + 1) * rows)
        upto = (block + 1) * rows
        allowed = allowed_block(col_ref, row_ref, block, rows)
        dq = jnp.zeros((PAIR, rows), f32)
        for head in range(2):
            query = keep_head(query_ref[0, span, :], head) * score_scale
            grad = keep_head(grad_ref[0, block], head)
            scores = jnp.where(allowed, nt(key_ref[0, :upto, :], query), neg_large)
            probs = jnp.exp(scores - total_ref[0, 0, head : head + 1, span])
            prob_grad = nt(value_ref[0, :upto, :], grad)
            inner = jnp.sum(probs * prob_grad, axis=0, keepdims=True)
            score_grad = (probs * (prob_grad - inner)).astype(bf16)
            dk_ref[:upto, :] += nn(score_grad, query)
            dv_ref[:upto, :] += nn(probs.astype(bf16), grad)
            dq = dq + tn(keep_head(key_ref[0, :upto, :], head), score_grad)
        put(block, 0, turned(jnp.transpose(dq) * score_scale, cos_ref[0, span, :], -sin_ref[0, span, :], first))
    for block in range(blocks):
        span = slice(block * rows, (block + 1) * rows)
        put(block, 1, turned(dk_ref[span, :], cos_ref[0, span, :], -sin_ref[0, span, :], first))
        put(block, 2, dv_ref[span, :])


def limits(lead=0):
    return dict(
        compiler_params=pltpu.CompilerParams(vmem_limit_bytes=56 * 1024 * 1024),
        cost_estimate=pl.CostEstimate(flops=lead * 10**9, bytes_accessed=lead * 3 * 10**6, transcendentals=0),
    )


def qkv_parts(seq, pairs):
    return [
        pl.BlockSpec((1, seq, PAIR), lambda p, h, place, which=which: (p, 0, which * pairs + h))
        for which in range(3)
    ]


def at_pack(*shape):
    rest = (0,) * len(shape)
    return pl.BlockSpec((1, *shape), lambda p, h, place: (jnp.bitwise_xor(p, place[2]), *rest))


def attention(place, qkv, blocks, seg_col, seg_row, lead=0):
    packs, seq, width = qkv.shape
    width //= 3
    rows, pairs = seq // blocks, width // PAIR
    return pl.pallas_call(
        functools.partial(attend_kernel, blocks),
        grid_spec=pltpu.PrefetchScalarGridSpec(
            num_scalar_prefetch=1,
            grid=(packs, pairs),
            in_specs=[*qkv_parts(seq, pairs), at_pack(seq, 1), at_pack(1, seq)],
            out_specs=[
                pl.BlockSpec(
                    (1, blocks, rows, PAIR), lambda p, h, place: (jnp.bitwise_xor(p, place[2]), 0, 0, h)
                ),
                pl.BlockSpec((2, 1, 2, rows, PAIR), lambda p, h, place: (0, p, 0, 0, h)),
                pl.BlockSpec((1, 1, 2, seq), lambda p, h, place: (p, h, 0, 0)),
            ],
        ),
        out_shape=[
            jax.ShapeDtypeStruct((packs, blocks, rows, width), bf16),
            jax.ShapeDtypeStruct((2, packs, 2, rows, width), bf16),
            jax.ShapeDtypeStruct((packs, pairs, 2, seq), f32),
        ],
        **limits(lead),
    )(place, qkv, qkv, qkv, seg_col, seg_row)


def attention_back(place, qkv, grad, totals, cosine, sine, seg_col, seg_row, lead=0):
    packs, blocks, rows, width = grad.shape
    pairs, seq = width // PAIR, blocks * rows
    return pl.pallas_call(
        functools.partial(attend_back_kernel, blocks),
        grid_spec=pltpu.PrefetchScalarGridSpec(
            num_scalar_prefetch=1,
            grid=(packs, pairs),
            in_specs=[
                *qkv_parts(seq, pairs),
                pl.BlockSpec(
                    (1, blocks, rows, PAIR), lambda p, h, place: (jnp.bitwise_xor(p, place[2]), 0, 0, h)
                ),
                pl.BlockSpec((1, 1, 2, seq), lambda p, h, place: (p, h, 0, 0)),
                at_pack(seq, PAIR), at_pack(seq, PAIR), at_pack(seq, 1), at_pack(1, seq),
            ],
            out_specs=pl.BlockSpec((2, 1, 2, rows, 3 * width), lambda p, h, place: (0, p, 0, 0, 0)),
            scratch_shapes=[pltpu.VMEM((seq, PAIR), f32)] * 2,
        ),
        out_shape=jax.ShapeDtypeStruct((2, packs, 2, rows, 3 * width), bf16),
        **limits(lead),
    )(place, qkv, qkv, qkv, grad, totals, cosine, sine, seg_col, seg_row)


def norm_kernel(*refs):
    *piece_refs, gain_ref, shift_ref, act_ref = refs
    step, at = 64, 0
    for piece in piece_refs:
        for row in range(0, piece.shape[0], step):
            normed = layer_stats(piece[row : row + step, :].astype(f32))[0]
            act_ref[at : at + step, :] = (normed * gain_ref[...] + shift_ref[...]).astype(bf16)
            at += step


def norm_rows(pieces, gain, shift, lead=0):
    count, width = sum(piece.shape[0] for piece in pieces), gain.shape[1]
    return pl.pallas_call(
        norm_kernel,
        out_shape=jax.ShapeDtypeStruct((count, width), bf16),
        **limits(lead),
    )(*pieces, gain, shift)


def pick(halves, steps):
    return jnp.where(pl.program_id(0) < steps // 2, halves[0][...], halves[1][...])


def project_kernel(place, act0_ref, act1_ref, weight_ref, bias_ref, cos_ref, sin_ref, out_ref, act_ref):
    act = pick((act0_ref, act1_ref), 8)
    act_ref[...] = act
    projected = nn(act, weight_ref[...]) + bias_ref[...]
    rows, width = projected.shape
    first = lanes_of(rows) % HEAD_DIM < ROT_DIMS // 2
    cosine, sine = cos_ref[0], sin_ref[0]
    for at in range(0, width, PAIR):
        part = projected[:, at : at + PAIR]
        if at < 2 * width // 3:
            part = turned(part, cosine, sine, first)
        out_ref[0, :, at : at + PAIR] = part.astype(bf16)


def project(place, act, weight, bias, cosine, sine, lead=0):
    count, depth = act[0].shape
    width = weight.shape[1]
    packs, seq, _ = cosine.shape
    rows = count // 4

    def block_of(s, place):
        return jnp.bitwise_xor(place[0], s % 2) * 2 + jnp.bitwise_xor(place[1], s // 4)

    def table(s, place):
        return (jnp.bitwise_xor(place[2], s // 2 % 2), block_of(s, place), 0)

    return pl.pallas_call(
        project_kernel,
        grid_spec=pltpu.PrefetchScalarGridSpec(
            num_scalar_prefetch=1,
            grid=(8,),
            in_specs=[
                *half_specs(rows, depth),
                pl.BlockSpec((depth, width), lambda s, place: (0, 0)),
                pl.BlockSpec((1, width), lambda s, place: (0, 0)),
                pl.BlockSpec((1, rows, PAIR), table),
                pl.BlockSpec((1, rows, PAIR), table),
            ],
            out_specs=[
                pl.BlockSpec((1, rows, width), lambda s, place: (s // 2 % 2, block_of(s, place), 0)),
                pl.BlockSpec((rows, depth), lambda s, place: (s, 0)),
            ],
        ),
        out_shape=[
            jax.ShapeDtypeStruct((packs, seq, width), bf16), jax.ShapeDtypeStruct((2 * count, depth), bf16)
        ],
        **limits(lead),
    )(place, *act, weight, bias, cosine, sine)


def slot_of(s, place):
    return jnp.bitwise_xor(place[3], s // 4 + (s // 2 % 2) * 4 + (s % 2) * 2)


def half_specs(rows, width, steps=8):
    half = steps // 2
    return [
        pl.BlockSpec((rows, width), lambda s, *place: (jnp.minimum(s, half - 1), 0)),
        pl.BlockSpec((rows, width), lambda s, *place: (jnp.maximum(s - half, 0), 0)),
    ]


def out_kernel(place, mixed_ref, w0_ref, w1_ref, token_ref, gain_ref, shift_ref, hidden_ref, act_ref, sum_ref):
    s = pl.program_id(0)

    @pl.when(s == 0)
    def _():
        sum_ref[...] = token_ref[...].astype(f32)

    @pl.when(s < 4)
    def _():
        sum_ref[...] += nn(mixed_ref[0], w0_ref[...])

    @pl.when(s >= 4)
    def _():
        sum_ref[...] += nn(mixed_ref[0], w1_ref[...])

    @pl.when(s == 7)
    def _():
        hidden = sum_ref[...]
        hidden_ref[...] = hidden
        act_ref[...] = (layer_stats(hidden)[0] * gain_ref[...] + shift_ref[...]).astype(bf16)


def out_rows_of(place, mixed, weight, tokens, gain, shift, lead=0):
    rows, width = tokens.shape
    part = mixed.shape[2]
    whole = pl.BlockSpec((rows, width), lambda s, place: (0, 0))
    vector = pl.BlockSpec((1, width), lambda s, place: (0, 0))
    return pl.pallas_call(
        out_kernel,
        grid_spec=pltpu.PrefetchScalarGridSpec(
            num_scalar_prefetch=1,
            grid=(8,),
            in_specs=[
                pl.BlockSpec((1, rows, part), lambda s, place: (slot_of(s, place), 0, 0)),
                *half_specs(part, width), whole, vector, vector,
            ],
            out_specs=[whole, whole],
            scratch_shapes=[pltpu.VMEM((rows, width), f32)],
        ),
        out_shape=[jax.ShapeDtypeStruct((rows, width), f32), jax.ShapeDtypeStruct((rows, width), bf16)],
        **limits(lead),
    )(place, mixed, *weight, tokens, gain, shift)


def out_back_kernel(
    place, own_ref, x_ref, y_ref, far_ref, hidden_ref, grad_ref, gain_ref, w0_ref, w1_ref,
    mixed_ref, total_ref, low_ref, vector_ref,
):
    s = pl.program_id(0)

    @pl.when(s == 0)
    def _():
        norm_grad = own_ref[...] + x_ref[...].astype(f32) + y_ref[...].astype(f32) + far_ref[...].astype(f32)
        normed, inv_std = layer_stats(hidden_ref[...])
        vector_ref[0:1, :] = jnp.sum(norm_grad * normed, axis=0, keepdims=True)
        vector_ref[1:2, :] = jnp.sum(norm_grad, axis=0, keepdims=True)
        total = grad_ref[...].astype(f32) + norm_back(norm_grad, normed, inv_std, gain_ref[...])
        total_ref[...] = total
        low_ref[...] = total.astype(bf16)

    @pl.when(s < 4)
    def _():
        mixed_ref[0] = nt(low_ref[...], w0_ref[...]).astype(bf16)

    @pl.when(s >= 4)
    def _():
        mixed_ref[0] = nt(low_ref[...], w1_ref[...]).astype(bf16)


def out_back_rows(place, terms, hidden, out_grad, gain, weight, lead=0):
    rows, width = hidden.shape
    part = weight[0].shape[0] // 4
    whole = pl.BlockSpec((rows, width), lambda s, place: (0, 0))
    vector = pl.BlockSpec((1, width), lambda s, place: (0, 0))
    return pl.pallas_call(
        out_back_kernel,
        grid_spec=pltpu.PrefetchScalarGridSpec(
            num_scalar_prefetch=1,
            grid=(8,),
            in_specs=[*[whole] * 6, vector, *half_specs(part, width)],
            out_specs=[
                pl.BlockSpec((1, rows, part), lambda s, place: (slot_of(s, place), 0, 0)),
                whole, whole, pl.BlockSpec((2, width), lambda s, place: (0, 0)),
            ],
        ),
        out_shape=[
            jax.ShapeDtypeStruct((8, rows, part), bf16),
            jax.ShapeDtypeStruct((rows, width), f32),
            jax.ShapeDtypeStruct((rows, width), bf16),
            jax.ShapeDtypeStruct((2, width), f32),
        ],
        **limits(lead),
    )(place, *terms, hidden, out_grad, gain, *weight)


STEPS = 4


def gate_kernel(act0_ref, act1_ref, weight_ref, middle_ref, by_gate_ref, by_up_ref, act_ref):
    act = pick((act0_ref, act1_ref), STEPS)
    act_ref[...] = act
    both = nn(act, weight_ref[...])
    half = both.shape[1] // 2
    gate, up = both[:, :half], both[:, half:]
    sigmoid = jax.nn.sigmoid(gate)
    silu = gate * sigmoid
    middle_ref[...] = (silu * up).astype(bf16)
    by_gate_ref[...] = (up * (sigmoid * (1.0 + gate * (1.0 - sigmoid)))).astype(bf16)
    by_up_ref[...] = silu.astype(bf16)


def gate_rows(act, weight, lead=0):
    count, depth = act[0].shape
    count *= 2
    half, rows = weight.shape[1] // 3, count // STEPS
    out = pl.BlockSpec((rows, half), lambda s: (s, 0))
    return pl.pallas_call(
        gate_kernel,
        grid=(STEPS,),
        in_specs=[*half_specs(rows, depth, STEPS), pl.BlockSpec((depth, 2 * half), lambda s: (0, 0))],
        out_specs=[out] * 3 + [pl.BlockSpec((rows, depth), lambda s: (s, 0))],
        out_shape=[jax.ShapeDtypeStruct((count, half), bf16)] * 3 + [jax.ShapeDtypeStruct((count, depth), bf16)],
        **limits(lead),
    )(*act, weight)


def gate_back_kernel(grad0_ref, grad1_ref, weight_ref, by_gate_ref, by_up_ref, out_ref):
    middle = nn(pick((grad0_ref, grad1_ref), STEPS), weight_ref[...])
    half = middle.shape[1]
    out_ref[:, :half] = (middle * by_gate_ref[...].astype(f32)).astype(bf16)
    out_ref[:, half:] = (middle * by_up_ref[...].astype(f32)).astype(bf16)


def gate_back_rows(grad, weight, by_gate, by_up, lead=0):
    count, depth = grad[0].shape
    count *= 2
    half, rows = weight.shape[1] // 3, count // STEPS
    part = pl.BlockSpec((rows, half), lambda s: (s, 0))
    return pl.pallas_call(
        gate_back_kernel,
        grid=(STEPS,),
        in_specs=[
            *half_specs(rows, depth, STEPS), pl.BlockSpec((depth, half), lambda s: (0, 2)), part, part
        ],
        out_specs=pl.BlockSpec((rows, 2 * half), lambda s: (s, 0)),
        out_shape=jax.ShapeDtypeStruct((count, 2 * half), bf16),
        **limits(lead),
    )(*grad, weight, by_gate, by_up)


def halves(low_part, low_at, high_part, high_at):
    low_part = low_part if low_at == 0 else pltpu.roll(low_part, HEAD_DIM, 1)
    high_part = high_part if high_at else pltpu.roll(high_part, HEAD_DIM, 1)
    return jnp.where(lanes_of(low_part.shape[0]) < HEAD_DIM, low_part, high_part)


def lane_group(load, at):
    return load(at // PAIR * PAIR), at % PAIR


def split_heads_kernel(team, weight_ref, out_ref):
    def load(at):
        return weight_ref[:, at : at + PAIR].astype(f32)

    chunks = weight_ref.shape[1] // (team * HEAD_DIM)
    for p in range(team):
        for chunk in range(0, chunks, 2):
            low = lane_group(load, (chunk * team + p) * HEAD_DIM)
            high = lane_group(load, ((chunk + 1) * team + p) * HEAD_DIM)
            out_ref[p, :, chunk * HEAD_DIM : (chunk + 2) * HEAD_DIM] = halves(*low, *high).astype(bf16)


def split_heads(weight, team, lead=0):
    rows, width = weight.shape
    return pl.pallas_call(
        functools.partial(split_heads_kernel, team),
        out_shape=jax.ShapeDtypeStruct((team, rows, width // team), bf16),
        **limits(lead),
    )(weight)


def merge_heads_kernel(part_ref, out_ref):
    team = part_ref.shape[0]
    chunks = part_ref.shape[2] // HEAD_DIM
    for chunk in range(chunks):
        for p in range(0, team, 2):
            at = chunk * HEAD_DIM

            def load(at, p=p):
                return part_ref[p, :, at : at + PAIR].astype(f32)

            def load_next(at, p=p):
                return part_ref[p + 1, :, at : at + PAIR].astype(f32)

            to = (chunk * team + p) * HEAD_DIM
            out_ref[:, to : to + PAIR] = halves(*lane_group(load, at), *lane_group(load_next, at))


def merge_heads(parts, lead=0):
    team, rows, width = parts.shape
    return pl.pallas_call(
        merge_heads_kernel,
        out_shape=jax.ShapeDtypeStruct((rows, team * width), f32),
        **limits(lead),
    )(parts)


def split_ffn_kernel(team, my_ffn, *refs):
    *weight_refs, out_ref = refs
    pad = out_ref.shape[2] // len(weight_refs)
    for which, weight_ref in enumerate(weight_refs):

        def load(at):
            return weight_ref[:, at : at + PAIR].astype(f32)

        for p in range(team):
            for at in range(0, pad, PAIR):
                source = p * my_ffn + at
                low = lane_group(load, source)
                if at + HEAD_DIM < my_ffn:
                    part = halves(*low, *lane_group(load, source + HEAD_DIM))
                else:
                    part = halves(*low, jnp.zeros_like(low[0]), HEAD_DIM)
                out_ref[p, :, which * pad + at : which * pad + at + PAIR] = part.astype(bf16)


def split_ffn(weights, team, pad, lead=0):
    rows, width = weights[0].shape
    return pl.pallas_call(
        functools.partial(split_ffn_kernel, team, width // team),
        out_shape=jax.ShapeDtypeStruct((team, rows, len(weights) * pad), bf16),
        **limits(lead),
    )(*weights)


def merge_ffn_kernel(my_ffn, part_ref, *out_refs):
    team = part_ref.shape[0]
    pad = part_ref.shape[2] // len(out_refs)
    for which, out_ref in enumerate(out_refs):

        def chunk(at):
            p, inside = at // my_ffn, at % my_ffn
            return lane_group(
                lambda lane: part_ref[p, :, which * pad + lane : which * pad + lane + PAIR].astype(f32), inside
            )

        for at in range(0, team * my_ffn, PAIR):
            out_ref[:, at : at + PAIR] = halves(*chunk(at), *chunk(at + HEAD_DIM))


def merge_ffn(parts, count, ffn, lead=0):
    team, rows, width = parts.shape
    return pl.pallas_call(
        functools.partial(merge_ffn_kernel, ffn // team),
        out_shape=[jax.ShapeDtypeStruct((rows, ffn), f32)] * count,
        **limits(lead),
    )(parts)


def local(
    tokens, segments, positions, out_grad, ln1_gain, ln1_bias, qkv_weight, qkv_bias, o_weight,
    ln2_gain, ln2_bias, gate_weight, up_weight, down_weight,
):
    rows, width = tokens.shape
    shard = qkv_weight.shape[0]
    ffn = gate_weight.shape[1]
    heads = width // HEAD_DIM
    team = lax.axis_size(PLANE)
    depth = lax.axis_size("g")
    devices = team * depth
    packs = lax.axis_size("y")
    blocks = team // packs
    seq = blocks * rows
    my_heads = heads // team
    my_width = my_heads * HEAD_DIM
    my_ffn = ffn // team
    pad_ffn = -(-my_ffn // 128) * 128
    me = lax.axis_index(PLANE)
    place = jnp.stack(
        [lax.axis_index("x"), lax.axis_index("c"), lax.axis_index("y"), me]
    ).astype(jnp.int32)
    aligned = shard == HEAD_DIM

    vectors = jnp.stack([ln1_gain, ln1_bias, ln2_gain, ln2_bias], axis=0)
    vectors = jnp.concatenate([vectors, jnp.transpose(qkv_bias)], axis=0).astype(f32).reshape(-1)
    small = jnp.concatenate([vectors, segments.astype(f32), positions.astype(f32)])
    small = lax.all_to_all(
        jnp.broadcast_to(small[None], (devices, small.shape[0])), ALL, 0, 0, tiled=True
    )
    vectors = jnp.transpose(small[:, : 7 * shard].reshape(devices, 7, shard), (1, 0, 2)).reshape(7, width)
    gain_one, shift_one, gain_two, shift_two = (vectors[i][None, :] for i in range(4))
    my_plane = lax.dynamic_slice_in_dim(small[:, 7 * shard :], lax.axis_index("g") * team, team, 0)
    segment_all = my_plane[:, :rows].reshape(packs, seq)
    position_all = my_plane[:, rows:].reshape(packs, seq)
    bias_mine = lax.dynamic_slice_in_dim(
        vectors[4:7].reshape(3, my_heads, team, HEAD_DIM), me, 1, 2
    ).reshape(1, 3 * my_width)

    token_pieces = chip_pieces(tokens)
    qkv_send = after(split_heads(qkv_weight, team), small)
    qkv_mine = plane_all_to_all(qkv_send).reshape(team * shard, 3 * my_width)
    ffn_send = split_ffn([gate_weight, up_weight, down_weight], team, pad_ffn)
    ffn_send = after(ffn_send, qkv_mine, *token_pieces)
    ffn_mine = plane_all_to_all(ffn_send).reshape(team * shard, 3 * pad_ffn)

    frequency = rope_base ** (-jnp.arange(0, ROT_DIMS, 2, dtype=f32) / ROT_DIMS)
    within = jnp.arange(PAIR) % HEAD_DIM
    phases = position_all[:, :, None] * jnp.where(within < ROT_DIMS, frequency[within % (ROT_DIMS // 2)], 0.0)
    cosine = jnp.cos(phases)
    sine = jnp.sin(phases) * jnp.where(within < ROT_DIMS // 2, -1.0, 1.0)
    seg_col, seg_row = segment_all[:, :, None], segment_all[:, None, :]

    def over_g(piece):
        return lax.all_gather(piece, "g", axis=0, tiled=True)

    act_one = norm_rows(token_pieces, gain_one, shift_one)
    ffn_mine = after(ffn_mine, act_one, cosine, sine, seg_col)
    act_one = act_one, swap(act_one, "c")
    if aligned:
        out_rows = after(over_g(o_weight), ffn_mine, act_one[0])
    else:
        out_abs = lax.all_gather(o_weight, ALL, axis=0, tiled=True)
        out_abs = out_abs.reshape(my_heads, team, HEAD_DIM, width)
        out_full = [
            jnp.concatenate(
                [jnp.take(out_abs, slot_of(s, place), axis=1).reshape(my_width, width) for s in span], axis=0
            )
            for span in (range(4), range(4, 8))
        ]
    qkv_full = over_g(qkv_mine)
    ffn_full = over_g(ffn_mine)
    qkv_full = after(qkv_full, act_one[0], ffn_mine)

    qkv, act_one = project(place, act_one, qkv_full, bias_mine, cosine, sine, lead=40)
    mixed, mixed_halves, totals = attention(place, qkv, blocks, seg_col, seg_row, lead=40)
    if aligned:
        out_full = halves_of(chip_pieces(out_rows, qkv), mixed)
    hidden, act_two = out_rows_of(
        place, plane_all_to_all(mixed.reshape(team, rows, my_width)), out_full, tokens, gain_two, shift_two
    )

    act_two = halves_of(chip_pieces(act_two))
    cotangent = halves_of(chip_pieces(after(out_grad, act_two[0])))
    middle_low, by_gate, by_up, act_all = gate_rows(act_two, ffn_full)
    down_sum = row_sum(cotangent, (middle_low[: 4 * rows], middle_low[4 * rows :]))

    def own_rows(grad_sum):
        return lax.psum_scatter(grad_sum, "g", scatter_dimension=0, tiled=True)

    def back_to_rows(columns):
        return plane_all_to_all(columns.reshape(team, shard, columns.shape[1]))

    gate_up_grad = gate_back_rows(after(cotangent, down_sum), ffn_full, by_gate, by_up)
    norm_two_other = plane_send(gate_up_grad, ffn_full, 0)
    norm_two_kept = plane_keep(gate_up_grad, ffn_full, 0, norm_two_other, bf16)
    gate_up_sum = row_sum([act_all], [after(gate_up_grad, norm_two_kept[0])], lead=60)
    down_own = own_rows(down_sum)
    gate_up_own = own_rows(gate_up_sum)
    norm_two_terms = plane_direct(norm_two_kept)
    output_other = plane_send(after(middle_low, gate_up_sum), ffn_full, 2)
    output_kept = plane_keep(middle_low, ffn_full, 2, output_other)
    norm_two_terms = after(norm_two_terms, output_kept[0], down_own)
    mixed_grad, hidden_grad, hidden_low, two_sums = out_back_rows(
        place, norm_two_terms, hidden, out_grad, gain_two, out_full
    )

    output_terms = plane_corner(after(output_kept, mixed_grad))
    mixed_grad = plane_all_to_all(mixed_grad).reshape(packs, blocks, rows, my_width)
    mixed_grad = after(mixed_grad, output_terms)
    qkv_grad = attention_back(place, qkv, mixed_grad, totals, cosine, sine, seg_col, seg_row, lead=40)
    qkv_grad = qkv_grad.reshape(8 * rows, 3 * my_width)
    output = (hidden + total_of(plane_neighbours(output_terms))).astype(bf16)
    qkv_sum = row_sum([act_one], [after(qkv_grad, output)], lead=40)
    qkv_own = own_rows(qkv_sum)
    norm_one_other = plane_send(after(qkv_grad, qkv_sum, gate_up_own), qkv_full, 0)
    hidden_pieces = chip_pieces(after(hidden_low, qkv_grad), norm_one_other)
    norm_one_kept = plane_keep(qkv_grad, qkv_full, 0, norm_one_other, bf16, lead=30)
    hidden_all = halves_of(hidden_pieces, norm_one_kept[0], lead=60)
    mixed_halves = mixed_halves.reshape(2, 4 * rows, my_width)
    out_sum = row_sum((mixed_halves[0], mixed_halves[1]), hidden_all)
    if aligned and depth == 4:
        out_share = deep_reduce(out_sum.reshape(4, shard, width))
    elif aligned:
        out_share = own_rows(out_sum).astype(f32)
    else:
        spread = jnp.zeros((my_heads, team, HEAD_DIM, width), bf16)
        spread = lax.dynamic_update_slice_in_dim(
            spread, out_sum.reshape(my_heads, 1, HEAD_DIM, width), me, 1
        )
        out_share = lax.psum_scatter(
            spread.reshape(width, width).astype(f32), ALL, scatter_dimension=0, tiled=True
        )
    down_share = merge_ffn(back_to_rows(after(down_own, qkv_sum)), 1, ffn)
    gate_up_share = merge_ffn(back_to_rows(gate_up_own), 2, ffn)
    norm_grad_one = total_of(
        after(plane_direct(norm_one_kept), qkv_own, out_share, down_share, gate_up_share)
    )
    normed_one, inv_one = layer_stats(tokens.astype(f32))
    input_grad = (hidden_grad + norm_back(norm_grad_one, normed_one, inv_one, gain_one)).astype(bf16)

    bias_sum = jnp.sum(qkv_grad.astype(f32), axis=0).reshape(3, my_heads, 1, HEAD_DIM)
    mine = (jnp.arange(team) == me).astype(f32)[None, None, :, None]
    terms = jnp.concatenate(
        [
            jnp.sum(norm_grad_one * normed_one, axis=0)[None],
            jnp.sum(norm_grad_one, axis=0)[None],
            (bias_sum * mine).reshape(3, width),
            two_sums,
        ],
        axis=0,
    )
    terms = jnp.transpose(terms.reshape(7, devices, shard), (1, 0, 2)).reshape(devices, 7 * shard)
    vector_share = jnp.sum(lax.all_to_all(terms, ALL, 0, 0, tiled=True), axis=0).reshape(7, shard)
    qkv_share = merge_heads(back_to_rows(qkv_own))
    return (
        output,
        input_grad,
        vector_share[0],
        vector_share[1],
        qkv_share,
        jnp.transpose(vector_share[2:5]),
        out_share,
        vector_share[5],
        vector_share[6],
        *gate_up_share,
        *down_share,
    )


def solution(mesh):
    dp, ctx = mesh.shape["dp"], mesh.shape["ctx"]
    split = Mesh(mesh.devices.reshape(dp // 2, 2, ctx // 2, 2), ALL)
    row, flat = P(ALL, None), P(ALL)
    return jax.shard_map(
        local,
        mesh=split,
        in_specs=(row, flat, flat, row, flat, flat, row, row, row, flat, flat, row, row, row),
        out_specs=(row, row, flat, flat, row, row, row, flat, flat, row, row, row),
        check_vma=False,
    )
```

time: 775 us -> 713 us (0.920)
  Pallas kernels: 42.8 us -> 265 us
  matrix products: 163 us -> 0 us
  local copies, waits for them, and re-layouts: 127 us -> 32.1 us
  other arithmetic: 42.3 us -> 29.3 us
    pallas_call x0 -> x25, Pallas kernels: none -> 224 us  [the longest x4 47.4 us: row_sum(): pl.pallas_call(functools.partial(sum_kernel, len(left)), grid=(width // s...]
    dot_general x33 -> x0, matrix products: 163 us -> none  [contract(): lax.dot_general(left, right, (((left_dim,), (right_dim,)), ((), ())), pre...]
    unnamed x145 -> x82, local copies, waits for them, and re-layouts: 64 us -> 8.63 us
    reduce_scatter x4 -> x3, waiting for transfers between devices: 40.6 us -> 0.5 us  [own_rows(): return lax.psum_scatter(grad_sum, 'g', scatter_dimension=0, tiled=True)]
    all_to_all x3 -> x5, waiting for transfers between devices: 5.57 us -> 39.6 us  [plane_all_to_all(): return lax.all_to_all(blocks, PLANE, 0, 0, tiled=True)]
    ppermute x69 -> x36, waiting for transfers between devices: 167 us -> 192 us  [swap(): return lax.ppermute(values, axis, [(0, 1), (1, 0)])]
    reshape x12 -> x0, local copies, waits for them, and re-layouts: 19.7 us -> none  [the longest x6 9.19 us: ffn_rows(): return jnp.transpose(part, (1, 0, 2)).reshape(shard, ffn)]
    ppermute x14 -> x6, waiting for transfers between devices: 24.6 us -> 5.28 us  [the longest x1 4.39 us: deep_reduce(): near = lax.ppermute(slots[1], 'g', [(0, 1), (1, 0), (2, 3), (3, 2)])]
  transfers between devices with their start and end apart: 96 -> 55, of which waited for: 35 -> 32; matrix products, arithmetic and copies ran while one was open for 39% -> 7% of each run, Pallas kernels for 6% -> 31%
where the time goes in v2:
time: 713 us; the launch traced here: 706 us
  Pallas kernels  265 us (37%)
  waiting for transfers between devices  259 us (36%)
  starting transfers between devices  73.3 us (10%)
  blocking collectives  33 us (5%)
  local copies, waits for them, and re-layouts  32.1 us (5%)
  other arithmetic  29.3 us (4%)
  between operations  15 us (2%)
    ppermute x36, waiting for transfers between devices, swap(): return lax.ppermute(values, axis, [(0, 1), (1, 0)])  192 us
    pallas_call x4, Pallas kernels, row_sum(): pl.pallas_call(functools.partial(sum_kernel, len(left)), grid=(width // s...  47.4 us
    all_to_all x5, waiting for transfers between devices, plane_all_to_all(): return lax.all_to_all(blocks, PLANE, 0, 0, tiled=True)  39.6 us
    pallas_call x3, Pallas kernels, plane_keep(): pl.pallas_call(keep_kernel, grid=(4,), in_specs=[pl.BlockSpec((rows, dept...  33.5 us
    all_to_all x2, blocking collectives, plane_all_to_all(): return lax.all_to_all(blocks, PLANE, 0, 0, tiled=True)  33 us
    ppermute x36, starting transfers between devices, swap(): return lax.ppermute(values, axis, [(0, 1), (1, 0)])  32.7 us
    pallas_call x3, Pallas kernels, plane_send(): pl.pallas_call(send_kernel, grid=(2,), in_specs=[pl.BlockSpec((2 * rows,...  26.1 us
    pallas_call x1, Pallas kernels, attention_back(): pl.pallas_call(functools.partial(attend_back_kernel, blocks), grid_spec=p...  25.9 us
  transfers between devices with their start and end apart: 55, of which 32 were waited for; matrix products, arithmetic and copies ran while one was open for 7% of the time, Pallas kernels for 31%

profile of v2, /device:TPU:0, one launch (start us, length us, event | category | flops | bytes accessed | tf_op | source)
XLA Modules:
  0.0 706.4 jit_solution(12297272749057328374)
XLA Ops:
  7.9 3.0 collective-permute-start.1
  15.5 4.0 all-to-all-start
  21.8 15.2 %all-to-all-done = f32[32,1,960]{2,1,0:T(1,128)S(1)} async-done(((f32[32,1,960]{2,1,0:T(1,128)}), f32[32,1,960]{2,1,0:T(1,128)S(1)}, u32[]{:S(2)}, u32[]{:S(2)}) %all-to-all-start) | async-done | bytes 122912 | tf_op jit(solution)/shard_map/all_to_all | solution.py:762
  37.1 16.8 %all_to_all.54 = bf16[8,64,768]{2,1,0:T(8,128)(2,1)} all-to-all(bf16[8,64,768]{2,1,0:T(8,128)(2,1)} %shard_map.230), channel_id=1, replica_groups=mesh['g'=4,'y'=2,'x'=2,'c'=2] {'y','x','c'}, dimensions={0} | all-to-all | bytes 1572864 | tf_op jit(solution)/shard_map/all_to_all | solution.py:217
  58.9 9.1 %collective-permute-done.2.refs_3_ = bf16[128,2048]{1,0:T(8,128)(2,1)S(1)} collective-permute-done((bf16[128,2048]{1,0:T(8,128)(2,1)}, bf16[128,2048]{1,0:T(8,128)(2,1)S(1)}, u32[]{:S(2)}, u32[]{:S(2)}) %collective-permute-start.2) | collective-permute-done | bytes 524320 | tf_op jit(solution)/shard_map/ppermute | solution.py:59
  70.7 7.3 %shard_map.229.act0_ref = bf16[1024,2048]{1,0:T(8,128)(2,1)} custom-call(bf16[256,2048]{1,0:T(8,128)(2,1)} %token_ref.1, bf16[256,2048]{1,0:T(8,128)(2,1)} %copy-done.8, bf16[256,2048]{1,0:T(8,128)(2,1)} %copy-done.7, bf16[128,2048]{1,0:T(8,128)(2,1)} %copy-done.23, bf16[128,2048]{1,0:T(8,128)(2,1)} %copy-done.24, f32[1,2048]{1,0:T(1,128)} %slice.138.refs_5_, ...), custom_call_target="tpu_custom_call" | custom-call | tf_op jit(solution)/shard_map/pallas_call | solution.py:403
  78.0 3.7 shard_map.231
  81.7 3.6 all-to-all-start.2
  86.9 5.2 compare_select_fusion.9
  94.9 5.5 fusion.12
  100.4 14.3 %all-to-all-done.2 = bf16[8,64,2304]{2,1,0:T(8,128)(2,1)S(1)} async-done(((bf16[8,64,2304]{2,1,0:T(8,128)(2,1)}), bf16[8,64,2304]{2,1,0:T(8,128)(2,1)S(1)}, u32[]{:S(2)}, u32[]{:S(2)}) %all-to-all-start.2) | async-done | bytes 2359328 | tf_op jit(solution)/shard_map/all_to_all | solution.py:217
  117.0 15.6 %shard_map.232 = (bf16[2,1024,768]{2,1,0:T(8,128)(2,1)}, bf16[2048,2048]{1,0:T(8,128)(2,1)}) custom-call(s32[4]{0:T(128)} %pad_add_fusion.place, bf16[1024,2048]{1,0:T(8,128)(2,1)} %shard_map.229.act0_ref, bf16[1024,2048]{1,0:T(8,128)(2,1)} %collective-permute-done.4.act1_ref, bf16[2048,768]{1,0:T(8,128)(2,1)} %all-gather.4.cloned.1.call-done.weight_ref.right_ref, ...), custom_call_target="tpu_custom_call" | custom-call | flops 40000000000 | bytes 120000000 | tf_op jit(solution)/shard_map/pallas_call | solution.py:440
  132.6 4.6 collective-permute-done.6.refs_2_
  143.7 15.8 %shard_map.233 = (bf16[2,4,256,256]{3,2,1,0:T(8,128)(2,1)}, bf16[2,2,2,256,256]{4,3,2,1,0:T(8,128)(2,1)}, f32[2,2,2,1024]{3,2,1,0:T(2,128)}) custom-call(s32[4]{0:T(128)} %pad_add_fusion.place, bf16[2,1024,768]{2,1,0:T(8,128)(2,1)} %get-tuple-element.86.query_ref.key_ref.value_ref, bf16[2,1024,768]{2,1,0:T(8,128)(2,1)} %get-tuple-element.86.query_ref.key_ref.value_ref, ...), custom_call_target="tpu_custom_call" | custom-call | flops 40000000000 | bytes 120000000 | tf_op jit(solution)/shard_map/pallas_call | solution.py:344
  160.5 4.8 shard_map.234.w0_ref
  165.3 3.6 all-to-all-start.3
  170.8 13.4 %all-to-all-done.3.mixed_ref = bf16[8,256,256]{2,1,0:T(8,128)(2,1)S(1)} async-done(((bf16[8,256,256]{2,1,0:T(8,128)(2,1)}), bf16[8,256,256]{2,1,0:T(8,128)(2,1)S(1)}, u32[]{:S(2)}, u32[]{:S(2)}) %all-to-all-start.3) | async-done | bytes 1048608 | tf_op jit(solution)/shard_map/all_to_all | solution.py:217
  185.1 11.8 %shard_map.235 = (f32[256,2048]{1,0:T(8,128)}, bf16[256,2048]{1,0:T(8,128)(2,1)}) custom-call(s32[4]{0:T(128)} %pad_add_fusion.place, bf16[8,256,256]{2,1,0:T(8,128)(2,1)} %copy-done.5, bf16[1024,2048]{1,0:T(8,128)(2,1)} %shard_map.234.w0_ref, bf16[1024,2048]{1,0:T(8,128)(2,1)} %collective-permute-done.9.w1_ref, bf16[256,2048]{1,0:T(8,128)(2,1)} %token_ref.1, ...), custom_call_target="tpu_custom_call" | custom-call | tf_op jit(solution)/shard_map/pallas_call | solution.py:503
  198.2 21.1 %collective-permute-done.11.refs_2_ = bf16[256,2048]{1,0:T(8,128)(2,1)S(1)} collective-permute-done((bf16[256,2048]{1,0:T(8,128)(2,1)}, bf16[256,2048]{1,0:T(8,128)(2,1)S(1)}, u32[]{:S(2)}, u32[]{:S(2)}) %collective-permute-start.11) | collective-permute-done | bytes 1048608 | tf_op jit(solution)/shard_map/ppermute | solution.py:59
  219.3 3.7 collective-permute-start.12
  223.6 11.0 %collective-permute-done.12.refs_3_ = bf16[128,2048]{1,0:T(8,128)(2,1)S(1)} collective-permute-done((bf16[128,2048]{1,0:T(8,128)(2,1)S(1)}, bf16[128,2048]{1,0:T(8,128)(2,1)S(1)}, u32[]{:S(2)}, u32[]{:S(2)}) %collective-permute-start.12) | collective-permute-done | bytes 524320 | tf_op jit(solution)/shard_map/ppermute | solution.py:59
  237.0 4.7 shard_map.236.act0_ref
  243.3 21.8 %collective-permute-done.16.refs_2_ = bf16[256,2048]{1,0:T(8,128)(2,1)S(1)} collective-permute-done((bf16[256,2048]{1,0:T(8,128)(2,1)S(1)}, bf16[256,2048]{1,0:T(8,128)(2,1)S(1)}, u32[]{:S(2)}, u32[]{:S(2)}) %collective-permute-start.16) | collective-permute-done | bytes 1048608 | tf_op jit(solution)/shard_map/ppermute | solution.py:59
  268.2 8.5 %collective-permute-done.17.refs_3_ = bf16[128,2048]{1,0:T(8,128)(2,1)S(1)} collective-permute-done((bf16[128,2048]{1,0:T(8,128)(2,1)S(1)}, bf16[128,2048]{1,0:T(8,128)(2,1)S(1)}, u32[]{:S(2)}, u32[]{:S(2)}) %collective-permute-start.17) | collective-permute-done | bytes 524320 | tf_op jit(solution)/shard_map/ppermute | solution.py:59
  278.8 4.7 shard_map.238.refs_0_.grad0_ref
  284.1 19.7 %shard_map.237 = (bf16[2048,768]{1,0:T(8,128)(2,1)}, bf16[2048,768]{1,0:T(8,128)(2,1)}, bf16[2048,768]{1,0:T(8,128)(2,1)}, bf16[2048,2048]{1,0:T(8,128)(2,1)}) custom-call(bf16[1024,2048]{1,0:T(8,128)(2,1)} %shard_map.236.act0_ref, bf16[1024,2048]{1,0:T(8,128)(2,1)} %collective-permute-done.14.act1_ref, ...), custom_call_target="tpu_custom_call" | custom-call | tf_op jit(solution)/shard_map/pallas_call | solution.py:592
  303.8 3.8 fusion.18
  307.6 10.8 %shard_map.239 = bf16[2048,768]{1,0:T(8,128)(2,1)} custom-call(bf16[1024,2048]{1,0:T(8,128)(2,1)} %shard_map.238.refs_0_.grad0_ref, bf16[1024,2048]{1,0:T(8,128)(2,1)} %collective-permute-done.19.refs_1_.grad1_ref, bf16[1024,768]{1,0:T(8,128)(2,1)} %get-tuple-element.162.refs_2_, bf16[1024,768]{1,0:T(8,128)(2,1)} %get-tuple-element.161.refs_3_), custom_call_target="tpu_custom_call" | custom-call | tf_op jit(solution)/shard_map/pallas_call | solution.py:191
  318.4 13.0 %shard_map.240.left_ref.refs_1_ = bf16[2048,1536]{1,0:T(8,128)(2,1)} custom-call(bf16[1024,2048]{1,0:T(8,128)(2,1)} %shard_map.238.refs_0_.grad0_ref, bf16[1024,2048]{1,0:T(8,128)(2,1)} %collective-permute-done.19.refs_1_.grad1_ref, bf16[2048,2304]{1,0:T(8,128)(2,1)} %all-gather.8.cloned.1.call-done.weight_ref.right_ref, ...), custom_call_target="tpu_custom_call" | custom-call | tf_op jit(solution)/shard_map/pallas_call | solution.py:614
  331.4 11.6 %shard_map.241 = bf16[1024,2048]{1,0:T(8,128)(2,1)} custom-call(bf16[2048,1536]{1,0:T(8,128)(2,1)} %shard_map.240.left_ref.refs_1_, bf16[2048,2304]{1,0:T(8,128)(2,1)} %all-gather.8.cloned.1.call-done.weight_ref.right_ref), custom_call_target="tpu_custom_call" | custom-call | tf_op jit(solution)/shard_map/pallas_call | solution.py:123
  343.2 7.2 %collective-permute-done.20.other_ref = bf16[1024,2048]{1,0:T(8,128)(2,1)} collective-permute-done((bf16[1024,2048]{1,0:T(8,128)(2,1)}, bf16[1024,2048]{1,0:T(8,128)(2,1)}, u32[]{:S(2)}, u32[]{:S(2)}) %collective-permute-start.20) | collective-permute-done | bytes 4194336 | tf_op jit(solution)/shard_map/ppermute | solution.py:59
  350.4 13.6 %shard_map.242 = (bf16[256,2048]{1,0:T(8,128)(2,1)}, bf16[256,2048]{1,0:T(8,128)(2,1)}, bf16[256,2048]{1,0:T(8,128)(2,1)}, f32[256,2048]{1,0:T(8,128)}) custom-call(bf16[2048,1536]{1,0:T(8,128)(2,1)} %shard_map.240.left_ref.refs_1_, bf16[2048,2304]{1,0:T(8,128)(2,1)} %all-gather.8.cloned.1.call-done.weight_ref.right_ref, ...), custom_call_target="tpu_custom_call" | custom-call | tf_op jit(solution)/shard_map/pallas_call | solution.py:140
  364.0 18.5 %shard_map.243 = bf16[2048,1536]{1,0:T(8,128)(2,1)} custom-call(bf16[2048,2048]{1,0:T(8,128)(2,1)} %get-tuple-element.99.refs_0_, bf16[2048,1536]{1,0:T(8,128)(2,1)} %shard_map.240.left_ref.refs_1_), custom_call_target="tpu_custom_call" | custom-call | flops 60000002048 | bytes 180000000 | tf_op jit(solution)/shard_map/pallas_call | solution.py:191
  382.5 7.2 %shard_map.244 = bf16[1024,2048]{1,0:T(8,128)(2,1)} custom-call(bf16[2048,768]{1,0:T(8,128)(2,1)} %get-tuple-element.107.left_ref, bf16[2048,2304]{1,0:T(8,128)(2,1)} %all-gather.8.cloned.1.call-done.weight_ref.right_ref), custom_call_target="tpu_custom_call" | custom-call | tf_op jit(solution)/shard_map/pallas_call | solution.py:123
  393.5 3.8 collective-permute-done.21.other_ref
  397.2 10.3 %shard_map.245 = (bf16[256,2048]{1,0:T(8,128)(2,1)}, f32[256,2048]{1,0:T(8,128)}, f32[256,2048]{1,0:T(8,128)}, f32[256,2048]{1,0:T(8,128)}) custom-call(bf16[2048,768]{1,0:T(8,128)(2,1)} %get-tuple-element.107.left_ref, bf16[2048,2304]{1,0:T(8,128)(2,1)} %all-gather.8.cloned.1.call-done.weight_ref.right_ref, bf16[1024,2048]{1,0:T(8,128)(2,1)} %collective-permute-done.21.other_ref), custom_call_target="tpu_custom_call" | custom-call | tf_op jit(solution)/shard_map/pallas_call | solution.py:140
  407.6 8.6 %collective-permute-done.22.x_ref = bf16[256,2048]{1,0:T(8,128)(2,1)S(1)} collective-permute-done((bf16[256,2048]{1,0:T(8,128)(2,1)}, bf16[256,2048]{1,0:T(8,128)(2,1)S(1)}, u32[]{:S(2)}, u32[]{:S(2)}) %collective-permute-start.22) | collective-permute-done | bytes 1048608 | tf_op jit(solution)/shard_map/ppermute | solution.py:59
  416.2 23.1 %collective-permute-done.23.y_ref = bf16[256,2048]{1,0:T(8,128)(2,1)S(1)} collective-permute-done((bf16[256,2048]{1,0:T(8,128)(2,1)}, bf16[256,2048]{1,0:T(8,128)(2,1)S(1)}, u32[]{:S(2)}, u32[]{:S(2)}) %collective-permute-start.23) | collective-permute-done | bytes 1048608 | tf_op jit(solution)/shard_map/ppermute | solution.py:59
  440.6 15.2 %shard_map.246 = (bf16[8,256,256]{2,1,0:T(8,128)(2,1)}, f32[256,2048]{1,0:T(8,128)}, bf16[256,2048]{1,0:T(8,128)(2,1)}, f32[2,2048]{1,0:T(2,128)}) custom-call(s32[4]{0:T(128)} %pad_add_fusion.place, f32[256,2048]{1,0:T(8,128)} %get-tuple-element.115.own_ref, bf16[256,2048]{1,0:T(8,128)(2,1)} %copy-done.18, bf16[256,2048]{1,0:T(8,128)(2,1)} %copy-done.19, ...), custom_call_target="tpu_custom_call" | custom-call | tf_op jit(solution)/shard_map/pallas_call | solution.py:550
  457.6 4.2 all-to-all-start.4
  465.6 6.0 collective-permute-done.27
  474.3 13.6 %collective-permute-done.25 = bf16[128,2048]{1,0:T(8,128)(2,1)S(1)} collective-permute-done((bf16[128,2048]{1,0:T(8,128)(2,1)}, bf16[128,2048]{1,0:T(8,128)(2,1)S(1)}, u32[]{:S(2)}, u32[]{:S(2)}) %collective-permute-start.25) | collective-permute-done | bytes 524320 | tf_op jit(solution)/shard_map/ppermute | solution.py:59
  489.7 25.9 %shard_map.247 = bf16[2,2,2,256,768]{4,3,2,1,0:T(8,128)(2,1)} custom-call(s32[4]{0:T(128)} %pad_add_fusion.place, bf16[2,1024,768]{2,1,0:T(8,128)(2,1)} %get-tuple-element.86.query_ref.key_ref.value_ref, bf16[2,1024,768]{2,1,0:T(8,128)(2,1)} %get-tuple-element.86.query_ref.key_ref.value_ref, ...), custom_call_target="tpu_custom_call" | custom-call | flops 40000000000 | bytes 120000000 | tf_op jit(solution)/shard_map/pallas_call | solution.py:370
  517.2 10.9 %shard_map.248 = bf16[2048,768]{1,0:T(8,128)(2,1)} custom-call(bf16[2048,2048]{1,0:T(8,128)(2,1)} %get-tuple-element.127.refs_0_, bf16[2048,768]{1,0:T(8,128)(2,1)} %bitcast.61), custom_call_target="tpu_custom_call" | custom-call | flops 40000000000 | bytes 120000000 | tf_op jit(solution)/shard_map/pallas_call | solution.py:191
  528.2 7.3 %shard_map.249 = bf16[1024,2048]{1,0:T(8,128)(2,1)} custom-call(bf16[2048,768]{1,0:T(8,128)(2,1)} %bitcast.62, bf16[2048,768]{1,0:T(8,128)(2,1)} %all-gather.4.cloned.1.call-done.weight_ref.right_ref), custom_call_target="tpu_custom_call" | custom-call | tf_op jit(solution)/shard_map/pallas_call | solution.py:123
  536.2 24.8 %collective-permute-done.34.refs_2_ = bf16[256,2048]{1,0:T(8,128)(2,1)S(1)} collective-permute-done((bf16[256,2048]{1,0:T(8,128)(2,1)S(1)}, bf16[256,2048]{1,0:T(8,128)(2,1)S(1)}, u32[]{:S(2)}, u32[]{:S(2)}) %collective-permute-start.34) | collective-permute-done | bytes 1048608 | tf_op jit(solution)/shard_map/ppermute | solution.py:59
  563.5 9.6 %shard_map.250 = (bf16[256,2048]{1,0:T(8,128)(2,1)}, bf16[256,2048]{1,0:T(8,128)(2,1)}, bf16[256,2048]{1,0:T(8,128)(2,1)}, f32[256,2048]{1,0:T(8,128)}) custom-call(bf16[2048,768]{1,0:T(8,128)(2,1)} %bitcast.63, bf16[2048,768]{1,0:T(8,128)(2,1)} %all-gather.4.cloned.1.call-done.weight_ref.right_ref, bf16[1024,2048]{1,0:T(8,128)(2,1)} %collective-permute-done.29.other_ref), custom_call_target="tpu_custom_call" | custom-call | flops 30000001024 | bytes 90000000 | tf_op jit(solution)/shard_map/pallas_call | solution.py:140
  575.8 4.8 shard_map.251.refs_2_
  580.7 16.2 %all_to_all.55.part_ref = bf16[8,64,768]{2,1,0:T(8,128)(2,1)} all-to-all(bf16[8,64,768]{2,1,0:T(8,128)(2,1)S(1)} %bitcast.72), channel_id=1, replica_groups=mesh['g'=4,'y'=2,'x'=2,'c'=2] {'y','x','c'}, dimensions={0} | all-to-all | bytes 1572864 | tf_op jit(solution)/shard_map/all_to_all | solution.py:217
  597.4 3.9 all-to-all-start.8
  602.0 11.9 %all-to-all-done.8.part_ref = bf16[8,64,768]{2,1,0:T(8,128)(2,1)S(1)} async-done(((bf16[8,64,768]{2,1,0:T(8,128)(2,1)}), bf16[8,64,768]{2,1,0:T(8,128)(2,1)S(1)}, u32[]{:S(2)}, u32[]{:S(2)}) %all-to-all-start.8) | async-done | bytes 786464 | tf_op jit(solution)/shard_map/all_to_all | solution.py:217
  613.9 3.6 all-to-all-start.6
  619.7 7.2 %shard_map.252 = bf16[256,2048]{1,0:T(8,128)(2,1)} custom-call(bf16[1024,256]{1,0:T(8,128)(2,1)} %bitcast.70, bf16[1024,256]{1,0:T(8,128)(2,1)} %bitcast.69, bf16[1024,2048]{1,0:T(8,128)(2,1)} %shard_map.251.refs_2_, bf16[1024,2048]{1,0:T(8,128)(2,1)} %collective-permute-done.37.refs_3_), custom_call_target="tpu_custom_call" | custom-call | tf_op jit(solution)/shard_map/pallas_call | solution.py:191
  628.0 2.9 collective-permute-start.40
  631.2 2.9 collective-permute-start.32
  641.2 4.4 collective-permute-done.39
  646.3 3.2 collective-permute-start.41
  654.6 2.6 shard_map.255
  658.4 3.6 shard_map.254
  664.0 18.6 %collective-permute-done.30 = bf16[256,2048]{1,0:T(8,128)(2,1)} collective-permute-done((bf16[256,2048]{1,0:T(8,128)(2,1)}, bf16[256,2048]{1,0:T(8,128)(2,1)}, u32[]{:S(2)}, u32[]{:S(2)}) %collective-permute-start.30) | collective-permute-done | bytes 1048608 | tf_op jit(solution)/shard_map/ppermute | solution.py:59
  683.5 3.2 fusion.10
  687.7 2.9 all-to-all-start.7
  690.6 3.4 fusion.9
  694.0 4.0 all-to-all-done.7
  (239 shorter events, 90.4 us)
Async XLA Ops:
  7.2 107.5 %all-gather.6.cloned.1.call-start = ((), (), s32[]{:S(2)}) async-start(), calls=%async_computation.13 | async-start | bytes 1310720 | tf_op jit(solution)/shard_map/all_gather | solution.py:789
  7.9 46.0 %collective-permute-start.1 = (bf16[256,2048]{1,0:T(8,128)(2,1)}, bf16[256,2048]{1,0:T(8,128)(2,1)S(1)}, u32[]{:S(2)}, u32[]{:S(2)}) collective-permute-start(bf16[256,2048]{1,0:T(8,128)(2,1)} %token_ref.1), channel_id=1, source_target_pairs={{0,4},{4,0},{1,5},{5,1},{2,6},{6,2},{3,7},{7,3},{8,12},{12,8},{9,1... | collective-permute-start | bytes 3145736 | tf_op jit(solution)/shard_map/ppermute | solution.py:59
  10.9 44.4 %collective-permute-start = (bf16[256,2048]{1,0:T(8,128)(2,1)}, bf16[256,2048]{1,0:T(8,128)(2,1)S(1)}, u32[]{:S(2)}, u32[]{:S(2)}) collective-permute-start(bf16[256,2048]{1,0:T(8,128)(2,1)} %token_ref.1), channel_id=1, source_target_pairs={{0,2},{2,0},{1,3},{3,1},{4,6},{6,4},{5,7},{7,5},{8,10},{10,8},{9,1... | collective-permute-start | bytes 3145736 | tf_op jit(solution)/shard_map/ppermute | solution.py:59
  15.5 21.6 %all-to-all-start = ((f32[32,1,960]{2,1,0:T(1,128)}), f32[32,1,960]{2,1,0:T(1,128)S(1)}, u32[]{:S(2)}, u32[]{:S(2)}) async-start(f32[32,1,960]{2,1,0:T(1,128)} %broadcast_in_dim.14), calls=%async_computation | async-start | bytes 262144 | tf_op jit(solution)/shard_map/all_to_all | solution.py:762
  19.4 97.5 %all-gather.4.cloned.1.call-start = ((), (), s32[]{:S(2)}) async-start(), calls=%async_computation.12 | async-start | bytes 3932160 | tf_op jit(solution)/shard_map/all_gather | solution.py:789
  53.9 16.0 %copy-start.7 = (bf16[256,2048]{1,0:T(8,128)(2,1)}, bf16[256,2048]{1,0:T(8,128)(2,1)S(1)}, u32[]{:S(2)}) copy-start(bf16[256,2048]{1,0:T(8,128)(2,1)S(1)} %collective-permute-done.1.refs_2_) | copy-start | bytes 3145732
  54.8 13.2 %collective-permute-start.2 = (bf16[128,2048]{1,0:T(8,128)(2,1)}, bf16[128,2048]{1,0:T(8,128)(2,1)S(1)}, u32[]{:S(2)}, u32[]{:S(2)}) collective-permute-start(bf16[128,2048]{1,0:T(8,128)(2,1)} %slice.182), channel_id=1, source_target_pairs={{0,2},{2,0},{1,3},{3,1},{4,6},{6,4},{5,7},{7,5},{8,10},{10,8},{9,1... | collective-permute-start | bytes 1572872 | tf_op jit(solution)/shard_map/ppermute | solution.py:59
  56.2 13.7 %collective-permute-start.3 = (bf16[128,2048]{1,0:T(8,128)(2,1)}, bf16[128,2048]{1,0:T(8,128)(2,1)S(1)}, u32[]{:S(2)}, u32[]{:S(2)}) collective-permute-start(bf16[128,2048]{1,0:T(8,128)(2,1)} %slice.183), channel_id=1, source_target_pairs={{0,4},{4,0},{1,5},{5,1},{2,6},{6,2},{3,7},{7,3},{8,12},{12,8},{9,1... | collective-permute-start | bytes 1572872 | tf_op jit(solution)/shard_map/ppermute | solution.py:59
  78.0 39.0 %collective-permute-start.4 = (bf16[1024,2048]{1,0:T(8,128)(2,1)}, bf16[1024,2048]{1,0:T(8,128)(2,1)}, u32[]{:S(2)}, u32[]{:S(2)}) collective-permute-start(bf16[1024,2048]{1,0:T(8,128)(2,1)} %shard_map.229.act0_ref), channel_id=1, source_target_pairs={{0,1},{1,0},{2,3},{3,2},{4,5},{5,4},{6,7},{7,6},{8,9},{9,8},{10,11... | collective-permute-start | bytes 12582920 | tf_op jit(solution)/shard_map/ppermute | solution.py:59
  81.7 33.0 %all-to-all-start.2 = ((bf16[8,64,2304]{2,1,0:T(8,128)(2,1)}), bf16[8,64,2304]{2,1,0:T(8,128)(2,1)S(1)}, u32[]{:S(2)}, u32[]{:S(2)}) async-start(bf16[8,64,2304]{2,1,0:T(8,128)(2,1)} %shard_map.231), calls=%async_computation.2 | async-start | bytes 4718592 | tf_op jit(solution)/shard_map/all_to_all | solution.py:217
  85.3 198.8 %all-gather.8.cloned.1.call-start = ((), (), s32[]{:S(2)}) async-start(), calls=%async_computation.14 | async-start | bytes 11796480 | tf_op jit(solution)/shard_map/all_gather | solution.py:789
  114.7 22.5 %collective-permute-start.6 = (bf16[256,2048]{1,0:T(8,128)(2,1)}, bf16[256,2048]{1,0:T(8,128)(2,1)S(1)}, u32[]{:S(2)}, u32[]{:S(2)}) collective-permute-start(bf16[256,2048]{1,0:T(8,128)(2,1)} %all-gather.6.cloned.1.call-done.refs_0_), channel_id=1, source_target_pairs={{0,4},{4,0},{1,5},{5,1},{2,6},{6,2},{3,7},{7,3},{8,12},{12,8},{9,1... | collective-permute-start | bytes 3145736 | tf_op jit(solution)/shard_map/ppermute | solution.py:59
  115.2 23.9 %collective-permute-start.5 = (bf16[256,2048]{1,0:T(8,128)(2,1)}, bf16[256,2048]{1,0:T(8,128)(2,1)}, u32[]{:S(2)}, u32[]{:S(2)}) collective-permute-start(bf16[256,2048]{1,0:T(8,128)(2,1)} %all-gather.6.cloned.1.call-done.refs_0_), channel_id=1, source_target_pairs={{0,2},{2,0},{1,3},{3,1},{4,6},{6,4},{5,7},{7,5},{8,10},{10,8},{9,1... | collective-permute-start | bytes 3145736 | tf_op jit(solution)/shard_map/ppermute | solution.py:59
  137.2 22.3 %copy-start.9 = (bf16[256,2048]{1,0:T(8,128)(2,1)}, bf16[256,2048]{1,0:T(8,128)(2,1)S(1)}, u32[]{:S(2)}) copy-start(bf16[256,2048]{1,0:T(8,128)(2,1)S(1)} %collective-permute-done.6.refs_2_) | copy-start | bytes 3145732
  140.3 19.2 %collective-permute-start.7 = (bf16[128,2048]{1,0:T(8,128)(2,1)S(1)}, bf16[128,2048]{1,0:T(8,128)(2,1)S(1)}, u32[]{:S(2)}, u32[]{:S(2)}) collective-permute-start(bf16[128,2048]{1,0:T(8,128)(2,1)S(1)} %slice.145), channel_id=1, source_target_pairs={{0,2},{2,0},{1,3},{3,1},{4,6},{6,4},{5,7},{7,5},{8,10},{10,8},{9,1... | collective-permute-start | bytes 1572872 | tf_op jit(solution)/shard_map/ppermute | solution.py:59
  142.2 17.2 %collective-permute-start.8 = (bf16[128,2048]{1,0:T(8,128)(2,1)S(1)}, bf16[128,2048]{1,0:T(8,128)(2,1)S(1)}, u32[]{:S(2)}, u32[]{:S(2)}) collective-permute-start(bf16[128,2048]{1,0:T(8,128)(2,1)S(1)} %slice.146), channel_id=1, source_target_pairs={{0,4},{4,0},{1,5},{5,1},{2,6},{6,2},{3,7},{7,3},{8,12},{12,8},{9,1... | collective-permute-start | bytes 1572872 | tf_op jit(solution)/shard_map/ppermute | solution.py:59
  165.3 18.9 %collective-permute-start.9 = (bf16[1024,2048]{1,0:T(8,128)(2,1)}, bf16[1024,2048]{1,0:T(8,128)(2,1)}, u32[]{:S(2)}, u32[]{:S(2)}) collective-permute-start(bf16[1024,2048]{1,0:T(8,128)(2,1)} %shard_map.234.w0_ref), channel_id=1, source_target_pairs={{0,1},{1,0},{2,3},{3,2},{4,5},{5,4},{6,7},{7,6},{8,9},{9,8},{10,11... | collective-permute-start | bytes 12582920 | tf_op jit(solution)/shard_map/ppermute | solution.py:59
  165.3 18.9 %all-to-all-start.3 = ((bf16[8,256,256]{2,1,0:T(8,128)(2,1)}), bf16[8,256,256]{2,1,0:T(8,128)(2,1)S(1)}, u32[]{:S(2)}, u32[]{:S(2)}) async-start(bf16[8,256,256]{2,1,0:T(8,128)(2,1)} %bitcast.23), calls=%async_computation.3 | async-start | bytes 2097152 | tf_op jit(solution)/shard_map/all_to_all | solution.py:217
  168.8 270.5 %reduce-scatter.4.cloned.1.call-start = ((), (), s32[]{:S(2)}) async-start(), calls=%async_computation.15 | async-start | bytes 3932160 | tf_op jit(solution)/shard_map/reduce_scatter | solution.py:823
  197.0 22.3 %collective-permute-start.11 = (bf16[256,2048]{1,0:T(8,128)(2,1)}, bf16[256,2048]{1,0:T(8,128)(2,1)S(1)}, u32[]{:S(2)}, u32[]{:S(2)}) collective-permute-start(bf16[256,2048]{1,0:T(8,128)(2,1)} %get-tuple-element.97.refs_0_), channel_id=1, source_target_pairs={{0,4},{4,0},{1,5},{5,1},{2,6},{6,2},{3,7},{7,3},{8,12},{12,8},{9,1... | collective-permute-start | bytes 3145736 | tf_op jit(solution)/shard_map/ppermute | solution.py:59
  197.5 25.5 %collective-permute-start.10 = (bf16[256,2048]{1,0:T(8,128)(2,1)}, bf16[256,2048]{1,0:T(8,128)(2,1)S(1)}, u32[]{:S(2)}, u32[]{:S(2)}) collective-permute-start(bf16[256,2048]{1,0:T(8,128)(2,1)} %get-tuple-element.97.refs_0_), channel_id=1, source_target_pairs={{0,2},{2,0},{1,3},{3,1},{4,6},{6,4},{5,7},{7,5},{8,10},{10,8},{9,1... | collective-permute-start | bytes 3145736 | tf_op jit(solution)/shard_map/ppermute | solution.py:59
  219.3 16.9 %copy-start.11 = (bf16[256,2048]{1,0:T(8,128)(2,1)}, bf16[256,2048]{1,0:T(8,128)(2,1)S(1)}, u32[]{:S(2)}) copy-start(bf16[256,2048]{1,0:T(8,128)(2,1)S(1)} %collective-permute-done.11.refs_2_) | copy-start | bytes 3145732
  219.3 15.2 %collective-permute-start.12 = (bf16[128,2048]{1,0:T(8,128)(2,1)S(1)}, bf16[128,2048]{1,0:T(8,128)(2,1)S(1)}, u32[]{:S(2)}, u32[]{:S(2)}) collective-permute-start(bf16[128,2048]{1,0:T(8,128)(2,1)S(1)} %slice.191), channel_id=1, source_target_pairs={{0,2},{2,0},{1,3},{3,1},{4,6},{6,4},{5,7},{7,5},{8,10},{10,8},{9,1... | collective-permute-start | bytes 1572872 | tf_op jit(solution)/shard_map/ppermute | solution.py:59
  223.1 18.6 %copy-start.4 = (bf16[256,2048]{1,0:T(8,128)(2,1)S(1)}, bf16[256,2048]{1,0:T(8,128)(2,1)}, u32[]{:S(2)}) copy-start(bf16[256,2048]{1,0:T(8,128)(2,1)} %grad_ref.1) | copy-start | bytes 3145732
  223.1 13.1 %collective-permute-start.13 = (bf16[128,2048]{1,0:T(8,128)(2,1)S(1)}, bf16[128,2048]{1,0:T(8,128)(2,1)S(1)}, u32[]{:S(2)}, u32[]{:S(2)}) collective-permute-start(bf16[128,2048]{1,0:T(8,128)(2,1)S(1)} %slice.192), channel_id=1, source_target_pairs={{0,4},{4,0},{1,5},{5,1},{2,6},{6,2},{3,7},{7,3},{8,12},{12,8},{9,1... | collective-permute-start | bytes 1572872 | tf_op jit(solution)/shard_map/ppermute | solution.py:59
  241.7 23.4 %collective-permute-start.16 = (bf16[256,2048]{1,0:T(8,128)(2,1)S(1)}, bf16[256,2048]{1,0:T(8,128)(2,1)S(1)}, u32[]{:S(2)}, u32[]{:S(2)}) collective-permute-start(bf16[256,2048]{1,0:T(8,128)(2,1)S(1)} %copy-done.4), channel_id=1, source_target_pairs={{0,4},{4,0},{1,5},{5,1},{2,6},{6,2},{3,7},{7,3},{8,12},{12,8},{9,1... | collective-permute-start | bytes 3145736 | tf_op jit(solution)/shard_map/ppermute | solution.py:59
  242.0 24.4 %collective-permute-start.15 = (bf16[256,2048]{1,0:T(8,128)(2,1)S(1)}, bf16[256,2048]{1,0:T(8,128)(2,1)S(1)}, u32[]{:S(2)}, u32[]{:S(2)}) collective-permute-start(bf16[256,2048]{1,0:T(8,128)(2,1)S(1)} %copy-done.4), channel_id=1, source_target_pairs={{0,2},{2,0},{1,3},{3,1},{4,6},{6,4},{5,7},{7,5},{8,10},{10,8},{9,1... | collective-permute-start | bytes 3145736 | tf_op jit(solution)/shard_map/ppermute | solution.py:59
  265.2 11.4 %collective-permute-start.17 = (bf16[128,2048]{1,0:T(8,128)(2,1)S(1)}, bf16[128,2048]{1,0:T(8,128)(2,1)S(1)}, u32[]{:S(2)}, u32[]{:S(2)}) collective-permute-start(bf16[128,2048]{1,0:T(8,128)(2,1)S(1)} %slice.193), channel_id=1, source_target_pairs={{0,2},{2,0},{1,3},{3,1},{4,6},{6,4},{5,7},{7,5},{8,10},{10,8},{9,1... | collective-permute-start | bytes 1572872 | tf_op jit(solution)/shard_map/ppermute | solution.py:59
  266.5 11.4 %collective-permute-start.18 = (bf16[128,2048]{1,0:T(8,128)(2,1)S(1)}, bf16[128,2048]{1,0:T(8,128)(2,1)S(1)}, u32[]{:S(2)}, u32[]{:S(2)}) collective-permute-start(bf16[128,2048]{1,0:T(8,128)(2,1)S(1)} %slice.194), channel_id=1, source_target_pairs={{0,4},{4,0},{1,5},{5,1},{2,6},{6,2},{3,7},{7,3},{8,12},{12,8},{9,1... | collective-permute-start | bytes 1572872 | tf_op jit(solution)/shard_map/ppermute | solution.py:59
  268.2 15.3 %collective-permute-start.14 = (bf16[1024,2048]{1,0:T(8,128)(2,1)}, bf16[1024,2048]{1,0:T(8,128)(2,1)}, u32[]{:S(2)}, u32[]{:S(2)}) collective-permute-start(bf16[1024,2048]{1,0:T(8,128)(2,1)} %shard_map.236.act0_ref), channel_id=1, source_target_pairs={{0,1},{1,0},{2,3},{3,2},{4,5},{5,4},{6,7},{7,6},{8,9},{9,8},{10,11... | collective-permute-start | bytes 12582920 | tf_op jit(solution)/shard_map/ppermute | solution.py:59
  283.5 24.1 %collective-permute-start.19 = (bf16[1024,2048]{1,0:T(8,128)(2,1)}, bf16[1024,2048]{1,0:T(8,128)(2,1)}, u32[]{:S(2)}, u32[]{:S(2)}) collective-permute-start(bf16[1024,2048]{1,0:T(8,128)(2,1)} %shard_map.238.refs_0_.grad0_ref), channel_id=1, source_target_pairs={{0,1},{1,0},{2,3},{3,2},{4,5},{5,4},{6,7},{7,6},{8,9},{9,8},{10,11... | collective-permute-start | bytes 12582920 | tf_op jit(solution)/shard_map/ppermute | solution.py:59
  342.9 7.5 %collective-permute-start.20 = (bf16[1024,2048]{1,0:T(8,128)(2,1)}, bf16[1024,2048]{1,0:T(8,128)(2,1)}, u32[]{:S(2)}, u32[]{:S(2)}) collective-permute-start(bf16[1024,2048]{1,0:T(8,128)(2,1)} %shard_map.241), channel_id=1, source_target_pairs={{0,1},{1,0},{2,3},{3,2},{4,5},{5,4},{6,7},{7,6},{8,9},{9,8},{10,11... | collective-permute-start | bytes 12582920 | tf_op jit(solution)/shard_map/ppermute | solution.py:59
  343.0 185.1 %reduce-scatter.6.cloned.1.call-start = ((), (), s32[]{:S(2)}) async-start(), calls=%async_computation.16 | async-start | bytes 7864320 | tf_op jit(solution)/shard_map/reduce_scatter | solution.py:823
  389.7 7.5 %collective-permute-start.21 = (bf16[1024,2048]{1,0:T(8,128)(2,1)}, bf16[1024,2048]{1,0:T(8,128)(2,1)}, u32[]{:S(2)}, u32[]{:S(2)}) collective-permute-start(bf16[1024,2048]{1,0:T(8,128)(2,1)} %shard_map.244), channel_id=1, source_target_pairs={{0,1},{1,0},{2,3},{3,2},{4,5},{5,4},{6,7},{7,6},{8,9},{9,8},{10,11... | collective-permute-start | bytes 12582920 | tf_op jit(solution)/shard_map/ppermute | solution.py:59
  389.9 26.3 %collective-permute-start.22 = (bf16[256,2048]{1,0:T(8,128)(2,1)}, bf16[256,2048]{1,0:T(8,128)(2,1)S(1)}, u32[]{:S(2)}, u32[]{:S(2)}) collective-permute-start(bf16[256,2048]{1,0:T(8,128)(2,1)} %get-tuple-element.113), channel_id=1, source_target_pairs={{0,2},{2,0},{1,3},{3,1},{4,6},{6,4},{5,7},{7,5},{8,10},{10,8},{9,1... | collective-permute-start | bytes 3145736 | tf_op jit(solution)/shard_map/ppermute | solution.py:59
  391.5 47.8 %collective-permute-start.23 = (bf16[256,2048]{1,0:T(8,128)(2,1)}, bf16[256,2048]{1,0:T(8,128)(2,1)S(1)}, u32[]{:S(2)}, u32[]{:S(2)}) collective-permute-start(bf16[256,2048]{1,0:T(8,128)(2,1)} %get-tuple-element.114), channel_id=1, source_target_pairs={{0,4},{4,0},{1,5},{5,1},{2,6},{6,2},{3,7},{7,3},{8,12},{12,8},{9,1... | collective-permute-start | bytes 3145736 | tf_op jit(solution)/shard_map/ppermute | solution.py:59
  392.9 46.4 %collective-permute-start.24 = (bf16[256,2048]{1,0:T(8,128)(2,1)}, bf16[256,2048]{1,0:T(8,128)(2,1)S(1)}, u32[]{:S(2)}, u32[]{:S(2)}) collective-permute-start(bf16[256,2048]{1,0:T(8,128)(2,1)} %get-tuple-element.105), channel_id=1, source_target_pairs={{0,6},{2,4},{4,2},{6,0},{1,7},{3,5},{5,3},{7,1},{8,14},{10,12},{12... | collective-permute-start | bytes 3145736 | tf_op jit(solution)/shard_map/ppermute | solution.py:156
  416.2 23.2 %copy-start.18 = (bf16[256,2048]{1,0:T(8,128)(2,1)}, bf16[256,2048]{1,0:T(8,128)(2,1)S(1)}, u32[]{:S(2)}) copy-start(bf16[256,2048]{1,0:T(8,128)(2,1)S(1)} %collective-permute-done.22.x_ref) | copy-start | bytes 3145732
  456.7 14.9 %collective-permute-start.27 = (bf16[128,2048]{1,0:T(8,128)(2,1)S(1)}, bf16[128,2048]{1,0:T(8,128)(2,1)S(1)}, u32[]{:S(2)}, u32[]{:S(2)}) collective-permute-start(bf16[128,2048]{1,0:T(8,128)(2,1)S(1)} %get-tuple-element.168), channel_id=1, source_target_pairs={{0,2},{2,0},{1,3},{3,1},{4,6},{6,4},{5,7},{7,5},{8,10},{10,8},{9,1... | collective-permute-start | bytes 1572872 | tf_op jit(solution)/shard_map/ppermute | solution.py:59
  457.6 32.1 %all-to-all-start.4 = ((bf16[8,256,256]{2,1,0:T(8,128)(2,1)}), bf16[8,256,256]{2,1,0:T(8,128)(2,1)}, u32[]{:S(2)}, u32[]{:S(2)}) async-start(bf16[8,256,256]{2,1,0:T(8,128)(2,1)} %get-tuple-element.119), calls=%async_computation.5 | async-start | bytes 2097152 | tf_op jit(solution)/shard_map/all_to_all | solution.py:217
  461.9 135.5 %reduce-scatter.8.cloned.1.call-start = ((), (), s32[]{:S(2)}) async-start(), calls=%async_computation.17 | async-start | bytes 3932160 | tf_op jit(solution)/shard_map/reduce_scatter | solution.py:823
  463.7 24.3 %collective-permute-start.25 = (bf16[128,2048]{1,0:T(8,128)(2,1)}, bf16[128,2048]{1,0:T(8,128)(2,1)S(1)}, u32[]{:S(2)}, u32[]{:S(2)}) collective-permute-start(bf16[128,2048]{1,0:T(8,128)(2,1)} %get-tuple-element.167), channel_id=1, source_target_pairs={{0,4},{4,0},{1,5},{5,1},{2,6},{6,2},{3,7},{7,3},{8,12},{12,8},{9,1... | collective-permute-start | bytes 1572872 | tf_op jit(solution)/shard_map/ppermute | solution.py:59
  472.8 42.8 %collective-permute-start.28 = (bf16[256,2048]{1,0:T(8,128)(2,1)}, bf16[256,2048]{1,0:T(8,128)(2,1)S(1)}, u32[]{:S(2)}, u32[]{:S(2)}) collective-permute-start(bf16[256,2048]{1,0:T(8,128)(2,1)} %pad_maximum_fusion.1), channel_id=1, source_target_pairs={{0,4},{4,0},{1,5},{5,1},{2,6},{6,2},{3,7},{7,3},{8,12},{12,8},{9,1... | collective-permute-start | bytes 3145736 | tf_op jit(solution)/shard_map/ppermute | solution.py:59
  488.2 27.5 %collective-permute-start.26 = (bf16[256,2048]{1,0:T(8,128)(2,1)S(1)}, bf16[256,2048]{1,0:T(8,128)(2,1)S(1)}, u32[]{:S(2)}, u32[]{:S(2)}) collective-permute-start(bf16[256,2048]{1,0:T(8,128)(2,1)S(1)} %pad_maximum_fusion), channel_id=1, source_target_pairs={{0,2},{2,0},{1,3},{3,1},{4,6},{6,4},{5,7},{7,5},{8,10},{10,8},{9,1... | collective-permute-start | bytes 3145736 | tf_op jit(solution)/shard_map/ppermute | solution.py:59
  489.7 25.9 %copy-start.2 = (f32[256,2048]{1,0:T(8,128)S(1)}, f32[256,2048]{1,0:T(8,128)}, u32[]{:S(2)}) copy-start(f32[256,2048]{1,0:T(8,128)} %get-tuple-element.96.hidden_ref) | copy-start | bytes 6291460
  489.7 25.9 %copy-start.15 = (f32[256,2048]{1,0:T(8,128)S(1)}, f32[256,2048]{1,0:T(8,128)}, u32[]{:S(2)}) copy-start(f32[256,2048]{1,0:T(8,128)} %get-tuple-element.123) | copy-start | bytes 6291460
  535.5 25.8 %collective-permute-start.29 = (bf16[1024,2048]{1,0:T(8,128)(2,1)}, bf16[1024,2048]{1,0:T(8,128)(2,1)}, u32[]{:S(2)}, u32[]{:S(2)}) collective-permute-start(bf16[1024,2048]{1,0:T(8,128)(2,1)} %shard_map.249), channel_id=1, source_target_pairs={{0,1},{1,0},{2,3},{3,2},{4,5},{5,4},{6,7},{7,6},{8,9},{9,8},{10,11... | collective-permute-start | bytes 12582920 | tf_op jit(solution)/shard_map/ppermute | solution.py:59
  535.5 25.6 %collective-permute-start.34 = (bf16[256,2048]{1,0:T(8,128)(2,1)S(1)}, bf16[256,2048]{1,0:T(8,128)(2,1)S(1)}, u32[]{:S(2)}, u32[]{:S(2)}) collective-permute-start(bf16[256,2048]{1,0:T(8,128)(2,1)S(1)} %copy-done.37), channel_id=1, source_target_pairs={{0,4},{4,0},{1,5},{5,1},{2,6},{6,2},{3,7},{7,3},{8,12},{12,8},{9,1... | collective-permute-start | bytes 3145736 | tf_op jit(solution)/shard_map/ppermute | solution.py:59
  536.0 25.2 %collective-permute-start.33 = (bf16[256,2048]{1,0:T(8,128)(2,1)S(1)}, bf16[256,2048]{1,0:T(8,128)(2,1)S(1)}, u32[]{:S(2)}, u32[]{:S(2)}) collective-permute-start(bf16[256,2048]{1,0:T(8,128)(2,1)S(1)} %copy-done.37), channel_id=1, source_target_pairs={{0,2},{2,0},{1,3},{3,1},{4,6},{6,4},{5,7},{7,5},{8,10},{10,8},{9,1... | collective-permute-start | bytes 3145736 | tf_op jit(solution)/shard_map/ppermute | solution.py:59
  561.4 13.5 %collective-permute-start.35 = (bf16[128,2048]{1,0:T(8,128)(2,1)S(1)}, bf16[128,2048]{1,0:T(8,128)(2,1)S(1)}, u32[]{:S(2)}, u32[]{:S(2)}) collective-permute-start(bf16[128,2048]{1,0:T(8,128)(2,1)S(1)} %slice.165), channel_id=1, source_target_pairs={{0,2},{2,0},{1,3},{3,1},{4,6},{6,4},{5,7},{7,5},{8,10},{10,8},{9,1... | collective-permute-start | bytes 1572872 | tf_op jit(solution)/shard_map/ppermute | solution.py:59
  561.7 13.3 %collective-permute-start.36 = (bf16[128,2048]{1,0:T(8,128)(2,1)S(1)}, bf16[128,2048]{1,0:T(8,128)(2,1)S(1)}, u32[]{:S(2)}, u32[]{:S(2)}) collective-permute-start(bf16[128,2048]{1,0:T(8,128)(2,1)S(1)} %slice.166), channel_id=1, source_target_pairs={{0,4},{4,0},{1,5},{5,1},{2,6},{6,2},{3,7},{7,3},{8,12},{12,8},{9,1... | collective-permute-start | bytes 1572872 | tf_op jit(solution)/shard_map/ppermute | solution.py:59
  580.7 20.7 %copy-start = (bf16[256,2048]{1,0:T(8,128)(2,1)S(1)}, bf16[256,2048]{1,0:T(8,128)(2,1)}, u32[]{:S(2)}) copy-start(bf16[256,2048]{1,0:T(8,128)(2,1)} %token_ref.1) | copy-start | bytes 3145732
  580.7 39.1 %collective-permute-start.37 = (bf16[1024,2048]{1,0:T(8,128)(2,1)}, bf16[1024,2048]{1,0:T(8,128)(2,1)}, u32[]{:S(2)}, u32[]{:S(2)}) collective-permute-start(bf16[1024,2048]{1,0:T(8,128)(2,1)} %shard_map.251.refs_2_), channel_id=1, source_target_pairs={{0,1},{1,0},{2,3},{3,2},{4,5},{5,4},{6,7},{7,6},{8,9},{9,8},{10,11... | collective-permute-start | bytes 12582920 | tf_op jit(solution)/shard_map/ppermute | solution.py:59
  597.4 16.5 %all-to-all-start.8 = ((bf16[8,64,768]{2,1,0:T(8,128)(2,1)}), bf16[8,64,768]{2,1,0:T(8,128)(2,1)S(1)}, u32[]{:S(2)}, u32[]{:S(2)}) async-start(bf16[8,64,768]{2,1,0:T(8,128)(2,1)} %bitcast.73), calls=%async_computation.11 | async-start | bytes 1572864 | tf_op jit(solution)/shard_map/all_to_all | solution.py:217
  613.9 43.3 %all-to-all-start.6 = ((bf16[8,64,1536]{2,1,0:T(8,128)(2,1)}), bf16[8,64,1536]{2,1,0:T(8,128)(2,1)S(1)}, u32[]{:S(2)}, u32[]{:S(2)}) async-start(bf16[8,64,1536]{2,1,0:T(8,128)(2,1)} %bitcast.71), calls=%async_computation.9 | async-start | bytes 3145728 | tf_op jit(solution)/shard_map/all_to_all | solution.py:217
  628.0 9.0 %collective-permute-start.40 = (bf16[64,2048]{1,0:T(8,128)(2,1)S(1)}, bf16[64,2048]{1,0:T(8,128)(2,1)S(1)}, u32[]{:S(2)}, u32[]{:S(2)}) collective-permute-start(bf16[64,2048]{1,0:T(8,128)(2,1)S(1)} %get-tuple-element.164), channel_id=1, source_target_pairs={{0,8},{24,16},{1,9},{25,17},{2,10},{26,18},{3,11},{27,19},{4,12},{... | collective-permute-start | bytes 786440 | tf_op jit(solution)/shard_map/ppermute | solution.py:207
  631.2 52.3 %collective-permute-start.32 = (bf16[256,2048]{1,0:T(8,128)(2,1)}, bf16[256,2048]{1,0:T(8,128)(2,1)}, u32[]{:S(2)}, u32[]{:S(2)}) collective-permute-start(bf16[256,2048]{1,0:T(8,128)(2,1)} %get-tuple-element.133), channel_id=1, source_target_pairs={{0,6},{2,4},{4,2},{6,0},{1,7},{3,5},{5,3},{7,1},{8,14},{10,12},{12... | collective-permute-start | bytes 3145736 | tf_op jit(solution)/shard_map/ppermute | solution.py:156
  634.1 48.5 %collective-permute-start.30 = (bf16[256,2048]{1,0:T(8,128)(2,1)}, bf16[256,2048]{1,0:T(8,128)(2,1)}, u32[]{:S(2)}, u32[]{:S(2)}) collective-permute-start(bf16[256,2048]{1,0:T(8,128)(2,1)} %get-tuple-element.131), channel_id=1, source_target_pairs={{0,2},{2,0},{1,3},{3,1},{4,6},{6,4},{5,7},{7,5},{8,10},{10,8},{9,1... | collective-permute-start | bytes 3145736 | tf_op jit(solution)/shard_map/ppermute | solution.py:59
  634.7 48.8 %collective-permute-start.31 = (bf16[256,2048]{1,0:T(8,128)(2,1)}, bf16[256,2048]{1,0:T(8,128)(2,1)}, u32[]{:S(2)}, u32[]{:S(2)}) collective-permute-start(bf16[256,2048]{1,0:T(8,128)(2,1)} %get-tuple-element.132), channel_id=1, source_target_pairs={{0,4},{4,0},{1,5},{5,1},{2,6},{6,2},{3,7},{7,3},{8,12},{12,8},{9,1... | collective-permute-start | bytes 3145736 | tf_op jit(solution)/shard_map/ppermute | solution.py:59
  634.8 27.2 %collective-permute-start.38 = (bf16[64,2048]{1,0:T(8,128)(2,1)S(1)}, bf16[64,2048]{1,0:T(8,128)(2,1)}, u32[]{:S(2)}, u32[]{:S(2)}) collective-permute-start(bf16[64,2048]{1,0:T(8,128)(2,1)S(1)} %get-tuple-element.164), channel_id=1, source_target_pairs={{8,16},{16,8},{9,17},{17,9},{10,18},{18,10},{11,19},{19,11},{12,20... | collective-permute-start | bytes 786440 | tf_op jit(solution)/shard_map/ppermute | solution.py:208
  637.0 8.6 %collective-permute-start.39 = (bf16[64,2048]{1,0:T(8,128)(2,1)S(1)}, bf16[64,2048]{1,0:T(8,128)(2,1)S(1)}, u32[]{:S(2)}, u32[]{:S(2)}) collective-permute-start(bf16[64,2048]{1,0:T(8,128)(2,1)S(1)} %get-tuple-element.163), channel_id=1, source_target_pairs={{0,8},{8,0},{16,24},{24,16},{1,9},{9,1},{17,25},{25,17},{2,10},{10... | collective-permute-start | bytes 786440 | tf_op jit(solution)/shard_map/ppermute | solution.py:209
  646.3 15.6 %collective-permute-start.41 = (bf16[64,2048]{1,0:T(8,128)(2,1)}, bf16[64,2048]{1,0:T(8,128)(2,1)}, u32[]{:S(2)}, u32[]{:S(2)}) collective-permute-start(bf16[64,2048]{1,0:T(8,128)(2,1)} %fusion.13), channel_id=1, source_target_pairs={{0,16},{8,24},{16,0},{24,8},{1,17},{9,25},{17,1},{25,9},{2,18},{10... | collective-permute-start | bytes 786440 | tf_op jit(solution)/shard_map/ppermute | solution.py:210
  658.4 25.1 %copy-start.14 = (f32[256,2048]{1,0:T(8,128)S(1)}, f32[256,2048]{1,0:T(8,128)}, u32[]{:S(2)}) copy-start(f32[256,2048]{1,0:T(8,128)} %get-tuple-element.150) | copy-start | bytes 6291460
  687.7 10.3 %all-to-all-start.7 = ((f32[32,1,448]{2,1,0:T(1,128)}), f32[32,1,448]{2,1,0:T(1,128)S(1)}, u32[]{:S(2)}, u32[]{:S(2)}) async-start(f32[32,1,448]{2,1,0:T(1,128)} %all_to_all.44), calls=%async_computation.10 | async-start | bytes 131072 | tf_op jit(solution)/shard_map/all_to_all | solution.py:888
  (31 other events, 171.9 us)
Sparse Core Ops, SparseCore 0:
  9.6 33.6 all-gather.5
  54.0 62.9 all-gather.3
  118.5 165.5 all-gather.7
  343.1 60.6 reduce-scatter.3
  406.0 110.7 reduce-scatter.5
  536.4 60.9 reduce-scatter.7

commit v3 on v2

--- a/solution.py
+++ b/solution.py
@@ -67,7 +67,7 @@
         at += piece.shape[0]
 
 
-def join(pieces, lead=0):
+def join(pieces, time=5):
     rows, width = sum(piece.shape[0] for piece in pieces), pieces[0].shape[1]
     return pl.pallas_call(
         join_kernel,
@@ -75,23 +75,26 @@
         in_specs=[pl.BlockSpec((piece.shape[0], width // 4), lambda i: (0, i)) for piece in pieces],
         out_specs=pl.BlockSpec((rows, width // 4), lambda i: (0, i)),
         out_shape=jax.ShapeDtypeStruct((rows, width), pieces[0].dtype),
-        **limits(lead),
+        **limits(time),
     )(*pieces)
 
 
-def chip_pieces(rows, *first):
+def near_pieces(rows):
+    return swap(rows, "x"), swap(rows, "y")
+
+
+def chip_pieces(rows, *first, near=None):
     half = rows.shape[0] // 2
-    over_x = swap(rows, "x")
-    over_y = swap(rows, "y")
+    over_x, over_y = near or near_pieces(rows)
     if first:
         over_x, over_y = lax.optimization_barrier((over_x, over_y, *first))[:2]
     return [rows, over_x, over_y, swap(over_y[:half], "x"), swap(over_x[half:], "y")]
 
 
-def halves_of(pieces, *first, lead=0):
+def halves_of(pieces, *first, time=5):
     if first:
         pieces = lax.optimization_barrier((*pieces, *first))[: len(pieces)]
-    mine = join(pieces, lead)
+    mine = join(pieces, time)
     return mine, swap(mine, "c")
 
 
@@ -118,23 +121,29 @@
     return jnp.where(s == 0, 3, jnp.where(s == 3, 0, s))
 
 
-def plane_send(left, right, at, lead=0):
+def columns_of(right, at, depth):
+    if right.shape[1] == depth:
+        return pl.BlockSpec(right.shape, lambda s: (0, 0))
+    return pl.BlockSpec((pl.Element(right.shape[0]), pl.Element(depth)), lambda s: (0, at))
+
+
+def plane_send(left, right, at, time=None):
     rows, depth, width = left.shape[0] // 8, left.shape[1], right.shape[0]
     terms = pl.pallas_call(
         send_kernel,
         grid=(2,),
         in_specs=[
             pl.BlockSpec((2 * rows, depth), lambda s: (s + 2, 0)),
-            pl.BlockSpec((width, depth), lambda s: (0, at)),
+            columns_of(right, at, depth),
         ],
         out_specs=pl.BlockSpec((2 * rows, width), lambda s: (s, 0)),
         out_shape=jax.ShapeDtypeStruct((4 * rows, width), bf16),
-        **limits(lead),
+        **limits(depth // 134 if time is None else time),
     )(left, right)
     return swap(terms, "c")
 
 
-def plane_keep(left, right, at, other, kind=f32, lead=0):
+def plane_keep(left, right, at, other, kind=f32, time=None):
     rows, depth, width = left.shape[0] // 8, left.shape[1], right.shape[0]
     whole = pl.BlockSpec((rows, width), lambda s: (0, 0))
     return pl.pallas_call(
@@ -142,12 +151,12 @@
         grid=(4,),
         in_specs=[
             pl.BlockSpec((rows, depth), lambda s: (corner_first(s), 0)),
-            pl.BlockSpec((width, depth), lambda s: (0, at)),
+            columns_of(right, at, depth),
             pl.BlockSpec((rows, width), lambda s: (corner_first(s), 0)),
         ],
         out_specs=[whole] * 4,
         out_shape=[jax.ShapeDtypeStruct((rows, width), kind) for kind in (bf16, kind, kind, f32)],
-        **limits(lead),
+        **limits(depth // 114 if time is None else time),
     )(left, right, other)
 
 
@@ -176,41 +185,54 @@
     return sum(term.astype(f32) for term in terms[1:]) + terms[0]
 
 
-def sum_kernel(count, *refs):
-    *in_refs, out_ref = refs
-    total = tn(in_refs[0][...], in_refs[count][...])
-    for left_ref, right_ref in zip(in_refs[1:count], in_refs[count + 1 :]):
-        total += tn(left_ref[...], right_ref[...])
-    out_ref[...] = total.astype(bf16)
-
-
-def row_sum(left, right, lead=0):
-    width, columns = left[0].shape[1], right[0].shape[1]
+def sum_kernel(*refs):
+    *left_refs, right_ref, out_ref = refs
+    total, at = None, 0
+    for left_ref in left_refs:
+        part = tn(left_ref[...], right_ref[at : at + left_ref.shape[0], :])
+        total = part if total is None else total + part
+        at += left_ref.shape[0]
+    out_ref[...] = total[:, : out_ref.shape[1]].astype(bf16)
+
+
+def row_sum(left, right, kept=None, time=None):
+    width, (rows, columns) = left[0].shape[1], right.shape
+    kept = kept or columns
     step = min(width, 512)
-    rows = sum(piece.shape[0] for piece in left)
-    return pl.pallas_call(
-        functools.partial(sum_kernel, len(left)),
+    return pl.pallas_call(
+        sum_kernel,
         grid=(width // step,),
         in_specs=[
             *[pl.BlockSpec((piece.shape[0], step), lambda i: (0, i)) for piece in left],
-            *[pl.BlockSpec(piece.shape, lambda i: (0, 0)) for piece in right],
+            pl.BlockSpec((rows, columns), lambda i: (0, 0)),
         ],
-        out_specs=pl.BlockSpec((step, columns), lambda i: (i, 0)),
+        out_specs=pl.BlockSpec((step, kept), lambda i: (i, 0)),
+        out_shape=jax.ShapeDtypeStruct((width, kept), bf16),
+        **limits(columns // 83 if time is None else time),
+    )(*left, right)
+
+
+def pair_kernel(left0_ref, left1_ref, right0_ref, right1_ref, out_ref):
+    out_ref[...] = (tn(left0_ref[0], right0_ref[...]) + tn(left1_ref[0], right1_ref[...])).astype(bf16)
+
+
+def pair_sum(left, right, time):
+    _, rows, width = left.shape
+    columns = right[0].shape[1]
+    step = columns // 4
+    return pl.pallas_call(
+        pair_kernel,
+        grid=(4,),
+        in_specs=[
+            pl.BlockSpec((1, rows, width), lambda i: (0, 0, 0)),
+            pl.BlockSpec((1, rows, width), lambda i: (1, 0, 0)),
+            pl.BlockSpec((rows, step), lambda i: (0, i)),
+            pl.BlockSpec((rows, step), lambda i: (0, i)),
+        ],
+        out_specs=pl.BlockSpec((width, step), lambda i: (0, i)),
         out_shape=jax.ShapeDtypeStruct((width, columns), bf16),
-        **limits(lead),
-    )(*left, *right)
-
-
-def deep_reduce(blocks):
-    depth = lax.axis_index("g")
-    slots = [lax.dynamic_index_in_dim(blocks, jnp.bitwise_xor(depth, j), 0, False) for j in range(4)]
-    ends = lax.ppermute(slots[3], "g", [(0, 1), (3, 2)])
-    middle = lax.ppermute(slots[3], "g", [(1, 2), (2, 1)])
-    near = lax.ppermute(slots[1], "g", [(0, 1), (1, 0), (2, 3), (3, 2)])
-    far = lax.ppermute(
-        (slots[2].astype(f32) + ends.astype(f32)).astype(bf16), "g", [(0, 2), (1, 3), (2, 0), (3, 1)]
-    )
-    return slots[0].astype(f32) + middle.astype(f32) + near.astype(f32) + far.astype(f32)
+        **limits(time),
+    )(left, left, *right)
 
 
 def plane_all_to_all(blocks):
@@ -318,10 +340,13 @@
         put(block, 2, dv_ref[span, :])
 
 
-def limits(lead=0):
+SHORT = 6
+
+
+def limits(time):
     return dict(
         compiler_params=pltpu.CompilerParams(vmem_limit_bytes=56 * 1024 * 1024),
-        cost_estimate=pl.CostEstimate(flops=lead * 10**9, bytes_accessed=lead * 3 * 10**6, transcendentals=0),
+        cost_estimate=pl.CostEstimate(flops=time * 10**9 // SHORT, bytes_accessed=time * 3 * 10**6 // SHORT, transcendentals=0),
     )
 
 
@@ -337,7 +362,7 @@
     return pl.BlockSpec((1, *shape), lambda p, h, place: (jnp.bitwise_xor(p, place[2]), *rest))
 
 
-def attention(place, qkv, blocks, seg_col, seg_row, lead=0):
+def attention(place, qkv, blocks, seg_col, seg_row):
     packs, seq, width = qkv.shape
     width //= 3
     rows, pairs = seq // blocks, width // PAIR
@@ -360,11 +385,11 @@
             jax.ShapeDtypeStruct((2, packs, 2, rows, width), bf16),
             jax.ShapeDtypeStruct((packs, pairs, 2, seq), f32),
         ],
-        **limits(lead),
+        **limits(16),
     )(place, qkv, qkv, qkv, seg_col, seg_row)
 
 
-def attention_back(place, qkv, grad, totals, cosine, sine, seg_col, seg_row, lead=0):
+def attention_back(place, qkv, grad, totals, cosine, sine, seg_col, seg_row, time=25):
     packs, blocks, rows, width = grad.shape
     pairs, seq = width // PAIR, blocks * rows
     return pl.pallas_call(
@@ -384,7 +409,7 @@
             scratch_shapes=[pltpu.VMEM((seq, PAIR), f32)] * 2,
         ),
         out_shape=jax.ShapeDtypeStruct((2, packs, 2, rows, 3 * width), bf16),
-        **limits(lead),
+        **limits(time),
     )(place, qkv, qkv, qkv, grad, totals, cosine, sine, seg_col, seg_row)
 
 
@@ -398,12 +423,12 @@
             at += step
 
 
-def norm_rows(pieces, gain, shift, lead=0):
+def norm_rows(pieces, gain, shift):
     count, width = sum(piece.shape[0] for piece in pieces), gain.shape[1]
     return pl.pallas_call(
         norm_kernel,
         out_shape=jax.ShapeDtypeStruct((count, width), bf16),
-        **limits(lead),
+        **limits(7),
     )(*pieces, gain, shift)
 
 
@@ -425,7 +450,7 @@
         out_ref[0, :, at : at + PAIR] = part.astype(bf16)
 
 
-def project(place, act, weight, bias, cosine, sine, lead=0):
+def project(place, act, weight, bias, cosine, sine):
     count, depth = act[0].shape
     width = weight.shape[1]
     packs, seq, _ = cosine.shape
@@ -457,7 +482,7 @@
         out_shape=[
             jax.ShapeDtypeStruct((packs, seq, width), bf16), jax.ShapeDtypeStruct((2 * count, depth), bf16)
         ],
-        **limits(lead),
+        **limits(15),
     )(place, *act, weight, bias, cosine, sine)
 
 
@@ -495,7 +520,7 @@
         act_ref[...] = (layer_stats(hidden)[0] * gain_ref[...] + shift_ref[...]).astype(bf16)
 
 
-def out_rows_of(place, mixed, weight, tokens, gain, shift, lead=0):
+def out_rows_of(place, mixed, weight, tokens, gain, shift):
     rows, width = tokens.shape
     part = mixed.shape[2]
     whole = pl.BlockSpec((rows, width), lambda s, place: (0, 0))
@@ -513,7 +538,7 @@
             scratch_shapes=[pltpu.VMEM((rows, width), f32)],
         ),
         out_shape=[jax.ShapeDtypeStruct((rows, width), f32), jax.ShapeDtypeStruct((rows, width), bf16)],
-        **limits(lead),
+        **limits(12),
     )(place, mixed, *weight, tokens, gain, shift)
 
 
@@ -542,7 +567,7 @@
         mixed_ref[0] = nt(low_ref[...], w1_ref[...]).astype(bf16)
 
 
-def out_back_rows(place, terms, hidden, out_grad, gain, weight, lead=0):
+def out_back_rows(place, terms, hidden, out_grad, gain, weight, time=15):
     rows, width = hidden.shape
     part = weight[0].shape[0] // 4
     whole = pl.BlockSpec((rows, width), lambda s, place: (0, 0))
@@ -564,7 +589,7 @@
             jax.ShapeDtypeStruct((rows, width), bf16),
             jax.ShapeDtypeStruct((2, width), f32),
         ],
-        **limits(lead),
+        **limits(time),
     )(place, *terms, hidden, out_grad, gain, *weight)
 
 
@@ -575,8 +600,10 @@
     act = pick((act0_ref, act1_ref), STEPS)
     act_ref[...] = act
     both = nn(act, weight_ref[...])
-    half = both.shape[1] // 2
-    gate, up = both[:, :half], both[:, half:]
+    half, wide = both.shape[1] // 2, middle_ref.shape[1]
+    inside = lax.broadcasted_iota(jnp.int32, (both.shape[0], wide), 1) < half
+    gate = jnp.where(inside, both[:, :wide], 0.0)
+    up = jnp.where(inside, pltpu.roll(both[:, 2 * half - wide :], half, 1), 0.0)
     sigmoid = jax.nn.sigmoid(gate)
     silu = gate * sigmoid
     middle_ref[...] = (silu * up).astype(bf16)
@@ -584,42 +611,46 @@
     by_up_ref[...] = silu.astype(bf16)
 
 
-def gate_rows(act, weight, lead=0):
+def gate_rows(act, weight, half):
     count, depth = act[0].shape
     count *= 2
-    half, rows = weight.shape[1] // 3, count // STEPS
-    out = pl.BlockSpec((rows, half), lambda s: (s, 0))
+    wide, rows = -(-half // PAIR) * PAIR, count // STEPS
+    out = pl.BlockSpec((rows, wide), lambda s: (s, 0))
     return pl.pallas_call(
         gate_kernel,
         grid=(STEPS,),
         in_specs=[*half_specs(rows, depth, STEPS), pl.BlockSpec((depth, 2 * half), lambda s: (0, 0))],
         out_specs=[out] * 3 + [pl.BlockSpec((rows, depth), lambda s: (s, 0))],
-        out_shape=[jax.ShapeDtypeStruct((count, half), bf16)] * 3 + [jax.ShapeDtypeStruct((count, depth), bf16)],
-        **limits(lead),
+        out_shape=[jax.ShapeDtypeStruct((count, wide), bf16)] * 3 + [jax.ShapeDtypeStruct((count, depth), bf16)],
+        **limits(20),
     )(*act, weight)
 
 
 def gate_back_kernel(grad0_ref, grad1_ref, weight_ref, by_gate_ref, by_up_ref, out_ref):
     middle = nn(pick((grad0_ref, grad1_ref), STEPS), weight_ref[...])
-    half = middle.shape[1]
-    out_ref[:, :half] = (middle * by_gate_ref[...].astype(f32)).astype(bf16)
-    out_ref[:, half:] = (middle * by_up_ref[...].astype(f32)).astype(bf16)
-
-
-def gate_back_rows(grad, weight, by_gate, by_up, lead=0):
+    gate = middle * by_gate_ref[...].astype(f32)
+    half, wide = out_ref.shape[1] // 2, middle.shape[1]
+    up = pltpu.roll(middle * by_up_ref[...].astype(f32), half - (2 * half - wide), 1)
+    cut = 2 * half - wide
+    out_ref[:, :cut] = gate[:, :cut].astype(bf16)
+    out_ref[:, cut:wide] = (gate[:, cut:] + up[:, : wide - cut]).astype(bf16)
+    out_ref[:, wide:] = up[:, wide - cut :].astype(bf16)
+
+
+def gate_back_rows(grad, weight, by_gate, by_up, half):
     count, depth = grad[0].shape
     count *= 2
-    half, rows = weight.shape[1] // 3, count // STEPS
-    part = pl.BlockSpec((rows, half), lambda s: (s, 0))
+    wide, rows = by_gate.shape[1], count // STEPS
+    part = pl.BlockSpec((rows, wide), lambda s: (s, 0))
     return pl.pallas_call(
         gate_back_kernel,
         grid=(STEPS,),
         in_specs=[
-            *half_specs(rows, depth, STEPS), pl.BlockSpec((depth, half), lambda s: (0, 2)), part, part
+            *half_specs(rows, depth, STEPS), columns_of(weight, 2 * half, wide), part, part
         ],
         out_specs=pl.BlockSpec((rows, 2 * half), lambda s: (s, 0)),
         out_shape=jax.ShapeDtypeStruct((count, 2 * half), bf16),
-        **limits(lead),
+        **limits(13),
     )(*grad, weight, by_gate, by_up)
 
 
@@ -645,12 +676,12 @@
             out_ref[p, :, chunk * HEAD_DIM : (chunk + 2) * HEAD_DIM] = halves(*low, *high).astype(bf16)
 
 
-def split_heads(weight, team, lead=0):
+def split_heads(weight, team):
     rows, width = weight.shape
     return pl.pallas_call(
         functools.partial(split_heads_kernel, team),
         out_shape=jax.ShapeDtypeStruct((team, rows, width // team), bf16),
-        **limits(lead),
+        **limits(2),
     )(weight)
 
 
@@ -671,64 +702,62 @@
             out_ref[:, to : to + PAIR] = halves(*lane_group(load, at), *lane_group(load_next, at))
 
 
-def merge_heads(parts, lead=0):
+def merge_heads(parts):
     team, rows, width = parts.shape
     return pl.pallas_call(
         merge_heads_kernel,
         out_shape=jax.ShapeDtypeStruct((rows, team * width), f32),
-        **limits(lead),
+        **limits(2),
     )(parts)
 
 
 def split_ffn_kernel(team, my_ffn, *refs):
     *weight_refs, out_ref = refs
-    pad = out_ref.shape[2] // len(weight_refs)
-    for which, weight_ref in enumerate(weight_refs):
-
-        def load(at):
-            return weight_ref[:, at : at + PAIR].astype(f32)
-
-        for p in range(team):
-            for at in range(0, pad, PAIR):
-                source = p * my_ffn + at
-                low = lane_group(load, source)
-                if at + HEAD_DIM < my_ffn:
-                    part = halves(*low, *lane_group(load, source + HEAD_DIM))
-                else:
-                    part = halves(*low, jnp.zeros_like(low[0]), HEAD_DIM)
-                out_ref[p, :, which * pad + at : which * pad + at + PAIR] = part.astype(bf16)
-
-
-def split_ffn(weights, team, pad, lead=0):
+    steps = my_ffn // HEAD_DIM
+
+    def chunk(p, at):
+        which, inside = at // steps, at % steps * HEAD_DIM
+        if which == len(weight_refs):
+            return jnp.zeros((out_ref.shape[1], PAIR), f32), at % 2 * HEAD_DIM
+        return lane_group(
+            lambda lane: weight_refs[which][:, lane : lane + PAIR].astype(f32), p * my_ffn + inside
+        )
+
+    for p in range(team):
+        for at in range(0, out_ref.shape[2], PAIR):
+            first = at // HEAD_DIM
+            out_ref[p, :, at : at + PAIR] = halves(*chunk(p, first), *chunk(p, first + 1)).astype(bf16)
+
+
+def split_ffn(weights, team, packed):
     rows, width = weights[0].shape
     return pl.pallas_call(
         functools.partial(split_ffn_kernel, team, width // team),
-        out_shape=jax.ShapeDtypeStruct((team, rows, len(weights) * pad), bf16),
-        **limits(lead),
+        out_shape=jax.ShapeDtypeStruct((team, rows, packed), bf16),
+        **limits(3),
     )(*weights)
 
 
 def merge_ffn_kernel(my_ffn, part_ref, *out_refs):
     team = part_ref.shape[0]
-    pad = part_ref.shape[2] // len(out_refs)
     for which, out_ref in enumerate(out_refs):
 
         def chunk(at):
             p, inside = at // my_ffn, at % my_ffn
-            return lane_group(
-                lambda lane: part_ref[p, :, which * pad + lane : which * pad + lane + PAIR].astype(f32), inside
-            )
+            group, lane = (which * my_ffn + inside) // PAIR * PAIR, (which * my_ffn + inside) % PAIR
+            return part_ref[p, :, group : group + PAIR].astype(f32), lane
 
         for at in range(0, team * my_ffn, PAIR):
             out_ref[:, at : at + PAIR] = halves(*chunk(at), *chunk(at + HEAD_DIM))
 
 
-def merge_ffn(parts, count, ffn, lead=0):
+def merge_ffn(parts, count, ffn):
     team, rows, width = parts.shape
+    parts = jnp.pad(parts, ((0, 0), (0, 0), (0, -width % PAIR)))
     return pl.pallas_call(
         functools.partial(merge_ffn_kernel, ffn // team),
         out_shape=[jax.ShapeDtypeStruct((rows, ffn), f32)] * count,
-        **limits(lead),
+        **limits(3),
     )(parts)
 
 
@@ -749,7 +778,7 @@
     my_heads = heads // team
     my_width = my_heads * HEAD_DIM
     my_ffn = ffn // team
-    pad_ffn = -(-my_ffn // 128) * 128
+    packed = -(-3 * my_ffn // PAIR) * PAIR
     me = lax.axis_index(PLANE)
     place = jnp.stack(
         [lax.axis_index("x"), lax.axis_index("c"), lax.axis_index("y"), me]
@@ -774,9 +803,9 @@
     token_pieces = chip_pieces(tokens)
     qkv_send = after(split_heads(qkv_weight, team), small)
     qkv_mine = plane_all_to_all(qkv_send).reshape(team * shard, 3 * my_width)
-    ffn_send = split_ffn([gate_weight, up_weight, down_weight], team, pad_ffn)
+    ffn_send = split_ffn([gate_weight, up_weight, down_weight], team, packed)
     ffn_send = after(ffn_send, qkv_mine, *token_pieces)
-    ffn_mine = plane_all_to_all(ffn_send).reshape(team * shard, 3 * pad_ffn)
+    ffn_mine = plane_all_to_all(ffn_send).reshape(team * shard, packed)
 
     frequency = rope_base ** (-jnp.arange(0, ROT_DIMS, 2, dtype=f32) / ROT_DIMS)
     within = jnp.arange(PAIR) % HEAD_DIM
@@ -806,8 +835,8 @@
     ffn_full = over_g(ffn_mine)
     qkv_full = after(qkv_full, act_one[0], ffn_mine)
 
-    qkv, act_one = project(place, act_one, qkv_full, bias_mine, cosine, sine, lead=40)
-    mixed, mixed_halves, totals = attention(place, qkv, blocks, seg_col, seg_row, lead=40)
+    qkv, act_one = project(place, act_one, qkv_full, bias_mine, cosine, sine)
+    mixed, mixed_halves, totals = attention(place, qkv, blocks, seg_col, seg_row)
     if aligned:
         out_full = halves_of(chip_pieces(out_rows, qkv), mixed)
     hidden, act_two = out_rows_of(
@@ -815,9 +844,12 @@
     )
 
     act_two = halves_of(chip_pieces(act_two))
-    cotangent = halves_of(chip_pieces(after(out_grad, act_two[0])))
-    middle_low, by_gate, by_up, act_all = gate_rows(act_two, ffn_full)
-    down_sum = row_sum(cotangent, (middle_low[: 4 * rows], middle_low[4 * rows :]))
+    cotangent = chip_pieces(after(out_grad, act_two[0]))
+    middle_low, by_gate, by_up, act_all = gate_rows(act_two, ffn_full, my_ffn)
+    cotangent = halves_of(cotangent, middle_low)
+    output_other = plane_send(middle_low, ffn_full, 2 * my_ffn)
+    down_sum = row_sum(cotangent, middle_low, kept=my_ffn)
+    output_kept = plane_keep(after(middle_low, down_sum), ffn_full, 2 * my_ffn, output_other)
 
     def own_rows(grad_sum):
         return lax.psum_scatter(grad_sum, "g", scatter_dimension=0, tiled=True)
@@ -825,37 +857,33 @@
     def back_to_rows(columns):
         return plane_all_to_all(columns.reshape(team, shard, columns.shape[1]))
 
-    gate_up_grad = gate_back_rows(after(cotangent, down_sum), ffn_full, by_gate, by_up)
-    norm_two_other = plane_send(gate_up_grad, ffn_full, 0)
+    down_own = own_rows(down_sum)
+    gate_up_grad = gate_back_rows(after(cotangent, output_kept[0]), ffn_full, by_gate, by_up, my_ffn)
+    output_terms = after(plane_corner(output_kept), gate_up_grad)
+    norm_two_other = plane_send(after(gate_up_grad, output_terms[0]), ffn_full, 0)
     norm_two_kept = plane_keep(gate_up_grad, ffn_full, 0, norm_two_other, bf16)
-    gate_up_sum = row_sum([act_all], [after(gate_up_grad, norm_two_kept[0])], lead=60)
-    down_own = own_rows(down_sum)
+    gate_up_sum = row_sum([act_all], after(gate_up_grad, norm_two_kept[0], down_own), time=60)
+    output = (hidden + total_of(after(plane_neighbours(output_terms), gate_up_sum))).astype(bf16)
     gate_up_own = own_rows(gate_up_sum)
-    norm_two_terms = plane_direct(norm_two_kept)
-    output_other = plane_send(after(middle_low, gate_up_sum), ffn_full, 2)
-    output_kept = plane_keep(middle_low, ffn_full, 2, output_other)
-    norm_two_terms = after(norm_two_terms, output_kept[0], down_own)
+    norm_two_terms = after(plane_direct(norm_two_kept), output)
     mixed_grad, hidden_grad, hidden_low, two_sums = out_back_rows(
-        place, norm_two_terms, hidden, out_grad, gain_two, out_full
+        place, norm_two_terms, hidden, out_grad, gain_two, out_full, time=130
     )
-
-    output_terms = plane_corner(after(output_kept, mixed_grad))
-    mixed_grad = plane_all_to_all(mixed_grad).reshape(packs, blocks, rows, my_width)
-    mixed_grad = after(mixed_grad, output_terms)
-    qkv_grad = attention_back(place, qkv, mixed_grad, totals, cosine, sine, seg_col, seg_row, lead=40)
+    down_recv = back_to_rows(after(down_own, norm_two_terms))
+
+    mixed_grad = plane_all_to_all(after(mixed_grad, down_recv)).reshape(packs, blocks, rows, my_width)
+    qkv_grad = attention_back(place, qkv, mixed_grad, totals, cosine, sine, seg_col, seg_row, time=130)
     qkv_grad = qkv_grad.reshape(8 * rows, 3 * my_width)
-    output = (hidden + total_of(plane_neighbours(output_terms))).astype(bf16)
-    qkv_sum = row_sum([act_one], [after(qkv_grad, output)], lead=40)
+    hidden_pieces = chip_pieces(after(hidden_low, mixed_grad), qkv_grad)
+    qkv_sum = row_sum([act_one], after(qkv_grad, hidden_pieces[1]), time=130)
     qkv_own = own_rows(qkv_sum)
-    norm_one_other = plane_send(after(qkv_grad, qkv_sum, gate_up_own), qkv_full, 0)
-    hidden_pieces = chip_pieces(after(hidden_low, qkv_grad), norm_one_other)
-    norm_one_kept = plane_keep(qkv_grad, qkv_full, 0, norm_one_other, bf16, lead=30)
-    hidden_all = halves_of(hidden_pieces, norm_one_kept[0], lead=60)
+    norm_one_other = plane_send(after(qkv_grad, qkv_sum, hidden_pieces), qkv_full, 0, time=60)
+    hidden_all = halves_of(hidden_pieces, norm_one_other, time=60)
+    gate_up_recv = back_to_rows(after(gate_up_own, norm_one_other))
+    norm_one_kept = plane_keep(after(qkv_grad, hidden_all[0]), qkv_full, 0, norm_one_other, bf16)
     mixed_halves = mixed_halves.reshape(2, 4 * rows, my_width)
-    out_sum = row_sum((mixed_halves[0], mixed_halves[1]), hidden_all)
-    if aligned and depth == 4:
-        out_share = deep_reduce(out_sum.reshape(4, shard, width))
-    elif aligned:
+    out_sum = pair_sum(mixed_halves, after(hidden_all, norm_one_kept[0], gate_up_recv), time=60)
+    if aligned:
         out_share = own_rows(out_sum).astype(f32)
     else:
         spread = jnp.zeros((my_heads, team, HEAD_DIM, width), bf16)
@@ -865,13 +893,12 @@
         out_share = lax.psum_scatter(
             spread.reshape(width, width).astype(f32), ALL, scatter_dimension=0, tiled=True
         )
-    down_share = merge_ffn(back_to_rows(after(down_own, qkv_sum)), 1, ffn)
-    gate_up_share = merge_ffn(back_to_rows(gate_up_own), 2, ffn)
-    norm_grad_one = total_of(
-        after(plane_direct(norm_one_kept), qkv_own, out_share, down_share, gate_up_share)
-    )
+    norm_one_terms = after(plane_direct(norm_one_kept), out_sum)
+    norm_grad_one = total_of(norm_one_terms)
     normed_one, inv_one = layer_stats(tokens.astype(f32))
     input_grad = (hidden_grad + norm_back(norm_grad_one, normed_one, inv_one, gain_one)).astype(bf16)
+    down_share = merge_ffn(down_recv, 1, ffn)
+    gate_up_share = merge_ffn(gate_up_recv, 2, ffn)
 
     bias_sum = jnp.sum(qkv_grad.astype(f32), axis=0).reshape(3, my_heads, 1, HEAD_DIM)
     mine = (jnp.arange(team) == me).astype(f32)[None, None, :, None]
@@ -884,9 +911,11 @@
         ],
         axis=0,
     )
+    qkv_recv = back_to_rows(after(qkv_own, out_sum))
+    terms = after(terms, qkv_recv)
     terms = jnp.transpose(terms.reshape(7, devices, shard), (1, 0, 2)).reshape(devices, 7 * shard)
     vector_share = jnp.sum(lax.all_to_all(terms, ALL, 0, 0, tiled=True), axis=0).reshape(7, shard)
-    qkv_share = merge_heads(back_to_rows(qkv_own))
+    qkv_share = merge_heads(qkv_recv)
     return (
         output,
         input_grad,

time: 713 us -> 649 us (0.910)
  waiting for transfers between devices: 259 us -> 207 us
  starting transfers between devices: 73.3 us -> 60.3 us
    ppermute x36, waiting for transfers between devices: 192 us -> 167 us  [swap(): return lax.ppermute(values, axis, [(0, 1), (1, 0)])]
    ppermute x4 -> x0, starting transfers between devices: 9.95 us -> none  [the longest x1 3.2 us: deep_reduce(): lax.ppermute((slots[2].astype(f32) + ends.astype(f32)).astype(bf16), 'g',...]
    all_to_all x1, waiting for transfers between devices: 15.2 us -> 6.09 us  [local(): lax.all_to_all(jnp.broadcast_to(small[None], (devices, small.shape[0])),...]
    all_to_all x5, waiting for transfers between devices: 39.6 us -> 31.5 us  [plane_all_to_all(): return lax.all_to_all(blocks, PLANE, 0, 0, tiled=True)]
  transfers between devices with their start and end apart: 55 -> 52, of which waited for: 32 -> 21; matrix products, arithmetic and copies ran while one was open for 7% -> 7% of each run, Pallas kernels for 31% -> 39%
where the time goes in v3:
time: 649 us; the launch traced here: 644 us
  Pallas kernels  265 us (41%)
  waiting for transfers between devices  207 us (32%)
  starting transfers between devices  60.3 us (9%)
  blocking collectives  36.5 us (6%)
  other arithmetic  29.9 us (5%)
  local copies, waits for them, and re-layouts  29.7 us (5%)
  between operations  15 us (2%)
    ppermute x36, waiting for transfers between devices, swap(): return lax.ppermute(values, axis, [(0, 1), (1, 0)])  167 us
    pallas_call x3, Pallas kernels, row_sum(): pl.pallas_call(sum_kernel, grid=(width // step,), in_specs=[*[pl.BlockSpe...  40 us
    all_to_all x2, blocking collectives, plane_all_to_all(): return lax.all_to_all(blocks, PLANE, 0, 0, tiled=True)  36.5 us
    pallas_call x3, Pallas kernels, plane_keep(): pl.pallas_call(keep_kernel, grid=(4,), in_specs=[pl.BlockSpec((rows, dept...  33.1 us
    all_to_all x5, waiting for transfers between devices, plane_all_to_all(): return lax.all_to_all(blocks, PLANE, 0, 0, tiled=True)  31.5 us
    ppermute x36, starting transfers between devices, swap(): return lax.ppermute(values, axis, [(0, 1), (1, 0)])  26.2 us
    pallas_call x3, Pallas kernels, plane_send(): pl.pallas_call(send_kernel, grid=(2,), in_specs=[pl.BlockSpec((2 * rows,...  25.8 us
    pallas_call x1, Pallas kernels, attention_back(): pl.pallas_call(functools.partial(attend_back_kernel, blocks), grid_spec=p...  25.2 us
  transfers between devices with their start and end apart: 52, of which 21 were waited for; matrix products, arithmetic and copies ran while one was open for 7% of the time, Pallas kernels for 39%

profile of v3, /device:TPU:0, one launch (start us, length us, event | category | flops | bytes accessed | tf_op | source)
XLA Modules:
  0.0 643.6 jit_solution(18177532143334267361)
XLA Ops:
  10.9 7.3 %all-to-all-start = ((f32[32,1,960]{2,1,0:T(1,128)}), f32[32,1,960]{2,1,0:T(1,128)S(1)}, u32[]{:S(2)}, u32[]{:S(2)}) async-start(f32[32,1,960]{2,1,0:T(1,128)} %broadcast_in_dim.18), calls=%async_computation | async-start | bytes 262144 | tf_op jit(solution)/shard_map/all_to_all | solution.py:791
  18.3 2.5 shard_map.230
  20.8 6.1 all-to-all-done
  26.9 16.8 %all_to_all.54 = bf16[8,64,768]{2,1,0:T(8,128)(2,1)} all-to-all(bf16[8,64,768]{2,1,0:T(8,128)(2,1)} %shard_map.230), channel_id=1, replica_groups=mesh['g'=4,'y'=2,'x'=2,'c'=2] {'y','x','c'}, dimensions={0} | all-to-all | bytes 1572864 | tf_op jit(solution)/shard_map/all_to_all | solution.py:239
  44.9 23.1 %collective-permute-done.1.refs_2_ = bf16[256,2048]{1,0:T(8,128)(2,1)S(1)} collective-permute-done((bf16[256,2048]{1,0:T(8,128)(2,1)S(1)}, bf16[256,2048]{1,0:T(8,128)(2,1)S(1)}, u32[]{:S(2)}, u32[]{:S(2)}) %collective-permute-start.1) | collective-permute-done | bytes 1048608 | tf_op jit(solution)/shard_map/ppermute | solution.py:59
  71.0 3.7 shard_map.231
  76.7 5.1 collective-permute-done.2.refs_3_
  83.9 3.6 all-to-all-start.2
  87.8 7.2 %shard_map.229.act0_ref = bf16[1024,2048]{1,0:T(8,128)(2,1)} custom-call(bf16[256,2048]{1,0:T(8,128)(2,1)} %token_ref.1, bf16[256,2048]{1,0:T(8,128)(2,1)} %copy-done.10, bf16[256,2048]{1,0:T(8,128)(2,1)} %copy-done.9, bf16[128,2048]{1,0:T(8,128)(2,1)} %collective-permute-done.2.refs_3_, bf16[128,2048]{1,0:T(8,128)(2,1)} %copy-done.20, ...), custom_call_target="tpu_custom_call" | custom-call | flops 1166666624 | bytes 3500000 | tf_op jit(solution)/shard_map/pallas_call | solution.py:428
  96.1 5.2 compare_select_fusion.9
  101.4 5.5 fusion.12
  106.9 8.6 %all-to-all-done.2 = bf16[8,64,2176]{2,1,0:T(8,128)(2,1)S(1)} async-done(((bf16[8,64,2176]{2,1,0:T(8,128)(2,1)}), bf16[8,64,2176]{2,1,0:T(8,128)(2,1)S(1)}, u32[]{:S(2)}, u32[]{:S(2)}) %all-to-all-start.2) | async-done | bytes 2228256 | tf_op jit(solution)/shard_map/all_to_all | solution.py:239
  119.5 15.9 %shard_map.232 = (bf16[2,1024,768]{2,1,0:T(8,128)(2,1)}, bf16[2048,2048]{1,0:T(8,128)(2,1)}) custom-call(s32[4]{0:T(128)} %pad_add_fusion.place, bf16[1024,2048]{1,0:T(8,128)(2,1)} %shard_map.229.act0_ref, bf16[1024,2048]{1,0:T(8,128)(2,1)} %collective-permute-done.4.act1_ref, bf16[2048,768]{1,0:T(8,128)(2,1)} %all-gather.4.cloned.1.call-done.weight_ref.right_ref, ...), custom_call_target="tpu_custom_call" | custom-call | flops 2500000000 | bytes 7500000 | tf_op jit(solution)/shard_map/pallas_call | solution.py:465
  135.4 5.7 collective-permute-done.5.refs_1_
  147.0 15.8 %shard_map.233 = (bf16[2,4,256,256]{3,2,1,0:T(8,128)(2,1)}, bf16[2,2,2,256,256]{4,3,2,1,0:T(8,128)(2,1)}, f32[2,2,2,1024]{3,2,1,0:T(2,128)}) custom-call(s32[4]{0:T(128)} %pad_add_fusion.place, bf16[2,1024,768]{2,1,0:T(8,128)(2,1)} %get-tuple-element.100.query_ref.key_ref.value_ref, bf16[2,1024,768]{2,1,0:T(8,128)(2,1)} %get-tuple-element.100.query_ref.key_ref.value_ref, ...), custom_call_target="tpu_custom_call" | custom-call | flops 2666666752 | bytes 8000000 | tf_op jit(solution)/shard_map/pallas_call | solution.py:369
  163.8 4.8 shard_map.234.w0_ref
  168.5 4.2 all-to-all-start.3
  174.6 13.5 %all-to-all-done.3.mixed_ref = bf16[8,256,256]{2,1,0:T(8,128)(2,1)S(1)} async-done(((bf16[8,256,256]{2,1,0:T(8,128)(2,1)}), bf16[8,256,256]{2,1,0:T(8,128)(2,1)S(1)}, u32[]{:S(2)}, u32[]{:S(2)}) %all-to-all-start.3) | async-done | bytes 1048608 | tf_op jit(solution)/shard_map/all_to_all | solution.py:239
  189.1 11.9 %shard_map.235 = (f32[256,2048]{1,0:T(8,128)}, bf16[256,2048]{1,0:T(8,128)(2,1)}) custom-call(s32[4]{0:T(128)} %pad_add_fusion.place, bf16[8,256,256]{2,1,0:T(8,128)(2,1)} %copy-done.6, bf16[1024,2048]{1,0:T(8,128)(2,1)} %shard_map.234.w0_ref, bf16[1024,2048]{1,0:T(8,128)(2,1)} %collective-permute-done.9.w1_ref, bf16[256,2048]{1,0:T(8,128)(2,1)} %token_ref.1, ...), custom_call_target="tpu_custom_call" | custom-call | flops 2000000000 | bytes 6000000 | tf_op jit(solution)/shard_map/pallas_call | solution.py:528
  202.1 21.1 %collective-permute-done.11.refs_2_ = bf16[256,2048]{1,0:T(8,128)(2,1)S(1)} collective-permute-done((bf16[256,2048]{1,0:T(8,128)(2,1)}, bf16[256,2048]{1,0:T(8,128)(2,1)S(1)}, u32[]{:S(2)}, u32[]{:S(2)}) %collective-permute-start.11) | collective-permute-done | bytes 1048608 | tf_op jit(solution)/shard_map/ppermute | solution.py:59
  223.3 3.7 collective-permute-start.12
  227.5 11.1 %collective-permute-done.12.refs_3_ = bf16[128,2048]{1,0:T(8,128)(2,1)S(1)} collective-permute-done((bf16[128,2048]{1,0:T(8,128)(2,1)S(1)}, bf16[128,2048]{1,0:T(8,128)(2,1)S(1)}, u32[]{:S(2)}, u32[]{:S(2)}) %collective-permute-start.12) | collective-permute-done | bytes 524320 | tf_op jit(solution)/shard_map/ppermute | solution.py:59
  238.6 1.6 collective-permute-done.13.refs_4_
  241.0 4.7 shard_map.236.act0_ref
  247.4 23.9 %collective-permute-done.16.refs_2_ = bf16[256,2048]{1,0:T(8,128)(2,1)S(1)} collective-permute-done((bf16[256,2048]{1,0:T(8,128)(2,1)S(1)}, bf16[256,2048]{1,0:T(8,128)(2,1)S(1)}, u32[]{:S(2)}, u32[]{:S(2)}) %collective-permute-start.16) | collective-permute-done | bytes 1048608 | tf_op jit(solution)/shard_map/ppermute | solution.py:59
  274.1 20.0 %shard_map.237 = (bf16[2048,768]{1,0:T(8,128)(2,1)}, bf16[2048,768]{1,0:T(8,128)(2,1)}, bf16[2048,768]{1,0:T(8,128)(2,1)}, bf16[2048,2048]{1,0:T(8,128)(2,1)}) custom-call(bf16[1024,2048]{1,0:T(8,128)(2,1)} %shard_map.236.act0_ref, bf16[1024,2048]{1,0:T(8,128)(2,1)} %collective-permute-done.14.act1_ref, ...), custom_call_target="tpu_custom_call" | custom-call | flops 3333333248 | bytes 10000000 | tf_op jit(solution)/shard_map/pallas_call | solution.py:619
  294.9 4.7 shard_map.238.refs_0_.grad0_ref
  299.7 7.1 %shard_map.240 = bf16[1024,2048]{1,0:T(8,128)(2,1)} custom-call(bf16[2048,768]{1,0:T(8,128)(2,1)} %get-tuple-element.119.refs_2_.left_ref, bf16[2048,2176]{1,0:T(8,128)(2,1)} %all-gather.8.cloned.1.call-done.weight_ref.right_ref), custom_call_target="tpu_custom_call" | custom-call | flops 833333312 | bytes 2500000 | tf_op jit(solution)/shard_map/pallas_call | solution.py:132
  307.3 2.0 copy-done.2
  309.3 10.8 %shard_map.239 = bf16[2048,704]{1,0:T(8,128)(2,1)} custom-call(bf16[1024,2048]{1,0:T(8,128)(2,1)} %shard_map.238.refs_0_.grad0_ref, bf16[1024,2048]{1,0:T(8,128)(2,1)} %copy-done.2, bf16[2048,768]{1,0:T(8,128)(2,1)} %get-tuple-element.119.refs_2_.left_ref), custom_call_target="tpu_custom_call" | custom-call | flops 1500000000 | bytes 4500000 | tf_op jit(solution)/shard_map/pallas_call | solution.py:202
  320.1 10.3 %shard_map.241 = (bf16[256,2048]{1,0:T(8,128)(2,1)}, f32[256,2048]{1,0:T(8,128)}, f32[256,2048]{1,0:T(8,128)}, f32[256,2048]{1,0:T(8,128)}) custom-call(bf16[2048,768]{1,0:T(8,128)(2,1)} %get-tuple-element.119.refs_2_.left_ref, bf16[2048,2176]{1,0:T(8,128)(2,1)} %all-gather.8.cloned.1.call-done.weight_ref.right_ref, ...), custom_call_target="tpu_custom_call" | custom-call | flops 1000000000 | bytes 3000000 | tf_op jit(solution)/shard_map/pallas_call | solution.py:149
  336.3 14.1 %shard_map.242.left_ref.refs_1_ = bf16[2048,1408]{1,0:T(8,128)(2,1)} custom-call(bf16[1024,2048]{1,0:T(8,128)(2,1)} %shard_map.238.refs_0_.grad0_ref, bf16[1024,2048]{1,0:T(8,128)(2,1)} %copy-done.2, bf16[2048,2176]{1,0:T(8,128)(2,1)} %all-gather.8.cloned.1.call-done.weight_ref.right_ref, bf16[2048,768]{1,0:T(8,128)(2,1)} %get-tuple-element.126.by_gate_ref, ...), custom_call_target="tpu_custom_call" | custom-call | flops 2166666752 | bytes 6500000 | tf_op jit(solution)/shard_map/pallas_call | solution.py:645
  353.9 11.4 %shard_map.243 = bf16[1024,2048]{1,0:T(8,128)(2,1)} custom-call(bf16[2048,1408]{1,0:T(8,128)(2,1)} %shard_map.242.left_ref.refs_1_, bf16[2048,2176]{1,0:T(8,128)(2,1)} %all-gather.8.cloned.1.call-done.weight_ref.right_ref), custom_call_target="tpu_custom_call" | custom-call | flops 1666666624 | bytes 5000000 | tf_op jit(solution)/shard_map/pallas_call | solution.py:132
  365.7 7.0 %collective-permute-done.25.other_ref = bf16[1024,2048]{1,0:T(8,128)(2,1)S(1)} collective-permute-done((bf16[1024,2048]{1,0:T(8,128)(2,1)}, bf16[1024,2048]{1,0:T(8,128)(2,1)S(1)}, u32[]{:S(2)}, u32[]{:S(2)}) %collective-permute-start.25) | collective-permute-done | bytes 4194336 | tf_op jit(solution)/shard_map/ppermute | solution.py:59
  372.6 2.0 copy-done.5
  374.6 13.3 %shard_map.244 = (bf16[256,2048]{1,0:T(8,128)(2,1)}, bf16[256,2048]{1,0:T(8,128)(2,1)}, bf16[256,2048]{1,0:T(8,128)(2,1)}, f32[256,2048]{1,0:T(8,128)}) custom-call(bf16[2048,1408]{1,0:T(8,128)(2,1)} %shard_map.242.left_ref.refs_1_, bf16[2048,2176]{1,0:T(8,128)(2,1)} %all-gather.8.cloned.1.call-done.weight_ref.right_ref, bf16[1024,2048]{1,0:T(8,128)(2,1)} %copy-done.5), custom_call_target="tpu_custom_call" | custom-call | flops 2000000000 | bytes 6000000 | tf_op jit(solution)/shard_map/pallas_call | solution.py:149
  388.5 2.9 collective-permute-start.28
  392.7 18.2 %shard_map.245 = bf16[2048,1408]{1,0:T(8,128)(2,1)} custom-call(bf16[2048,2048]{1,0:T(8,128)(2,1)} %get-tuple-element.131.refs_0_, bf16[2048,1408]{1,0:T(8,128)(2,1)} %shard_map.242.left_ref.refs_1_), custom_call_target="tpu_custom_call" | custom-call | flops 10000000000 | bytes 30000000 | tf_op jit(solution)/shard_map/pallas_call | solution.py:202
  410.9 1.5 copy-done.15
  412.5 3.4 add_convert_fusion
  415.9 20.2 %collective-permute-done.27.y_ref = bf16[256,2048]{1,0:T(8,128)(2,1)} collective-permute-done((bf16[256,2048]{1,0:T(8,128)(2,1)}, bf16[256,2048]{1,0:T(8,128)(2,1)}, u32[]{:S(2)}, u32[]{:S(2)}) %collective-permute-start.27) | collective-permute-done | bytes 1048608 | tf_op jit(solution)/shard_map/ppermute | solution.py:59
  436.1 3.5 all-to-all-start.4
  439.9 15.1 %shard_map.246 = (bf16[8,256,256]{2,1,0:T(8,128)(2,1)}, f32[256,2048]{1,0:T(8,128)}, bf16[256,2048]{1,0:T(8,128)(2,1)}, f32[2,2048]{1,0:T(2,128)}) custom-call(s32[4]{0:T(128)} %pad_add_fusion.place, f32[256,2048]{1,0:T(8,128)} %get-tuple-element.141.own_ref, bf16[256,2048]{1,0:T(8,128)(2,1)} %collective-permute-done.26.x_ref, ...), custom_call_target="tpu_custom_call" | custom-call | flops 21666666496 | bytes 65000000 | tf_op jit(solution)/shard_map/pallas_call | solution.py:575
  455.1 19.7 %all_to_all.55 = bf16[8,256,256]{2,1,0:T(8,128)(2,1)} all-to-all(bf16[8,256,256]{2,1,0:T(8,128)(2,1)} %get-tuple-element.148), channel_id=1, replica_groups=mesh['g'=4,'y'=2,'x'=2,'c'=2] {'y','x','c'}, dimensions={0} | all-to-all | bytes 2097152 | tf_op jit(solution)/shard_map/all_to_all | solution.py:239
  475.9 25.2 %shard_map.247 = bf16[2,2,2,256,768]{4,3,2,1,0:T(8,128)(2,1)} custom-call(s32[4]{0:T(128)} %pad_add_fusion.place, bf16[2,1024,768]{2,1,0:T(8,128)(2,1)} %get-tuple-element.100.query_ref.key_ref.value_ref, bf16[2,1024,768]{2,1,0:T(8,128)(2,1)} %get-tuple-element.100.query_ref.key_ref.value_ref, ...), custom_call_target="tpu_custom_call" | custom-call | flops 21666666496 | bytes 65000000 | tf_op jit(solution)/shard_map/pallas_call | solution.py:395
  504.3 11.0 %shard_map.248 = bf16[2048,768]{1,0:T(8,128)(2,1)} custom-call(bf16[2048,2048]{1,0:T(8,128)(2,1)} %get-tuple-element.154.refs_0_, bf16[2048,768]{1,0:T(8,128)(2,1)} %bitcast.50), custom_call_target="tpu_custom_call" | custom-call | flops 21666666496 | bytes 65000000 | tf_op jit(solution)/shard_map/pallas_call | solution.py:202
  515.3 7.3 %shard_map.249 = bf16[1024,2048]{1,0:T(8,128)(2,1)} custom-call(bf16[2048,768]{1,0:T(8,128)(2,1)} %bitcast.51, bf16[2048,768]{1,0:T(8,128)(2,1)} %all-gather.4.cloned.1.call-done.weight_ref.right_ref), custom_call_target="tpu_custom_call" | custom-call | flops 10000000000 | bytes 30000000 | tf_op jit(solution)/shard_map/pallas_call | solution.py:132
  522.7 7.5 %collective-permute-done.33.other_ref = bf16[1024,2048]{1,0:T(8,128)(2,1)} collective-permute-done((bf16[1024,2048]{1,0:T(8,128)(2,1)}, bf16[1024,2048]{1,0:T(8,128)(2,1)}, u32[]{:S(2)}, u32[]{:S(2)}) %collective-permute-start.33) | collective-permute-done | bytes 4194336 | tf_op jit(solution)/shard_map/ppermute | solution.py:59
  530.1 4.8 shard_map.250.right0_ref
  535.0 3.7 all-to-all-start.6
  540.9 2.8 shard_map.255
  544.4 9.6 %shard_map.251 = (bf16[256,2048]{1,0:T(8,128)(2,1)}, bf16[256,2048]{1,0:T(8,128)(2,1)}, bf16[256,2048]{1,0:T(8,128)(2,1)}, f32[256,2048]{1,0:T(8,128)}) custom-call(bf16[2048,768]{1,0:T(8,128)(2,1)} %bitcast.52, bf16[2048,768]{1,0:T(8,128)(2,1)} %all-gather.4.cloned.1.call-done.weight_ref.right_ref, bf16[1024,2048]{1,0:T(8,128)(2,1)} %collective-permute-done.33.other_ref), custom_call_target="tpu_custom_call" | custom-call | flops 1000000000 | bytes 3000000 | tf_op jit(solution)/shard_map/pallas_call | solution.py:149
  554.0 1.9 collective-permute-start.34
  558.3 7.2 %shard_map.252 = bf16[256,2048]{1,0:T(8,128)(2,1)} custom-call(bf16[2,1024,256]{2,1,0:T(8,128)(2,1)} %bitcast.74, bf16[2,1024,256]{2,1,0:T(8,128)(2,1)} %bitcast.75, bf16[1024,2048]{1,0:T(8,128)(2,1)} %shard_map.250.right0_ref, bf16[1024,2048]{1,0:T(8,128)(2,1)} %collective-permute-done.37.right1_ref), custom_call_target="tpu_custom_call" | custom-call | flops 10000000000 | bytes 30000000 | tf_op jit(solution)/shard_map/pallas_call | solution.py:223
  565.6 14.7 %collective-permute-done.34 = bf16[256,2048]{1,0:T(8,128)(2,1)} collective-permute-done((bf16[256,2048]{1,0:T(8,128)(2,1)}, bf16[256,2048]{1,0:T(8,128)(2,1)}, u32[]{:S(2)}, u32[]{:S(2)}) %collective-permute-start.34) | collective-permute-done | bytes 1048608 | tf_op jit(solution)/shard_map/ppermute | solution.py:59
  580.3 23.3 %collective-permute-done.35 = bf16[256,2048]{1,0:T(8,128)(2,1)} collective-permute-done((bf16[256,2048]{1,0:T(8,128)(2,1)}, bf16[256,2048]{1,0:T(8,128)(2,1)}, u32[]{:S(2)}, u32[]{:S(2)}) %collective-permute-start.35) | collective-permute-done | bytes 1048608 | tf_op jit(solution)/shard_map/ppermute | solution.py:59
  603.6 4.2 all-to-all-start.7
  607.8 3.9 fusion.10
  611.8 8.7 %all-to-all-done.7.part_ref = bf16[8,64,768]{2,1,0:T(8,128)(2,1)} async-done(((bf16[8,64,768]{2,1,0:T(8,128)(2,1)}), bf16[8,64,768]{2,1,0:T(8,128)(2,1)}, u32[]{:S(2)}, u32[]{:S(2)}) %all-to-all-start.7) | async-done | bytes 786464 | tf_op jit(solution)/shard_map/all_to_all | solution.py:239
  621.4 2.7 all-to-all-start.8
  624.1 3.4 fusion.9
  627.5 3.4 shard_map.254
  630.8 2.6 shard_map.253
  634.7 1.8 convert_element_type.77
  (214 shorter events, 59.2 us)
Async XLA Ops:
  7.2 109.8 %all-gather.6.cloned.1.call-start = ((), (), s32[]{:S(2)}) async-start(), calls=%async_computation.14 | async-start | bytes 1310720 | tf_op jit(solution)/shard_map/all_gather | solution.py:818
  10.9 15.9 %all-to-all-start = ((f32[32,1,960]{2,1,0:T(1,128)}), f32[32,1,960]{2,1,0:T(1,128)S(1)}, u32[]{:S(2)}, u32[]{:S(2)}) async-start(f32[32,1,960]{2,1,0:T(1,128)} %broadcast_in_dim.18), calls=%async_computation | async-start | bytes 262144 | tf_op jit(solution)/shard_map/all_to_all | solution.py:791
  18.2 25.5 %copy-start = (bf16[256,2048]{1,0:T(8,128)(2,1)S(1)}, bf16[256,2048]{1,0:T(8,128)(2,1)}, u32[]{:S(2)}) copy-start(bf16[256,2048]{1,0:T(8,128)(2,1)} %token_ref.1) | copy-start | bytes 3145732
  18.2 101.2 %all-gather.4.cloned.1.call-start = ((), (), s32[]{:S(2)}) async-start(), calls=%async_computation.13 | async-start | bytes 3932160 | tf_op jit(solution)/shard_map/all_gather | solution.py:818
  43.7 24.3 %collective-permute-start.1 = (bf16[256,2048]{1,0:T(8,128)(2,1)S(1)}, bf16[256,2048]{1,0:T(8,128)(2,1)S(1)}, u32[]{:S(2)}, u32[]{:S(2)}) collective-permute-start(bf16[256,2048]{1,0:T(8,128)(2,1)S(1)} %copy-done), channel_id=1, source_target_pairs={{0,4},{4,0},{1,5},{5,1},{2,6},{6,2},{3,7},{7,3},{8,12},{12,8},{9,1... | collective-permute-start | bytes 3145736 | tf_op jit(solution)/shard_map/ppermute | solution.py:59
  44.3 25.9 %collective-permute-start = (bf16[256,2048]{1,0:T(8,128)(2,1)S(1)}, bf16[256,2048]{1,0:T(8,128)(2,1)S(1)}, u32[]{:S(2)}, u32[]{:S(2)}) collective-permute-start(bf16[256,2048]{1,0:T(8,128)(2,1)S(1)} %copy-done), channel_id=1, source_target_pairs={{0,2},{2,0},{1,3},{3,1},{4,6},{6,4},{5,7},{7,5},{8,10},{10,8},{9,1... | collective-permute-start | bytes 3145736 | tf_op jit(solution)/shard_map/ppermute | solution.py:59
  68.9 12.9 %collective-permute-start.2 = (bf16[128,2048]{1,0:T(8,128)(2,1)}, bf16[128,2048]{1,0:T(8,128)(2,1)}, u32[]{:S(2)}, u32[]{:S(2)}) collective-permute-start(bf16[128,2048]{1,0:T(8,128)(2,1)} %slice.164), channel_id=1, source_target_pairs={{0,2},{2,0},{1,3},{3,1},{4,6},{6,4},{5,7},{7,5},{8,10},{10,8},{9,1... | collective-permute-start | bytes 1572872 | tf_op jit(solution)/shard_map/ppermute | solution.py:59
  70.3 12.8 %collective-permute-start.3 = (bf16[128,2048]{1,0:T(8,128)(2,1)S(1)}, bf16[128,2048]{1,0:T(8,128)(2,1)S(1)}, u32[]{:S(2)}, u32[]{:S(2)}) collective-permute-start(bf16[128,2048]{1,0:T(8,128)(2,1)S(1)} %slice.165), channel_id=1, source_target_pairs={{0,4},{4,0},{1,5},{5,1},{2,6},{6,2},{3,7},{7,3},{8,12},{12,8},{9,1... | collective-permute-start | bytes 1572872 | tf_op jit(solution)/shard_map/ppermute | solution.py:59
  83.9 31.6 %all-to-all-start.2 = ((bf16[8,64,2176]{2,1,0:T(8,128)(2,1)}), bf16[8,64,2176]{2,1,0:T(8,128)(2,1)S(1)}, u32[]{:S(2)}, u32[]{:S(2)}) async-start(bf16[8,64,2176]{2,1,0:T(8,128)(2,1)} %shard_map.231), calls=%async_computation.2 | async-start | bytes 4456448 | tf_op jit(solution)/shard_map/all_to_all | solution.py:239
  87.5 186.6 %all-gather.8.cloned.1.call-start = ((), (), s32[]{:S(2)}) async-start(), calls=%async_computation.15 | async-start | bytes 11141120 | tf_op jit(solution)/shard_map/all_gather | solution.py:818
  95.0 24.4 %collective-permute-start.4 = (bf16[1024,2048]{1,0:T(8,128)(2,1)}, bf16[1024,2048]{1,0:T(8,128)(2,1)}, u32[]{:S(2)}, u32[]{:S(2)}) collective-permute-start(bf16[1024,2048]{1,0:T(8,128)(2,1)} %shard_map.229.act0_ref), channel_id=1, source_target_pairs={{0,1},{1,0},{2,3},{3,2},{4,5},{5,4},{6,7},{7,6},{8,9},{9,8},{10,11... | collective-permute-start | bytes 12582920 | tf_op jit(solution)/shard_map/ppermute | solution.py:59
  116.9 24.2 %collective-permute-start.5 = (bf16[256,2048]{1,0:T(8,128)(2,1)}, bf16[256,2048]{1,0:T(8,128)(2,1)S(1)}, u32[]{:S(2)}, u32[]{:S(2)}) collective-permute-start(bf16[256,2048]{1,0:T(8,128)(2,1)} %all-gather.6.cloned.1.call-done.refs_0_), channel_id=1, source_target_pairs={{0,2},{2,0},{1,3},{3,1},{4,6},{6,4},{5,7},{7,5},{8,10},{10,8},{9,1... | collective-permute-start | bytes 3145736 | tf_op jit(solution)/shard_map/ppermute | solution.py:59
  117.5 25.1 %collective-permute-start.6 = (bf16[256,2048]{1,0:T(8,128)(2,1)}, bf16[256,2048]{1,0:T(8,128)(2,1)S(1)}, u32[]{:S(2)}, u32[]{:S(2)}) collective-permute-start(bf16[256,2048]{1,0:T(8,128)(2,1)} %all-gather.6.cloned.1.call-done.refs_0_), channel_id=1, source_target_pairs={{0,4},{4,0},{1,5},{5,1},{2,6},{6,2},{3,7},{7,3},{8,12},{12,8},{9,1... | collective-permute-start | bytes 3145736 | tf_op jit(solution)/shard_map/ppermute | solution.py:59
  141.1 21.7 %copy-start.7 = (bf16[256,2048]{1,0:T(8,128)(2,1)}, bf16[256,2048]{1,0:T(8,128)(2,1)S(1)}, u32[]{:S(2)}) copy-start(bf16[256,2048]{1,0:T(8,128)(2,1)S(1)} %collective-permute-done.5.refs_1_) | copy-start | bytes 3145732
  142.6 20.2 %copy-start.8 = (bf16[256,2048]{1,0:T(8,128)(2,1)}, bf16[256,2048]{1,0:T(8,128)(2,1)S(1)}, u32[]{:S(2)}) copy-start(bf16[256,2048]{1,0:T(8,128)(2,1)S(1)} %collective-permute-done.6.refs_2_) | copy-start | bytes 3145732
  143.5 19.3 %collective-permute-start.7 = (bf16[128,2048]{1,0:T(8,128)(2,1)}, bf16[128,2048]{1,0:T(8,128)(2,1)S(1)}, u32[]{:S(2)}, u32[]{:S(2)}) collective-permute-start(bf16[128,2048]{1,0:T(8,128)(2,1)} %slice.131), channel_id=1, source_target_pairs={{0,2},{2,0},{1,3},{3,1},{4,6},{6,4},{5,7},{7,5},{8,10},{10,8},{9,1... | collective-permute-start | bytes 1572872 | tf_op jit(solution)/shard_map/ppermute | solution.py:59
  144.7 18.1 %collective-permute-start.8 = (bf16[128,2048]{1,0:T(8,128)(2,1)}, bf16[128,2048]{1,0:T(8,128)(2,1)S(1)}, u32[]{:S(2)}, u32[]{:S(2)}) collective-permute-start(bf16[128,2048]{1,0:T(8,128)(2,1)} %slice.132), channel_id=1, source_target_pairs={{0,4},{4,0},{1,5},{5,1},{2,6},{6,2},{3,7},{7,3},{8,12},{12,8},{9,1... | collective-permute-start | bytes 1572872 | tf_op jit(solution)/shard_map/ppermute | solution.py:59
  168.5 19.6 %collective-permute-start.9 = (bf16[1024,2048]{1,0:T(8,128)(2,1)}, bf16[1024,2048]{1,0:T(8,128)(2,1)}, u32[]{:S(2)}, u32[]{:S(2)}) collective-permute-start(bf16[1024,2048]{1,0:T(8,128)(2,1)} %shard_map.234.w0_ref), channel_id=1, source_target_pairs={{0,1},{1,0},{2,3},{3,2},{4,5},{5,4},{6,7},{7,6},{8,9},{9,8},{10,11... | collective-permute-start | bytes 12582920 | tf_op jit(solution)/shard_map/ppermute | solution.py:59
  168.5 19.6 %all-to-all-start.3 = ((bf16[8,256,256]{2,1,0:T(8,128)(2,1)}), bf16[8,256,256]{2,1,0:T(8,128)(2,1)S(1)}, u32[]{:S(2)}, u32[]{:S(2)}) async-start(bf16[8,256,256]{2,1,0:T(8,128)(2,1)} %bitcast.23), calls=%async_computation.3 | async-start | bytes 2097152 | tf_op jit(solution)/shard_map/all_to_all | solution.py:239
  172.7 220.0 %reduce-scatter.5.cloned.1.call-start = ((), (), s32[]{:S(2)}) async-start(), calls=%async_computation.16 | async-start | bytes 3932160 | tf_op jit(solution)/shard_map/reduce_scatter | solution.py:855
  200.9 22.3 %collective-permute-start.11 = (bf16[256,2048]{1,0:T(8,128)(2,1)}, bf16[256,2048]{1,0:T(8,128)(2,1)S(1)}, u32[]{:S(2)}, u32[]{:S(2)}) collective-permute-start(bf16[256,2048]{1,0:T(8,128)(2,1)} %get-tuple-element.111.refs_0_), channel_id=1, source_target_pairs={{0,4},{4,0},{1,5},{5,1},{2,6},{6,2},{3,7},{7,3},{8,12},{12,8},{9,1... | collective-permute-start | bytes 3145736 | tf_op jit(solution)/shard_map/ppermute | solution.py:59
  201.5 25.5 %collective-permute-start.10 = (bf16[256,2048]{1,0:T(8,128)(2,1)}, bf16[256,2048]{1,0:T(8,128)(2,1)S(1)}, u32[]{:S(2)}, u32[]{:S(2)}) collective-permute-start(bf16[256,2048]{1,0:T(8,128)(2,1)} %get-tuple-element.111.refs_0_), channel_id=1, source_target_pairs={{0,2},{2,0},{1,3},{3,1},{4,6},{6,4},{5,7},{7,5},{8,10},{10,8},{9,1... | collective-permute-start | bytes 3145736 | tf_op jit(solution)/shard_map/ppermute | solution.py:59
  223.2 16.9 %copy-start.13 = (bf16[256,2048]{1,0:T(8,128)(2,1)}, bf16[256,2048]{1,0:T(8,128)(2,1)S(1)}, u32[]{:S(2)}) copy-start(bf16[256,2048]{1,0:T(8,128)(2,1)S(1)} %collective-permute-done.11.refs_2_) | copy-start | bytes 3145732
  223.3 15.3 %collective-permute-start.12 = (bf16[128,2048]{1,0:T(8,128)(2,1)S(1)}, bf16[128,2048]{1,0:T(8,128)(2,1)S(1)}, u32[]{:S(2)}, u32[]{:S(2)}) collective-permute-start(bf16[128,2048]{1,0:T(8,128)(2,1)S(1)} %slice.173), channel_id=1, source_target_pairs={{0,2},{2,0},{1,3},{3,1},{4,6},{6,4},{5,7},{7,5},{8,10},{10,8},{9,1... | collective-permute-start | bytes 1572872 | tf_op jit(solution)/shard_map/ppermute | solution.py:59
  227.0 13.1 %copy-start.14 = (bf16[256,2048]{1,0:T(8,128)(2,1)}, bf16[256,2048]{1,0:T(8,128)(2,1)S(1)}, u32[]{:S(2)}) copy-start(bf16[256,2048]{1,0:T(8,128)(2,1)S(1)} %collective-permute-done.10.refs_1_) | copy-start | bytes 3145732
  227.1 18.6 %copy-start.19 = (bf16[256,2048]{1,0:T(8,128)(2,1)S(1)}, bf16[256,2048]{1,0:T(8,128)(2,1)}, u32[]{:S(2)}) copy-start(bf16[256,2048]{1,0:T(8,128)(2,1)} %grad_ref.1) | copy-start | bytes 3145732
  227.1 13.1 %collective-permute-start.13 = (bf16[128,2048]{1,0:T(8,128)(2,1)S(1)}, bf16[128,2048]{1,0:T(8,128)(2,1)S(1)}, u32[]{:S(2)}, u32[]{:S(2)}) collective-permute-start(bf16[128,2048]{1,0:T(8,128)(2,1)S(1)} %slice.174), channel_id=1, source_target_pairs={{0,4},{4,0},{1,5},{5,1},{2,6},{6,2},{3,7},{7,3},{8,12},{12,8},{9,1... | collective-permute-start | bytes 1572872 | tf_op jit(solution)/shard_map/ppermute | solution.py:59
  245.7 28.2 %collective-permute-start.14 = (bf16[1024,2048]{1,0:T(8,128)(2,1)}, bf16[1024,2048]{1,0:T(8,128)(2,1)}, u32[]{:S(2)}, u32[]{:S(2)}) collective-permute-start(bf16[1024,2048]{1,0:T(8,128)(2,1)} %shard_map.236.act0_ref), channel_id=1, source_target_pairs={{0,1},{1,0},{2,3},{3,2},{4,5},{5,4},{6,7},{7,6},{8,9},{9,8},{10,11... | collective-permute-start | bytes 12582920 | tf_op jit(solution)/shard_map/ppermute | solution.py:59
  245.7 25.6 %collective-permute-start.16 = (bf16[256,2048]{1,0:T(8,128)(2,1)S(1)}, bf16[256,2048]{1,0:T(8,128)(2,1)S(1)}, u32[]{:S(2)}, u32[]{:S(2)}) collective-permute-start(bf16[256,2048]{1,0:T(8,128)(2,1)S(1)} %copy-done.19), channel_id=1, source_target_pairs={{0,4},{4,0},{1,5},{5,1},{2,6},{6,2},{3,7},{7,3},{8,12},{12,8},{9,1... | collective-permute-start | bytes 3145736 | tf_op jit(solution)/shard_map/ppermute | solution.py:59
  246.1 27.0 %collective-permute-start.15 = (bf16[256,2048]{1,0:T(8,128)(2,1)S(1)}, bf16[256,2048]{1,0:T(8,128)(2,1)S(1)}, u32[]{:S(2)}, u32[]{:S(2)}) collective-permute-start(bf16[256,2048]{1,0:T(8,128)(2,1)S(1)} %copy-done.19), channel_id=1, source_target_pairs={{0,2},{2,0},{1,3},{3,1},{4,6},{6,4},{5,7},{7,5},{8,10},{10,8},{9,1... | collective-permute-start | bytes 3145736 | tf_op jit(solution)/shard_map/ppermute | solution.py:59
  271.3 22.8 %copy-start.11 = (bf16[256,2048]{1,0:T(8,128)(2,1)}, bf16[256,2048]{1,0:T(8,128)(2,1)S(1)}, u32[]{:S(2)}) copy-start(bf16[256,2048]{1,0:T(8,128)(2,1)S(1)} %collective-permute-done.16.refs_2_) | copy-start | bytes 3145732
  272.2 21.9 %collective-permute-start.17 = (bf16[128,2048]{1,0:T(8,128)(2,1)}, bf16[128,2048]{1,0:T(8,128)(2,1)}, u32[]{:S(2)}, u32[]{:S(2)}) collective-permute-start(bf16[128,2048]{1,0:T(8,128)(2,1)} %slice.175), channel_id=1, source_target_pairs={{0,2},{2,0},{1,3},{3,1},{4,6},{6,4},{5,7},{7,5},{8,10},{10,8},{9,1... | collective-permute-start | bytes 1572872 | tf_op jit(solution)/shard_map/ppermute | solution.py:59
  273.1 21.0 %copy-start.12 = (bf16[256,2048]{1,0:T(8,128)(2,1)}, bf16[256,2048]{1,0:T(8,128)(2,1)S(1)}, u32[]{:S(2)}) copy-start(bf16[256,2048]{1,0:T(8,128)(2,1)S(1)} %collective-permute-done.15.refs_1_) | copy-start | bytes 3145732
  273.1 21.0 %collective-permute-start.18 = (bf16[128,2048]{1,0:T(8,128)(2,1)S(1)}, bf16[128,2048]{1,0:T(8,128)(2,1)S(1)}, u32[]{:S(2)}, u32[]{:S(2)}) collective-permute-start(bf16[128,2048]{1,0:T(8,128)(2,1)S(1)} %slice.176), channel_id=1, source_target_pairs={{0,4},{4,0},{1,5},{5,1},{2,6},{6,2},{3,7},{7,3},{8,12},{12,8},{9,1... | collective-permute-start | bytes 1572872 | tf_op jit(solution)/shard_map/ppermute | solution.py:59
  299.6 7.6 %collective-permute-start.19 = (bf16[1024,2048]{1,0:T(8,128)(2,1)}, bf16[1024,2048]{1,0:T(8,128)(2,1)S(1)}, u32[]{:S(2)}, u32[]{:S(2)}) collective-permute-start(bf16[1024,2048]{1,0:T(8,128)(2,1)} %shard_map.238.refs_0_.grad0_ref), channel_id=1, source_target_pairs={{0,1},{1,0},{2,3},{3,2},{4,5},{5,4},{6,7},{7,6},{8,9},{9,8},{10,11... | collective-permute-start | bytes 12582920 | tf_op jit(solution)/shard_map/ppermute | solution.py:59
  306.8 13.3 %collective-permute-start.20 = (bf16[1024,2048]{1,0:T(8,128)(2,1)}, bf16[1024,2048]{1,0:T(8,128)(2,1)}, u32[]{:S(2)}, u32[]{:S(2)}) collective-permute-start(bf16[1024,2048]{1,0:T(8,128)(2,1)} %shard_map.240), channel_id=1, source_target_pairs={{0,1},{1,0},{2,3},{3,2},{4,5},{5,4},{6,7},{7,6},{8,9},{9,8},{10,11... | collective-permute-start | bytes 12582920 | tf_op jit(solution)/shard_map/ppermute | solution.py:59
  331.6 18.8 %collective-permute-start.21 = (bf16[128,2048]{1,0:T(8,128)(2,1)S(1)}, bf16[128,2048]{1,0:T(8,128)(2,1)}, u32[]{:S(2)}, u32[]{:S(2)}) collective-permute-start(bf16[128,2048]{1,0:T(8,128)(2,1)S(1)} %get-tuple-element.190), channel_id=1, source_target_pairs={{0,4},{4,0},{1,5},{5,1},{2,6},{6,2},{3,7},{7,3},{8,12},{12,8},{9,1... | collective-permute-start | bytes 1572872 | tf_op jit(solution)/shard_map/ppermute | solution.py:59
  333.2 201.9 %reduce-scatter.7.cloned.1.call-start = ((), (), s32[]{:S(2)}) async-start(), calls=%async_computation.17 | async-start | bytes 7208960 | tf_op jit(solution)/shard_map/reduce_scatter | solution.py:855
  334.8 17.9 %collective-permute-start.22 = (bf16[128,2048]{1,0:T(8,128)(2,1)S(1)}, bf16[128,2048]{1,0:T(8,128)(2,1)S(1)}, u32[]{:S(2)}, u32[]{:S(2)}) collective-permute-start(bf16[128,2048]{1,0:T(8,128)(2,1)S(1)} %get-tuple-element.189), channel_id=1, source_target_pairs={{0,2},{2,0},{1,3},{3,1},{4,6},{6,4},{5,7},{7,5},{8,10},{10,8},{9,1... | collective-permute-start | bytes 1572872 | tf_op jit(solution)/shard_map/ppermute | solution.py:59
  336.3 14.1 %copy-start.18 = (f32[256,2048]{1,0:T(8,128)S(1)}, f32[256,2048]{1,0:T(8,128)}, u32[]{:S(2)}) copy-start(f32[256,2048]{1,0:T(8,128)} %get-tuple-element.121) | copy-start | bytes 6291460
  365.2 7.4 %collective-permute-start.25 = (bf16[1024,2048]{1,0:T(8,128)(2,1)}, bf16[1024,2048]{1,0:T(8,128)(2,1)S(1)}, u32[]{:S(2)}, u32[]{:S(2)}) collective-permute-start(bf16[1024,2048]{1,0:T(8,128)(2,1)} %shard_map.243), channel_id=1, source_target_pairs={{0,1},{1,0},{2,3},{3,2},{4,5},{5,4},{6,7},{7,6},{8,9},{9,8},{10,11... | collective-permute-start | bytes 12582920 | tf_op jit(solution)/shard_map/ppermute | solution.py:59
  365.2 45.7 %collective-permute-start.23 = (bf16[256,2048]{1,0:T(8,128)(2,1)}, bf16[256,2048]{1,0:T(8,128)(2,1)S(1)}, u32[]{:S(2)}, u32[]{:S(2)}) collective-permute-start(bf16[256,2048]{1,0:T(8,128)(2,1)} %pad_maximum_fusion), channel_id=1, source_target_pairs={{0,2},{2,0},{1,3},{3,1},{4,6},{6,4},{5,7},{7,5},{8,10},{10,8},{9,1... | collective-permute-start | bytes 3145736 | tf_op jit(solution)/shard_map/ppermute | solution.py:59
  365.6 45.4 %collective-permute-start.24 = (bf16[256,2048]{1,0:T(8,128)(2,1)}, bf16[256,2048]{1,0:T(8,128)(2,1)}, u32[]{:S(2)}, u32[]{:S(2)}) collective-permute-start(bf16[256,2048]{1,0:T(8,128)(2,1)} %pad_maximum_fusion.1), channel_id=1, source_target_pairs={{0,4},{4,0},{1,5},{5,1},{2,6},{6,2},{3,7},{7,3},{8,12},{12,8},{9,1... | collective-permute-start | bytes 3145736 | tf_op jit(solution)/shard_map/ppermute | solution.py:59
  387.9 28.0 %collective-permute-start.26 = (bf16[256,2048]{1,0:T(8,128)(2,1)}, bf16[256,2048]{1,0:T(8,128)(2,1)}, u32[]{:S(2)}, u32[]{:S(2)}) collective-permute-start(bf16[256,2048]{1,0:T(8,128)(2,1)} %get-tuple-element.139), channel_id=1, source_target_pairs={{0,2},{2,0},{1,3},{3,1},{4,6},{6,4},{5,7},{7,5},{8,10},{10,8},{9,1... | collective-permute-start | bytes 3145736 | tf_op jit(solution)/shard_map/ppermute | solution.py:59
  388.3 47.9 %collective-permute-start.27 = (bf16[256,2048]{1,0:T(8,128)(2,1)}, bf16[256,2048]{1,0:T(8,128)(2,1)}, u32[]{:S(2)}, u32[]{:S(2)}) collective-permute-start(bf16[256,2048]{1,0:T(8,128)(2,1)} %get-tuple-element.140), channel_id=1, source_target_pairs={{0,4},{4,0},{1,5},{5,1},{2,6},{6,2},{3,7},{7,3},{8,12},{12,8},{9,1... | collective-permute-start | bytes 3145736 | tf_op jit(solution)/shard_map/ppermute | solution.py:59
  388.5 47.7 %collective-permute-start.28 = (bf16[256,2048]{1,0:T(8,128)(2,1)}, bf16[256,2048]{1,0:T(8,128)(2,1)}, u32[]{:S(2)}, u32[]{:S(2)}) collective-permute-start(bf16[256,2048]{1,0:T(8,128)(2,1)} %get-tuple-element.133), channel_id=1, source_target_pairs={{0,6},{2,4},{4,2},{6,0},{1,7},{3,5},{5,3},{7,1},{8,14},{10,12},{12... | collective-permute-start | bytes 3145736 | tf_op jit(solution)/shard_map/ppermute | solution.py:165
  436.1 19.0 %all-to-all-start.4 = ((bf16[8,64,704]{2,1,0:T(8,128)(2,1)}), bf16[8,64,704]{2,1,0:T(8,128)(2,1)S(1)}, u32[]{:S(2)}, u32[]{:S(2)}) async-start(bf16[8,64,704]{2,1,0:T(8,128)(2,1)} %bitcast.58), calls=%async_computation.5 | async-start | bytes 1572864 | tf_op jit(solution)/shard_map/all_to_all | solution.py:239
  439.7 163.9 %reduce-scatter.9.cloned.1.call-start = ((), (), s32[]{:S(2)}) async-start(), calls=%async_computation.18 | async-start | bytes 3932160 | tf_op jit(solution)/shard_map/reduce_scatter | solution.py:855
  455.1 19.7 %copy-start.30 = (bf16[256,2048]{1,0:T(8,128)(2,1)S(1)}, bf16[256,2048]{1,0:T(8,128)(2,1)}, u32[]{:S(2)}) copy-start(bf16[256,2048]{1,0:T(8,128)(2,1)} %get-tuple-element.157.refs_0_) | copy-start | bytes 3145732
  474.8 26.3 %collective-permute-start.29 = (bf16[256,2048]{1,0:T(8,128)(2,1)S(1)}, bf16[256,2048]{1,0:T(8,128)(2,1)S(1)}, u32[]{:S(2)}, u32[]{:S(2)}) collective-permute-start(bf16[256,2048]{1,0:T(8,128)(2,1)S(1)} %copy-done.30), channel_id=1, source_target_pairs={{0,2},{2,0},{1,3},{3,1},{4,6},{6,4},{5,7},{7,5},{8,10},{10,8},{9,1... | collective-permute-start | bytes 3145736 | tf_op jit(solution)/shard_map/ppermute | solution.py:59
  475.4 25.8 %collective-permute-start.30 = (bf16[256,2048]{1,0:T(8,128)(2,1)S(1)}, bf16[256,2048]{1,0:T(8,128)(2,1)S(1)}, u32[]{:S(2)}, u32[]{:S(2)}) collective-permute-start(bf16[256,2048]{1,0:T(8,128)(2,1)S(1)} %copy-done.30), channel_id=1, source_target_pairs={{0,4},{4,0},{1,5},{5,1},{2,6},{6,2},{3,7},{7,3},{8,12},{12,8},{9,1... | collective-permute-start | bytes 3145736 | tf_op jit(solution)/shard_map/ppermute | solution.py:59
  501.2 14.1 %copy-start.26 = (bf16[256,2048]{1,0:T(8,128)(2,1)}, bf16[256,2048]{1,0:T(8,128)(2,1)S(1)}, u32[]{:S(2)}) copy-start(bf16[256,2048]{1,0:T(8,128)(2,1)S(1)} %collective-permute-done.29.refs_1_) | copy-start | bytes 3145732
  501.3 14.0 %collective-permute-start.31 = (bf16[128,2048]{1,0:T(8,128)(2,1)S(1)}, bf16[128,2048]{1,0:T(8,128)(2,1)S(1)}, u32[]{:S(2)}, u32[]{:S(2)}) collective-permute-start(bf16[128,2048]{1,0:T(8,128)(2,1)S(1)} %slice.147), channel_id=1, source_target_pairs={{0,2},{2,0},{1,3},{3,1},{4,6},{6,4},{5,7},{7,5},{8,10},{10,8},{9,1... | collective-permute-start | bytes 1572872 | tf_op jit(solution)/shard_map/ppermute | solution.py:59
  502.8 12.5 %collective-permute-start.32 = (bf16[128,2048]{1,0:T(8,128)(2,1)S(1)}, bf16[128,2048]{1,0:T(8,128)(2,1)}, u32[]{:S(2)}, u32[]{:S(2)}) collective-permute-start(bf16[128,2048]{1,0:T(8,128)(2,1)S(1)} %slice.148), channel_id=1, source_target_pairs={{0,4},{4,0},{1,5},{5,1},{2,6},{6,2},{3,7},{7,3},{8,12},{12,8},{9,1... | collective-permute-start | bytes 1572872 | tf_op jit(solution)/shard_map/ppermute | solution.py:59
  515.3 7.4 %copy-start.31 = (bf16[128,2048]{1,0:T(8,128)(2,1)}, bf16[128,2048]{1,0:T(8,128)(2,1)S(1)}, u32[]{:S(2)}) copy-start(bf16[128,2048]{1,0:T(8,128)(2,1)S(1)} %collective-permute-done.31.refs_3_) | copy-start | bytes 1572868
  522.6 7.5 %collective-permute-start.33 = (bf16[1024,2048]{1,0:T(8,128)(2,1)}, bf16[1024,2048]{1,0:T(8,128)(2,1)}, u32[]{:S(2)}, u32[]{:S(2)}) collective-permute-start(bf16[1024,2048]{1,0:T(8,128)(2,1)} %shard_map.249), channel_id=1, source_target_pairs={{0,1},{1,0},{2,3},{3,2},{4,5},{5,4},{6,7},{7,6},{8,9},{9,8},{10,11... | collective-permute-start | bytes 12582920 | tf_op jit(solution)/shard_map/ppermute | solution.py:59
  534.9 22.6 %collective-permute-start.37 = (bf16[1024,2048]{1,0:T(8,128)(2,1)}, bf16[1024,2048]{1,0:T(8,128)(2,1)}, u32[]{:S(2)}, u32[]{:S(2)}) collective-permute-start(bf16[1024,2048]{1,0:T(8,128)(2,1)} %shard_map.250.right0_ref), channel_id=1, source_target_pairs={{0,1},{1,0},{2,3},{3,2},{4,5},{5,4},{6,7},{7,6},{8,9},{9,8},{10,11... | collective-permute-start | bytes 12582920 | tf_op jit(solution)/shard_map/ppermute | solution.py:59
  535.0 23.3 %all-to-all-start.6 = ((bf16[8,64,1408]{2,1,0:T(8,128)(2,1)}), bf16[8,64,1408]{2,1,0:T(8,128)(2,1)S(1)}, u32[]{:S(2)}, u32[]{:S(2)}) async-start(bf16[8,64,1408]{2,1,0:T(8,128)(2,1)} %bitcast.55), calls=%async_computation.8 | async-start | bytes 2883584 | tf_op jit(solution)/shard_map/all_to_all | solution.py:239
  538.8 96.0 %reduce-scatter.11.cloned.1.call-start = ((), (), s32[]{:S(2)}) async-start(), calls=%async_computation.19 | async-start | bytes 1310720 | tf_op jit(solution)/shard_map/reduce_scatter | solution.py:855
  554.0 26.3 %collective-permute-start.34 = (bf16[256,2048]{1,0:T(8,128)(2,1)}, bf16[256,2048]{1,0:T(8,128)(2,1)}, u32[]{:S(2)}, u32[]{:S(2)}) collective-permute-start(bf16[256,2048]{1,0:T(8,128)(2,1)} %get-tuple-element.164), channel_id=1, source_target_pairs={{0,2},{2,0},{1,3},{3,1},{4,6},{6,4},{5,7},{7,5},{8,10},{10,8},{9,1... | collective-permute-start | bytes 3145736 | tf_op jit(solution)/shard_map/ppermute | solution.py:59
  555.9 47.8 %collective-permute-start.35 = (bf16[256,2048]{1,0:T(8,128)(2,1)}, bf16[256,2048]{1,0:T(8,128)(2,1)}, u32[]{:S(2)}, u32[]{:S(2)}) collective-permute-start(bf16[256,2048]{1,0:T(8,128)(2,1)} %get-tuple-element.165), channel_id=1, source_target_pairs={{0,4},{4,0},{1,5},{5,1},{2,6},{6,2},{3,7},{7,3},{8,12},{12,8},{9,1... | collective-permute-start | bytes 3145736 | tf_op jit(solution)/shard_map/ppermute | solution.py:59
  557.3 46.3 %collective-permute-start.36 = (bf16[256,2048]{1,0:T(8,128)(2,1)}, bf16[256,2048]{1,0:T(8,128)(2,1)}, u32[]{:S(2)}, u32[]{:S(2)}) collective-permute-start(bf16[256,2048]{1,0:T(8,128)(2,1)} %get-tuple-element.166), channel_id=1, source_target_pairs={{0,6},{2,4},{4,2},{6,0},{1,7},{3,5},{5,3},{7,1},{8,14},{10,12},{12... | collective-permute-start | bytes 3145736 | tf_op jit(solution)/shard_map/ppermute | solution.py:165
  603.6 16.8 %all-to-all-start.7 = ((bf16[8,64,768]{2,1,0:T(8,128)(2,1)}), bf16[8,64,768]{2,1,0:T(8,128)(2,1)}, u32[]{:S(2)}, u32[]{:S(2)}) async-start(bf16[8,64,768]{2,1,0:T(8,128)(2,1)} %bitcast.57), calls=%async_computation.10 | async-start | bytes 1572864 | tf_op jit(solution)/shard_map/all_to_all | solution.py:239
  621.4 12.1 %all-to-all-start.8 = ((f32[32,1,448]{2,1,0:T(1,128)}), f32[32,1,448]{2,1,0:T(1,128)S(1)}, u32[]{:S(2)}, u32[]{:S(2)}) async-start(f32[32,1,448]{2,1,0:T(1,128)} %all_to_all.44), calls=%async_computation.11 | async-start | bytes 131072 | tf_op jit(solution)/shard_map/all_to_all | solution.py:917
  (20 other events, 55.0 us)
Sparse Core Ops, SparseCore 0:
  9.6 32.4 all-gather.5
  43.8 62.3 all-gather.3
  117.0 157.0 all-gather.7
  333.3 59.3 reduce-scatter.4
  411.0 102.2 reduce-scatter.6
  522.8 59.7 reduce-scatter.8
  584.9 27.1 reduce-scatter.10

commit v4 on v3

--- a/solution.py
+++ b/solution.py
@@ -129,7 +129,7 @@
 
 def plane_send(left, right, at, time=None):
     rows, depth, width = left.shape[0] // 8, left.shape[1], right.shape[0]
-    terms = pl.pallas_call(
+    return pl.pallas_call(
         send_kernel,
         grid=(2,),
         in_specs=[
@@ -140,7 +140,6 @@
         out_shape=jax.ShapeDtypeStruct((4 * rows, width), bf16),
         **limits(depth // 134 if time is None else time),
     )(left, right)
-    return swap(terms, "c")
 
 
 def plane_keep(left, right, at, other, kind=f32, time=None):
@@ -847,7 +846,7 @@
     cotangent = chip_pieces(after(out_grad, act_two[0]))
     middle_low, by_gate, by_up, act_all = gate_rows(act_two, ffn_full, my_ffn)
     cotangent = halves_of(cotangent, middle_low)
-    output_other = plane_send(middle_low, ffn_full, 2 * my_ffn)
+    output_other = swap(plane_send(middle_low, ffn_full, 2 * my_ffn), "c")
     down_sum = row_sum(cotangent, middle_low, kept=my_ffn)
     output_kept = plane_keep(after(middle_low, down_sum), ffn_full, 2 * my_ffn, output_other)
 
@@ -860,7 +859,7 @@
     down_own = own_rows(down_sum)
     gate_up_grad = gate_back_rows(after(cotangent, output_kept[0]), ffn_full, by_gate, by_up, my_ffn)
     output_terms = after(plane_corner(output_kept), gate_up_grad)
-    norm_two_other = plane_send(after(gate_up_grad, output_terms[0]), ffn_full, 0)
+    norm_two_other = swap(plane_send(after(gate_up_grad, output_terms[0]), ffn_full, 0), "c")
     norm_two_kept = plane_keep(gate_up_grad, ffn_full, 0, norm_two_other, bf16)
     gate_up_sum = row_sum([act_all], after(gate_up_grad, norm_two_kept[0], down_own), time=60)
     output = (hidden + total_of(after(plane_neighbours(output_terms), gate_up_sum))).astype(bf16)
@@ -877,7 +876,8 @@
     hidden_pieces = chip_pieces(after(hidden_low, mixed_grad), qkv_grad)
     qkv_sum = row_sum([act_one], after(qkv_grad, hidden_pieces[1]), time=130)
     qkv_own = own_rows(qkv_sum)
-    norm_one_other = plane_send(after(qkv_grad, qkv_sum, hidden_pieces), qkv_full, 0, time=60)
+    norm_one_sent = plane_send(after(qkv_grad, qkv_sum, hidden_pieces), qkv_full, 0, time=60)
+    norm_one_other = swap(norm_one_sent, "c")
     hidden_all = halves_of(hidden_pieces, norm_one_other, time=60)
     gate_up_recv = back_to_rows(after(gate_up_own, norm_one_other))
     norm_one_kept = plane_keep(after(qkv_grad, hidden_all[0]), qkv_full, 0, norm_one_other, bf16)
@@ -894,10 +894,11 @@
             spread.reshape(width, width).astype(f32), ALL, scatter_dimension=0, tiled=True
         )
     norm_one_terms = after(plane_direct(norm_one_kept), out_sum)
-    norm_grad_one = total_of(norm_one_terms)
+    qkv_recv = back_to_rows(after(qkv_own, out_sum))
+    norm_grad_one = total_of(after(norm_one_terms, qkv_recv))
     normed_one, inv_one = layer_stats(tokens.astype(f32))
     input_grad = (hidden_grad + norm_back(norm_grad_one, normed_one, inv_one, gain_one)).astype(bf16)
-    down_share = merge_ffn(down_recv, 1, ffn)
+    down_share = merge_ffn(after(down_recv, out_sum), 1, ffn)
     gate_up_share = merge_ffn(gate_up_recv, 2, ffn)
 
     bias_sum = jnp.sum(qkv_grad.astype(f32), axis=0).reshape(3, my_heads, 1, HEAD_DIM)
@@ -911,8 +912,6 @@
         ],
         axis=0,
     )
-    qkv_recv = back_to_rows(after(qkv_own, out_sum))
-    terms = after(terms, qkv_recv)
     terms = jnp.transpose(terms.reshape(7, devices, shard), (1, 0, 2)).reshape(devices, 7 * shard)
     vector_share = jnp.sum(lax.all_to_all(terms, ALL, 0, 0, tiled=True), axis=0).reshape(7, shard)
     qkv_share = merge_heads(qkv_recv)

time: 649 us -> 644 us (level)
  waiting for transfers between devices: 207 us -> 198 us
    ppermute x36, waiting for transfers between devices: 167 us -> 127 us  [swap(): return lax.ppermute(values, axis, [(0, 1), (1, 0)])]
    reduce_scatter x4, waiting for transfers between devices: 1.25 us -> 17.7 us  [own_rows(): return lax.psum_scatter(grad_sum, 'g', scatter_dimension=0, tiled=True)]
    ppermute x2, waiting for transfers between devices: 0.01 us -> 14.7 us  [plane_direct(): far = lax.ppermute(corner, ('y', 'x'), [(0, 3), (1, 2), (2, 1), (3, 0)])]
  transfers between devices with their start and end apart: 52 -> 52, of which waited for: 21 -> 22; matrix products, arithmetic and copies ran while one was open for 7% -> 7% of each run, Pallas kernels for 39% -> 39%
where the time goes in v4:
time: 644 us; the launch traced here: 639 us
  Pallas kernels  265 us (41%)
  waiting for transfers between devices  198 us (31%)
  starting transfers between devices  62.9 us (10%)
  blocking collectives  36.5 us (6%)
  other arithmetic  31.9 us (5%)
  local copies, waits for them, and re-layouts  29.8 us (5%)
  between operations  15 us (2%)
    ppermute x36, waiting for transfers between devices, swap(): return lax.ppermute(values, axis, [(0, 1), (1, 0)])  127 us
    pallas_call x3, Pallas kernels, row_sum(): pl.pallas_call(sum_kernel, grid=(width // step,), in_specs=[*[pl.BlockSpe...  40.1 us
    all_to_all x2, blocking collectives, plane_all_to_all(): return lax.all_to_all(blocks, PLANE, 0, 0, tiled=True)  36.5 us
    pallas_call x3, Pallas kernels, plane_keep(): pl.pallas_call(keep_kernel, grid=(4,), in_specs=[pl.BlockSpec((rows, dept...  33.2 us
    all_to_all x5, waiting for transfers between devices, plane_all_to_all(): return lax.all_to_all(blocks, PLANE, 0, 0, tiled=True)  29.8 us
    ppermute x36, starting transfers between devices, swap(): return lax.ppermute(values, axis, [(0, 1), (1, 0)])  29.6 us
    pallas_call x3, Pallas kernels, plane_send(): pl.pallas_call(send_kernel, grid=(2,), in_specs=[pl.BlockSpec((2 * rows,...  25.7 us
    pallas_call x1, Pallas kernels, attention_back(): pl.pallas_call(functools.partial(attend_back_kernel, blocks), grid_spec=p...  25.1 us
  transfers between devices with their start and end apart: 52, of which 22 were waited for; matrix products, arithmetic and copies ran while one was open for 7% of the time, Pallas kernels for 39%

profile of v4, /device:TPU:0, one launch (start us, length us, event | category | flops | bytes accessed | tf_op | source)
XLA Modules:
  0.0 638.7 jit_solution(2765039272056302361)
XLA Ops:
  10.9 7.3 %all-to-all-start = ((f32[32,1,960]{2,1,0:T(1,128)}), f32[32,1,960]{2,1,0:T(1,128)S(1)}, u32[]{:S(2)}, u32[]{:S(2)}) async-start(f32[32,1,960]{2,1,0:T(1,128)} %broadcast_in_dim.14), calls=%async_computation | async-start | bytes 262144 | tf_op jit(solution)/shard_map/all_to_all | solution.py:790
  18.3 2.5 shard_map.230
  20.8 6.1 all-to-all-done
  26.9 16.8 %all_to_all.54 = bf16[8,64,768]{2,1,0:T(8,128)(2,1)} all-to-all(bf16[8,64,768]{2,1,0:T(8,128)(2,1)} %shard_map.230), channel_id=1, replica_groups=mesh['g'=4,'y'=2,'x'=2,'c'=2] {'y','x','c'}, dimensions={0} | all-to-all | bytes 1572864 | tf_op jit(solution)/shard_map/all_to_all | solution.py:238
  44.9 23.1 %collective-permute-done.1.refs_2_ = bf16[256,2048]{1,0:T(8,128)(2,1)S(1)} collective-permute-done((bf16[256,2048]{1,0:T(8,128)(2,1)S(1)}, bf16[256,2048]{1,0:T(8,128)(2,1)S(1)}, u32[]{:S(2)}, u32[]{:S(2)}) %collective-permute-start.1) | collective-permute-done | bytes 1048608 | tf_op jit(solution)/shard_map/ppermute | solution.py:59
  71.0 3.7 shard_map.231
  76.7 5.1 collective-permute-done.2.refs_3_
  83.9 3.6 all-to-all-start.2
  87.8 7.2 %shard_map.229.act0_ref = bf16[1024,2048]{1,0:T(8,128)(2,1)} custom-call(bf16[256,2048]{1,0:T(8,128)(2,1)} %token_ref.1, bf16[256,2048]{1,0:T(8,128)(2,1)} %copy-done.9, bf16[256,2048]{1,0:T(8,128)(2,1)} %copy-done.8, bf16[128,2048]{1,0:T(8,128)(2,1)} %collective-permute-done.2.refs_3_, bf16[128,2048]{1,0:T(8,128)(2,1)} %copy-done.19, ...), custom_call_target="tpu_custom_call" | custom-call | flops 1166666624 | bytes 3500000 | tf_op jit(solution)/shard_map/pallas_call | solution.py:427
  96.0 5.2 compare_select_fusion.9
  101.4 5.5 fusion.12
  106.9 8.6 %all-to-all-done.2 = bf16[8,64,2176]{2,1,0:T(8,128)(2,1)S(1)} async-done(((bf16[8,64,2176]{2,1,0:T(8,128)(2,1)}), bf16[8,64,2176]{2,1,0:T(8,128)(2,1)S(1)}, u32[]{:S(2)}, u32[]{:S(2)}) %all-to-all-start.2) | async-done | bytes 2228256 | tf_op jit(solution)/shard_map/all_to_all | solution.py:238
  119.5 15.9 %shard_map.232 = (bf16[2,1024,768]{2,1,0:T(8,128)(2,1)}, bf16[2048,2048]{1,0:T(8,128)(2,1)}) custom-call(s32[4]{0:T(128)} %pad_add_fusion.place, bf16[1024,2048]{1,0:T(8,128)(2,1)} %shard_map.229.act0_ref, bf16[1024,2048]{1,0:T(8,128)(2,1)} %collective-permute-done.4.act1_ref, bf16[2048,768]{1,0:T(8,128)(2,1)} %all-gather.4.cloned.1.call-done.weight_ref.right_ref, ...), custom_call_target="tpu_custom_call" | custom-call | flops 2500000000 | bytes 7500000 | tf_op jit(solution)/shard_map/pallas_call | solution.py:464
  135.3 3.9 collective-permute-done.6.refs_2_
  139.2 1.9 collective-permute-done.5.refs_1_
  148.3 15.8 %shard_map.233 = (bf16[2,4,256,256]{3,2,1,0:T(8,128)(2,1)}, bf16[2,2,2,256,256]{4,3,2,1,0:T(8,128)(2,1)}, f32[2,2,2,1024]{3,2,1,0:T(2,128)}) custom-call(s32[4]{0:T(128)} %pad_add_fusion.place, bf16[2,1024,768]{2,1,0:T(8,128)(2,1)} %get-tuple-element.104.query_ref.key_ref.value_ref, bf16[2,1024,768]{2,1,0:T(8,128)(2,1)} %get-tuple-element.104.query_ref.key_ref.value_ref, ...), custom_call_target="tpu_custom_call" | custom-call | flops 2666666752 | bytes 8000000 | tf_op jit(solution)/shard_map/pallas_call | solution.py:368
  165.1 4.8 shard_map.234.w0_ref
  169.8 3.6 all-to-all-start.3
  175.3 13.4 %all-to-all-done.3.mixed_ref = bf16[8,256,256]{2,1,0:T(8,128)(2,1)S(1)} async-done(((bf16[8,256,256]{2,1,0:T(8,128)(2,1)}), bf16[8,256,256]{2,1,0:T(8,128)(2,1)S(1)}, u32[]{:S(2)}, u32[]{:S(2)}) %all-to-all-start.3) | async-done | bytes 1048608 | tf_op jit(solution)/shard_map/all_to_all | solution.py:238
  189.7 11.9 %shard_map.235 = (f32[256,2048]{1,0:T(8,128)}, bf16[256,2048]{1,0:T(8,128)(2,1)}) custom-call(s32[4]{0:T(128)} %pad_add_fusion.place, bf16[8,256,256]{2,1,0:T(8,128)(2,1)} %copy-done.5, bf16[1024,2048]{1,0:T(8,128)(2,1)} %shard_map.234.w0_ref, bf16[1024,2048]{1,0:T(8,128)(2,1)} %collective-permute-done.9.w1_ref, bf16[256,2048]{1,0:T(8,128)(2,1)} %token_ref.1, ...), custom_call_target="tpu_custom_call" | custom-call | flops 2000000000 | bytes 6000000 | tf_op jit(solution)/shard_map/pallas_call | solution.py:527
  202.7 21.1 %collective-permute-done.11.refs_2_ = bf16[256,2048]{1,0:T(8,128)(2,1)S(1)} collective-permute-done((bf16[256,2048]{1,0:T(8,128)(2,1)}, bf16[256,2048]{1,0:T(8,128)(2,1)S(1)}, u32[]{:S(2)}, u32[]{:S(2)}) %collective-permute-start.11) | collective-permute-done | bytes 1048608 | tf_op jit(solution)/shard_map/ppermute | solution.py:59
  223.9 3.7 collective-permute-start.12
  228.1 11.1 %collective-permute-done.12.refs_3_ = bf16[128,2048]{1,0:T(8,128)(2,1)S(1)} collective-permute-done((bf16[128,2048]{1,0:T(8,128)(2,1)S(1)}, bf16[128,2048]{1,0:T(8,128)(2,1)S(1)}, u32[]{:S(2)}, u32[]{:S(2)}) %collective-permute-start.12) | collective-permute-done | bytes 524320 | tf_op jit(solution)/shard_map/ppermute | solution.py:59
  241.6 4.7 shard_map.236.act0_ref
  247.9 23.9 %collective-permute-done.16.refs_2_ = bf16[256,2048]{1,0:T(8,128)(2,1)S(1)} collective-permute-done((bf16[256,2048]{1,0:T(8,128)(2,1)S(1)}, bf16[256,2048]{1,0:T(8,128)(2,1)S(1)}, u32[]{:S(2)}, u32[]{:S(2)}) %collective-permute-start.16) | collective-permute-done | bytes 1048608 | tf_op jit(solution)/shard_map/ppermute | solution.py:59
  274.4 20.0 %shard_map.237 = (bf16[2048,768]{1,0:T(8,128)(2,1)}, bf16[2048,768]{1,0:T(8,128)(2,1)}, bf16[2048,768]{1,0:T(8,128)(2,1)}, bf16[2048,2048]{1,0:T(8,128)(2,1)}) custom-call(bf16[1024,2048]{1,0:T(8,128)(2,1)} %shard_map.236.act0_ref, bf16[1024,2048]{1,0:T(8,128)(2,1)} %collective-permute-done.14.act1_ref, ...), custom_call_target="tpu_custom_call" | custom-call | flops 3333333248 | bytes 10000000 | tf_op jit(solution)/shard_map/pallas_call | solution.py:618
  295.3 4.8 shard_map.238.refs_0_.grad0_ref
  300.1 7.1 %shard_map.240 = bf16[1024,2048]{1,0:T(8,128)(2,1)} custom-call(bf16[2048,768]{1,0:T(8,128)(2,1)} %get-tuple-element.123.refs_2_.left_ref, bf16[2048,2176]{1,0:T(8,128)(2,1)} %all-gather.8.cloned.1.call-done.weight_ref.right_ref), custom_call_target="tpu_custom_call" | custom-call | flops 833333312 | bytes 2500000 | tf_op jit(solution)/shard_map/pallas_call | solution.py:132
  307.7 2.0 copy-done.2
  309.7 10.8 %shard_map.239 = bf16[2048,704]{1,0:T(8,128)(2,1)} custom-call(bf16[1024,2048]{1,0:T(8,128)(2,1)} %shard_map.238.refs_0_.grad0_ref, bf16[1024,2048]{1,0:T(8,128)(2,1)} %copy-done.2, bf16[2048,768]{1,0:T(8,128)(2,1)} %get-tuple-element.123.refs_2_.left_ref), custom_call_target="tpu_custom_call" | custom-call | flops 1500000000 | bytes 4500000 | tf_op jit(solution)/shard_map/pallas_call | solution.py:201
  320.5 10.3 %shard_map.241 = (bf16[256,2048]{1,0:T(8,128)(2,1)}, f32[256,2048]{1,0:T(8,128)}, f32[256,2048]{1,0:T(8,128)}, f32[256,2048]{1,0:T(8,128)}) custom-call(bf16[2048,768]{1,0:T(8,128)(2,1)} %get-tuple-element.123.refs_2_.left_ref, bf16[2048,2176]{1,0:T(8,128)(2,1)} %all-gather.8.cloned.1.call-done.weight_ref.right_ref, ...), custom_call_target="tpu_custom_call" | custom-call | flops 1000000000 | bytes 3000000 | tf_op jit(solution)/shard_map/pallas_call | solution.py:148
  336.4 14.1 %shard_map.242.left_ref.refs_1_ = bf16[2048,1408]{1,0:T(8,128)(2,1)} custom-call(bf16[1024,2048]{1,0:T(8,128)(2,1)} %shard_map.238.refs_0_.grad0_ref, bf16[1024,2048]{1,0:T(8,128)(2,1)} %copy-done.2, bf16[2048,2176]{1,0:T(8,128)(2,1)} %all-gather.8.cloned.1.call-done.weight_ref.right_ref, bf16[2048,768]{1,0:T(8,128)(2,1)} %get-tuple-element.130.by_gate_ref, ...), custom_call_target="tpu_custom_call" | custom-call | flops 2166666752 | bytes 6500000 | tf_op jit(solution)/shard_map/pallas_call | solution.py:644
  354.0 11.4 %shard_map.243 = bf16[1024,2048]{1,0:T(8,128)(2,1)} custom-call(bf16[2048,1408]{1,0:T(8,128)(2,1)} %shard_map.242.left_ref.refs_1_, bf16[2048,2176]{1,0:T(8,128)(2,1)} %all-gather.8.cloned.1.call-done.weight_ref.right_ref), custom_call_target="tpu_custom_call" | custom-call | flops 1666666624 | bytes 5000000 | tf_op jit(solution)/shard_map/pallas_call | solution.py:132
  366.4 6.4 collective-permute-done.25.other_ref
  372.7 2.0 copy-done.4
  374.7 13.3 %shard_map.244 = (bf16[256,2048]{1,0:T(8,128)(2,1)}, bf16[256,2048]{1,0:T(8,128)(2,1)}, bf16[256,2048]{1,0:T(8,128)(2,1)}, f32[256,2048]{1,0:T(8,128)}) custom-call(bf16[2048,1408]{1,0:T(8,128)(2,1)} %shard_map.242.left_ref.refs_1_, bf16[2048,2176]{1,0:T(8,128)(2,1)} %all-gather.8.cloned.1.call-done.weight_ref.right_ref, bf16[1024,2048]{1,0:T(8,128)(2,1)} %copy-done.4), custom_call_target="tpu_custom_call" | custom-call | flops 2000000000 | bytes 6000000 | tf_op jit(solution)/shard_map/pallas_call | solution.py:148
  389.2 2.4 collective-permute-start.28
  391.5 2.1 reduce-scatter.5.cloned.1.call-done
  393.6 18.2 %shard_map.245 = bf16[2048,1408]{1,0:T(8,128)(2,1)} custom-call(bf16[2048,2048]{1,0:T(8,128)(2,1)} %get-tuple-element.135.refs_0_, bf16[2048,1408]{1,0:T(8,128)(2,1)} %shard_map.242.left_ref.refs_1_), custom_call_target="tpu_custom_call" | custom-call | flops 10000000000 | bytes 30000000 | tf_op jit(solution)/shard_map/pallas_call | solution.py:201
  413.4 3.4 add_convert_fusion
  416.8 19.8 %collective-permute-done.27.y_ref = bf16[256,2048]{1,0:T(8,128)(2,1)} collective-permute-done((bf16[256,2048]{1,0:T(8,128)(2,1)}, bf16[256,2048]{1,0:T(8,128)(2,1)}, u32[]{:S(2)}, u32[]{:S(2)}) %collective-permute-start.27) | collective-permute-done | bytes 1048608 | tf_op jit(solution)/shard_map/ppermute | solution.py:59
  436.6 3.5 all-to-all-start.4
  440.5 15.1 %shard_map.246 = (bf16[8,256,256]{2,1,0:T(8,128)(2,1)}, f32[256,2048]{1,0:T(8,128)}, bf16[256,2048]{1,0:T(8,128)(2,1)}, f32[2,2048]{1,0:T(2,128)}) custom-call(s32[4]{0:T(128)} %pad_add_fusion.place, f32[256,2048]{1,0:T(8,128)} %get-tuple-element.145.own_ref, bf16[256,2048]{1,0:T(8,128)(2,1)} %collective-permute-done.26.x_ref, ...), custom_call_target="tpu_custom_call" | custom-call | flops 21666666496 | bytes 65000000 | tf_op jit(solution)/shard_map/pallas_call | solution.py:574
  455.6 19.8 %all_to_all.55 = bf16[8,256,256]{2,1,0:T(8,128)(2,1)} all-to-all(bf16[8,256,256]{2,1,0:T(8,128)(2,1)} %get-tuple-element.152), channel_id=1, replica_groups=mesh['g'=4,'y'=2,'x'=2,'c'=2] {'y','x','c'}, dimensions={0} | all-to-all | bytes 2097152 | tf_op jit(solution)/shard_map/all_to_all | solution.py:238
  476.4 25.1 %shard_map.247 = bf16[2,2,2,256,768]{4,3,2,1,0:T(8,128)(2,1)} custom-call(s32[4]{0:T(128)} %pad_add_fusion.place, bf16[2,1024,768]{2,1,0:T(8,128)(2,1)} %get-tuple-element.104.query_ref.key_ref.value_ref, bf16[2,1024,768]{2,1,0:T(8,128)(2,1)} %get-tuple-element.104.query_ref.key_ref.value_ref, ...), custom_call_target="tpu_custom_call" | custom-call | flops 21666666496 | bytes 65000000 | tf_op jit(solution)/shard_map/pallas_call | solution.py:394
  504.7 11.0 %shard_map.248 = bf16[2048,768]{1,0:T(8,128)(2,1)} custom-call(bf16[2048,2048]{1,0:T(8,128)(2,1)} %get-tuple-element.158.refs_0_, bf16[2048,768]{1,0:T(8,128)(2,1)} %bitcast.49), custom_call_target="tpu_custom_call" | custom-call | flops 21666666496 | bytes 65000000 | tf_op jit(solution)/shard_map/pallas_call | solution.py:201
  516.3 7.2 %shard_map.249 = bf16[1024,2048]{1,0:T(8,128)(2,1)} custom-call(bf16[2048,768]{1,0:T(8,128)(2,1)} %bitcast.50, bf16[2048,768]{1,0:T(8,128)(2,1)} %all-gather.4.cloned.1.call-done.weight_ref.right_ref), custom_call_target="tpu_custom_call" | custom-call | flops 10000000000 | bytes 30000000 | tf_op jit(solution)/shard_map/pallas_call | solution.py:132
  523.5 7.5 %collective-permute-done.33.other_ref = bf16[1024,2048]{1,0:T(8,128)(2,1)} collective-permute-done((bf16[1024,2048]{1,0:T(8,128)(2,1)}, bf16[1024,2048]{1,0:T(8,128)(2,1)}, u32[]{:S(2)}, u32[]{:S(2)}) %collective-permute-start.33) | collective-permute-done | bytes 4194336 | tf_op jit(solution)/shard_map/ppermute | solution.py:59
  531.0 4.8 shard_map.250.right0_ref
  535.9 4.0 all-to-all-start.6
  540.2 9.6 %shard_map.251 = (bf16[256,2048]{1,0:T(8,128)(2,1)}, bf16[256,2048]{1,0:T(8,128)(2,1)}, bf16[256,2048]{1,0:T(8,128)(2,1)}, f32[256,2048]{1,0:T(8,128)}) custom-call(bf16[2048,768]{1,0:T(8,128)(2,1)} %bitcast.51, bf16[2048,768]{1,0:T(8,128)(2,1)} %all-gather.4.cloned.1.call-done.weight_ref.right_ref, bf16[1024,2048]{1,0:T(8,128)(2,1)} %collective-permute-done.33.other_ref), custom_call_target="tpu_custom_call" | custom-call | flops 1000000000 | bytes 3000000 | tf_op jit(solution)/shard_map/pallas_call | solution.py:148
  549.8 1.9 collective-permute-start.34
  553.3 6.6 %all-to-all-done.6.part_ref = bf16[8,64,1408]{2,1,0:T(8,128)(2,1)S(1)} async-done(((bf16[8,64,1408]{2,1,0:T(8,128)(2,1)}), bf16[8,64,1408]{2,1,0:T(8,128)(2,1)S(1)}, u32[]{:S(2)}, u32[]{:S(2)}) %all-to-all-start.6) | async-done | bytes 1441824 | tf_op jit(solution)/shard_map/all_to_all | solution.py:238
  559.9 7.2 %shard_map.252 = bf16[256,2048]{1,0:T(8,128)(2,1)} custom-call(bf16[2,1024,256]{2,1,0:T(8,128)(2,1)} %bitcast.70, bf16[2,1024,256]{2,1,0:T(8,128)(2,1)} %bitcast.71, bf16[1024,2048]{1,0:T(8,128)(2,1)} %shard_map.250.right0_ref, bf16[1024,2048]{1,0:T(8,128)(2,1)} %collective-permute-done.37.right1_ref), custom_call_target="tpu_custom_call" | custom-call | flops 10000000000 | bytes 30000000 | tf_op jit(solution)/shard_map/pallas_call | solution.py:222
  567.1 15.7 %reduce-scatter.9.cloned.1.call-done = bf16[512,768]{1,0:T(8,128)(2,1)} async-done(((bf16[2048,768]{1,0:T(8,128)(2,1)}), bf16[512,768]{1,0:T(8,128)(2,1)}) %reduce-scatter.9.cloned.1.call-update) | async-done | bytes 786448 | tf_op jit(solution)/shard_map/reduce_scatter | solution.py:854
  582.8 4.2 all-to-all-start.7
  587.7 2.4 convert_reduce_fusion
  590.4 14.7 %collective-permute-done.36 = bf16[256,2048]{1,0:T(8,128)(2,1)} collective-permute-done((bf16[256,2048]{1,0:T(8,128)(2,1)}, bf16[256,2048]{1,0:T(8,128)(2,1)}, u32[]{:S(2)}, u32[]{:S(2)}) %collective-permute-start.36) | collective-permute-done | bytes 1048608 | tf_op jit(solution)/shard_map/ppermute | solution.py:164
  606.0 2.5 shard_map.255
  608.5 3.4 shard_map.254
  613.0 3.9 fusion.10
  617.9 3.1 all-to-all-start.8
  621.1 3.4 fusion.9
  624.4 2.6 shard_map.253
  (213 shorter events, 66.4 us)
Async XLA Ops:
  7.2 109.7 %all-gather.6.cloned.1.call-start = ((), (), s32[]{:S(2)}) async-start(), calls=%async_computation.14 | async-start | bytes 1310720 | tf_op jit(solution)/shard_map/all_gather | solution.py:817
  10.9 15.9 %all-to-all-start = ((f32[32,1,960]{2,1,0:T(1,128)}), f32[32,1,960]{2,1,0:T(1,128)S(1)}, u32[]{:S(2)}, u32[]{:S(2)}) async-start(f32[32,1,960]{2,1,0:T(1,128)} %broadcast_in_dim.14), calls=%async_computation | async-start | bytes 262144 | tf_op jit(solution)/shard_map/all_to_all | solution.py:790
  18.2 25.5 %copy-start = (bf16[256,2048]{1,0:T(8,128)(2,1)S(1)}, bf16[256,2048]{1,0:T(8,128)(2,1)}, u32[]{:S(2)}) copy-start(bf16[256,2048]{1,0:T(8,128)(2,1)} %token_ref.1) | copy-start | bytes 3145732
  18.2 101.2 %all-gather.4.cloned.1.call-start = ((), (), s32[]{:S(2)}) async-start(), calls=%async_computation.13 | async-start | bytes 3932160 | tf_op jit(solution)/shard_map/all_gather | solution.py:817
  43.7 24.3 %collective-permute-start.1 = (bf16[256,2048]{1,0:T(8,128)(2,1)S(1)}, bf16[256,2048]{1,0:T(8,128)(2,1)S(1)}, u32[]{:S(2)}, u32[]{:S(2)}) collective-permute-start(bf16[256,2048]{1,0:T(8,128)(2,1)S(1)} %copy-done), channel_id=1, source_target_pairs={{0,4},{4,0},{1,5},{5,1},{2,6},{6,2},{3,7},{7,3},{8,12},{12,8},{9,1... | collective-permute-start | bytes 3145736 | tf_op jit(solution)/shard_map/ppermute | solution.py:59
  44.3 25.9 %collective-permute-start = (bf16[256,2048]{1,0:T(8,128)(2,1)S(1)}, bf16[256,2048]{1,0:T(8,128)(2,1)S(1)}, u32[]{:S(2)}, u32[]{:S(2)}) collective-permute-start(bf16[256,2048]{1,0:T(8,128)(2,1)S(1)} %copy-done), channel_id=1, source_target_pairs={{0,2},{2,0},{1,3},{3,1},{4,6},{6,4},{5,7},{7,5},{8,10},{10,8},{9,1... | collective-permute-start | bytes 3145736 | tf_op jit(solution)/shard_map/ppermute | solution.py:59
  68.9 12.9 %collective-permute-start.2 = (bf16[128,2048]{1,0:T(8,128)(2,1)}, bf16[128,2048]{1,0:T(8,128)(2,1)}, u32[]{:S(2)}, u32[]{:S(2)}) collective-permute-start(bf16[128,2048]{1,0:T(8,128)(2,1)} %slice.164), channel_id=1, source_target_pairs={{0,2},{2,0},{1,3},{3,1},{4,6},{6,4},{5,7},{7,5},{8,10},{10,8},{9,1... | collective-permute-start | bytes 1572872 | tf_op jit(solution)/shard_map/ppermute | solution.py:59
  70.3 12.8 %collective-permute-start.3 = (bf16[128,2048]{1,0:T(8,128)(2,1)S(1)}, bf16[128,2048]{1,0:T(8,128)(2,1)S(1)}, u32[]{:S(2)}, u32[]{:S(2)}) collective-permute-start(bf16[128,2048]{1,0:T(8,128)(2,1)S(1)} %slice.165), channel_id=1, source_target_pairs={{0,4},{4,0},{1,5},{5,1},{2,6},{6,2},{3,7},{7,3},{8,12},{12,8},{9,1... | collective-permute-start | bytes 1572872 | tf_op jit(solution)/shard_map/ppermute | solution.py:59
  83.9 31.6 %all-to-all-start.2 = ((bf16[8,64,2176]{2,1,0:T(8,128)(2,1)}), bf16[8,64,2176]{2,1,0:T(8,128)(2,1)S(1)}, u32[]{:S(2)}, u32[]{:S(2)}) async-start(bf16[8,64,2176]{2,1,0:T(8,128)(2,1)} %shard_map.231), calls=%async_computation.2 | async-start | bytes 4456448 | tf_op jit(solution)/shard_map/all_to_all | solution.py:238
  87.5 187.0 %all-gather.8.cloned.1.call-start = ((), (), s32[]{:S(2)}) async-start(), calls=%async_computation.15 | async-start | bytes 11141120 | tf_op jit(solution)/shard_map/all_gather | solution.py:817
  95.0 24.4 %collective-permute-start.4 = (bf16[1024,2048]{1,0:T(8,128)(2,1)}, bf16[1024,2048]{1,0:T(8,128)(2,1)}, u32[]{:S(2)}, u32[]{:S(2)}) collective-permute-start(bf16[1024,2048]{1,0:T(8,128)(2,1)} %shard_map.229.act0_ref), channel_id=1, source_target_pairs={{0,1},{1,0},{2,3},{3,2},{4,5},{5,4},{6,7},{7,6},{8,9},{9,8},{10,11... | collective-permute-start | bytes 12582920 | tf_op jit(solution)/shard_map/ppermute | solution.py:59
  116.9 22.3 %collective-permute-start.6 = (bf16[256,2048]{1,0:T(8,128)(2,1)}, bf16[256,2048]{1,0:T(8,128)(2,1)S(1)}, u32[]{:S(2)}, u32[]{:S(2)}) collective-permute-start(bf16[256,2048]{1,0:T(8,128)(2,1)} %all-gather.6.cloned.1.call-done.refs_0_), channel_id=1, source_target_pairs={{0,4},{4,0},{1,5},{5,1},{2,6},{6,2},{3,7},{7,3},{8,12},{12,8},{9,1... | collective-permute-start | bytes 3145736 | tf_op jit(solution)/shard_map/ppermute | solution.py:59
  117.5 23.7 %collective-permute-start.5 = (bf16[256,2048]{1,0:T(8,128)(2,1)}, bf16[256,2048]{1,0:T(8,128)(2,1)S(1)}, u32[]{:S(2)}, u32[]{:S(2)}) collective-permute-start(bf16[256,2048]{1,0:T(8,128)(2,1)} %all-gather.6.cloned.1.call-done.refs_0_), channel_id=1, source_target_pairs={{0,2},{2,0},{1,3},{3,1},{4,6},{6,4},{5,7},{7,5},{8,10},{10,8},{9,1... | collective-permute-start | bytes 3145736 | tf_op jit(solution)/shard_map/ppermute | solution.py:59
  139.2 24.8 %copy-start.6 = (bf16[256,2048]{1,0:T(8,128)(2,1)}, bf16[256,2048]{1,0:T(8,128)(2,1)S(1)}, u32[]{:S(2)}) copy-start(bf16[256,2048]{1,0:T(8,128)(2,1)S(1)} %collective-permute-done.6.refs_2_) | copy-start | bytes 3145732
  141.2 22.9 %copy-start.7 = (bf16[256,2048]{1,0:T(8,128)(2,1)}, bf16[256,2048]{1,0:T(8,128)(2,1)S(1)}, u32[]{:S(2)}) copy-start(bf16[256,2048]{1,0:T(8,128)(2,1)S(1)} %collective-permute-done.5.refs_1_) | copy-start | bytes 3145732
  142.9 21.1 %collective-permute-start.7 = (bf16[128,2048]{1,0:T(8,128)(2,1)}, bf16[128,2048]{1,0:T(8,128)(2,1)S(1)}, u32[]{:S(2)}, u32[]{:S(2)}) collective-permute-start(bf16[128,2048]{1,0:T(8,128)(2,1)} %slice.131), channel_id=1, source_target_pairs={{0,2},{2,0},{1,3},{3,1},{4,6},{6,4},{5,7},{7,5},{8,10},{10,8},{9,1... | collective-permute-start | bytes 1572872 | tf_op jit(solution)/shard_map/ppermute | solution.py:59
  144.7 19.4 %collective-permute-start.8 = (bf16[128,2048]{1,0:T(8,128)(2,1)}, bf16[128,2048]{1,0:T(8,128)(2,1)S(1)}, u32[]{:S(2)}, u32[]{:S(2)}) collective-permute-start(bf16[128,2048]{1,0:T(8,128)(2,1)} %slice.132), channel_id=1, source_target_pairs={{0,4},{4,0},{1,5},{5,1},{2,6},{6,2},{3,7},{7,3},{8,12},{12,8},{9,1... | collective-permute-start | bytes 1572872 | tf_op jit(solution)/shard_map/ppermute | solution.py:59
  169.8 18.9 %collective-permute-start.9 = (bf16[1024,2048]{1,0:T(8,128)(2,1)}, bf16[1024,2048]{1,0:T(8,128)(2,1)}, u32[]{:S(2)}, u32[]{:S(2)}) collective-permute-start(bf16[1024,2048]{1,0:T(8,128)(2,1)} %shard_map.234.w0_ref), channel_id=1, source_target_pairs={{0,1},{1,0},{2,3},{3,2},{4,5},{5,4},{6,7},{7,6},{8,9},{9,8},{10,11... | collective-permute-start | bytes 12582920 | tf_op jit(solution)/shard_map/ppermute | solution.py:59
  169.8 18.9 %all-to-all-start.3 = ((bf16[8,256,256]{2,1,0:T(8,128)(2,1)}), bf16[8,256,256]{2,1,0:T(8,128)(2,1)S(1)}, u32[]{:S(2)}, u32[]{:S(2)}) async-start(bf16[8,256,256]{2,1,0:T(8,128)(2,1)} %bitcast.23), calls=%async_computation.3 | async-start | bytes 2097152 | tf_op jit(solution)/shard_map/all_to_all | solution.py:238
  173.4 220.2 %reduce-scatter.5.cloned.1.call-start = ((), (), s32[]{:S(2)}) async-start(), calls=%async_computation.16 | async-start | bytes 3932160 | tf_op jit(solution)/shard_map/reduce_scatter | solution.py:854
  201.6 22.3 %collective-permute-start.11 = (bf16[256,2048]{1,0:T(8,128)(2,1)}, bf16[256,2048]{1,0:T(8,128)(2,1)S(1)}, u32[]{:S(2)}, u32[]{:S(2)}) collective-permute-start(bf16[256,2048]{1,0:T(8,128)(2,1)} %get-tuple-element.115.refs_0_), channel_id=1, source_target_pairs={{0,4},{4,0},{1,5},{5,1},{2,6},{6,2},{3,7},{7,3},{8,12},{12,8},{9,1... | collective-permute-start | bytes 3145736 | tf_op jit(solution)/shard_map/ppermute | solution.py:59
  202.1 25.5 %collective-permute-start.10 = (bf16[256,2048]{1,0:T(8,128)(2,1)}, bf16[256,2048]{1,0:T(8,128)(2,1)S(1)}, u32[]{:S(2)}, u32[]{:S(2)}) collective-permute-start(bf16[256,2048]{1,0:T(8,128)(2,1)} %get-tuple-element.115.refs_0_), channel_id=1, source_target_pairs={{0,2},{2,0},{1,3},{3,1},{4,6},{6,4},{5,7},{7,5},{8,10},{10,8},{9,1... | collective-permute-start | bytes 3145736 | tf_op jit(solution)/shard_map/ppermute | solution.py:59
  223.8 16.9 %copy-start.12 = (bf16[256,2048]{1,0:T(8,128)(2,1)}, bf16[256,2048]{1,0:T(8,128)(2,1)S(1)}, u32[]{:S(2)}) copy-start(bf16[256,2048]{1,0:T(8,128)(2,1)S(1)} %collective-permute-done.11.refs_2_) | copy-start | bytes 3145732
  223.9 15.3 %collective-permute-start.12 = (bf16[128,2048]{1,0:T(8,128)(2,1)S(1)}, bf16[128,2048]{1,0:T(8,128)(2,1)S(1)}, u32[]{:S(2)}, u32[]{:S(2)}) collective-permute-start(bf16[128,2048]{1,0:T(8,128)(2,1)S(1)} %slice.173), channel_id=1, source_target_pairs={{0,2},{2,0},{1,3},{3,1},{4,6},{6,4},{5,7},{7,5},{8,10},{10,8},{9,1... | collective-permute-start | bytes 1572872 | tf_op jit(solution)/shard_map/ppermute | solution.py:59
  227.7 18.6 %copy-start.18 = (bf16[256,2048]{1,0:T(8,128)(2,1)S(1)}, bf16[256,2048]{1,0:T(8,128)(2,1)}, u32[]{:S(2)}) copy-start(bf16[256,2048]{1,0:T(8,128)(2,1)} %grad_ref.1) | copy-start | bytes 3145732
  227.7 13.1 %collective-permute-start.13 = (bf16[128,2048]{1,0:T(8,128)(2,1)S(1)}, bf16[128,2048]{1,0:T(8,128)(2,1)S(1)}, u32[]{:S(2)}, u32[]{:S(2)}) collective-permute-start(bf16[128,2048]{1,0:T(8,128)(2,1)S(1)} %slice.174), channel_id=1, source_target_pairs={{0,4},{4,0},{1,5},{5,1},{2,6},{6,2},{3,7},{7,3},{8,12},{12,8},{9,1... | collective-permute-start | bytes 1572872 | tf_op jit(solution)/shard_map/ppermute | solution.py:59
  246.3 28.2 %collective-permute-start.14 = (bf16[1024,2048]{1,0:T(8,128)(2,1)}, bf16[1024,2048]{1,0:T(8,128)(2,1)}, u32[]{:S(2)}, u32[]{:S(2)}) collective-permute-start(bf16[1024,2048]{1,0:T(8,128)(2,1)} %shard_map.236.act0_ref), channel_id=1, source_target_pairs={{0,1},{1,0},{2,3},{3,2},{4,5},{5,4},{6,7},{7,6},{8,9},{9,8},{10,11... | collective-permute-start | bytes 12582920 | tf_op jit(solution)/shard_map/ppermute | solution.py:59
  246.3 25.6 %collective-permute-start.16 = (bf16[256,2048]{1,0:T(8,128)(2,1)S(1)}, bf16[256,2048]{1,0:T(8,128)(2,1)S(1)}, u32[]{:S(2)}, u32[]{:S(2)}) collective-permute-start(bf16[256,2048]{1,0:T(8,128)(2,1)S(1)} %copy-done.18), channel_id=1, source_target_pairs={{0,4},{4,0},{1,5},{5,1},{2,6},{6,2},{3,7},{7,3},{8,12},{12,8},{9,1... | collective-permute-start | bytes 3145736 | tf_op jit(solution)/shard_map/ppermute | solution.py:59
  246.6 27.0 %collective-permute-start.15 = (bf16[256,2048]{1,0:T(8,128)(2,1)S(1)}, bf16[256,2048]{1,0:T(8,128)(2,1)S(1)}, u32[]{:S(2)}, u32[]{:S(2)}) collective-permute-start(bf16[256,2048]{1,0:T(8,128)(2,1)S(1)} %copy-done.18), channel_id=1, source_target_pairs={{0,2},{2,0},{1,3},{3,1},{4,6},{6,4},{5,7},{7,5},{8,10},{10,8},{9,1... | collective-permute-start | bytes 3145736 | tf_op jit(solution)/shard_map/ppermute | solution.py:59
  271.9 22.6 %copy-start.10 = (bf16[256,2048]{1,0:T(8,128)(2,1)}, bf16[256,2048]{1,0:T(8,128)(2,1)S(1)}, u32[]{:S(2)}) copy-start(bf16[256,2048]{1,0:T(8,128)(2,1)S(1)} %collective-permute-done.16.refs_2_) | copy-start | bytes 3145732
  272.7 21.8 %collective-permute-start.17 = (bf16[128,2048]{1,0:T(8,128)(2,1)}, bf16[128,2048]{1,0:T(8,128)(2,1)}, u32[]{:S(2)}, u32[]{:S(2)}) collective-permute-start(bf16[128,2048]{1,0:T(8,128)(2,1)} %slice.175), channel_id=1, source_target_pairs={{0,2},{2,0},{1,3},{3,1},{4,6},{6,4},{5,7},{7,5},{8,10},{10,8},{9,1... | collective-permute-start | bytes 1572872 | tf_op jit(solution)/shard_map/ppermute | solution.py:59
  273.7 20.8 %copy-start.11 = (bf16[256,2048]{1,0:T(8,128)(2,1)}, bf16[256,2048]{1,0:T(8,128)(2,1)S(1)}, u32[]{:S(2)}) copy-start(bf16[256,2048]{1,0:T(8,128)(2,1)S(1)} %collective-permute-done.15.refs_1_) | copy-start | bytes 3145732
  273.7 20.8 %collective-permute-start.18 = (bf16[128,2048]{1,0:T(8,128)(2,1)S(1)}, bf16[128,2048]{1,0:T(8,128)(2,1)S(1)}, u32[]{:S(2)}, u32[]{:S(2)}) collective-permute-start(bf16[128,2048]{1,0:T(8,128)(2,1)S(1)} %slice.176), channel_id=1, source_target_pairs={{0,4},{4,0},{1,5},{5,1},{2,6},{6,2},{3,7},{7,3},{8,12},{12,8},{9,1... | collective-permute-start | bytes 1572872 | tf_op jit(solution)/shard_map/ppermute | solution.py:59
  300.1 7.6 %collective-permute-start.19 = (bf16[1024,2048]{1,0:T(8,128)(2,1)}, bf16[1024,2048]{1,0:T(8,128)(2,1)S(1)}, u32[]{:S(2)}, u32[]{:S(2)}) collective-permute-start(bf16[1024,2048]{1,0:T(8,128)(2,1)} %shard_map.238.refs_0_.grad0_ref), channel_id=1, source_target_pairs={{0,1},{1,0},{2,3},{3,2},{4,5},{5,4},{6,7},{7,6},{8,9},{9,8},{10,11... | collective-permute-start | bytes 12582920 | tf_op jit(solution)/shard_map/ppermute | solution.py:59
  307.2 13.3 %collective-permute-start.20 = (bf16[1024,2048]{1,0:T(8,128)(2,1)}, bf16[1024,2048]{1,0:T(8,128)(2,1)}, u32[]{:S(2)}, u32[]{:S(2)}) collective-permute-start(bf16[1024,2048]{1,0:T(8,128)(2,1)} %shard_map.240), channel_id=1, source_target_pairs={{0,1},{1,0},{2,3},{3,2},{4,5},{5,4},{6,7},{7,6},{8,9},{9,8},{10,11... | collective-permute-start | bytes 12582920 | tf_op jit(solution)/shard_map/ppermute | solution.py:59
  332.0 18.5 %collective-permute-start.22 = (bf16[128,2048]{1,0:T(8,128)(2,1)S(1)}, bf16[128,2048]{1,0:T(8,128)(2,1)}, u32[]{:S(2)}, u32[]{:S(2)}) collective-permute-start(bf16[128,2048]{1,0:T(8,128)(2,1)S(1)} %get-tuple-element.197), channel_id=1, source_target_pairs={{0,2},{2,0},{1,3},{3,1},{4,6},{6,4},{5,7},{7,5},{8,10},{10,8},{9,1... | collective-permute-start | bytes 1572872 | tf_op jit(solution)/shard_map/ppermute | solution.py:59
  333.2 202.7 %reduce-scatter.7.cloned.1.call-start = ((), (), s32[]{:S(2)}) async-start(), calls=%async_computation.17 | async-start | bytes 7208960 | tf_op jit(solution)/shard_map/reduce_scatter | solution.py:854
  335.0 17.8 %collective-permute-start.21 = (bf16[128,2048]{1,0:T(8,128)(2,1)S(1)}, bf16[128,2048]{1,0:T(8,128)(2,1)S(1)}, u32[]{:S(2)}, u32[]{:S(2)}) collective-permute-start(bf16[128,2048]{1,0:T(8,128)(2,1)S(1)} %get-tuple-element.198), channel_id=1, source_target_pairs={{0,4},{4,0},{1,5},{5,1},{2,6},{6,2},{3,7},{7,3},{8,12},{12,8},{9,1... | collective-permute-start | bytes 1572872 | tf_op jit(solution)/shard_map/ppermute | solution.py:59
  336.4 14.1 %copy-start.17 = (f32[256,2048]{1,0:T(8,128)S(1)}, f32[256,2048]{1,0:T(8,128)}, u32[]{:S(2)}) copy-start(f32[256,2048]{1,0:T(8,128)} %get-tuple-element.127) | copy-start | bytes 6291460
  365.4 7.4 %collective-permute-start.25 = (bf16[1024,2048]{1,0:T(8,128)(2,1)}, bf16[1024,2048]{1,0:T(8,128)(2,1)S(1)}, u32[]{:S(2)}, u32[]{:S(2)}) collective-permute-start(bf16[1024,2048]{1,0:T(8,128)(2,1)} %shard_map.243), channel_id=1, source_target_pairs={{0,1},{1,0},{2,3},{3,2},{4,5},{5,4},{6,7},{7,6},{8,9},{9,8},{10,11... | collective-permute-start | bytes 12582920 | tf_op jit(solution)/shard_map/ppermute | solution.py:59
  365.4 46.5 %collective-permute-start.23 = (bf16[256,2048]{1,0:T(8,128)(2,1)}, bf16[256,2048]{1,0:T(8,128)(2,1)S(1)}, u32[]{:S(2)}, u32[]{:S(2)}) collective-permute-start(bf16[256,2048]{1,0:T(8,128)(2,1)} %pad_maximum_fusion), channel_id=1, source_target_pairs={{0,2},{2,0},{1,3},{3,1},{4,6},{6,4},{5,7},{7,5},{8,10},{10,8},{9,1... | collective-permute-start | bytes 3145736 | tf_op jit(solution)/shard_map/ppermute | solution.py:59
  366.1 45.8 %collective-permute-start.24 = (bf16[256,2048]{1,0:T(8,128)(2,1)}, bf16[256,2048]{1,0:T(8,128)(2,1)}, u32[]{:S(2)}, u32[]{:S(2)}) collective-permute-start(bf16[256,2048]{1,0:T(8,128)(2,1)} %pad_maximum_fusion.1), channel_id=1, source_target_pairs={{0,4},{4,0},{1,5},{5,1},{2,6},{6,2},{3,7},{7,3},{8,12},{12,8},{9,1... | collective-permute-start | bytes 3145736 | tf_op jit(solution)/shard_map/ppermute | solution.py:59
  388.0 28.8 %collective-permute-start.26 = (bf16[256,2048]{1,0:T(8,128)(2,1)}, bf16[256,2048]{1,0:T(8,128)(2,1)}, u32[]{:S(2)}, u32[]{:S(2)}) collective-permute-start(bf16[256,2048]{1,0:T(8,128)(2,1)} %get-tuple-element.143), channel_id=1, source_target_pairs={{0,2},{2,0},{1,3},{3,1},{4,6},{6,4},{5,7},{7,5},{8,10},{10,8},{9,1... | collective-permute-start | bytes 3145736 | tf_op jit(solution)/shard_map/ppermute | solution.py:59
  388.8 47.9 %collective-permute-start.27 = (bf16[256,2048]{1,0:T(8,128)(2,1)}, bf16[256,2048]{1,0:T(8,128)(2,1)}, u32[]{:S(2)}, u32[]{:S(2)}) collective-permute-start(bf16[256,2048]{1,0:T(8,128)(2,1)} %get-tuple-element.144), channel_id=1, source_target_pairs={{0,4},{4,0},{1,5},{5,1},{2,6},{6,2},{3,7},{7,3},{8,12},{12,8},{9,1... | collective-permute-start | bytes 3145736 | tf_op jit(solution)/shard_map/ppermute | solution.py:59
  389.2 47.5 %collective-permute-start.28 = (bf16[256,2048]{1,0:T(8,128)(2,1)}, bf16[256,2048]{1,0:T(8,128)(2,1)}, u32[]{:S(2)}, u32[]{:S(2)}) collective-permute-start(bf16[256,2048]{1,0:T(8,128)(2,1)} %get-tuple-element.137), channel_id=1, source_target_pairs={{0,6},{2,4},{4,2},{6,0},{1,7},{3,5},{5,3},{7,1},{8,14},{10,12},{12... | collective-permute-start | bytes 3145736 | tf_op jit(solution)/shard_map/ppermute | solution.py:164
  436.6 18.9 %all-to-all-start.4 = ((bf16[8,64,704]{2,1,0:T(8,128)(2,1)}), bf16[8,64,704]{2,1,0:T(8,128)(2,1)S(1)}, u32[]{:S(2)}, u32[]{:S(2)}) async-start(bf16[8,64,704]{2,1,0:T(8,128)(2,1)} %bitcast.56), calls=%async_computation.5 | async-start | bytes 1572864 | tf_op jit(solution)/shard_map/all_to_all | solution.py:238
  440.2 142.6 %reduce-scatter.9.cloned.1.call-start = ((), (), s32[]{:S(2)}) async-start(), calls=%async_computation.18 | async-start | bytes 3932160 | tf_op jit(solution)/shard_map/reduce_scatter | solution.py:854
  455.5 19.8 %copy-start.29 = (bf16[256,2048]{1,0:T(8,128)(2,1)S(1)}, bf16[256,2048]{1,0:T(8,128)(2,1)}, u32[]{:S(2)}) copy-start(bf16[256,2048]{1,0:T(8,128)(2,1)} %get-tuple-element.161.refs_0_) | copy-start | bytes 3145732
  475.3 26.3 %collective-permute-start.30 = (bf16[256,2048]{1,0:T(8,128)(2,1)S(1)}, bf16[256,2048]{1,0:T(8,128)(2,1)S(1)}, u32[]{:S(2)}, u32[]{:S(2)}) collective-permute-start(bf16[256,2048]{1,0:T(8,128)(2,1)S(1)} %copy-done.29), channel_id=1, source_target_pairs={{0,4},{4,0},{1,5},{5,1},{2,6},{6,2},{3,7},{7,3},{8,12},{12,8},{9,1... | collective-permute-start | bytes 3145736 | tf_op jit(solution)/shard_map/ppermute | solution.py:59
  475.9 25.7 %collective-permute-start.29 = (bf16[256,2048]{1,0:T(8,128)(2,1)S(1)}, bf16[256,2048]{1,0:T(8,128)(2,1)S(1)}, u32[]{:S(2)}, u32[]{:S(2)}) collective-permute-start(bf16[256,2048]{1,0:T(8,128)(2,1)S(1)} %copy-done.29), channel_id=1, source_target_pairs={{0,2},{2,0},{1,3},{3,1},{4,6},{6,4},{5,7},{7,5},{8,10},{10,8},{9,1... | collective-permute-start | bytes 3145736 | tf_op jit(solution)/shard_map/ppermute | solution.py:59
  501.6 14.1 %copy-start.25 = (bf16[256,2048]{1,0:T(8,128)(2,1)}, bf16[256,2048]{1,0:T(8,128)(2,1)S(1)}, u32[]{:S(2)}) copy-start(bf16[256,2048]{1,0:T(8,128)(2,1)S(1)} %collective-permute-done.30.refs_2_) | copy-start | bytes 3145732
  501.7 14.0 %collective-permute-start.32 = (bf16[128,2048]{1,0:T(8,128)(2,1)S(1)}, bf16[128,2048]{1,0:T(8,128)(2,1)S(1)}, u32[]{:S(2)}, u32[]{:S(2)}) collective-permute-start(bf16[128,2048]{1,0:T(8,128)(2,1)S(1)} %slice.148), channel_id=1, source_target_pairs={{0,4},{4,0},{1,5},{5,1},{2,6},{6,2},{3,7},{7,3},{8,12},{12,8},{9,1... | collective-permute-start | bytes 1572872 | tf_op jit(solution)/shard_map/ppermute | solution.py:59
  503.2 13.0 %collective-permute-start.31 = (bf16[128,2048]{1,0:T(8,128)(2,1)S(1)}, bf16[128,2048]{1,0:T(8,128)(2,1)}, u32[]{:S(2)}, u32[]{:S(2)}) collective-permute-start(bf16[128,2048]{1,0:T(8,128)(2,1)S(1)} %slice.147), channel_id=1, source_target_pairs={{0,2},{2,0},{1,3},{3,1},{4,6},{6,4},{5,7},{7,5},{8,10},{10,8},{9,1... | collective-permute-start | bytes 1572872 | tf_op jit(solution)/shard_map/ppermute | solution.py:59
  523.5 7.5 %collective-permute-start.33 = (bf16[1024,2048]{1,0:T(8,128)(2,1)}, bf16[1024,2048]{1,0:T(8,128)(2,1)}, u32[]{:S(2)}, u32[]{:S(2)}) collective-permute-start(bf16[1024,2048]{1,0:T(8,128)(2,1)} %shard_map.249), channel_id=1, source_target_pairs={{0,1},{1,0},{2,3},{3,2},{4,5},{5,4},{6,7},{7,6},{8,9},{9,8},{10,11... | collective-permute-start | bytes 12582920 | tf_op jit(solution)/shard_map/ppermute | solution.py:59
  535.8 17.5 %collective-permute-start.37 = (bf16[1024,2048]{1,0:T(8,128)(2,1)}, bf16[1024,2048]{1,0:T(8,128)(2,1)}, u32[]{:S(2)}, u32[]{:S(2)}) collective-permute-start(bf16[1024,2048]{1,0:T(8,128)(2,1)} %shard_map.250.right0_ref), channel_id=1, source_target_pairs={{0,1},{1,0},{2,3},{3,2},{4,5},{5,4},{6,7},{7,6},{8,9},{9,8},{10,11... | collective-permute-start | bytes 12582920 | tf_op jit(solution)/shard_map/ppermute | solution.py:59
  535.9 24.0 %all-to-all-start.6 = ((bf16[8,64,1408]{2,1,0:T(8,128)(2,1)}), bf16[8,64,1408]{2,1,0:T(8,128)(2,1)S(1)}, u32[]{:S(2)}, u32[]{:S(2)}) async-start(bf16[8,64,1408]{2,1,0:T(8,128)(2,1)} %bitcast.54), calls=%async_computation.8 | async-start | bytes 2883584 | tf_op jit(solution)/shard_map/all_to_all | solution.py:238
  549.8 40.5 %collective-permute-start.34 = (bf16[256,2048]{1,0:T(8,128)(2,1)}, bf16[256,2048]{1,0:T(8,128)(2,1)}, u32[]{:S(2)}, u32[]{:S(2)}) collective-permute-start(bf16[256,2048]{1,0:T(8,128)(2,1)} %get-tuple-element.168), channel_id=1, source_target_pairs={{0,2},{2,0},{1,3},{3,1},{4,6},{6,4},{5,7},{7,5},{8,10},{10,8},{9,1... | collective-permute-start | bytes 3145736 | tf_op jit(solution)/shard_map/ppermute | solution.py:59
  551.8 38.6 %collective-permute-start.35 = (bf16[256,2048]{1,0:T(8,128)(2,1)}, bf16[256,2048]{1,0:T(8,128)(2,1)}, u32[]{:S(2)}, u32[]{:S(2)}) collective-permute-start(bf16[256,2048]{1,0:T(8,128)(2,1)} %get-tuple-element.169), channel_id=1, source_target_pairs={{0,4},{4,0},{1,5},{5,1},{2,6},{6,2},{3,7},{7,3},{8,12},{12,8},{9,1... | collective-permute-start | bytes 3145736 | tf_op jit(solution)/shard_map/ppermute | solution.py:59
  553.2 51.8 %collective-permute-start.36 = (bf16[256,2048]{1,0:T(8,128)(2,1)}, bf16[256,2048]{1,0:T(8,128)(2,1)}, u32[]{:S(2)}, u32[]{:S(2)}) collective-permute-start(bf16[256,2048]{1,0:T(8,128)(2,1)} %get-tuple-element.170), channel_id=1, source_target_pairs={{0,6},{2,4},{4,2},{6,0},{1,7},{3,5},{5,3},{7,1},{8,14},{10,12},{12... | collective-permute-start | bytes 3145736 | tf_op jit(solution)/shard_map/ppermute | solution.py:164
  567.1 20.4 %copy-start.27 = (f32[1,32,64]{2,0,1:T(1,128)S(1)}, f32[1,32,64]{2,0,1:T(1,128)}, u32[]{:S(2)}) copy-start(f32[1,32,64]{2,0,1:T(1,128)} %get-tuple-element.199) | copy-start | bytes 24580
  567.1 20.5 %copy-start.28 = (f32[2,2048]{1,0:T(2,128)S(1)}, f32[2,2048]{1,0:T(2,128)}, u32[]{:S(2)}) copy-start(f32[2,2048]{1,0:T(2,128)} %get-tuple-element.184) | copy-start | bytes 49156
  582.8 30.3 %all-to-all-start.7 = ((bf16[8,64,768]{2,1,0:T(8,128)(2,1)}), bf16[8,64,768]{2,1,0:T(8,128)(2,1)}, u32[]{:S(2)}, u32[]{:S(2)}) async-start(bf16[8,64,768]{2,1,0:T(8,128)(2,1)} %bitcast.57), calls=%async_computation.10 | async-start | bytes 1572864 | tf_op jit(solution)/shard_map/all_to_all | solution.py:238
  587.0 42.8 %reduce-scatter.11.cloned.1.call-start = ((), (), s32[]{:S(2)}) async-start(), calls=%async_computation.19 | async-start | bytes 1310720 | tf_op jit(solution)/shard_map/reduce_scatter | solution.py:854
  617.9 10.6 %all-to-all-start.8 = ((f32[32,1,448]{2,1,0:T(1,128)}), f32[32,1,448]{2,1,0:T(1,128)S(1)}, u32[]{:S(2)}, u32[]{:S(2)}) async-start(f32[32,1,448]{2,1,0:T(1,128)} %all_to_all.44), calls=%async_computation.11 | async-start | bytes 131072 | tf_op jit(solution)/shard_map/all_to_all | solution.py:916
  (19 other events, 61.7 us)
Sparse Core Ops, SparseCore 0:
  9.6 32.4 all-gather.5
  43.8 62.3 all-gather.3
  117.0 157.0 all-gather.7
  333.3 60.2 reduce-scatter.4
  412.0 102.2 reduce-scatter.6
  523.6 59.0 reduce-scatter.8
  590.1 27.6 reduce-scatter.10

commit v5 on v4

--- a/solution.py
+++ b/solution.py
@@ -435,9 +435,8 @@
     return jnp.where(pl.program_id(0) < steps // 2, halves[0][...], halves[1][...])
 
 
-def project_kernel(place, act0_ref, act1_ref, weight_ref, bias_ref, cos_ref, sin_ref, out_ref, act_ref):
+def project_kernel(place, act0_ref, act1_ref, weight_ref, bias_ref, cos_ref, sin_ref, out_ref):
     act = pick((act0_ref, act1_ref), 8)
-    act_ref[...] = act
     projected = nn(act, weight_ref[...]) + bias_ref[...]
     rows, width = projected.shape
     first = lanes_of(rows) % HEAD_DIM < ROT_DIMS // 2
@@ -473,14 +472,9 @@
                 pl.BlockSpec((1, rows, PAIR), table),
                 pl.BlockSpec((1, rows, PAIR), table),
             ],
-            out_specs=[
-                pl.BlockSpec((1, rows, width), lambda s, place: (s // 2 % 2, block_of(s, place), 0)),
-                pl.BlockSpec((rows, depth), lambda s, place: (s, 0)),
-            ],
+            out_specs=pl.BlockSpec((1, rows, width), lambda s, place: (s // 2 % 2, block_of(s, place), 0)),
         ),
-        out_shape=[
-            jax.ShapeDtypeStruct((packs, seq, width), bf16), jax.ShapeDtypeStruct((2 * count, depth), bf16)
-        ],
+        out_shape=jax.ShapeDtypeStruct((packs, seq, width), bf16),
         **limits(15),
     )(place, *act, weight, bias, cosine, sine)
 
@@ -595,9 +589,8 @@
 STEPS = 4
 
 
-def gate_kernel(act0_ref, act1_ref, weight_ref, middle_ref, by_gate_ref, by_up_ref, act_ref):
+def gate_kernel(act0_ref, act1_ref, weight_ref, middle_ref, by_gate_ref, by_up_ref):
     act = pick((act0_ref, act1_ref), STEPS)
-    act_ref[...] = act
     both = nn(act, weight_ref[...])
     half, wide = both.shape[1] // 2, middle_ref.shape[1]
     inside = lax.broadcasted_iota(jnp.int32, (both.shape[0], wide), 1) < half
@@ -619,8 +612,8 @@
         gate_kernel,
         grid=(STEPS,),
         in_specs=[*half_specs(rows, depth, STEPS), pl.BlockSpec((depth, 2 * half), lambda s: (0, 0))],
-        out_specs=[out] * 3 + [pl.BlockSpec((rows, depth), lambda s: (s, 0))],
-        out_shape=[jax.ShapeDtypeStruct((count, wide), bf16)] * 3 + [jax.ShapeDtypeStruct((count, depth), bf16)],
+        out_specs=[out] * 3,
+        out_shape=[jax.ShapeDtypeStruct((count, wide), bf16)] * 3,
         **limits(20),
     )(*act, weight)
 
@@ -834,7 +827,7 @@
     ffn_full = over_g(ffn_mine)
     qkv_full = after(qkv_full, act_one[0], ffn_mine)
 
-    qkv, act_one = project(place, act_one, qkv_full, bias_mine, cosine, sine)
+    qkv = project(place, act_one, qkv_full, bias_mine, cosine, sine)
     mixed, mixed_halves, totals = attention(place, qkv, blocks, seg_col, seg_row)
     if aligned:
         out_full = halves_of(chip_pieces(out_rows, qkv), mixed)
@@ -844,7 +837,7 @@
 
     act_two = halves_of(chip_pieces(act_two))
     cotangent = chip_pieces(after(out_grad, act_two[0]))
-    middle_low, by_gate, by_up, act_all = gate_rows(act_two, ffn_full, my_ffn)
+    middle_low, by_gate, by_up = gate_rows(act_two, ffn_full, my_ffn)
     cotangent = halves_of(cotangent, middle_low)
     output_other = swap(plane_send(middle_low, ffn_full, 2 * my_ffn), "c")
     down_sum = row_sum(cotangent, middle_low, kept=my_ffn)
@@ -861,7 +854,7 @@
     output_terms = after(plane_corner(output_kept), gate_up_grad)
     norm_two_other = swap(plane_send(after(gate_up_grad, output_terms[0]), ffn_full, 0), "c")
     norm_two_kept = plane_keep(gate_up_grad, ffn_full, 0, norm_two_other, bf16)
-    gate_up_sum = row_sum([act_all], after(gate_up_grad, norm_two_kept[0], down_own), time=60)
+    gate_up_sum = row_sum(act_two, after(gate_up_grad, norm_two_kept[0], down_own), time=60)
     output = (hidden + total_of(after(plane_neighbours(output_terms), gate_up_sum))).astype(bf16)
     gate_up_own = own_rows(gate_up_sum)
     norm_two_terms = after(plane_direct(norm_two_kept), output)
@@ -874,7 +867,7 @@
     qkv_grad = attention_back(place, qkv, mixed_grad, totals, cosine, sine, seg_col, seg_row, time=130)
     qkv_grad = qkv_grad.reshape(8 * rows, 3 * my_width)
     hidden_pieces = chip_pieces(after(hidden_low, mixed_grad), qkv_grad)
-    qkv_sum = row_sum([act_one], after(qkv_grad, hidden_pieces[1]), time=130)
+    qkv_sum = row_sum(act_one, after(qkv_grad, hidden_pieces[1]), time=130)
     qkv_own = own_rows(qkv_sum)
     norm_one_sent = plane_send(after(qkv_grad, qkv_sum, hidden_pieces), qkv_full, 0, time=60)
     norm_one_other = swap(norm_one_sent, "c")

time: 644 us -> 644 us (level)
  no operation moved by 1% of the time
where the time goes in v5:
time: 644 us; the launch traced here: 639 us
  Pallas kernels  264 us (41%)
  waiting for transfers between devices  199 us (31%)
  starting transfers between devices  62.7 us (10%)
  blocking collectives  36.5 us (6%)
  other arithmetic  31.9 us (5%)
  local copies, waits for them, and re-layouts  29.6 us (5%)
  between operations  15 us (2%)
    ppermute x36, waiting for transfers between devices, swap(): return lax.ppermute(values, axis, [(0, 1), (1, 0)])  129 us
    pallas_call x3, Pallas kernels, row_sum(): pl.pallas_call(sum_kernel, grid=(width // step,), in_specs=[*[pl.BlockSpe...  40 us
    all_to_all x2, blocking collectives, plane_all_to_all(): return lax.all_to_all(blocks, PLANE, 0, 0, tiled=True)  36.5 us
    pallas_call x3, Pallas kernels, plane_keep(): pl.pallas_call(keep_kernel, grid=(4,), in_specs=[pl.BlockSpec((rows, dept...  33.1 us
    all_to_all x5, waiting for transfers between devices, plane_all_to_all(): return lax.all_to_all(blocks, PLANE, 0, 0, tiled=True)  29.8 us
    ppermute x36, starting transfers between devices, swap(): return lax.ppermute(values, axis, [(0, 1), (1, 0)])  29.7 us
    pallas_call x3, Pallas kernels, plane_send(): pl.pallas_call(send_kernel, grid=(2,), in_specs=[pl.BlockSpec((2 * rows,...  25.7 us
    pallas_call x1, Pallas kernels, attention_back(): pl.pallas_call(functools.partial(attend_back_kernel, blocks), grid_spec=p...  25.2 us
  transfers between devices with their start and end apart: 52, of which 22 were waited for; matrix products, arithmetic and copies ran while one was open for 7% of the time, Pallas kernels for 39%

profile of v5, /device:TPU:0, one launch (start us, length us, event | category | flops | bytes accessed | tf_op | source)
XLA Modules:
  0.0 638.5 jit_solution(12094740454590331872)
XLA Ops:
  10.9 7.3 %all-to-all-start = ((f32[32,1,960]{2,1,0:T(1,128)}), f32[32,1,960]{2,1,0:T(1,128)S(1)}, u32[]{:S(2)}, u32[]{:S(2)}) async-start(f32[32,1,960]{2,1,0:T(1,128)} %broadcast_in_dim.14), calls=%async_computation | async-start | bytes 262144 | tf_op jit(solution)/shard_map/all_to_all | solution.py:783
  18.3 2.5 shard_map.230
  20.8 6.1 all-to-all-done
  26.9 16.8 %all_to_all.54 = bf16[8,64,768]{2,1,0:T(8,128)(2,1)} all-to-all(bf16[8,64,768]{2,1,0:T(8,128)(2,1)} %shard_map.230), channel_id=1, replica_groups=mesh['g'=4,'y'=2,'x'=2,'c'=2] {'y','x','c'}, dimensions={0} | all-to-all | bytes 1572864 | tf_op jit(solution)/shard_map/all_to_all | solution.py:238
  44.9 23.1 %collective-permute-done.1.refs_2_ = bf16[256,2048]{1,0:T(8,128)(2,1)S(1)} collective-permute-done((bf16[256,2048]{1,0:T(8,128)(2,1)S(1)}, bf16[256,2048]{1,0:T(8,128)(2,1)S(1)}, u32[]{:S(2)}, u32[]{:S(2)}) %collective-permute-start.1) | collective-permute-done | bytes 1048608 | tf_op jit(solution)/shard_map/ppermute | solution.py:59
  71.0 3.7 shard_map.231
  76.7 5.1 collective-permute-done.2.refs_3_
  83.9 3.6 all-to-all-start.2
  87.8 7.2 %shard_map.229.act0_ref.refs_0_ = bf16[1024,2048]{1,0:T(8,128)(2,1)} custom-call(bf16[256,2048]{1,0:T(8,128)(2,1)} %token_ref.1, bf16[256,2048]{1,0:T(8,128)(2,1)} %copy-done.9, bf16[256,2048]{1,0:T(8,128)(2,1)} %copy-done.8, bf16[128,2048]{1,0:T(8,128)(2,1)} %collective-permute-done.2.refs_3_, bf16[128,2048]{1,0:T(8,128)(2,1)} %copy-done.19, ...), custom_call_target="tpu_custom_call" | custom-call | flops 1166666624 | bytes 3500000 | tf_op jit(solution)/shard_map/pallas_call | solution.py:427
  96.0 5.2 compare_select_fusion.9
  101.3 5.5 fusion.12
  106.8 8.6 %all-to-all-done.2 = bf16[8,64,2176]{2,1,0:T(8,128)(2,1)S(1)} async-done(((bf16[8,64,2176]{2,1,0:T(8,128)(2,1)}), bf16[8,64,2176]{2,1,0:T(8,128)(2,1)S(1)}, u32[]{:S(2)}, u32[]{:S(2)}) %all-to-all-start.2) | async-done | bytes 2228256 | tf_op jit(solution)/shard_map/all_to_all | solution.py:238
  119.4 14.7 %shard_map.232.query_ref.key_ref.value_ref = bf16[2,1024,768]{2,1,0:T(8,128)(2,1)} custom-call(s32[4]{0:T(128)} %pad_add_fusion.place, bf16[1024,2048]{1,0:T(8,128)(2,1)} %shard_map.229.act0_ref.refs_0_, bf16[1024,2048]{1,0:T(8,128)(2,1)} %collective-permute-done.4.act1_ref.refs_1_, bf16[2048,768]{1,0:T(8,128)(2,1)} %all-gather.4.cloned.1.call-done.weight_ref.right_ref, ...), custom_call_target="tpu_custom_call" | custom-call | flops 2500000000 | bytes 7500000 | tf_op jit(solution)/shard_map/pallas_call | solution.py:463
  134.1 5.1 collective-permute-done.6.refs_2_
  139.2 1.9 collective-permute-done.5.refs_1_
  148.1 15.8 %shard_map.233 = (bf16[2,4,256,256]{3,2,1,0:T(8,128)(2,1)}, bf16[2,2,2,256,256]{4,3,2,1,0:T(8,128)(2,1)}, f32[2,2,2,1024]{3,2,1,0:T(2,128)}) custom-call(s32[4]{0:T(128)} %pad_add_fusion.place, bf16[2,1024,768]{2,1,0:T(8,128)(2,1)} %shard_map.232.query_ref.key_ref.value_ref, bf16[2,1024,768]{2,1,0:T(8,128)(2,1)} %shard_map.232.query_ref.key_ref.value_ref, ...), custom_call_target="tpu_custom_call" | custom-call | flops 2666666752 | bytes 8000000 | tf_op jit(solution)/shard_map/pallas_call | solution.py:368
  164.9 4.8 shard_map.234.w0_ref
  169.7 3.6 all-to-all-start.3
  175.2 13.4 %all-to-all-done.3.mixed_ref = bf16[8,256,256]{2,1,0:T(8,128)(2,1)S(1)} async-done(((bf16[8,256,256]{2,1,0:T(8,128)(2,1)}), bf16[8,256,256]{2,1,0:T(8,128)(2,1)S(1)}, u32[]{:S(2)}, u32[]{:S(2)}) %all-to-all-start.3) | async-done | bytes 1048608 | tf_op jit(solution)/shard_map/all_to_all | solution.py:238
  189.5 11.9 %shard_map.235 = (f32[256,2048]{1,0:T(8,128)}, bf16[256,2048]{1,0:T(8,128)(2,1)}) custom-call(s32[4]{0:T(128)} %pad_add_fusion.place, bf16[8,256,256]{2,1,0:T(8,128)(2,1)} %copy-done.5, bf16[1024,2048]{1,0:T(8,128)(2,1)} %shard_map.234.w0_ref, bf16[1024,2048]{1,0:T(8,128)(2,1)} %collective-permute-done.9.w1_ref, bf16[256,2048]{1,0:T(8,128)(2,1)} %token_ref.1, ...), custom_call_target="tpu_custom_call" | custom-call | flops 2000000000 | bytes 6000000 | tf_op jit(solution)/shard_map/pallas_call | solution.py:521
  202.5 21.1 %collective-permute-done.11.refs_2_ = bf16[256,2048]{1,0:T(8,128)(2,1)S(1)} collective-permute-done((bf16[256,2048]{1,0:T(8,128)(2,1)}, bf16[256,2048]{1,0:T(8,128)(2,1)S(1)}, u32[]{:S(2)}, u32[]{:S(2)}) %collective-permute-start.11) | collective-permute-done | bytes 1048608 | tf_op jit(solution)/shard_map/ppermute | solution.py:59
  223.7 3.7 collective-permute-start.12
  227.9 11.1 %collective-permute-done.12.refs_3_ = bf16[128,2048]{1,0:T(8,128)(2,1)S(1)} collective-permute-done((bf16[128,2048]{1,0:T(8,128)(2,1)S(1)}, bf16[128,2048]{1,0:T(8,128)(2,1)S(1)}, u32[]{:S(2)}, u32[]{:S(2)}) %collective-permute-start.12) | collective-permute-done | bytes 524320 | tf_op jit(solution)/shard_map/ppermute | solution.py:59
  241.4 4.8 shard_map.236.act0_ref.refs_0_
  247.8 23.9 %collective-permute-done.16.refs_2_ = bf16[256,2048]{1,0:T(8,128)(2,1)S(1)} collective-permute-done((bf16[256,2048]{1,0:T(8,128)(2,1)S(1)}, bf16[256,2048]{1,0:T(8,128)(2,1)S(1)}, u32[]{:S(2)}, u32[]{:S(2)}) %collective-permute-start.16) | collective-permute-done | bytes 1048608 | tf_op jit(solution)/shard_map/ppermute | solution.py:59
  274.4 20.1 %shard_map.237 = (bf16[2048,768]{1,0:T(8,128)(2,1)}, bf16[2048,768]{1,0:T(8,128)(2,1)}, bf16[2048,768]{1,0:T(8,128)(2,1)}) custom-call(bf16[1024,2048]{1,0:T(8,128)(2,1)} %shard_map.236.act0_ref.refs_0_, bf16[1024,2048]{1,0:T(8,128)(2,1)} %collective-permute-done.14.act1_ref.refs_1_, bf16[2048,2176]{1,0:T(8,128)(2,1)} %all-gather.8.cloned.1.call-done.weight_ref.right_ref), custom_call_target="tpu_custom_call" | custom-call | flops 3333333248 | bytes 10000000 | tf_op jit(solution)/shard_map/pallas_call | solution.py:611
  295.3 4.7 shard_map.238.refs_0_.grad0_ref
  300.0 7.1 %shard_map.240 = bf16[1024,2048]{1,0:T(8,128)(2,1)} custom-call(bf16[2048,768]{1,0:T(8,128)(2,1)} %get-tuple-element.119.refs_2_.left_ref, bf16[2048,2176]{1,0:T(8,128)(2,1)} %all-gather.8.cloned.1.call-done.weight_ref.right_ref), custom_call_target="tpu_custom_call" | custom-call | flops 833333312 | bytes 2500000 | tf_op jit(solution)/shard_map/pallas_call | solution.py:132
  307.7 2.0 copy-done.2
  309.7 10.8 %shard_map.239 = bf16[2048,704]{1,0:T(8,128)(2,1)} custom-call(bf16[1024,2048]{1,0:T(8,128)(2,1)} %shard_map.238.refs_0_.grad0_ref, bf16[1024,2048]{1,0:T(8,128)(2,1)} %copy-done.2, bf16[2048,768]{1,0:T(8,128)(2,1)} %get-tuple-element.119.refs_2_.left_ref), custom_call_target="tpu_custom_call" | custom-call | flops 1500000000 | bytes 4500000 | tf_op jit(solution)/shard_map/pallas_call | solution.py:201
  320.4 10.2 %shard_map.241 = (bf16[256,2048]{1,0:T(8,128)(2,1)}, f32[256,2048]{1,0:T(8,128)}, f32[256,2048]{1,0:T(8,128)}, f32[256,2048]{1,0:T(8,128)}) custom-call(bf16[2048,768]{1,0:T(8,128)(2,1)} %get-tuple-element.119.refs_2_.left_ref, bf16[2048,2176]{1,0:T(8,128)(2,1)} %all-gather.8.cloned.1.call-done.weight_ref.right_ref, ...), custom_call_target="tpu_custom_call" | custom-call | flops 1000000000 | bytes 3000000 | tf_op jit(solution)/shard_map/pallas_call | solution.py:148
  336.4 14.1 %shard_map.242.left_ref.refs_2_ = bf16[2048,1408]{1,0:T(8,128)(2,1)} custom-call(bf16[1024,2048]{1,0:T(8,128)(2,1)} %shard_map.238.refs_0_.grad0_ref, bf16[1024,2048]{1,0:T(8,128)(2,1)} %copy-done.2, bf16[2048,2176]{1,0:T(8,128)(2,1)} %all-gather.8.cloned.1.call-done.weight_ref.right_ref, bf16[2048,768]{1,0:T(8,128)(2,1)} %get-tuple-element.126.by_gate_ref, ...), custom_call_target="tpu_custom_call" | custom-call | flops 2166666752 | bytes 6500000 | tf_op jit(solution)/shard_map/pallas_call | solution.py:637
  353.9 11.4 %shard_map.243 = bf16[1024,2048]{1,0:T(8,128)(2,1)} custom-call(bf16[2048,1408]{1,0:T(8,128)(2,1)} %shard_map.242.left_ref.refs_2_, bf16[2048,2176]{1,0:T(8,128)(2,1)} %all-gather.8.cloned.1.call-done.weight_ref.right_ref), custom_call_target="tpu_custom_call" | custom-call | flops 1666666624 | bytes 5000000 | tf_op jit(solution)/shard_map/pallas_call | solution.py:132
  366.4 6.4 collective-permute-done.25.other_ref
  372.7 2.0 copy-done.4
  374.7 13.3 %shard_map.244 = (bf16[256,2048]{1,0:T(8,128)(2,1)}, bf16[256,2048]{1,0:T(8,128)(2,1)}, bf16[256,2048]{1,0:T(8,128)(2,1)}, f32[256,2048]{1,0:T(8,128)}) custom-call(bf16[2048,1408]{1,0:T(8,128)(2,1)} %shard_map.242.left_ref.refs_2_, bf16[2048,2176]{1,0:T(8,128)(2,1)} %all-gather.8.cloned.1.call-done.weight_ref.right_ref, bf16[1024,2048]{1,0:T(8,128)(2,1)} %copy-done.4), custom_call_target="tpu_custom_call" | custom-call | flops 2000000000 | bytes 6000000 | tf_op jit(solution)/shard_map/pallas_call | solution.py:148
  389.1 2.3 collective-permute-start.28
  391.5 2.0 reduce-scatter.5.cloned.1.call-done
  393.5 18.3 %shard_map.245 = bf16[2048,1408]{1,0:T(8,128)(2,1)} custom-call(bf16[1024,2048]{1,0:T(8,128)(2,1)} %shard_map.236.act0_ref.refs_0_, bf16[1024,2048]{1,0:T(8,128)(2,1)} %collective-permute-done.14.act1_ref.refs_1_, bf16[2048,1408]{1,0:T(8,128)(2,1)} %shard_map.242.left_ref.refs_2_), custom_call_target="tpu_custom_call" | custom-call | flops 10000000000 | bytes 30000000 | tf_op jit(solution)/shard_map/pallas_call | solution.py:201
  413.3 3.4 add_convert_fusion
  416.7 20.0 %collective-permute-done.27.y_ref = bf16[256,2048]{1,0:T(8,128)(2,1)} collective-permute-done((bf16[256,2048]{1,0:T(8,128)(2,1)}, bf16[256,2048]{1,0:T(8,128)(2,1)}, u32[]{:S(2)}, u32[]{:S(2)}) %collective-permute-start.27) | collective-permute-done | bytes 1048608 | tf_op jit(solution)/shard_map/ppermute | solution.py:59
  436.7 3.5 all-to-all-start.4
  440.6 15.1 %shard_map.246 = (bf16[8,256,256]{2,1,0:T(8,128)(2,1)}, f32[256,2048]{1,0:T(8,128)}, bf16[256,2048]{1,0:T(8,128)(2,1)}, f32[2,2048]{1,0:T(2,128)}) custom-call(s32[4]{0:T(128)} %pad_add_fusion.place, f32[256,2048]{1,0:T(8,128)} %get-tuple-element.140.own_ref, bf16[256,2048]{1,0:T(8,128)(2,1)} %collective-permute-done.26.x_ref, ...), custom_call_target="tpu_custom_call" | custom-call | flops 21666666496 | bytes 65000000 | tf_op jit(solution)/shard_map/pallas_call | solution.py:568
  455.7 19.8 %all_to_all.55 = bf16[8,256,256]{2,1,0:T(8,128)(2,1)} all-to-all(bf16[8,256,256]{2,1,0:T(8,128)(2,1)} %get-tuple-element.147), channel_id=1, replica_groups=mesh['g'=4,'y'=2,'x'=2,'c'=2] {'y','x','c'}, dimensions={0} | all-to-all | bytes 2097152 | tf_op jit(solution)/shard_map/all_to_all | solution.py:238
  476.5 25.2 %shard_map.247 = bf16[2,2,2,256,768]{4,3,2,1,0:T(8,128)(2,1)} custom-call(s32[4]{0:T(128)} %pad_add_fusion.place, bf16[2,1024,768]{2,1,0:T(8,128)(2,1)} %shard_map.232.query_ref.key_ref.value_ref, bf16[2,1024,768]{2,1,0:T(8,128)(2,1)} %shard_map.232.query_ref.key_ref.value_ref, bf16[2,1024,768]{2,1,0:T(8,128)(2,1)} %shard_map.232.query_ref.key_ref.value_ref, ...), custom_call_target="tpu_custom_call" | custom-call | flops 21666666496 | bytes 65000000 | tf_op jit(solution)/shard_map/pallas_call | solution.py:394
  504.9 11.0 %shard_map.248 = bf16[2048,768]{1,0:T(8,128)(2,1)} custom-call(bf16[1024,2048]{1,0:T(8,128)(2,1)} %shard_map.229.act0_ref.refs_0_, bf16[1024,2048]{1,0:T(8,128)(2,1)} %collective-permute-done.4.act1_ref.refs_1_, bf16[2048,768]{1,0:T(8,128)(2,1)} %bitcast.49), custom_call_target="tpu_custom_call" | custom-call | flops 21666666496 | bytes 65000000 | tf_op jit(solution)/shard_map/pallas_call | solution.py:201
  516.4 7.2 %shard_map.249 = bf16[1024,2048]{1,0:T(8,128)(2,1)} custom-call(bf16[2048,768]{1,0:T(8,128)(2,1)} %bitcast.50, bf16[2048,768]{1,0:T(8,128)(2,1)} %all-gather.4.cloned.1.call-done.weight_ref.right_ref), custom_call_target="tpu_custom_call" | custom-call | flops 10000000000 | bytes 30000000 | tf_op jit(solution)/shard_map/pallas_call | solution.py:132
  523.6 7.5 %collective-permute-done.33.other_ref = bf16[1024,2048]{1,0:T(8,128)(2,1)} collective-permute-done((bf16[1024,2048]{1,0:T(8,128)(2,1)}, bf16[1024,2048]{1,0:T(8,128)(2,1)}, u32[]{:S(2)}, u32[]{:S(2)}) %collective-permute-start.33) | collective-permute-done | bytes 4194336 | tf_op jit(solution)/shard_map/ppermute | solution.py:59
  531.1 4.8 shard_map.250.right0_ref
  536.0 4.0 all-to-all-start.6
  540.3 9.6 %shard_map.251 = (bf16[256,2048]{1,0:T(8,128)(2,1)}, bf16[256,2048]{1,0:T(8,128)(2,1)}, bf16[256,2048]{1,0:T(8,128)(2,1)}, f32[256,2048]{1,0:T(8,128)}) custom-call(bf16[2048,768]{1,0:T(8,128)(2,1)} %bitcast.51, bf16[2048,768]{1,0:T(8,128)(2,1)} %all-gather.4.cloned.1.call-done.weight_ref.right_ref, bf16[1024,2048]{1,0:T(8,128)(2,1)} %collective-permute-done.33.other_ref), custom_call_target="tpu_custom_call" | custom-call | flops 1000000000 | bytes 3000000 | tf_op jit(solution)/shard_map/pallas_call | solution.py:148
  549.9 2.0 collective-permute-start.34
  553.4 6.6 %all-to-all-done.6.part_ref = bf16[8,64,1408]{2,1,0:T(8,128)(2,1)S(1)} async-done(((bf16[8,64,1408]{2,1,0:T(8,128)(2,1)}), bf16[8,64,1408]{2,1,0:T(8,128)(2,1)S(1)}, u32[]{:S(2)}, u32[]{:S(2)}) %all-to-all-start.6) | async-done | bytes 1441824 | tf_op jit(solution)/shard_map/all_to_all | solution.py:238
  560.0 7.2 %shard_map.252 = bf16[256,2048]{1,0:T(8,128)(2,1)} custom-call(bf16[2,1024,256]{2,1,0:T(8,128)(2,1)} %bitcast.70, bf16[2,1024,256]{2,1,0:T(8,128)(2,1)} %bitcast.71, bf16[1024,2048]{1,0:T(8,128)(2,1)} %shard_map.250.right0_ref, bf16[1024,2048]{1,0:T(8,128)(2,1)} %collective-permute-done.37.right1_ref), custom_call_target="tpu_custom_call" | custom-call | flops 10000000000 | bytes 30000000 | tf_op jit(solution)/shard_map/pallas_call | solution.py:222
  567.2 15.4 %reduce-scatter.9.cloned.1.call-done = bf16[512,768]{1,0:T(8,128)(2,1)} async-done(((bf16[2048,768]{1,0:T(8,128)(2,1)}), bf16[512,768]{1,0:T(8,128)(2,1)}) %reduce-scatter.9.cloned.1.call-update) | async-done | bytes 786448 | tf_op jit(solution)/shard_map/reduce_scatter | solution.py:847
  582.7 4.2 all-to-all-start.7
  587.7 2.4 convert_reduce_fusion
  590.3 14.9 %collective-permute-done.36 = bf16[256,2048]{1,0:T(8,128)(2,1)} collective-permute-done((bf16[256,2048]{1,0:T(8,128)(2,1)}, bf16[256,2048]{1,0:T(8,128)(2,1)}, u32[]{:S(2)}, u32[]{:S(2)}) %collective-permute-start.36) | collective-permute-done | bytes 1048608 | tf_op jit(solution)/shard_map/ppermute | solution.py:164
  606.1 2.5 shard_map.255
  608.6 3.4 shard_map.254
  613.2 3.9 fusion.10
  618.0 2.9 all-to-all-start.8
  620.9 3.4 fusion.9
  624.3 2.6 shard_map.253
  (213 shorter events, 66.3 us)
Async XLA Ops:
  7.2 109.7 %all-gather.6.cloned.1.call-start = ((), (), s32[]{:S(2)}) async-start(), calls=%async_computation.14 | async-start | bytes 1310720 | tf_op jit(solution)/shard_map/all_gather | solution.py:810
  10.9 15.9 %all-to-all-start = ((f32[32,1,960]{2,1,0:T(1,128)}), f32[32,1,960]{2,1,0:T(1,128)S(1)}, u32[]{:S(2)}, u32[]{:S(2)}) async-start(f32[32,1,960]{2,1,0:T(1,128)} %broadcast_in_dim.14), calls=%async_computation | async-start | bytes 262144 | tf_op jit(solution)/shard_map/all_to_all | solution.py:783
  18.2 25.5 %copy-start = (bf16[256,2048]{1,0:T(8,128)(2,1)S(1)}, bf16[256,2048]{1,0:T(8,128)(2,1)}, u32[]{:S(2)}) copy-start(bf16[256,2048]{1,0:T(8,128)(2,1)} %token_ref.1) | copy-start | bytes 3145732
  18.2 101.1 %all-gather.4.cloned.1.call-start = ((), (), s32[]{:S(2)}) async-start(), calls=%async_computation.13 | async-start | bytes 3932160 | tf_op jit(solution)/shard_map/all_gather | solution.py:810
  43.7 24.3 %collective-permute-start.1 = (bf16[256,2048]{1,0:T(8,128)(2,1)S(1)}, bf16[256,2048]{1,0:T(8,128)(2,1)S(1)}, u32[]{:S(2)}, u32[]{:S(2)}) collective-permute-start(bf16[256,2048]{1,0:T(8,128)(2,1)S(1)} %copy-done), channel_id=1, source_target_pairs={{0,4},{4,0},{1,5},{5,1},{2,6},{6,2},{3,7},{7,3},{8,12},{12,8},{9,1... | collective-permute-start | bytes 3145736 | tf_op jit(solution)/shard_map/ppermute | solution.py:59
  44.3 25.9 %collective-permute-start = (bf16[256,2048]{1,0:T(8,128)(2,1)S(1)}, bf16[256,2048]{1,0:T(8,128)(2,1)S(1)}, u32[]{:S(2)}, u32[]{:S(2)}) collective-permute-start(bf16[256,2048]{1,0:T(8,128)(2,1)S(1)} %copy-done), channel_id=1, source_target_pairs={{0,2},{2,0},{1,3},{3,1},{4,6},{6,4},{5,7},{7,5},{8,10},{10,8},{9,1... | collective-permute-start | bytes 3145736 | tf_op jit(solution)/shard_map/ppermute | solution.py:59
  68.9 12.9 %collective-permute-start.2 = (bf16[128,2048]{1,0:T(8,128)(2,1)}, bf16[128,2048]{1,0:T(8,128)(2,1)}, u32[]{:S(2)}, u32[]{:S(2)}) collective-permute-start(bf16[128,2048]{1,0:T(8,128)(2,1)} %slice.164), channel_id=1, source_target_pairs={{0,2},{2,0},{1,3},{3,1},{4,6},{6,4},{5,7},{7,5},{8,10},{10,8},{9,1... | collective-permute-start | bytes 1572872 | tf_op jit(solution)/shard_map/ppermute | solution.py:59
  70.3 12.8 %collective-permute-start.3 = (bf16[128,2048]{1,0:T(8,128)(2,1)S(1)}, bf16[128,2048]{1,0:T(8,128)(2,1)S(1)}, u32[]{:S(2)}, u32[]{:S(2)}) collective-permute-start(bf16[128,2048]{1,0:T(8,128)(2,1)S(1)} %slice.165), channel_id=1, source_target_pairs={{0,4},{4,0},{1,5},{5,1},{2,6},{6,2},{3,7},{7,3},{8,12},{12,8},{9,1... | collective-permute-start | bytes 1572872 | tf_op jit(solution)/shard_map/ppermute | solution.py:59
  83.9 31.6 %all-to-all-start.2 = ((bf16[8,64,2176]{2,1,0:T(8,128)(2,1)}), bf16[8,64,2176]{2,1,0:T(8,128)(2,1)S(1)}, u32[]{:S(2)}, u32[]{:S(2)}) async-start(bf16[8,64,2176]{2,1,0:T(8,128)(2,1)} %shard_map.231), calls=%async_computation.2 | async-start | bytes 4456448 | tf_op jit(solution)/shard_map/all_to_all | solution.py:238
  87.5 186.9 %all-gather.8.cloned.1.call-start = ((), (), s32[]{:S(2)}) async-start(), calls=%async_computation.15 | async-start | bytes 11141120 | tf_op jit(solution)/shard_map/all_gather | solution.py:810
  95.0 24.4 %collective-permute-start.4 = (bf16[1024,2048]{1,0:T(8,128)(2,1)}, bf16[1024,2048]{1,0:T(8,128)(2,1)}, u32[]{:S(2)}, u32[]{:S(2)}) collective-permute-start(bf16[1024,2048]{1,0:T(8,128)(2,1)} %shard_map.229.act0_ref.refs_0_), channel_id=1, source_target_pairs={{0,1},{1,0},{2,3},{3,2},{4,5},{5,4},{6,7},{7,6},{8,9},{9,8},{10,11... | collective-permute-start | bytes 12582920 | tf_op jit(solution)/shard_map/ppermute | solution.py:59
  116.8 22.3 %collective-permute-start.6 = (bf16[256,2048]{1,0:T(8,128)(2,1)}, bf16[256,2048]{1,0:T(8,128)(2,1)S(1)}, u32[]{:S(2)}, u32[]{:S(2)}) collective-permute-start(bf16[256,2048]{1,0:T(8,128)(2,1)} %all-gather.6.cloned.1.call-done.refs_0_), channel_id=1, source_target_pairs={{0,4},{4,0},{1,5},{5,1},{2,6},{6,2},{3,7},{7,3},{8,12},{12,8},{9,1... | collective-permute-start | bytes 3145736 | tf_op jit(solution)/shard_map/ppermute | solution.py:59
  117.5 23.7 %collective-permute-start.5 = (bf16[256,2048]{1,0:T(8,128)(2,1)}, bf16[256,2048]{1,0:T(8,128)(2,1)S(1)}, u32[]{:S(2)}, u32[]{:S(2)}) collective-permute-start(bf16[256,2048]{1,0:T(8,128)(2,1)} %all-gather.6.cloned.1.call-done.refs_0_), channel_id=1, source_target_pairs={{0,2},{2,0},{1,3},{3,1},{4,6},{6,4},{5,7},{7,5},{8,10},{10,8},{9,1... | collective-permute-start | bytes 3145736 | tf_op jit(solution)/shard_map/ppermute | solution.py:59
  139.2 24.8 %copy-start.6 = (bf16[256,2048]{1,0:T(8,128)(2,1)}, bf16[256,2048]{1,0:T(8,128)(2,1)S(1)}, u32[]{:S(2)}) copy-start(bf16[256,2048]{1,0:T(8,128)(2,1)S(1)} %collective-permute-done.6.refs_2_) | copy-start | bytes 3145732
  141.1 22.8 %copy-start.7 = (bf16[256,2048]{1,0:T(8,128)(2,1)}, bf16[256,2048]{1,0:T(8,128)(2,1)S(1)}, u32[]{:S(2)}) copy-start(bf16[256,2048]{1,0:T(8,128)(2,1)S(1)} %collective-permute-done.5.refs_1_) | copy-start | bytes 3145732
  142.8 21.1 %collective-permute-start.7 = (bf16[128,2048]{1,0:T(8,128)(2,1)}, bf16[128,2048]{1,0:T(8,128)(2,1)S(1)}, u32[]{:S(2)}, u32[]{:S(2)}) collective-permute-start(bf16[128,2048]{1,0:T(8,128)(2,1)} %slice.131), channel_id=1, source_target_pairs={{0,2},{2,0},{1,3},{3,1},{4,6},{6,4},{5,7},{7,5},{8,10},{10,8},{9,1... | collective-permute-start | bytes 1572872 | tf_op jit(solution)/shard_map/ppermute | solution.py:59
  144.6 19.4 %collective-permute-start.8 = (bf16[128,2048]{1,0:T(8,128)(2,1)}, bf16[128,2048]{1,0:T(8,128)(2,1)S(1)}, u32[]{:S(2)}, u32[]{:S(2)}) collective-permute-start(bf16[128,2048]{1,0:T(8,128)(2,1)} %slice.132), channel_id=1, source_target_pairs={{0,4},{4,0},{1,5},{5,1},{2,6},{6,2},{3,7},{7,3},{8,12},{12,8},{9,1... | collective-permute-start | bytes 1572872 | tf_op jit(solution)/shard_map/ppermute | solution.py:59
  169.7 18.9 %collective-permute-start.9 = (bf16[1024,2048]{1,0:T(8,128)(2,1)}, bf16[1024,2048]{1,0:T(8,128)(2,1)}, u32[]{:S(2)}, u32[]{:S(2)}) collective-permute-start(bf16[1024,2048]{1,0:T(8,128)(2,1)} %shard_map.234.w0_ref), channel_id=1, source_target_pairs={{0,1},{1,0},{2,3},{3,2},{4,5},{5,4},{6,7},{7,6},{8,9},{9,8},{10,11... | collective-permute-start | bytes 12582920 | tf_op jit(solution)/shard_map/ppermute | solution.py:59
  169.7 18.9 %all-to-all-start.3 = ((bf16[8,256,256]{2,1,0:T(8,128)(2,1)}), bf16[8,256,256]{2,1,0:T(8,128)(2,1)S(1)}, u32[]{:S(2)}, u32[]{:S(2)}) async-start(bf16[8,256,256]{2,1,0:T(8,128)(2,1)} %bitcast.23), calls=%async_computation.3 | async-start | bytes 2097152 | tf_op jit(solution)/shard_map/all_to_all | solution.py:238
  173.2 220.2 %reduce-scatter.5.cloned.1.call-start = ((), (), s32[]{:S(2)}) async-start(), calls=%async_computation.16 | async-start | bytes 3932160 | tf_op jit(solution)/shard_map/reduce_scatter | solution.py:847
  201.4 22.3 %collective-permute-start.11 = (bf16[256,2048]{1,0:T(8,128)(2,1)}, bf16[256,2048]{1,0:T(8,128)(2,1)S(1)}, u32[]{:S(2)}, u32[]{:S(2)}) collective-permute-start(bf16[256,2048]{1,0:T(8,128)(2,1)} %get-tuple-element.111.refs_0_), channel_id=1, source_target_pairs={{0,4},{4,0},{1,5},{5,1},{2,6},{6,2},{3,7},{7,3},{8,12},{12,8},{9,1... | collective-permute-start | bytes 3145736 | tf_op jit(solution)/shard_map/ppermute | solution.py:59
  201.9 25.5 %collective-permute-start.10 = (bf16[256,2048]{1,0:T(8,128)(2,1)}, bf16[256,2048]{1,0:T(8,128)(2,1)S(1)}, u32[]{:S(2)}, u32[]{:S(2)}) collective-permute-start(bf16[256,2048]{1,0:T(8,128)(2,1)} %get-tuple-element.111.refs_0_), channel_id=1, source_target_pairs={{0,2},{2,0},{1,3},{3,1},{4,6},{6,4},{5,7},{7,5},{8,10},{10,8},{9,1... | collective-permute-start | bytes 3145736 | tf_op jit(solution)/shard_map/ppermute | solution.py:59
  223.7 16.9 %copy-start.12 = (bf16[256,2048]{1,0:T(8,128)(2,1)}, bf16[256,2048]{1,0:T(8,128)(2,1)S(1)}, u32[]{:S(2)}) copy-start(bf16[256,2048]{1,0:T(8,128)(2,1)S(1)} %collective-permute-done.11.refs_2_) | copy-start | bytes 3145732
  223.7 15.3 %collective-permute-start.12 = (bf16[128,2048]{1,0:T(8,128)(2,1)S(1)}, bf16[128,2048]{1,0:T(8,128)(2,1)S(1)}, u32[]{:S(2)}, u32[]{:S(2)}) collective-permute-start(bf16[128,2048]{1,0:T(8,128)(2,1)S(1)} %slice.173), channel_id=1, source_target_pairs={{0,2},{2,0},{1,3},{3,1},{4,6},{6,4},{5,7},{7,5},{8,10},{10,8},{9,1... | collective-permute-start | bytes 1572872 | tf_op jit(solution)/shard_map/ppermute | solution.py:59
  227.5 18.7 %copy-start.18 = (bf16[256,2048]{1,0:T(8,128)(2,1)S(1)}, bf16[256,2048]{1,0:T(8,128)(2,1)}, u32[]{:S(2)}) copy-start(bf16[256,2048]{1,0:T(8,128)(2,1)} %grad_ref.1) | copy-start | bytes 3145732
  227.5 13.1 %collective-permute-start.13 = (bf16[128,2048]{1,0:T(8,128)(2,1)S(1)}, bf16[128,2048]{1,0:T(8,128)(2,1)S(1)}, u32[]{:S(2)}, u32[]{:S(2)}) collective-permute-start(bf16[128,2048]{1,0:T(8,128)(2,1)S(1)} %slice.174), channel_id=1, source_target_pairs={{0,4},{4,0},{1,5},{5,1},{2,6},{6,2},{3,7},{7,3},{8,12},{12,8},{9,1... | collective-permute-start | bytes 1572872 | tf_op jit(solution)/shard_map/ppermute | solution.py:59
  246.2 28.2 %collective-permute-start.14 = (bf16[1024,2048]{1,0:T(8,128)(2,1)}, bf16[1024,2048]{1,0:T(8,128)(2,1)}, u32[]{:S(2)}, u32[]{:S(2)}) collective-permute-start(bf16[1024,2048]{1,0:T(8,128)(2,1)} %shard_map.236.act0_ref.refs_0_), channel_id=1, source_target_pairs={{0,1},{1,0},{2,3},{3,2},{4,5},{5,4},{6,7},{7,6},{8,9},{9,8},{10,11... | collective-permute-start | bytes 12582920 | tf_op jit(solution)/shard_map/ppermute | solution.py:59
  246.2 25.6 %collective-permute-start.16 = (bf16[256,2048]{1,0:T(8,128)(2,1)S(1)}, bf16[256,2048]{1,0:T(8,128)(2,1)S(1)}, u32[]{:S(2)}, u32[]{:S(2)}) collective-permute-start(bf16[256,2048]{1,0:T(8,128)(2,1)S(1)} %copy-done.18), channel_id=1, source_target_pairs={{0,4},{4,0},{1,5},{5,1},{2,6},{6,2},{3,7},{7,3},{8,12},{12,8},{9,1... | collective-permute-start | bytes 3145736 | tf_op jit(solution)/shard_map/ppermute | solution.py:59
  246.6 27.0 %collective-permute-start.15 = (bf16[256,2048]{1,0:T(8,128)(2,1)S(1)}, bf16[256,2048]{1,0:T(8,128)(2,1)S(1)}, u32[]{:S(2)}, u32[]{:S(2)}) collective-permute-start(bf16[256,2048]{1,0:T(8,128)(2,1)S(1)} %copy-done.18), channel_id=1, source_target_pairs={{0,2},{2,0},{1,3},{3,1},{4,6},{6,4},{5,7},{7,5},{8,10},{10,8},{9,1... | collective-permute-start | bytes 3145736 | tf_op jit(solution)/shard_map/ppermute | solution.py:59
  271.8 22.7 %copy-start.10 = (bf16[256,2048]{1,0:T(8,128)(2,1)}, bf16[256,2048]{1,0:T(8,128)(2,1)S(1)}, u32[]{:S(2)}) copy-start(bf16[256,2048]{1,0:T(8,128)(2,1)S(1)} %collective-permute-done.16.refs_2_) | copy-start | bytes 3145732
  272.7 21.8 %collective-permute-start.17 = (bf16[128,2048]{1,0:T(8,128)(2,1)}, bf16[128,2048]{1,0:T(8,128)(2,1)}, u32[]{:S(2)}, u32[]{:S(2)}) collective-permute-start(bf16[128,2048]{1,0:T(8,128)(2,1)} %slice.175), channel_id=1, source_target_pairs={{0,2},{2,0},{1,3},{3,1},{4,6},{6,4},{5,7},{7,5},{8,10},{10,8},{9,1... | collective-permute-start | bytes 1572872 | tf_op jit(solution)/shard_map/ppermute | solution.py:59
  273.6 20.9 %copy-start.11 = (bf16[256,2048]{1,0:T(8,128)(2,1)}, bf16[256,2048]{1,0:T(8,128)(2,1)S(1)}, u32[]{:S(2)}) copy-start(bf16[256,2048]{1,0:T(8,128)(2,1)S(1)} %collective-permute-done.15.refs_1_) | copy-start | bytes 3145732
  273.6 20.8 %collective-permute-start.18 = (bf16[128,2048]{1,0:T(8,128)(2,1)S(1)}, bf16[128,2048]{1,0:T(8,128)(2,1)S(1)}, u32[]{:S(2)}, u32[]{:S(2)}) collective-permute-start(bf16[128,2048]{1,0:T(8,128)(2,1)S(1)} %slice.176), channel_id=1, source_target_pairs={{0,4},{4,0},{1,5},{5,1},{2,6},{6,2},{3,7},{7,3},{8,12},{12,8},{9,1... | collective-permute-start | bytes 1572872 | tf_op jit(solution)/shard_map/ppermute | solution.py:59
  300.0 7.6 %collective-permute-start.19 = (bf16[1024,2048]{1,0:T(8,128)(2,1)}, bf16[1024,2048]{1,0:T(8,128)(2,1)S(1)}, u32[]{:S(2)}, u32[]{:S(2)}) collective-permute-start(bf16[1024,2048]{1,0:T(8,128)(2,1)} %shard_map.238.refs_0_.grad0_ref), channel_id=1, source_target_pairs={{0,1},{1,0},{2,3},{3,2},{4,5},{5,4},{6,7},{7,6},{8,9},{9,8},{10,11... | collective-permute-start | bytes 12582920 | tf_op jit(solution)/shard_map/ppermute | solution.py:59
  307.2 13.3 %collective-permute-start.20 = (bf16[1024,2048]{1,0:T(8,128)(2,1)}, bf16[1024,2048]{1,0:T(8,128)(2,1)}, u32[]{:S(2)}, u32[]{:S(2)}) collective-permute-start(bf16[1024,2048]{1,0:T(8,128)(2,1)} %shard_map.240), channel_id=1, source_target_pairs={{0,1},{1,0},{2,3},{3,2},{4,5},{5,4},{6,7},{7,6},{8,9},{9,8},{10,11... | collective-permute-start | bytes 12582920 | tf_op jit(solution)/shard_map/ppermute | solution.py:59
  332.0 18.5 %collective-permute-start.22 = (bf16[128,2048]{1,0:T(8,128)(2,1)S(1)}, bf16[128,2048]{1,0:T(8,128)(2,1)}, u32[]{:S(2)}, u32[]{:S(2)}) collective-permute-start(bf16[128,2048]{1,0:T(8,128)(2,1)S(1)} %get-tuple-element.191), channel_id=1, source_target_pairs={{0,2},{2,0},{1,3},{3,1},{4,6},{6,4},{5,7},{7,5},{8,10},{10,8},{9,1... | collective-permute-start | bytes 1572872 | tf_op jit(solution)/shard_map/ppermute | solution.py:59
  333.2 202.9 %reduce-scatter.7.cloned.1.call-start = ((), (), s32[]{:S(2)}) async-start(), calls=%async_computation.17 | async-start | bytes 7208960 | tf_op jit(solution)/shard_map/reduce_scatter | solution.py:847
  334.9 17.8 %collective-permute-start.21 = (bf16[128,2048]{1,0:T(8,128)(2,1)S(1)}, bf16[128,2048]{1,0:T(8,128)(2,1)S(1)}, u32[]{:S(2)}, u32[]{:S(2)}) collective-permute-start(bf16[128,2048]{1,0:T(8,128)(2,1)S(1)} %get-tuple-element.192), channel_id=1, source_target_pairs={{0,4},{4,0},{1,5},{5,1},{2,6},{6,2},{3,7},{7,3},{8,12},{12,8},{9,1... | collective-permute-start | bytes 1572872 | tf_op jit(solution)/shard_map/ppermute | solution.py:59
  336.4 14.1 %copy-start.17 = (f32[256,2048]{1,0:T(8,128)S(1)}, f32[256,2048]{1,0:T(8,128)}, u32[]{:S(2)}) copy-start(f32[256,2048]{1,0:T(8,128)} %get-tuple-element.123) | copy-start | bytes 6291460
  365.3 7.4 %collective-permute-start.25 = (bf16[1024,2048]{1,0:T(8,128)(2,1)}, bf16[1024,2048]{1,0:T(8,128)(2,1)S(1)}, u32[]{:S(2)}, u32[]{:S(2)}) collective-permute-start(bf16[1024,2048]{1,0:T(8,128)(2,1)} %shard_map.243), channel_id=1, source_target_pairs={{0,1},{1,0},{2,3},{3,2},{4,5},{5,4},{6,7},{7,6},{8,9},{9,8},{10,11... | collective-permute-start | bytes 12582920 | tf_op jit(solution)/shard_map/ppermute | solution.py:59
  365.4 46.4 %collective-permute-start.23 = (bf16[256,2048]{1,0:T(8,128)(2,1)}, bf16[256,2048]{1,0:T(8,128)(2,1)S(1)}, u32[]{:S(2)}, u32[]{:S(2)}) collective-permute-start(bf16[256,2048]{1,0:T(8,128)(2,1)} %pad_maximum_fusion), channel_id=1, source_target_pairs={{0,2},{2,0},{1,3},{3,1},{4,6},{6,4},{5,7},{7,5},{8,10},{10,8},{9,1... | collective-permute-start | bytes 3145736 | tf_op jit(solution)/shard_map/ppermute | solution.py:59
  366.2 45.6 %collective-permute-start.24 = (bf16[256,2048]{1,0:T(8,128)(2,1)}, bf16[256,2048]{1,0:T(8,128)(2,1)}, u32[]{:S(2)}, u32[]{:S(2)}) collective-permute-start(bf16[256,2048]{1,0:T(8,128)(2,1)} %pad_maximum_fusion.1), channel_id=1, source_target_pairs={{0,4},{4,0},{1,5},{5,1},{2,6},{6,2},{3,7},{7,3},{8,12},{12,8},{9,1... | collective-permute-start | bytes 3145736 | tf_op jit(solution)/shard_map/ppermute | solution.py:59
  388.0 28.8 %collective-permute-start.26 = (bf16[256,2048]{1,0:T(8,128)(2,1)}, bf16[256,2048]{1,0:T(8,128)(2,1)}, u32[]{:S(2)}, u32[]{:S(2)}) collective-permute-start(bf16[256,2048]{1,0:T(8,128)(2,1)} %get-tuple-element.138), channel_id=1, source_target_pairs={{0,2},{2,0},{1,3},{3,1},{4,6},{6,4},{5,7},{7,5},{8,10},{10,8},{9,1... | collective-permute-start | bytes 3145736 | tf_op jit(solution)/shard_map/ppermute | solution.py:59
  388.8 47.9 %collective-permute-start.27 = (bf16[256,2048]{1,0:T(8,128)(2,1)}, bf16[256,2048]{1,0:T(8,128)(2,1)}, u32[]{:S(2)}, u32[]{:S(2)}) collective-permute-start(bf16[256,2048]{1,0:T(8,128)(2,1)} %get-tuple-element.139), channel_id=1, source_target_pairs={{0,4},{4,0},{1,5},{5,1},{2,6},{6,2},{3,7},{7,3},{8,12},{12,8},{9,1... | collective-permute-start | bytes 3145736 | tf_op jit(solution)/shard_map/ppermute | solution.py:59
  389.1 47.6 %collective-permute-start.28 = (bf16[256,2048]{1,0:T(8,128)(2,1)}, bf16[256,2048]{1,0:T(8,128)(2,1)}, u32[]{:S(2)}, u32[]{:S(2)}) collective-permute-start(bf16[256,2048]{1,0:T(8,128)(2,1)} %get-tuple-element.132), channel_id=1, source_target_pairs={{0,6},{2,4},{4,2},{6,0},{1,7},{3,5},{5,3},{7,1},{8,14},{10,12},{12... | collective-permute-start | bytes 3145736 | tf_op jit(solution)/shard_map/ppermute | solution.py:164
  436.7 18.9 %all-to-all-start.4 = ((bf16[8,64,704]{2,1,0:T(8,128)(2,1)}), bf16[8,64,704]{2,1,0:T(8,128)(2,1)S(1)}, u32[]{:S(2)}, u32[]{:S(2)}) async-start(bf16[8,64,704]{2,1,0:T(8,128)(2,1)} %bitcast.56), calls=%async_computation.5 | async-start | bytes 1572864 | tf_op jit(solution)/shard_map/all_to_all | solution.py:238
  440.3 142.4 %reduce-scatter.9.cloned.1.call-start = ((), (), s32[]{:S(2)}) async-start(), calls=%async_computation.18 | async-start | bytes 3932160 | tf_op jit(solution)/shard_map/reduce_scatter | solution.py:847
  455.7 19.8 %copy-start.29 = (bf16[256,2048]{1,0:T(8,128)(2,1)S(1)}, bf16[256,2048]{1,0:T(8,128)(2,1)}, u32[]{:S(2)}) copy-start(bf16[256,2048]{1,0:T(8,128)(2,1)} %get-tuple-element.155.refs_0_) | copy-start | bytes 3145732
  475.4 26.3 %collective-permute-start.30 = (bf16[256,2048]{1,0:T(8,128)(2,1)S(1)}, bf16[256,2048]{1,0:T(8,128)(2,1)S(1)}, u32[]{:S(2)}, u32[]{:S(2)}) collective-permute-start(bf16[256,2048]{1,0:T(8,128)(2,1)S(1)} %copy-done.29), channel_id=1, source_target_pairs={{0,4},{4,0},{1,5},{5,1},{2,6},{6,2},{3,7},{7,3},{8,12},{12,8},{9,1... | collective-permute-start | bytes 3145736 | tf_op jit(solution)/shard_map/ppermute | solution.py:59
  476.0 25.8 %collective-permute-start.29 = (bf16[256,2048]{1,0:T(8,128)(2,1)S(1)}, bf16[256,2048]{1,0:T(8,128)(2,1)S(1)}, u32[]{:S(2)}, u32[]{:S(2)}) collective-permute-start(bf16[256,2048]{1,0:T(8,128)(2,1)S(1)} %copy-done.29), channel_id=1, source_target_pairs={{0,2},{2,0},{1,3},{3,1},{4,6},{6,4},{5,7},{7,5},{8,10},{10,8},{9,1... | collective-permute-start | bytes 3145736 | tf_op jit(solution)/shard_map/ppermute | solution.py:59
  501.7 14.1 %copy-start.25 = (bf16[256,2048]{1,0:T(8,128)(2,1)}, bf16[256,2048]{1,0:T(8,128)(2,1)S(1)}, u32[]{:S(2)}) copy-start(bf16[256,2048]{1,0:T(8,128)(2,1)S(1)} %collective-permute-done.30.refs_2_) | copy-start | bytes 3145732
  501.9 14.0 %collective-permute-start.32 = (bf16[128,2048]{1,0:T(8,128)(2,1)S(1)}, bf16[128,2048]{1,0:T(8,128)(2,1)S(1)}, u32[]{:S(2)}, u32[]{:S(2)}) collective-permute-start(bf16[128,2048]{1,0:T(8,128)(2,1)S(1)} %slice.148), channel_id=1, source_target_pairs={{0,4},{4,0},{1,5},{5,1},{2,6},{6,2},{3,7},{7,3},{8,12},{12,8},{9,1... | collective-permute-start | bytes 1572872 | tf_op jit(solution)/shard_map/ppermute | solution.py:59
  503.4 13.0 %collective-permute-start.31 = (bf16[128,2048]{1,0:T(8,128)(2,1)S(1)}, bf16[128,2048]{1,0:T(8,128)(2,1)}, u32[]{:S(2)}, u32[]{:S(2)}) collective-permute-start(bf16[128,2048]{1,0:T(8,128)(2,1)S(1)} %slice.147), channel_id=1, source_target_pairs={{0,2},{2,0},{1,3},{3,1},{4,6},{6,4},{5,7},{7,5},{8,10},{10,8},{9,1... | collective-permute-start | bytes 1572872 | tf_op jit(solution)/shard_map/ppermute | solution.py:59
  523.6 7.5 %collective-permute-start.33 = (bf16[1024,2048]{1,0:T(8,128)(2,1)}, bf16[1024,2048]{1,0:T(8,128)(2,1)}, u32[]{:S(2)}, u32[]{:S(2)}) collective-permute-start(bf16[1024,2048]{1,0:T(8,128)(2,1)} %shard_map.249), channel_id=1, source_target_pairs={{0,1},{1,0},{2,3},{3,2},{4,5},{5,4},{6,7},{7,6},{8,9},{9,8},{10,11... | collective-permute-start | bytes 12582920 | tf_op jit(solution)/shard_map/ppermute | solution.py:59
  535.9 17.5 %collective-permute-start.37 = (bf16[1024,2048]{1,0:T(8,128)(2,1)}, bf16[1024,2048]{1,0:T(8,128)(2,1)}, u32[]{:S(2)}, u32[]{:S(2)}) collective-permute-start(bf16[1024,2048]{1,0:T(8,128)(2,1)} %shard_map.250.right0_ref), channel_id=1, source_target_pairs={{0,1},{1,0},{2,3},{3,2},{4,5},{5,4},{6,7},{7,6},{8,9},{9,8},{10,11... | collective-permute-start | bytes 12582920 | tf_op jit(solution)/shard_map/ppermute | solution.py:59
  536.0 24.0 %all-to-all-start.6 = ((bf16[8,64,1408]{2,1,0:T(8,128)(2,1)}), bf16[8,64,1408]{2,1,0:T(8,128)(2,1)S(1)}, u32[]{:S(2)}, u32[]{:S(2)}) async-start(bf16[8,64,1408]{2,1,0:T(8,128)(2,1)} %bitcast.54), calls=%async_computation.8 | async-start | bytes 2883584 | tf_op jit(solution)/shard_map/all_to_all | solution.py:238
  549.9 40.3 %collective-permute-start.34 = (bf16[256,2048]{1,0:T(8,128)(2,1)}, bf16[256,2048]{1,0:T(8,128)(2,1)}, u32[]{:S(2)}, u32[]{:S(2)}) collective-permute-start(bf16[256,2048]{1,0:T(8,128)(2,1)} %get-tuple-element.162), channel_id=1, source_target_pairs={{0,2},{2,0},{1,3},{3,1},{4,6},{6,4},{5,7},{7,5},{8,10},{10,8},{9,1... | collective-permute-start | bytes 3145736 | tf_op jit(solution)/shard_map/ppermute | solution.py:59
  551.9 38.4 %collective-permute-start.35 = (bf16[256,2048]{1,0:T(8,128)(2,1)}, bf16[256,2048]{1,0:T(8,128)(2,1)}, u32[]{:S(2)}, u32[]{:S(2)}) collective-permute-start(bf16[256,2048]{1,0:T(8,128)(2,1)} %get-tuple-element.163), channel_id=1, source_target_pairs={{0,4},{4,0},{1,5},{5,1},{2,6},{6,2},{3,7},{7,3},{8,12},{12,8},{9,1... | collective-permute-start | bytes 3145736 | tf_op jit(solution)/shard_map/ppermute | solution.py:59
  553.4 51.8 %collective-permute-start.36 = (bf16[256,2048]{1,0:T(8,128)(2,1)}, bf16[256,2048]{1,0:T(8,128)(2,1)}, u32[]{:S(2)}, u32[]{:S(2)}) collective-permute-start(bf16[256,2048]{1,0:T(8,128)(2,1)} %get-tuple-element.164), channel_id=1, source_target_pairs={{0,6},{2,4},{4,2},{6,0},{1,7},{3,5},{5,3},{7,1},{8,14},{10,12},{12... | collective-permute-start | bytes 3145736 | tf_op jit(solution)/shard_map/ppermute | solution.py:164
  567.2 20.2 %copy-start.27 = (f32[1,32,64]{2,0,1:T(1,128)S(1)}, f32[1,32,64]{2,0,1:T(1,128)}, u32[]{:S(2)}) copy-start(f32[1,32,64]{2,0,1:T(1,128)} %get-tuple-element.193) | copy-start | bytes 24580
  567.2 20.2 %copy-start.28 = (f32[2,2048]{1,0:T(2,128)S(1)}, f32[2,2048]{1,0:T(2,128)}, u32[]{:S(2)}) copy-start(f32[2,2048]{1,0:T(2,128)} %get-tuple-element.178) | copy-start | bytes 49156
  582.7 30.5 %all-to-all-start.7 = ((bf16[8,64,768]{2,1,0:T(8,128)(2,1)}), bf16[8,64,768]{2,1,0:T(8,128)(2,1)}, u32[]{:S(2)}, u32[]{:S(2)}) async-start(bf16[8,64,768]{2,1,0:T(8,128)(2,1)} %bitcast.57), calls=%async_computation.10 | async-start | bytes 1572864 | tf_op jit(solution)/shard_map/all_to_all | solution.py:238
  586.9 42.7 %reduce-scatter.11.cloned.1.call-start = ((), (), s32[]{:S(2)}) async-start(), calls=%async_computation.19 | async-start | bytes 1310720 | tf_op jit(solution)/shard_map/reduce_scatter | solution.py:847
  618.0 10.3 %all-to-all-start.8 = ((f32[32,1,448]{2,1,0:T(1,128)}), f32[32,1,448]{2,1,0:T(1,128)S(1)}, u32[]{:S(2)}, u32[]{:S(2)}) async-start(f32[32,1,448]{2,1,0:T(1,128)} %all_to_all.44), calls=%async_computation.11 | async-start | bytes 131072 | tf_op jit(solution)/shard_map/all_to_all | solution.py:909
  (19 other events, 61.7 us)
Sparse Core Ops, SparseCore 0:
  9.6 32.4 all-gather.5
  43.8 62.3 all-gather.3
  116.9 157.0 all-gather.7
  333.3 60.1 reduce-scatter.4
  411.9 102.2 reduce-scatter.6
  523.8 58.8 reduce-scatter.8
  590.0 27.5 reduce-scatter.10
